TPU v7x, 32 devices: a whole 2x2x4 slice. The times are simulated.
32 devices in a mesh: band: 4 (over y, core), row: 8 (over z, x).
Axes of the slice: x: 2, y: 2, z: 4, core: 2. Of those that a mesh axis runs over, the one named last changes fastest.
Arguments:
- observed: bfloat16 [224, 256, 680], P('band', 'row'), may hold values from -60 to 60
- row_taps: float32 [224, 25], P('band'), may hold values from 0 to 0.08
- col_taps: float32 [224, 25], P('band'), may hold values from 0 to 0.08
- spectral_basis: bfloat16 [224, 32], replicated, may hold values from -0.375 to 0.375
- ridge_weights: float32 [32], replicated, may hold values from 0.05 to 0.5
Outputs:
- coefficients: float32 [32, 256, 680], P(None, 'row', 'band')
- residual: float32 [32, 256, 680], P(None, 'row', 'band')
All inputs are finite; a program needn't handle non-finite values.
Results may differ from a plain program's by a relative error of at most 0.01.
Values may be sent and summed in bfloat16 or wider, within the bound.
No kernel may reach another device: no remote copies, remote signals or barrier semaphores. Data moves between devices by JAX's collectives and lax.ppermute only.
A program may use at most 64 MiB of HBM per device.

v0:
```python
import jax
import jax.numpy as jnp
from jax import lax
from jax.sharding import PartitionSpec as P

ITERS = 2


def extended(cells, sides, width):
    for axis, dim in sides:
        count = lax.axis_size(axis)
        ends = count - 1
        head = lax.slice_in_dim(cells, 0, width, axis=dim)
        tail = lax.slice_in_dim(cells, cells.shape[dim] - width, cells.shape[dim], axis=dim)
        cells = jnp.concatenate(
            [
                lax.ppermute(tail, axis, [(i, (i + 1) % count) for i in range(ends)]),
                cells,
                lax.ppermute(head, axis, [((i + 1) % count, i) for i in range(ends)]),
            ],
            axis=dim,
        )
    return cells


def pass_rows(padded, kernel):
    length = padded.shape[1] - kernel.shape[1] + 1
    running = jnp.zeros((padded.shape[0], length, padded.shape[2]), jnp.float32)
    for offset in range(kernel.shape[1]):
        running = running + kernel[:, offset, None, None] * padded[
            :, offset : offset + length, :
        ].astype(jnp.float32)
    return running


def pass_cols(field, kernel):
    radius = (kernel.shape[1] - 1) // 2
    columns = field.shape[2]
    padded = jnp.pad(field, ((0, 0), (0, 0), (radius, radius)))
    running = jnp.zeros(field.shape, jnp.float32)
    for offset in range(kernel.shape[1]):
        running = running + kernel[:, offset, None, None] * padded[:, :, offset : offset + columns]
    return running


def two_products(residual, mapped):
    return lax.psum((jnp.sum(residual * residual), jnp.sum(residual * mapped)), ("band", "row"))


def local(observed, row_taps, col_taps, spectral_basis, ridge_weights):
    radius = (row_taps.shape[1] - 1) // 2
    row_flip = row_taps[:, ::-1]
    col_flip = col_taps[:, ::-1]
    basis_wide = spectral_basis.astype(jnp.float32)

    def project(gathered):
        return jnp.einsum(
            "bk,brc->krc", spectral_basis, gathered, preferred_element_type=jnp.float32
        )

    def to_subspace(band_field):
        return project(lax.all_to_all(band_field, "band", split_axis=2, concat_axis=0, tiled=True))

    def normal_map(direction):
        spectra = jnp.einsum(
            "bk,krc->brc", basis_wide, direction, precision=lax.Precision.HIGHEST
        ).astype(jnp.bfloat16)
        banded = lax.all_to_all(spectra, "band", split_axis=0, concat_axis=2, tiled=True)
        padded = extended(banded, (("row", 1),), radius)
        blurred = pass_cols(pass_rows(padded, row_taps), col_taps).astype(jnp.bfloat16)
        blurred = extended(blurred, (("row", 1),), radius)
        returned = pass_cols(pass_rows(blurred, row_flip), col_flip).astype(jnp.bfloat16)
        return to_subspace(returned) + ridge_weights[:, None, None] * direction

    padded_obs = extended(observed, (("row", 1),), radius)
    adjoint_obs = pass_cols(pass_rows(padded_obs, row_flip), col_flip).astype(jnp.bfloat16)
    rhs = to_subspace(adjoint_obs)
    solution = jnp.zeros_like(rhs)
    residual = rhs
    direction = rhs
    along = normal_map(residual)
    norm_now, product = two_products(residual, along)
    alpha = norm_now / product
    for iteration in range(ITERS):
        solution = solution + alpha * direction
        residual = residual - alpha * along
        if iteration + 1 < ITERS:
            mapped = normal_map(residual)
            norm_next, product = two_products(residual, mapped)
            ratio = norm_next / norm_now
            alpha = norm_next / (product - ratio * norm_next / alpha)
            direction = residual + ratio * direction
            along = mapped + ratio * along
            norm_now = norm_next
    return (solution, residual)


def solution(mesh):
    in_specs = (P("band", "row", None), P("band", None), P("band", None), P(), P())
    out_specs = (P(None, "row", "band"), P(None, "row", "band"))
    return jax.shard_map(local, mesh=mesh, in_specs=in_specs, out_specs=out_specs, check_vma=False)
```

profile of v0, /device:TPU:0, one launch (start us, length us, event | category | flops | bytes accessed | tf_op | source)
XLA Modules:
  0.0 1140.8 jit_solution(7169108547794464120)
XLA Ops:
  0.7 2.4 fusion.163
  3.4 4.9 collective-permute-start
  8.7 1.3 collective-permute-start.1
  10.5 0.7 slice_bitcast_fusion.49
  11.1 41.3 %collective-permute-done = bf16[56,12,680]{2,0,1:T(8,128)(2,1)S(1)} collective-permute-done((bf16[56,12,680]{2,0,1:T(8,128)(2,1)S(1)}, bf16[56,12,680]{2,0,1:T(8,128)(2,1)S(1)}, u32[]{:S(2)}, u32[]{:S(2)}) %collective-permute-start) | collective-permute-done | bytes 913952 | tf_op jit(solution)/shard_map/ppermute | solution.py:17
  52.9 22.1 %multiply_add_fusion.4 = f32[56,32,680]{2,1,0:T(8,128)S(1)} fusion(bf16[56,32,680]{2,1,0:T(8,128)(2,1)S(1)} %copy-done.4, bf16[56,12,680]{2,1,0:T(8,128)(2,1)S(1)} %copy.72, bf16[56,44,680]{2,1,0:T(8,128)(2,1)S(1)} %copy_dynamic-update-slice_fusion.2, f32[56]{0:T(128)S(1)} %get-tuple-element.80, f32[56]{0:T(128)S(1)} %get-tuple-element.81, ...), kind=kLoop, calls=%fused_computation.278 | loop fusion | flops 134041600 | bytes 37476320 | tf_op jit(solution)/shard_map/add | solution.py:30
  75.2 40.2 %add_convert_fusion.4 = bf16[56,32,680]{2,1,0:T(8,128)(2,1)S(1)} fusion(f32[56,32,680]{2,1,0:T(8,128)S(1)} %multiply_add_fusion.4, f32[56]{0:T(128)S(1)} %get-tuple-element.55, f32[56]{0:T(128)S(1)} %get-tuple-element.56, f32[56]{0:T(128)S(1)} %get-tuple-element.33, f32[56]{0:T(128)S(1)} %get-tuple-element.34, f32[56]{0:T(128)S(1)} %get-tuple-element.35, ...), kind=kLoop, calls=%fused_computation.254 | loop fusion | flops 60928000 | bytes 7316960 | tf_op jit(solution)/shard_map/convert_element_type | solution.py:76
  115.4 10.2 copy.75
  125.6 12.5 %reshape.106 = bf16[4,2,152320]{2,1,0:T(2,128)(2,1)S(1)} reshape(bf16[680,32,56]{2,1,0:T(8,128)(2,1)} %bitcast.161) | data formatting | bytes 4874240
  138.1 32.9 %all_to_all.90 = bf16[4,2,152320]{2,1,0:T(2,128)(2,1)} all-to-all(bf16[4,2,152320]{2,1,0:T(2,128)(2,1)S(1)} %reshape.106), channel_id=1, replica_groups=mesh['band'=4,'row'=8] {'band'}, dimensions={0} | all-to-all | bytes 4874240 | tf_op jit(solution)/shard_map/all_to_all | solution.py:62
  171.0 13.8 %reshape.107 = bf16[680,32,56]{2,1,0:T(8,128)(2,1)} reshape(bf16[4,2,152320]{2,1,0:T(2,128)(2,1)} %all_to_all.90) | data formatting | bytes 4874240
  184.8 8.3 copy.108
  193.1 2.7 convolution_bitcast_fusion.2
  195.9 1.0 copy-done.1
  196.8 2.6 convert_bitcast_fusion.1
  199.4 4.8 copy.78
  204.2 46.7 %all_to_all.91 = bf16[224,32,170]{2,1,0:T(8,128)(2,1)S(1)} all-to-all(bf16[224,32,170]{2,1,0:T(8,128)(2,1)} %copy.78), channel_id=1, replica_groups=mesh['band'=4,'row'=8] {'band'}, dimensions={0} | all-to-all | bytes 4874240 | tf_op jit(solution)/shard_map/all_to_all | solution.py:68
  250.9 8.5 copy.79
  259.4 6.3 all_to_all.72
  266.5 4.4 collective-permute-start.2
  271.5 1.5 collective-permute-start.3
  273.2 41.5 %collective-permute-done.2 = bf16[56,12,680]{2,0,1:T(8,128)(2,1)S(1)} collective-permute-done((bf16[56,12,680]{2,0,1:T(8,128)(2,1)S(1)}, bf16[56,12,680]{2,0,1:T(8,128)(2,1)S(1)}, u32[]{:S(2)}, u32[]{:S(2)}) %collective-permute-start.2) | collective-permute-done | bytes 913952 | tf_op jit(solution)/shard_map/ppermute | solution.py:17
  315.5 24.4 %multiply_add_fusion.3 = f32[56,32,680]{2,1,0:T(8,128)} fusion(bf16[56,32,680]{2,1,0:T(8,128)(2,1)S(1)} %all_to_all.72, bf16[56,12,680]{2,1,0:T(8,128)(2,1)S(1)} %copy.81, bf16[56,44,680]{2,1,0:T(8,128)(2,1)S(1)} %copy_dynamic-update-slice_fusion.1, f32[56]{0:T(128)S(1)} %copy-done.60, f32[56]{0:T(128)S(1)} %copy-done.65, f32[56]{0:T(128)S(1)} %copy-done.75, ...), kind=kLoop, calls=%fused_computation.253 | loop fusion | flops 134041600 | bytes 37476320 | tf_op jit(solution)/shard_map/add | solution.py:30
  340.1 82.1 %add_convert_fusion.3 = bf16[56,32,680]{2,1,0:T(8,128)(2,1)S(1)} fusion(f32[56,32,680]{2,1,0:T(8,128)} %multiply_add_fusion.3, f32[56]{0:T(128)S(1)} %get-tuple-element.55, f32[56]{0:T(128)S(1)} %get-tuple-element.56, f32[56]{0:T(128)S(1)} %get-tuple-element.33, f32[56]{0:T(128)S(1)} %get-tuple-element.34, f32[56]{0:T(128)S(1)} %get-tuple-element.35, ...), kind=kLoop, calls=%fused_computation.229 | loop fusion | flops 60928000 | bytes 7316960 | tf_op jit(solution)/shard_map/convert_element_type | solution.py:70
  423.3 1.3 collective-permute-start.5
  424.9 5.3 collective-permute-start.4
  430.2 19.0 %collective-permute-done.5 = bf16[56,12,680]{2,0,1:T(8,128)(2,1)S(1)} collective-permute-done((bf16[56,12,680]{2,0,1:T(8,128)(2,1)S(1)}, bf16[56,12,680]{2,0,1:T(8,128)(2,1)S(1)}, u32[]{:S(2)}, u32[]{:S(2)}) %collective-permute-start.5) | collective-permute-done | bytes 913952 | tf_op jit(solution)/shard_map/ppermute | solution.py:19
  449.4 23.4 %collective-permute-done.4 = bf16[56,12,680]{2,0,1:T(8,128)(2,1)S(1)} collective-permute-done((bf16[56,12,680]{2,0,1:T(8,128)(2,1)S(1)}, bf16[56,12,680]{2,0,1:T(8,128)(2,1)S(1)}, u32[]{:S(2)}, u32[]{:S(2)}) %collective-permute-start.4) | collective-permute-done | bytes 913952 | tf_op jit(solution)/shard_map/ppermute | solution.py:17
  473.3 24.6 %multiply_add_fusion.2 = f32[56,32,680]{2,1,0:T(8,128)S(1)} fusion(bf16[56,32,680]{2,1,0:T(8,128)(2,1)S(1)} %add_convert_fusion.3, bf16[56,12,680]{2,1,0:T(8,128)(2,1)S(1)} %copy.87, bf16[56,12,680]{2,1,0:T(8,128)(2,1)S(1)} %copy.85, f32[56]{0:T(128)S(1)} %copy-done.61, f32[56]{0:T(128)S(1)} %copy-done.66, f32[56]{0:T(128)S(1)} %copy-done.76, ...), kind=kLoop, calls=%fused_computation.228 | loop fusion | flops 177909760 | bytes 9144800 | tf_op jit(solution)/shard_map/add | solution.py:30
  497.9 40.9 %add_convert_fusion.2 = bf16[56,32,680]{2,1,0:T(8,128)(2,1)} fusion(f32[56,32,680]{2,1,0:T(8,128)S(1)} %multiply_add_fusion.2, f32[56]{0:T(128)S(1)} %get-tuple-element.55, f32[56]{0:T(128)S(1)} %get-tuple-element.56, f32[56]{0:T(128)S(1)} %get-tuple-element.33, f32[56]{0:T(128)S(1)} %get-tuple-element.34, f32[56]{0:T(128)S(1)} %get-tuple-element.35, ...), kind=kLoop, calls=%fused_computation.204 | loop fusion | flops 60928000 | bytes 7316960 | tf_op jit(solution)/shard_map/convert_element_type | solution.py:72
  538.8 11.7 %copy.88 = bf16[56,32,680]{0,1,2:T(8,128)(2,1)} copy(bf16[56,32,680]{2,1,0:T(8,128)(2,1)} %add_convert_fusion.2) | data formatting | bytes 4874240 | tf_op jit(solution)/shard_map/convert_element_type | solution.py:72
  550.5 12.5 %reshape.108 = bf16[4,2,152320]{2,1,0:T(2,128)(2,1)S(1)} reshape(bf16[680,32,56]{2,1,0:T(8,128)(2,1)} %bitcast.163) | data formatting | bytes 4874240
  563.0 33.1 %all_to_all.92 = bf16[4,2,152320]{2,1,0:T(2,128)(2,1)} all-to-all(bf16[4,2,152320]{2,1,0:T(2,128)(2,1)S(1)} %reshape.108), channel_id=1, replica_groups=mesh['band'=4,'row'=8] {'band'}, dimensions={0} | all-to-all | bytes 4874240 | tf_op jit(solution)/shard_map/all_to_all | solution.py:62
  596.1 13.8 %reshape.109 = bf16[680,32,56]{2,1,0:T(8,128)(2,1)} reshape(bf16[4,2,152320]{2,1,0:T(2,128)(2,1)} %all_to_all.92) | data formatting | bytes 4874240
  609.9 8.4 copy.109
  618.3 3.4 multiply_reduce_fusion.2
  621.7 41.6 %all-reduce.6 = (f32[]{:T(128)}, f32[]{:T(128)}) all-reduce(f32[]{:T(128)} %get-tuple-element.15, f32[]{:T(128)} %get-tuple-element.14), channel_id=1, replica_groups=mesh['band'=4,'row'=8] {'band','row'}, use_global_device_ids=true, to_apply=%region_1.2 | all-reduce | flops 2 | bytes 16 | tf_op jit(solution)/shard_map/psum | solution.py:47
  664.8 1.0 copy-done.5
  665.7 2.6 convert_bitcast_fusion
  668.3 4.8 copy.91
  673.1 46.5 %all_to_all.93 = bf16[224,32,170]{2,1,0:T(8,128)(2,1)S(1)} all-to-all(bf16[224,32,170]{2,1,0:T(8,128)(2,1)} %copy.91), channel_id=1, replica_groups=mesh['band'=4,'row'=8] {'band'}, dimensions={0} | all-to-all | bytes 4874240 | tf_op jit(solution)/shard_map/all_to_all | solution.py:68
  719.5 8.5 copy.92
  728.0 6.3 all_to_all.80
  735.2 4.2 collective-permute-start.6
  739.9 1.5 collective-permute-start.7
  741.6 41.5 %collective-permute-done.6 = bf16[56,12,680]{2,0,1:T(8,128)(2,1)S(1)} collective-permute-done((bf16[56,12,680]{2,0,1:T(8,128)(2,1)S(1)}, bf16[56,12,680]{2,0,1:T(8,128)(2,1)S(1)}, u32[]{:S(2)}, u32[]{:S(2)}) %collective-permute-start.6) | collective-permute-done | bytes 913952 | tf_op jit(solution)/shard_map/ppermute | solution.py:17
  784.0 24.4 %multiply_add_fusion.1 = f32[56,32,680]{2,1,0:T(8,128)} fusion(bf16[56,32,680]{2,1,0:T(8,128)(2,1)S(1)} %all_to_all.80, bf16[56,12,680]{2,1,0:T(8,128)(2,1)S(1)} %copy.94, bf16[56,44,680]{2,1,0:T(8,128)(2,1)S(1)} %copy_dynamic-update-slice_fusion, f32[56]{0:T(128)S(1)} %copy-done.62, f32[56]{0:T(128)S(1)} %copy-done.67, f32[56]{0:T(128)S(1)} %copy-done.77, ...), kind=kLoop, calls=%fused_computation.203 | loop fusion | flops 134041600 | bytes 37476320 | tf_op jit(solution)/shard_map/add | solution.py:30
  808.5 82.1 %add_convert_fusion.1 = bf16[56,32,680]{2,1,0:T(8,128)(2,1)S(1)} fusion(f32[56,32,680]{2,1,0:T(8,128)} %multiply_add_fusion.1, f32[56]{0:T(128)S(1)} %get-tuple-element.55, f32[56]{0:T(128)S(1)} %get-tuple-element.56, f32[56]{0:T(128)S(1)} %get-tuple-element.33, f32[56]{0:T(128)S(1)} %get-tuple-element.34, f32[56]{0:T(128)S(1)} %get-tuple-element.35, ...), kind=kLoop, calls=%fused_computation.179 | loop fusion | flops 60928000 | bytes 7316960 | tf_op jit(solution)/shard_map/convert_element_type | solution.py:70
  891.7 1.3 collective-permute-start.9
  893.3 5.3 collective-permute-start.8
  898.7 19.0 %collective-permute-done.9 = bf16[56,12,680]{2,0,1:T(8,128)(2,1)S(1)} collective-permute-done((bf16[56,12,680]{2,0,1:T(8,128)(2,1)S(1)}, bf16[56,12,680]{2,0,1:T(8,128)(2,1)S(1)}, u32[]{:S(2)}, u32[]{:S(2)}) %collective-permute-start.9) | collective-permute-done | bytes 913952 | tf_op jit(solution)/shard_map/ppermute | solution.py:19
  917.9 22.3 %collective-permute-done.8 = bf16[56,12,680]{2,0,1:T(8,128)(2,1)S(1)} collective-permute-done((bf16[56,12,680]{2,0,1:T(8,128)(2,1)S(1)}, bf16[56,12,680]{2,0,1:T(8,128)(2,1)S(1)}, u32[]{:S(2)}, u32[]{:S(2)}) %collective-permute-start.8) | collective-permute-done | bytes 913952 | tf_op jit(solution)/shard_map/ppermute | solution.py:17
  940.6 24.6 %multiply_add_fusion = f32[56,32,680]{2,1,0:T(8,128)S(1)} fusion(bf16[56,32,680]{2,1,0:T(8,128)(2,1)S(1)} %add_convert_fusion.1, bf16[56,12,680]{2,1,0:T(8,128)(2,1)S(1)} %copy.100, bf16[56,12,680]{2,1,0:T(8,128)(2,1)S(1)} %copy.98, f32[56]{0:T(128)S(1)} %copy-done.63, f32[56]{0:T(128)S(1)} %copy-done.68, f32[56]{0:T(128)S(1)} %copy-done.78, ...), kind=kLoop, calls=%fused_computation.178 | loop fusion | flops 177909760 | bytes 9144800 | tf_op jit(solution)/shard_map/add | solution.py:30
  965.2 40.9 %add_convert_fusion = bf16[56,32,680]{2,1,0:T(8,128)(2,1)} fusion(f32[56,32,680]{2,1,0:T(8,128)S(1)} %multiply_add_fusion, f32[56]{0:T(128)S(1)} %get-tuple-element.55, f32[56]{0:T(128)S(1)} %get-tuple-element.56, f32[56]{0:T(128)S(1)} %get-tuple-element.33, f32[56]{0:T(128)S(1)} %get-tuple-element.34, f32[56]{0:T(128)S(1)} %get-tuple-element.35, ...), kind=kLoop, calls=%fused_computation.154 | loop fusion | flops 60928000 | bytes 7316960 | tf_op jit(solution)/shard_map/convert_element_type | solution.py:72
  1006.1 11.7 %copy.101 = bf16[56,32,680]{0,1,2:T(8,128)(2,1)} copy(bf16[56,32,680]{2,1,0:T(8,128)(2,1)} %add_convert_fusion) | data formatting | bytes 4874240 | tf_op jit(solution)/shard_map/convert_element_type | solution.py:72
  1017.9 12.5 %reshape.110 = bf16[4,2,152320]{2,1,0:T(2,128)(2,1)S(1)} reshape(bf16[680,32,56]{2,1,0:T(8,128)(2,1)} %bitcast.165) | data formatting | bytes 4874240
  1030.4 32.9 %all_to_all.94 = bf16[4,2,152320]{2,1,0:T(2,128)(2,1)} all-to-all(bf16[4,2,152320]{2,1,0:T(2,128)(2,1)S(1)} %reshape.110), channel_id=1, replica_groups=mesh['band'=4,'row'=8] {'band'}, dimensions={0} | all-to-all | bytes 4874240 | tf_op jit(solution)/shard_map/all_to_all | solution.py:62
  1063.3 13.8 %reshape.111 = bf16[680,32,56]{2,1,0:T(8,128)(2,1)} reshape(bf16[4,2,152320]{2,1,0:T(2,128)(2,1)} %all_to_all.94) | data formatting | bytes 4874240
  1077.2 8.5 copy.110
  1085.6 4.4 multiply_reduce_fusion
  1090.0 41.0 %all-reduce.5 = (f32[]{:T(128)}, f32[]{:T(128)}) all-reduce(f32[]{:T(128)} %get-tuple-element.13, f32[]{:T(128)} %get-tuple-element.12), channel_id=1, replica_groups=mesh['band'=4,'row'=8] {'band','row'}, use_global_device_ids=true, to_apply=%region_5.6 | all-reduce | flops 2 | bytes 16 | tf_op jit(solution)/shard_map/psum | solution.py:47
  1135.4 1.7 multiply_subtract_fusion
  1137.1 1.6 copy.105
  1138.7 1.6 copy.104
  (368 shorter events, 8.8 us)
Async XLA Ops:
  0.6 192.5 %copy-start = (bf16[224,32]{0,1:T(8,128)(2,1)S(1)}, bf16[224,32]{0,1:T(8,128)(2,1)}, u32[]{:S(2)}) copy-start(bf16[224,32]{0,1:T(8,128)(2,1)} %param.8) | copy-start | bytes 43012
  3.4 49.0 %collective-permute-start = (bf16[56,12,680]{2,0,1:T(8,128)(2,1)S(1)}, bf16[56,12,680]{2,0,1:T(8,128)(2,1)S(1)}, u32[]{:S(2)}, u32[]{:S(2)}) collective-permute-start(bf16[56,12,680]{2,0,1:T(8,128)(2,1)S(1)} %copy.106), channel_id=1, source_target_pairs={{0,1},{1,2},{2,3},{3,4},{4,5},{5,6},{6,7},{8,9},{9,10},{10,11},{11... | collective-permute-start | bytes 2741768 | tf_op jit(solution)/shard_map/ppermute | solution.py:17
  8.7 44.0 %collective-permute-start.1 = (bf16[56,12,680]{2,0,1:T(8,128)(2,1)S(1)}, bf16[56,12,680]{2,0,1:T(8,128)(2,1)S(1)}, u32[]{:S(2)}, u32[]{:S(2)}) collective-permute-start(bf16[56,12,680]{2,0,1:T(8,128)(2,1)S(1)} %copy.107), channel_id=1, source_target_pairs={{1,0},{2,1},{3,2},{4,3},{5,4},{6,5},{7,6},{9,8},{10,9},{11,10},{12... | collective-permute-start | bytes 2741768 | tf_op jit(solution)/shard_map/ppermute | solution.py:19
  10.2 64.8 %copy-start.39 = (f32[56]{0:T(128)}, f32[56]{0:T(128)S(1)}, u32[]{:S(2)}) copy-start(f32[56]{0:T(128)S(1)} %get-tuple-element.76) | copy-start | bytes 676
  10.2 64.8 %copy-start.44 = (f32[56]{0:T(128)}, f32[56]{0:T(128)S(1)}, u32[]{:S(2)}) copy-start(f32[56]{0:T(128)S(1)} %get-tuple-element.77) | copy-start | bytes 676
  10.2 64.8 %copy-start.49 = (f32[56]{0:T(128)}, f32[56]{0:T(128)S(1)}, u32[]{:S(2)}) copy-start(f32[56]{0:T(128)S(1)} %get-tuple-element.78) | copy-start | bytes 676
  10.2 64.8 %copy-start.54 = (f32[56]{0:T(128)}, f32[56]{0:T(128)S(1)}, u32[]{:S(2)}) copy-start(f32[56]{0:T(128)S(1)} %get-tuple-element.79) | copy-start | bytes 676
  10.2 64.8 %copy-start.59 = (f32[56]{0:T(128)}, f32[56]{0:T(128)S(1)}, u32[]{:S(2)}) copy-start(f32[56]{0:T(128)S(1)} %get-tuple-element.80) | copy-start | bytes 676
  10.2 64.8 %copy-start.64 = (f32[56]{0:T(128)}, f32[56]{0:T(128)S(1)}, u32[]{:S(2)}) copy-start(f32[56]{0:T(128)S(1)} %get-tuple-element.81) | copy-start | bytes 676
  10.3 64.8 %copy-start.69 = (f32[56]{0:T(128)}, f32[56]{0:T(128)S(1)}, u32[]{:S(2)}) copy-start(f32[56]{0:T(128)S(1)} %get-tuple-element.57) | copy-start | bytes 676
  10.3 64.8 %copy-start.74 = (f32[56]{0:T(128)}, f32[56]{0:T(128)S(1)}, u32[]{:S(2)}) copy-start(f32[56]{0:T(128)S(1)} %get-tuple-element.58) | copy-start | bytes 676
  10.3 64.8 %copy-start.79 = (f32[56]{0:T(128)}, f32[56]{0:T(128)S(1)}, u32[]{:S(2)}) copy-start(f32[56]{0:T(128)S(1)} %get-tuple-element.59) | copy-start | bytes 676
  10.3 64.8 %copy-start.84 = (f32[56]{0:T(128)}, f32[56]{0:T(128)S(1)}, u32[]{:S(2)}) copy-start(f32[56]{0:T(128)S(1)} %get-tuple-element.60) | copy-start | bytes 676
  10.3 64.8 %copy-start.89 = (f32[56]{0:T(128)}, f32[56]{0:T(128)S(1)}, u32[]{:S(2)}) copy-start(f32[56]{0:T(128)S(1)} %get-tuple-element.61) | copy-start | bytes 676
  10.3 64.8 %copy-start.94 = (f32[56]{0:T(128)}, f32[56]{0:T(128)S(1)}, u32[]{:S(2)}) copy-start(f32[56]{0:T(128)S(1)} %get-tuple-element.62) | copy-start | bytes 676
  10.3 64.8 %copy-start.99 = (f32[56]{0:T(128)}, f32[56]{0:T(128)S(1)}, u32[]{:S(2)}) copy-start(f32[56]{0:T(128)S(1)} %get-tuple-element.63) | copy-start | bytes 676
  10.3 64.8 %copy-start.104 = (f32[56]{0:T(128)}, f32[56]{0:T(128)S(1)}, u32[]{:S(2)}) copy-start(f32[56]{0:T(128)S(1)} %get-tuple-element.64) | copy-start | bytes 676
  10.4 64.8 %copy-start.109 = (f32[56]{0:T(128)}, f32[56]{0:T(128)S(1)}, u32[]{:S(2)}) copy-start(f32[56]{0:T(128)S(1)} %get-tuple-element.65) | copy-start | bytes 676
  10.4 64.8 %copy-start.114 = (f32[56]{0:T(128)}, f32[56]{0:T(128)S(1)}, u32[]{:S(2)}) copy-start(f32[56]{0:T(128)S(1)} %get-tuple-element.66) | copy-start | bytes 676
  10.4 64.8 %copy-start.119 = (f32[56]{0:T(128)}, f32[56]{0:T(128)S(1)}, u32[]{:S(2)}) copy-start(f32[56]{0:T(128)S(1)} %get-tuple-element.67) | copy-start | bytes 676
  10.4 64.8 %copy-start.124 = (f32[56]{0:T(128)}, f32[56]{0:T(128)S(1)}, u32[]{:S(2)}) copy-start(f32[56]{0:T(128)S(1)} %get-tuple-element.68) | copy-start | bytes 676
  10.4 64.8 %copy-start.129 = (f32[56]{0:T(128)}, f32[56]{0:T(128)S(1)}, u32[]{:S(2)}) copy-start(f32[56]{0:T(128)S(1)} %get-tuple-element.69) | copy-start | bytes 676
  10.4 64.8 %copy-start.134 = (f32[56]{0:T(128)}, f32[56]{0:T(128)S(1)}, u32[]{:S(2)}) copy-start(f32[56]{0:T(128)S(1)} %get-tuple-element.70) | copy-start | bytes 676
  10.4 64.8 %copy-start.139 = (f32[56]{0:T(128)}, f32[56]{0:T(128)S(1)}, u32[]{:S(2)}) copy-start(f32[56]{0:T(128)S(1)} %get-tuple-element.71) | copy-start | bytes 676
  10.4 64.8 %copy-start.144 = (f32[56]{0:T(128)}, f32[56]{0:T(128)S(1)}, u32[]{:S(2)}) copy-start(f32[56]{0:T(128)S(1)} %get-tuple-element.72) | copy-start | bytes 676
  10.4 64.8 %copy-start.149 = (f32[56]{0:T(128)}, f32[56]{0:T(128)S(1)}, u32[]{:S(2)}) copy-start(f32[56]{0:T(128)S(1)} %get-tuple-element.73) | copy-start | bytes 676
  10.4 64.8 %copy-start.154 = (f32[56]{0:T(128)}, f32[56]{0:T(128)S(1)}, u32[]{:S(2)}) copy-start(f32[56]{0:T(128)S(1)} %get-tuple-element.74) | copy-start | bytes 676
  10.5 64.8 %copy-start.159 = (f32[56]{0:T(128)}, f32[56]{0:T(128)S(1)}, u32[]{:S(2)}) copy-start(f32[56]{0:T(128)S(1)} %get-tuple-element.75) | copy-start | bytes 676
  266.5 48.2 %collective-permute-start.2 = (bf16[56,12,680]{2,0,1:T(8,128)(2,1)S(1)}, bf16[56,12,680]{2,0,1:T(8,128)(2,1)S(1)}, u32[]{:S(2)}, u32[]{:S(2)}) collective-permute-start(bf16[56,12,680]{2,0,1:T(8,128)(2,1)S(1)} %copy.80), channel_id=1, source_target_pairs={{0,1},{1,2},{2,3},{3,4},{4,5},{5,6},{6,7},{8,9},{9,10},{10,11},{11... | collective-permute-start | bytes 2741768 | tf_op jit(solution)/shard_map/ppermute | solution.py:17
  271.5 43.4 %collective-permute-start.3 = (bf16[56,12,680]{2,0,1:T(8,128)(2,1)S(1)}, bf16[56,12,680]{2,0,1:T(8,128)(2,1)S(1)}, u32[]{:S(2)}, u32[]{:S(2)}) collective-permute-start(bf16[56,12,680]{2,0,1:T(8,128)(2,1)S(1)} %copy.82), channel_id=1, source_target_pairs={{1,0},{2,1},{3,2},{4,3},{5,4},{6,5},{7,6},{9,8},{10,9},{11,10},{12... | collective-permute-start | bytes 2741768 | tf_op jit(solution)/shard_map/ppermute | solution.py:19
  422.7 50.3 %copy-start.41 = (f32[56]{0:T(128)S(1)}, f32[56]{0:T(128)}, u32[]{:S(2)}) copy-start(f32[56]{0:T(128)} %copy-done.39) | copy-start | bytes 676
  422.7 50.3 %copy-start.46 = (f32[56]{0:T(128)S(1)}, f32[56]{0:T(128)}, u32[]{:S(2)}) copy-start(f32[56]{0:T(128)} %copy-done.44) | copy-start | bytes 676
  422.7 50.3 %copy-start.51 = (f32[56]{0:T(128)S(1)}, f32[56]{0:T(128)}, u32[]{:S(2)}) copy-start(f32[56]{0:T(128)} %copy-done.49) | copy-start | bytes 676
  422.8 50.3 %copy-start.56 = (f32[56]{0:T(128)S(1)}, f32[56]{0:T(128)}, u32[]{:S(2)}) copy-start(f32[56]{0:T(128)} %copy-done.54) | copy-start | bytes 676
  422.8 50.3 %copy-start.61 = (f32[56]{0:T(128)S(1)}, f32[56]{0:T(128)}, u32[]{:S(2)}) copy-start(f32[56]{0:T(128)} %copy-done.59) | copy-start | bytes 676
  422.8 50.3 %copy-start.66 = (f32[56]{0:T(128)S(1)}, f32[56]{0:T(128)}, u32[]{:S(2)}) copy-start(f32[56]{0:T(128)} %copy-done.64) | copy-start | bytes 676
  422.8 50.3 %copy-start.71 = (f32[56]{0:T(128)S(1)}, f32[56]{0:T(128)}, u32[]{:S(2)}) copy-start(f32[56]{0:T(128)} %copy-done.69) | copy-start | bytes 676
  422.8 50.3 %copy-start.76 = (f32[56]{0:T(128)S(1)}, f32[56]{0:T(128)}, u32[]{:S(2)}) copy-start(f32[56]{0:T(128)} %copy-done.74) | copy-start | bytes 676
  422.8 50.3 %copy-start.81 = (f32[56]{0:T(128)S(1)}, f32[56]{0:T(128)}, u32[]{:S(2)}) copy-start(f32[56]{0:T(128)} %copy-done.79) | copy-start | bytes 676
  422.8 50.3 %copy-start.86 = (f32[56]{0:T(128)S(1)}, f32[56]{0:T(128)}, u32[]{:S(2)}) copy-start(f32[56]{0:T(128)} %copy-done.84) | copy-start | bytes 676
  422.8 50.3 %copy-start.91 = (f32[56]{0:T(128)S(1)}, f32[56]{0:T(128)}, u32[]{:S(2)}) copy-start(f32[56]{0:T(128)} %copy-done.89) | copy-start | bytes 676
  422.8 50.3 %copy-start.96 = (f32[56]{0:T(128)S(1)}, f32[56]{0:T(128)}, u32[]{:S(2)}) copy-start(f32[56]{0:T(128)} %copy-done.94) | copy-start | bytes 676
  422.8 50.3 %copy-start.101 = (f32[56]{0:T(128)S(1)}, f32[56]{0:T(128)}, u32[]{:S(2)}) copy-start(f32[56]{0:T(128)} %copy-done.99) | copy-start | bytes 676
  422.9 50.3 %copy-start.106 = (f32[56]{0:T(128)S(1)}, f32[56]{0:T(128)}, u32[]{:S(2)}) copy-start(f32[56]{0:T(128)} %copy-done.104) | copy-start | bytes 676
  422.9 50.3 %copy-start.111 = (f32[56]{0:T(128)S(1)}, f32[56]{0:T(128)}, u32[]{:S(2)}) copy-start(f32[56]{0:T(128)} %copy-done.109) | copy-start | bytes 676
  422.9 50.3 %copy-start.116 = (f32[56]{0:T(128)S(1)}, f32[56]{0:T(128)}, u32[]{:S(2)}) copy-start(f32[56]{0:T(128)} %copy-done.114) | copy-start | bytes 676
  422.9 50.3 %copy-start.121 = (f32[56]{0:T(128)S(1)}, f32[56]{0:T(128)}, u32[]{:S(2)}) copy-start(f32[56]{0:T(128)} %copy-done.119) | copy-start | bytes 676
  422.9 50.3 %copy-start.126 = (f32[56]{0:T(128)S(1)}, f32[56]{0:T(128)}, u32[]{:S(2)}) copy-start(f32[56]{0:T(128)} %copy-done.124) | copy-start | bytes 676
  422.9 50.3 %copy-start.131 = (f32[56]{0:T(128)S(1)}, f32[56]{0:T(128)}, u32[]{:S(2)}) copy-start(f32[56]{0:T(128)} %copy-done.129) | copy-start | bytes 676
  422.9 50.3 %copy-start.136 = (f32[56]{0:T(128)S(1)}, f32[56]{0:T(128)}, u32[]{:S(2)}) copy-start(f32[56]{0:T(128)} %copy-done.134) | copy-start | bytes 676
  422.9 50.3 %copy-start.141 = (f32[56]{0:T(128)S(1)}, f32[56]{0:T(128)}, u32[]{:S(2)}) copy-start(f32[56]{0:T(128)} %copy-done.139) | copy-start | bytes 676
  422.9 50.3 %copy-start.146 = (f32[56]{0:T(128)S(1)}, f32[56]{0:T(128)}, u32[]{:S(2)}) copy-start(f32[56]{0:T(128)} %copy-done.144) | copy-start | bytes 676
  422.9 50.3 %copy-start.151 = (f32[56]{0:T(128)S(1)}, f32[56]{0:T(128)}, u32[]{:S(2)}) copy-start(f32[56]{0:T(128)} %copy-done.149) | copy-start | bytes 676
  423.0 50.3 %copy-start.156 = (f32[56]{0:T(128)S(1)}, f32[56]{0:T(128)}, u32[]{:S(2)}) copy-start(f32[56]{0:T(128)} %copy-done.154) | copy-start | bytes 676
  423.0 50.3 %copy-start.161 = (f32[56]{0:T(128)S(1)}, f32[56]{0:T(128)}, u32[]{:S(2)}) copy-start(f32[56]{0:T(128)} %copy-done.159) | copy-start | bytes 676
  423.3 25.9 %collective-permute-start.5 = (bf16[56,12,680]{2,0,1:T(8,128)(2,1)S(1)}, bf16[56,12,680]{2,0,1:T(8,128)(2,1)S(1)}, u32[]{:S(2)}, u32[]{:S(2)}) collective-permute-start(bf16[56,12,680]{2,0,1:T(8,128)(2,1)S(1)} %copy.86), channel_id=1, source_target_pairs={{1,0},{2,1},{3,2},{4,3},{5,4},{6,5},{7,6},{9,8},{10,9},{11,10},{12... | collective-permute-start | bytes 2741768 | tf_op jit(solution)/shard_map/ppermute | solution.py:19
  424.9 47.9 %collective-permute-start.4 = (bf16[56,12,680]{2,0,1:T(8,128)(2,1)S(1)}, bf16[56,12,680]{2,0,1:T(8,128)(2,1)S(1)}, u32[]{:S(2)}, u32[]{:S(2)}) collective-permute-start(bf16[56,12,680]{2,0,1:T(8,128)(2,1)S(1)} %copy.84), channel_id=1, source_target_pairs={{0,1},{1,2},{2,3},{3,4},{4,5},{5,6},{6,7},{8,9},{9,10},{10,11},{11... | collective-permute-start | bytes 2741768 | tf_op jit(solution)/shard_map/ppermute | solution.py:17
  735.2 47.9 %collective-permute-start.6 = (bf16[56,12,680]{2,0,1:T(8,128)(2,1)S(1)}, bf16[56,12,680]{2,0,1:T(8,128)(2,1)S(1)}, u32[]{:S(2)}, u32[]{:S(2)}) collective-permute-start(bf16[56,12,680]{2,0,1:T(8,128)(2,1)S(1)} %copy.93), channel_id=1, source_target_pairs={{0,1},{1,2},{2,3},{3,4},{4,5},{5,6},{6,7},{8,9},{9,10},{10,11},{11... | collective-permute-start | bytes 2741768 | tf_op jit(solution)/shard_map/ppermute | solution.py:17
  739.9 43.4 %collective-permute-start.7 = (bf16[56,12,680]{2,0,1:T(8,128)(2,1)S(1)}, bf16[56,12,680]{2,0,1:T(8,128)(2,1)S(1)}, u32[]{:S(2)}, u32[]{:S(2)}) collective-permute-start(bf16[56,12,680]{2,0,1:T(8,128)(2,1)S(1)} %copy.95), channel_id=1, source_target_pairs={{1,0},{2,1},{3,2},{4,3},{5,4},{6,5},{7,6},{9,8},{10,9},{11,10},{12... | collective-permute-start | bytes 2741768 | tf_op jit(solution)/shard_map/ppermute | solution.py:19
  891.2 49.2 %copy-start.43 = (f32[56]{0:T(128)S(1)}, f32[56]{0:T(128)}, u32[]{:S(2)}) copy-start(f32[56]{0:T(128)} %copy-done.39) | copy-start | bytes 676
  891.7 25.9 %collective-permute-start.9 = (bf16[56,12,680]{2,0,1:T(8,128)(2,1)S(1)}, bf16[56,12,680]{2,0,1:T(8,128)(2,1)S(1)}, u32[]{:S(2)}, u32[]{:S(2)}) collective-permute-start(bf16[56,12,680]{2,0,1:T(8,128)(2,1)S(1)} %copy.99), channel_id=1, source_target_pairs={{1,0},{2,1},{3,2},{4,3},{5,4},{6,5},{7,6},{9,8},{10,9},{11,10},{12... | collective-permute-start | bytes 2741768 | tf_op jit(solution)/shard_map/ppermute | solution.py:19
  893.3 46.8 %collective-permute-start.8 = (bf16[56,12,680]{2,0,1:T(8,128)(2,1)S(1)}, bf16[56,12,680]{2,0,1:T(8,128)(2,1)S(1)}, u32[]{:S(2)}, u32[]{:S(2)}) collective-permute-start(bf16[56,12,680]{2,0,1:T(8,128)(2,1)S(1)} %copy.97), channel_id=1, source_target_pairs={{0,1},{1,2},{2,3},{3,4},{4,5},{5,6},{6,7},{8,9},{9,10},{10,11},{11... | collective-permute-start | bytes 2741768 | tf_op jit(solution)/shard_map/ppermute | solution.py:17
  1077.2 58.3 %copy-start.3 = (f32[32,32,170]{2,0,1:T(8,128)S(1)}, f32[32,32,170]{2,0,1:T(8,128)}, u32[]{:S(2)}) copy-start(f32[32,32,170]{2,0,1:T(8,128)} %copy-done.1) | copy-start | bytes 2088964
  1077.2 58.3 %copy-start.8 = (f32[32,32,170]{2,0,1:T(8,128)S(1)}, f32[32,32,170]{2,0,1:T(8,128)}, u32[]{:S(2)}) copy-start(f32[32,32,170]{2,0,1:T(8,128)} %copy-done.7) | copy-start | bytes 2088964
  (114 other events, 4214.2 us)
where the time goes:
time: 1150 us; the launch traced here: 1140 us
  other arithmetic  408 us (35%)
  blocking collectives  275 us (24%)
  waiting for transfers between devices  208 us (18%)
  local copies, waits for them, and re-layouts  194 us (17%)
  starting transfers between devices  31 us (3%)
  matrix products  15.7 us (1%)
    ppermute x5, waiting for transfers between devices, extended(): lax.ppermute(tail, axis, [(i, (i + 1) % count) for i in range(ends)])  170 us
    convert_element_type x2, other arithmetic, normal_map(): pass_cols(pass_rows(padded, row_taps), col_taps).astype(jnp.bfloat16)  164 us
    add x5, other arithmetic, pass_rows(): running + kernel[:, offset, None, None] * padded[:, offset:offset + lengt...  120 us
    all_to_all x3, blocking collectives, to_subspace(): lax.all_to_all(band_field, 'band', split_axis=2, concat_axis=0, tiled=True)  98.9 us
    all_to_all x2, blocking collectives, normal_map(): lax.all_to_all(spectra, 'band', split_axis=0, concat_axis=2, tiled=True)  93.1 us
    unnamed x349, local copies, waits for them, and re-layouts  85.9 us
    psum x2, blocking collectives, two_products(): lax.psum((jnp.sum(residual * residual), jnp.sum(residual * mapped)), ('ba...  82.5 us
    convert_element_type x2, other arithmetic, normal_map(): pass_cols(pass_rows(blurred, row_flip), col_flip).astype(jnp.bfloat16)  81.8 us
  transfers between devices with their start and end apart: 10, of which 7 were waited for; matrix products, arithmetic and copies ran while one was open for 0% of the time, Pallas kernels for 0%

commit v1 on v0

v1 whole, which is shorter than its diff:
```python
import functools

import jax
import jax.numpy as jnp
from jax import lax
from jax.experimental import pallas as pl
from jax.experimental.pallas import tpu as pltpu
from jax.sharding import PartitionSpec as P

LANES = 128
SUB = 8
BF = jnp.bfloat16
F32 = jnp.float32
VMEM_LIMIT = 50 * 1024 * 1024


def round_up(value, unit):
    return (value + unit - 1) // unit * unit


def group_size(count, most):
    return max(size for size in range(1, most + 1) if count % size == 0)


def dot(lhs, rhs):
    return lax.dot_general(lhs, rhs, (((1,), (0,)), ((), ())), preferred_element_type=F32)


def toeplitz(taps, rows, shift):
    lanes = taps.shape[1]
    pieces = []
    for first in range(0, rows, LANES):
        count = min(LANES, rows - first)
        wide = jnp.broadcast_to(taps, (count, lanes))
        pieces.append(pltpu.roll(wide, (shift + first) % lanes, 1, stride=1, stride_axis=0))
    return jnp.concatenate(pieces, axis=0) if len(pieces) > 1 else pieces[0]


def spread_basis(basis, group, kinds):
    bands = basis.shape[0]
    rows = jnp.arange(bands * SUB)
    lanes = jnp.arange(SUB * kinds)
    up = (rows[:, None] // SUB == jnp.arange(bands)[None, :]).astype(BF)
    out = (jnp.arange(kinds)[:, None] == lanes[None, :] % kinds).astype(BF)
    same = (rows[:, None] % SUB) == (lanes[None, :] // kinds)
    wide = dot(dot(up, basis).astype(BF), out)
    return jnp.where(same, wide, 0.0).astype(BF).reshape(bands // group, group * SUB, SUB * kinds)


def adjoint_kernel(columns, radius, obs_ref, row_ref, col_ref, mix_ref, out_ref, acc, ys):
    step = pl.program_id(0)
    group, height, _ = obs_ref.shape
    span = ys.shape[3]
    tiles = span // (2 * LANES)
    chunks = ys.shape[0]
    ext = chunks * SUB

    @pl.when(step == 0)
    def _():
        acc[...] = jnp.zeros_like(acc)

    last = columns // LANES * LANES
    width = 2 * LANES

    def one(b):
        cells = obs_ref[b]
        tail = cells[:, last:]
        pieces = [jnp.zeros((height, LANES), BF), cells[:, :last]]
        if columns > last:
            pieces.append(
                jnp.concatenate([tail, jnp.zeros((height, LANES - (columns - last)), BF)], axis=1)
            )
        have = sum(piece.shape[1] for piece in pieces)
        if have < span + 2 * LANES:
            pieces.append(jnp.zeros((height, span + 2 * LANES - have), BF))
        padded = jnp.concatenate(pieces, axis=1)
        stacked = jnp.concatenate(
            [padded[:, t * width : t * width + 2 * width] for t in range(tiles)], axis=0
        )
        edge = 2 * SUB
        ring = toeplitz(col_ref[b], width, -round_up(radius, SUB)).astype(BF)
        top, bottom = ring[:edge], ring[width - edge :]
        blank = jnp.zeros((edge, width), BF)
        near = lax.broadcasted_iota(jnp.int32, (edge, width), 1) < LANES
        rest = jnp.zeros((LANES - edge, width), BF)
        matrix = jnp.concatenate(
            [
                rest,
                jnp.where(near, bottom, blank),
                jnp.where(near, top, blank),
                ring[edge : width - edge],
                jnp.where(near, blank, bottom),
                jnp.where(near, blank, top),
                rest,
            ],
            axis=0,
        )
        mixed = dot(stacked, matrix).astype(BF)
        field = jnp.concatenate(
            [mixed[t * height : (t + 1) * height] for t in range(tiles)], axis=1
        )
        rows = toeplitz(row_ref[b], ext, -2 * radius)[:, :height]
        high = rows.astype(BF)
        low = (rows - high.astype(F32)).astype(BF)
        done = dot(high, field) + dot(low, field)
        for c in range(chunks):
            ys[c, b] = done[c * SUB : (c + 1) * SUB]

    @pl.loop(0, group)
    def _(b):
        one(b)

    for c in range(chunks):
        cells = ys[c].reshape(group * SUB, span).astype(BF)
        acc[c] += dot(mix_ref[0], cells)

    @pl.when(step == pl.num_programs(0) - 1)
    def _():
        out_ref[...] = acc[...].reshape(out_ref.shape).astype(out_ref.dtype)


def gram_kernel(halo, row_ref, row_flip_ref, col_ref, col_flip_ref, row_mask_ref, col_mask_ref, gr_ref, gl_ref):
    group, height, row_lanes = gr_ref.shape
    size = gl_ref.shape[1]
    for b in range(group):
        left = (toeplitz(col_flip_ref[b], size, -halo) * col_mask_ref[...]).astype(BF)
        right = toeplitz(col_ref[b], size, -halo).astype(BF)
        gl_ref[b] = dot(left, right).astype(BF)
        left = (toeplitz(row_flip_ref[b], height, 0) * row_mask_ref[...]).astype(BF)
        right = toeplitz(row_ref[b], row_lanes, 0).astype(BF)
        gr_ref[b] = dot(left, right).astype(BF)


def normal_kernel(columns, p_ref, own_ref, ridge_ref, sk_ref, pk_ref, gr_ref, gl_ref, out_ref, acc, xs, ys):
    step = pl.program_id(0)
    group, height, _ = gr_ref.shape
    ext, kinds, lanes = p_ref.shape
    chunks = height // SUB

    @pl.when(step == 0)
    def _():
        acc[...] = jnp.zeros_like(acc)
        xs[...] = jnp.zeros_like(xs)

    for c in range(0, ext, 2 * SUB):
        halves = []
        for s in (c, c + SUB):
            cells = p_ref[s : s + SUB].reshape(SUB * kinds, lanes)
            halves.append(dot(sk_ref[0], cells).reshape(group, SUB, lanes))
        xs[:, c : c + 2 * SUB, :] = jnp.concatenate(halves, axis=1).astype(BF)

    @pl.loop(0, group, step=8)
    def _(first):
        mids = []
        for b in range(8):
            mids.append(dot(gr_ref[first + b], xs[first + b]).astype(BF))
        for b in range(8):
            done = dot(mids[b], gl_ref[first + b])
            for c in range(chunks):
                ys[c, first + b] = done[c * SUB : (c + 1) * SUB]

    for c in range(chunks):
        acc[c] += dot(pk_ref[0], ys[c].reshape(group * SUB, lanes).astype(BF))

    @pl.when(step == pl.num_programs(0) - 1)
    def _():
        total = acc[...].reshape(height, kinds, lanes) + ridge_ref[...] * own_ref[...]
        lane = lax.broadcasted_iota(jnp.int32, total.shape, 2)
        out_ref[...] = jnp.where(lane < columns, total, 0.0)


def shift_both(low_edge, high_edge, axis):
    count = lax.axis_size(axis)
    from_before = lax.ppermute(high_edge, axis, [(i, i + 1) for i in range(count - 1)])
    from_after = lax.ppermute(low_edge, axis, [(i + 1, i) for i in range(count - 1)])
    return from_before, from_after


def local(observed, row_taps, col_taps, spectral_basis, ridge_weights):
    bands_here, height, columns_all = observed.shape
    taps = row_taps.shape[1]
    radius = (taps - 1) // 2
    halo = 2 * radius
    bands, kinds = spectral_basis.shape
    n_band = lax.axis_size("band")
    n_row = lax.axis_size("row")
    columns = columns_all // n_band
    lanes = round_up(columns + 2 * halo, 2 * LANES)
    me_band = lax.axis_index("band")
    me_row = lax.axis_index("row")
    core = me_band % 2
    chip = me_band // 2
    chips = n_band // 2

    def widen(values, width, lead=0):
        return jnp.pad(values, ((0, 0), (lead, width - taps - lead)))[:, None, :]

    every = lax.all_gather(jnp.concatenate([row_taps, col_taps], axis=1), "band", tiled=True)
    row_all, col_all = every[:, :taps], every[:, taps:]

    size = lanes
    at = jnp.arange(size)
    edge = me_band * columns - radius + at
    col_mask = ((edge >= 0) & (edge < columns_all) & (at < columns + 2 * radius)).astype(F32)[None]
    at = jnp.arange(LANES)
    edge = me_row * height - radius + at
    row_mask = ((edge >= 0) & (edge < height * n_row) & (at < height + 2 * radius)).astype(F32)[None]
    part = group_size(bands, 16)
    spec = lambda width: pl.BlockSpec((part, 1, width), lambda i: (i, 0, 0))
    whole = lambda shape: pl.BlockSpec(shape, lambda i: (0,) * len(shape))
    gr, gl = pl.pallas_call(
        functools.partial(gram_kernel, halo),
        grid=(bands // part,),
        in_specs=[spec(LANES), spec(LANES), spec(size), spec(size), whole((1, LANES)), whole((1, size))],
        out_specs=[
            pl.BlockSpec((part, height, LANES), lambda i: (i, 0, 0)),
            pl.BlockSpec((part, size, size), lambda i: (i, 0, 0)),
        ],
        out_shape=[
            jax.ShapeDtypeStruct((bands, height, LANES), BF),
            jax.ShapeDtypeStruct((bands, size, size), BF),
        ],
        compiler_params=pltpu.CompilerParams(vmem_limit_bytes=VMEM_LIMIT),
        cost_estimate=pl.CostEstimate(
            flops=bands * 2 * size**3, bytes_accessed=bands * size * size * 2, transcendentals=0
        ),
        name="gram",
    )(
        widen(row_all, LANES),
        widen(row_all[:, ::-1], LANES),
        widen(col_all, size),
        widen(col_all[:, ::-1], size),
        row_mask,
        col_mask,
    )

    few = group_size(bands_here, 32)
    span = round_up(columns_all, 2 * LANES)
    ext = height + 2 * radius
    chunks = ext // SUB
    basis_here = lax.dynamic_slice_in_dim(spectral_basis, me_band * bands_here, bands_here, 0)
    mix = jnp.swapaxes(spread_basis(basis_here, few, kinds), 1, 2)
    summed = pl.pallas_call(
        functools.partial(adjoint_kernel, columns_all, radius),
        grid=(bands_here // few,),
        in_specs=[
            pl.BlockSpec((few, height, columns_all), lambda i: (i, 0, 0)),
            pl.BlockSpec((few, 1, LANES), lambda i: (i, 0, 0)),
            pl.BlockSpec((few, 1, 2 * LANES), lambda i: (i, 0, 0)),
            pl.BlockSpec((1,) + mix.shape[1:], lambda i: (i, 0, 0)),
        ],
        out_specs=whole((ext, kinds, span)),
        out_shape=jax.ShapeDtypeStruct((ext, kinds, span), BF),
        scratch_shapes=[
            pltpu.VMEM((chunks, SUB * kinds, span), F32),
            pltpu.VMEM((chunks, few, SUB, span), F32),
        ],
        compiler_params=pltpu.CompilerParams(vmem_limit_bytes=VMEM_LIMIT),
        cost_estimate=pl.CostEstimate(
            flops=bands_here * 2 * 96 * 512 * 256, bytes_accessed=observed.size * 2, transcendentals=0
        ),
        name="adjoint",
    )(observed, widen(row_taps[:, ::-1], LANES), widen(col_taps, 2 * LANES, -radius % SUB), mix)

    half = kinds // 2
    keep = lax.dynamic_slice_in_dim(summed, core * half, half, 1)
    give = lax.dynamic_slice_in_dim(summed, (1 - core) * half, half, 1)
    pairs = [(i, i ^ 1) for i in range(n_band)]
    got = lax.ppermute(give, "band", pairs)
    pair = keep.astype(F32) + got.astype(F32)
    before, after = shift_both(pair[:radius].astype(BF), pair[ext - radius :].astype(BF), "row")
    rows = pair[radius : ext - radius]
    pad = ((0, height - radius), (0, 0), (0, 0))
    rows = rows + jnp.pad(before.astype(F32), pad) + jnp.pad(after.astype(F32), (pad[0][::-1],) + pad[1:])
    rows = jnp.pad(rows[:, :, :columns_all], ((0, 0), (0, 0), (halo, halo)))
    wide = 2 * columns + 2 * halo
    total = lax.dynamic_slice_in_dim(rows, chip * 2 * columns, wide, 2)
    for hop in range(1, chips):
        target = (chip + hop) % chips
        piece = lax.dynamic_slice_in_dim(rows, target * 2 * columns, wide, 2).astype(BF)
        moves = [(i, (i + 2 * hop) % n_band) for i in range(n_band)]
        total = total + lax.ppermute(piece, "band", moves).astype(F32)
    other = lax.ppermute(total, "band", pairs)
    first = jnp.where(core == 0, total, other)
    second = jnp.where(core == 0, other, total)
    total = jnp.concatenate([first, second], axis=1)
    window = lax.dynamic_slice_in_dim(total, core * columns, columns + 2 * halo, 2)
    v0 = jnp.pad(window[:, :, halo : halo + columns], ((0, 0), (0, 0), (0, lanes - columns)))
    window = jnp.pad(window.astype(BF), ((0, 0), (0, 0), (0, lanes - columns - 2 * halo)))

    group = group_size(bands, 32)
    sk = spread_basis(spectral_basis, group, kinds)
    pk = jnp.swapaxes(sk, 1, 2)
    ridge = jnp.broadcast_to(ridge_weights[:, None], (kinds, lanes))
    tall = height + 2 * halo
    block = lambda shape: pl.BlockSpec((group,) + shape, lambda i: (i, 0, 0))

    def normal_map(window, own):
        before, after = shift_both(window[:halo], window[height - halo :], "row")
        cells = jnp.concatenate([before, window, after], axis=0)
        return pl.pallas_call(
            functools.partial(normal_kernel, columns),
            grid=(bands // group,),
            in_specs=[
                whole((tall, kinds, lanes)),
                whole((height, kinds, lanes)),
                whole((kinds, lanes)),
                pl.BlockSpec((1,) + sk.shape[1:], lambda i: (i, 0, 0)),
                pl.BlockSpec((1,) + pk.shape[1:], lambda i: (i, 0, 0)),
                block((height, LANES)),
                block((size, size)),
            ],
            out_specs=whole((height, kinds, lanes)),
            out_shape=jax.ShapeDtypeStruct((height, kinds, lanes), F32),
            scratch_shapes=[
                pltpu.VMEM((height // SUB, SUB * kinds, lanes), F32),
                pltpu.VMEM((group, LANES, lanes), BF),
                pltpu.VMEM((height // SUB, group, SUB, lanes), F32),
            ],
            compiler_params=pltpu.CompilerParams(vmem_limit_bytes=VMEM_LIMIT),
            cost_estimate=pl.CostEstimate(
                flops=bands * 2 * 32 * 512 * 256, bytes_accessed=bands * size * size * 2, transcendentals=0
            ),
            name="normal",
        )(cells, own, ridge, sk, pk, gr, gl)

    v1 = normal_map(window, v0)
    near = v1[:, :, :columns].astype(BF)
    before, after = shift_both(near[:, :, :halo], near[:, :, columns - halo :], "band")
    window = jnp.concatenate(
        [before, near, after, jnp.zeros((height, kinds, lanes - columns - 2 * halo), BF)], axis=2
    )
    v2 = normal_map(window, v1)

    sums = jnp.stack(
        [jnp.sum(v0 * v0), jnp.sum(v0 * v1), jnp.sum(v1 * v1), jnp.sum(v0 * v2), jnp.sum(v1 * v2)]
    )
    everyone = n_band * n_row
    mine = jnp.broadcast_to(jnp.pad(sums, (0, LANES - 5))[None, None], (everyone, SUB, LANES))
    shared = lax.all_to_all(mine, ("band", "row"), 0, 0, tiled=True)
    sums = jnp.sum(shared[:, 0, :], axis=0)
    v00, v01, v11, v02, v12 = [sums[i] for i in range(5)]
    alpha = v00 / v01
    norm = v00 - 2.0 * alpha * v01 + alpha * alpha * v11
    ratio = norm / v00
    lead = 1.0 + ratio
    product = lead * lead * v01 - lead * alpha * (v02 + v11) + alpha * alpha * v12
    second = norm / product
    coefficients = (alpha + second * lead) * v0 - (second * alpha) * v1
    residual = v0 - (alpha + second * lead) * v1 + (second * alpha) * v2
    give_back = lambda field: jnp.swapaxes(field[:, :, :columns], 0, 1)
    return give_back(coefficients), give_back(residual)


def solution(mesh):
    in_specs = (P("band", "row", None), P("band", None), P("band", None), P(), P())
    out_specs = (P(None, "row", "band"), P(None, "row", "band"))
    return jax.shard_map(local, mesh=mesh, in_specs=in_specs, out_specs=out_specs, check_vma=False)
```

time: 1150 us -> 213 us (0.19)
  other arithmetic: 408 us -> 13.9 us
  blocking collectives: 275 us -> 34.5 us
  waiting for transfers between devices: 208 us -> 25.9 us
  local copies, waits for them, and re-layouts: 194 us -> 15.8 us
  Pallas kernels: 0 us -> 89 us
  matrix products: 15.7 us -> 1.35 us
    convert_element_type x5 -> x3, other arithmetic: 286 us -> 0.4 us  [the longest x1 0.38 us: local(): window.astype(BF)]
    ppermute x10 -> x11, waiting for transfers between devices: 208 us -> 25.9 us  [the longest x4 14 us: shift_both(): lax.ppermute(high_edge, axis, [(i, i + 1) for i in range(count - 1)])]
    all_to_all x5 -> x1, blocking collectives: 192 us -> 21.5 us  [local(): shared = lax.all_to_all(mine, ('band', 'row'), 0, 0, tiled=True)]
    add x5 -> x2, other arithmetic: 120 us -> 1.54 us  [the longest x1 1.33 us: local(): total = total + lax.ppermute(piece, 'band', moves).astype(F32)]
    pallas_call x0 -> x4, Pallas kernels: none -> 89 us  [the longest x2 39.8 us: normal_map(): pl.pallas_call(functools.partial(normal_kernel, columns), grid=(bands //...]
    psum x2 -> x0, blocking collectives: 82.5 us -> none  [two_products(): lax.psum((jnp.sum(residual * residual), jnp.sum(residual * mapped)), ('ba...]
    unnamed x349 -> x18, local copies, waits for them, and re-layouts: 85.9 us -> 5.61 us
    all_to_all x7 -> x0, local copies, waits for them, and re-layouts: 54.8 us -> none  [the longest x4 29.6 us: normal_map(): lax.all_to_all(spectra, 'band', split_axis=0, concat_axis=2, tiled=True)]
  transfers between devices with their start and end apart: 10 -> 11, of which waited for: 7 -> 5; matrix products, arithmetic and copies ran while one was open for 0% -> 2% of each run, Pallas kernels for 0% -> 9%
where the time goes in v1:
time: 213 us
  Pallas kernels  89 us (42%)
  blocking collectives  34.5 us (16%)
  waiting for transfers between devices  25.9 us (12%)
  starting transfers between devices  24.6 us (12%)
  local copies, waits for them, and re-layouts  15.8 us (7%)
  other arithmetic  13.9 us (7%)
  between operations  7.54 us (4%)
    pallas_call x2, Pallas kernels, normal_map(): pl.pallas_call(functools.partial(normal_kernel, columns), grid=(bands //...  39.8 us
    pallas_call x1, Pallas kernels, local(): pl.pallas_call(functools.partial(adjoint_kernel, columns_all, radius), gr...  29.5 us
    all_to_all x1, blocking collectives, local(): shared = lax.all_to_all(mine, ('band', 'row'), 0, 0, tiled=True)  21.5 us
    pallas_call x1, Pallas kernels, local(): pl.pallas_call(functools.partial(gram_kernel, halo), grid=(bands // part,...  19.7 us
    ppermute x4, starting transfers between devices, shift_both(): lax.ppermute(high_edge, axis, [(i, i + 1) for i in range(count - 1)])  16.7 us
    ppermute x4, waiting for transfers between devices, shift_both(): lax.ppermute(high_edge, axis, [(i, i + 1) for i in range(count - 1)])  14 us
    all_gather x1, blocking collectives, local(): lax.all_gather(jnp.concatenate([row_taps, col_taps], axis=1), 'band', til...  13 us
    ppermute x4, waiting for transfers between devices, shift_both(): lax.ppermute(low_edge, axis, [(i + 1, i) for i in range(count - 1)])  8.79 us
  transfers between devices with their start and end apart: 11, of which 5 were waited for; matrix products, arithmetic and copies ran while one was open for 2% of the time, Pallas kernels for 9%

profile of v1, /device:TPU:0, one launch (start us, length us, event | category | flops | bytes accessed | tf_op | source)
XLA Modules:
  0.0 212.5 jit_solution(15734701146175074270)
XLA Ops:
  0.6 0.0 copy-start
  0.7 0.8 copy.40
  1.5 0.8 copy.41
  2.3 0.1 rev.9
  2.4 0.1 pad.53
  2.5 0.5 fusion.2
  3.0 0.1 copy.42
  3.2 29.5 %adjoint.1 = bf16[56,32,768]{2,1,0:T(8,128)(2,1)S(1)} custom-call(bf16[56,32,680]{2,1,0:T(8,128)(2,1)} %obs_ref.1, f32[56,1,128]{2,1,0:T(1,128)S(1)} %bitcast.36, f32[56,1,256]{2,1,0:T(1,128)S(1)} %broadcast_in_dim.27.col_ref, bf16[2,256,224]{2,1,0:T(8,128)(2,1)S(1)} %bitcast.35), custom_call_target="tpu_custom_call" | custom-call | flops 1409286144 | bytes 2437120 | tf_op jit(solution)/shard_map/adjoint/pallas_call | solution.py:243
  32.7 1.2 constant_dynamic-slice_fusion
  33.9 0.5 collective-permute-start
  34.3 3.1 %collective-permute-done = bf16[56,16,768]{2,1,0:T(8,128)(2,1)} collective-permute-done((bf16[56,16,768]{2,1,0:T(8,128)(2,1)}, bf16[56,16,768]{2,1,0:T(8,128)(2,1)}, u32[]{:S(2)}, u32[]{:S(2)}) %collective-permute-start) | collective-permute-done | bytes 1376288 | tf_op jit(solution)/shard_map/ppermute | solution.py:269
  37.4 3.4 %fusion.32 = (bf16[56,16,768]{2,1,0:T(8,128)(2,1)S(1)}, f32[56,16,768]{2,1,0:T(8,128)}) fusion(bf16[56,16,768]{2,1,0:T(8,128)(2,1)} %collective-permute-done, bf16[56,32,768]{2,1,0:T(8,128)(2,1)S(1)} %adjoint.1, s32[]{:T(128)S(6)} %select_n.131), kind=kLoop, calls=%fused_computation.74 | loop fusion | flops 2752512 | bytes 6881284 | tf_op jit(solution)/shard_map/convert.6
  40.8 4.8 %collective-permute-start.1 = (bf16[12,16,768]{2,1,0:T(8,128)(2,1)S(1)}, bf16[12,16,768]{2,1,0:T(8,128)(2,1)S(1)}, u32[]{:S(2)}, u32[]{:S(2)}) collective-permute-start(bf16[12,16,768]{2,1,0:T(8,128)(2,1)S(1)} %get-tuple-element.27), channel_id=1, source_target_pairs={{0,1},{1,2},{2,3},{3,4},{4,5},{5,6},{6,7},{8,9},{9,10},{10,11},{11... | collective-permute-start | bytes 884744 | tf_op jit(solution)/shard_map/ppermute | solution.py:174
  45.6 1.3 collective-permute-start.2
  47.0 1.5 slice.93
  48.5 10.0 %collective-permute-done.1 = bf16[12,16,768]{2,1,0:T(8,128)(2,1)S(1)} collective-permute-done((bf16[12,16,768]{2,1,0:T(8,128)(2,1)S(1)}, bf16[12,16,768]{2,1,0:T(8,128)(2,1)S(1)}, u32[]{:S(2)}, u32[]{:S(2)}) %collective-permute-start.1) | collective-permute-done | bytes 294944 | tf_op jit(solution)/shard_map/ppermute | solution.py:174
  58.5 0.2 fusion.1
  58.7 0.3 fusion.4
  58.9 1.6 collective-permute-start.3
  60.5 0.1 pad_maximum_fusion.3
  60.6 13.0 %all_gather.3 = f32[224,50]{1,0:T(8,128)S(1)} all-gather(f32[56,50]{1,0:T(8,128)S(1)} %pad_maximum_fusion.3), channel_id=1, replica_groups=mesh['band'=4,'row'=8] {'band'}, dimensions={0}, use_global_device_ids=true | all-gather | bytes 56000 | tf_op jit(solution)/shard_map/all_gather | solution.py:198
  73.6 1.3 fusion.3
  74.9 0.3 collective-permute-start.4
  75.3 0.1 fusion.36
  75.4 0.4 rev.10
  75.8 0.4 rev.11
  76.2 0.2 copy.48.col_ref
  76.4 0.2 broadcast_in_dim.63.col_flip_ref
  76.6 0.9 fusion
  77.5 0.6 copy.43
  78.2 2.2 %broadcast_select_fusion.1 = (f32[32,16,388]{2,1,0:T(8,128)S(1)}, f32[32,16,388]{2,1,0:T(8,128)S(1)}) fusion(f32[32,16,388]{2,1,0:T(8,128)} %fusion.3, f32[32,16,388]{2,1,0:T(8,128)} %collective-permute-done.4, pred[]{:T(512)S(6)} %eq.48), kind=kLoop, calls=%fused_computation.31 | loop fusion | flops 397312 | bytes 3178497 | tf_op jit(solution)/shard_map/jit(_where)/select_n | solution.py:284
  80.4 0.4 fusion.30
  80.8 0.1 pad_slice_fusion.1
  80.9 4.4 %collective-permute-start.5 = (bf16[24,32,256]{2,1,0:T(8,128)(2,1)S(1)}, bf16[24,32,256]{2,1,0:T(8,128)(2,1)S(1)}, u32[]{:S(2)}, u32[]{:S(2)}) collective-permute-start(bf16[24,32,256]{2,1,0:T(8,128)(2,1)S(1)} %get-tuple-element.33), channel_id=1, source_target_pairs={{0,1},{1,2},{2,3},{3,4},{4,5},{5,6},{6,7},{8,9},{9,10},{10,11},{11... | collective-permute-start | bytes 1179656 | tf_op jit(solution)/shard_map/ppermute | solution.py:174
  85.4 1.3 collective-permute-start.6
  86.7 19.7 %gram.1 = (bf16[224,32,128]{2,1,0:T(8,128)(2,1)S(1)}, bf16[224,256,256]{2,1,0:T(8,128)(2,1)}) custom-call(f32[224,1,128]{2,1,0:T(1,128)S(1)} %bitcast.37, f32[224,1,128]{2,1,0:T(1,128)S(1)} %bitcast.38, f32[224,1,256]{2,1,0:T(1,128)S(1)} %copy.48.col_ref, f32[224,1,256]{2,1,0:T(1,128)S(1)} %broadcast_in_dim.63.col_flip_ref, ...), custom_call_target="tpu_custom_call" | custom-call | flops 7516192768 | bytes 29360128 | tf_op jit(solution)/shard_map/gram/pallas_call | solution.py:211
  106.4 0.3 slice.97
  106.7 0.1 pad.60
  106.8 0.8 copy-done.4
  107.6 0.1 pad.59.own_ref
  107.7 0.0 copy-start.6
  107.8 1.2 pad_maximum_fusion.p_ref
  109.0 0.1 broadcast_in_dim.29.ridge_ref
  109.1 19.9 %normal.2.own_ref = f32[32,32,256]{2,1,0:T(8,128)S(1)} custom-call(bf16[80,32,256]{2,1,0:T(8,128)(2,1)} %pad_maximum_fusion.p_ref, f32[32,32,256]{2,1,0:T(8,128)S(1)} %pad.59.own_ref, f32[32,256]{1,0:T(8,128)S(1)} %broadcast_in_dim.29.ridge_ref, bf16[7,256,256]{2,1,0:T(8,128)(2,1)S(1)} %bitcast.31, bf16[7,256,256]{2,1,0:T(8,128)(2,1)S(1)} %bitcast.33, ...), custom_call_target="tpu_custom_call" | custom-call | flops 1879048192 | bytes 29360128 | tf_op jit(solution)/shard_map/normal/pallas_call | solution.py:301
  129.0 0.1 convert.12
  129.1 0.1 fusion.35
  129.2 1.8 collective-permute-start.7
  131.0 1.3 collective-permute-start.8
  132.3 3.3 %collective-permute-done.8 = bf16[32,32,24]{2,1,0:T(8,128)(2,1)S(1)} collective-permute-done((bf16[32,32,24]{2,1,0:T(8,128)(2,1)S(1)}, bf16[32,32,24]{2,1,0:T(8,128)(2,1)S(1)}, u32[]{:S(2)}, u32[]{:S(2)}) %collective-permute-start.8) | collective-permute-done | bytes 49184 | tf_op jit(solution)/shard_map/ppermute | solution.py:175
  135.7 0.5 pad_maximum_fusion.2
  136.2 0.1 fusion.34
  136.3 5.7 %collective-permute-start.9 = (bf16[24,32,256]{2,1,0:T(8,128)(2,1)S(1)}, bf16[24,32,256]{2,1,0:T(8,128)(2,1)S(1)}, u32[]{:S(2)}, u32[]{:S(2)}) collective-permute-start(bf16[24,32,256]{2,1,0:T(8,128)(2,1)S(1)} %get-tuple-element.29), channel_id=1, source_target_pairs={{0,1},{1,2},{2,3},{3,4},{4,5},{5,6},{6,7},{8,9},{9,10},{10,11},{11... | collective-permute-start | bytes 1179656 | tf_op jit(solution)/shard_map/ppermute | solution.py:174
  142.0 1.6 collective-permute-start.10
  143.6 4.0 %collective-permute-done.9 = bf16[24,32,256]{2,1,0:T(8,128)(2,1)S(1)} collective-permute-done((bf16[24,32,256]{2,1,0:T(8,128)(2,1)S(1)}, bf16[24,32,256]{2,1,0:T(8,128)(2,1)S(1)}, u32[]{:S(2)}, u32[]{:S(2)}) %collective-permute-start.9) | collective-permute-done | bytes 393248 | tf_op jit(solution)/shard_map/ppermute | solution.py:174
  147.6 5.4 %collective-permute-done.10 = bf16[24,32,256]{2,1,0:T(8,128)(2,1)S(1)} collective-permute-done((bf16[24,32,256]{2,1,0:T(8,128)(2,1)S(1)}, bf16[24,32,256]{2,1,0:T(8,128)(2,1)S(1)}, u32[]{:S(2)}, u32[]{:S(2)}) %collective-permute-start.10) | collective-permute-done | bytes 393248 | tf_op jit(solution)/shard_map/ppermute | solution.py:175
  153.1 1.6 pad_maximum_fusion.1.p_ref
  154.6 19.9 %normal.3 = f32[32,32,256]{2,1,0:T(8,128)S(1)} custom-call(bf16[80,32,256]{2,1,0:T(8,128)(2,1)} %pad_maximum_fusion.1.p_ref, f32[32,32,256]{2,1,0:T(8,128)S(1)} %normal.2.own_ref, f32[32,256]{1,0:T(8,128)S(1)} %broadcast_in_dim.29.ridge_ref, bf16[7,256,256]{2,1,0:T(8,128)(2,1)S(1)} %bitcast.32, bf16[7,256,256]{2,1,0:T(8,128)(2,1)S(1)} %bitcast.34, ...), custom_call_target="tpu_custom_call" | custom-call | flops 1879048192 | bytes 29360128 | tf_op jit(solution)/shard_map/normal/pallas_call | solution.py:301
  174.5 1.4 multiply_reduce_fusion
  175.9 3.2 %stack.23 = f32[5]{0:T(128)S(1)} concatenate(f32[1]{0:T(128)} %bitcast.3, f32[1]{0:T(128)} %bitcast.11, f32[1]{0:T(128)} %bitcast.12, f32[1]{0:T(128)} %bitcast.13, f32[1]{0:T(128)} %bitcast.14), dimensions={0} | concatenate | bytes 40 | tf_op jit(solution)/shard_map/stack | solution.py:335
  179.1 21.5 %all_to_all.5 = f32[32,8,128]{2,1,0:T(8,128)S(1)} all-to-all(f32[32,8,128]{2,1,0:T(8,128)S(1)} %broadcast_in_dim.65), channel_id=1, replica_groups=mesh['band'=4,'row'=8] {'band','row'}, dimensions={0} | all-to-all | bytes 262144 | tf_op jit(solution)/shard_map/all_to_all | solution.py:340
  200.7 0.7 fusion.37
  207.7 1.6 fusion.7
  209.3 1.6 copy.51
  210.9 1.6 copy.50
  (34 shorter events, 0.3 us)
Async XLA Ops:
  0.6 1.9 copy-start
  33.9 3.5 %collective-permute-start = (bf16[56,16,768]{2,1,0:T(8,128)(2,1)}, bf16[56,16,768]{2,1,0:T(8,128)(2,1)}, u32[]{:S(2)}, u32[]{:S(2)}) collective-permute-start(bf16[56,16,768]{2,1,0:T(8,128)(2,1)} %constant_dynamic-slice_fusion), channel_id=1, source_target_pairs={{0,8},{8,0},{16,24},{24,16},{1,9},{9,1},{17,25},{25,17},{2,10},{10... | collective-permute-start | bytes 4128776 | tf_op jit(solution)/shard_map/ppermute | solution.py:269
  40.8 17.6 %collective-permute-start.1 = (bf16[12,16,768]{2,1,0:T(8,128)(2,1)S(1)}, bf16[12,16,768]{2,1,0:T(8,128)(2,1)S(1)}, u32[]{:S(2)}, u32[]{:S(2)}) collective-permute-start(bf16[12,16,768]{2,1,0:T(8,128)(2,1)S(1)} %get-tuple-element.27), channel_id=1, source_target_pairs={{0,1},{1,2},{2,3},{3,4},{4,5},{5,6},{6,7},{8,9},{9,10},{10,11},{11... | collective-permute-start | bytes 884744 | tf_op jit(solution)/shard_map/ppermute | solution.py:174
  45.6 12.8 %collective-permute-start.2 = (bf16[12,16,768]{2,1,0:T(8,128)(2,1)S(1)}, bf16[12,16,768]{2,1,0:T(8,128)(2,1)S(1)}, u32[]{:S(2)}, u32[]{:S(2)}) collective-permute-start(bf16[12,16,768]{2,1,0:T(8,128)(2,1)S(1)} %get-tuple-element.28), channel_id=1, source_target_pairs={{1,0},{2,1},{3,2},{4,3},{5,4},{6,5},{7,6},{9,8},{10,9},{11,10},{12... | collective-permute-start | bytes 884744 | tf_op jit(solution)/shard_map/ppermute | solution.py:175
  58.9 14.6 %collective-permute-start.3 = (bf16[32,16,388]{2,1,0:T(8,128)(2,1)S(1)}, bf16[32,16,388]{2,1,0:T(8,128)(2,1)S(1)}, u32[]{:S(2)}, u32[]{:S(2)}) collective-permute-start(bf16[32,16,388]{2,1,0:T(8,128)(2,1)S(1)} %fusion.4), channel_id=1, source_target_pairs={{0,16},{8,24},{16,0},{24,8},{1,17},{9,25},{17,1},{25,9},{2,18},{10... | collective-permute-start | bytes 1191944 | tf_op jit(solution)/shard_map/ppermute | solution.py:282
  74.9 3.3 %collective-permute-start.4 = (f32[32,16,388]{2,1,0:T(8,128)}, f32[32,16,388]{2,1,0:T(8,128)}, u32[]{:S(2)}, u32[]{:S(2)}) collective-permute-start(f32[32,16,388]{2,1,0:T(8,128)} %fusion.3), channel_id=1, source_target_pairs={{0,8},{8,0},{16,24},{24,16},{1,9},{9,1},{17,25},{25,17},{2,10},{10... | collective-permute-start | bytes 2383880 | tf_op jit(solution)/shard_map/ppermute | solution.py:283
  78.1 30.9 %copy-start.2 = (bf16[7,256,256]{1,2,0:T(8,128)(2,1)}, bf16[7,256,256]{1,2,0:T(8,128)(2,1)S(1)}, u32[]{:S(2)}) copy-start(bf16[7,256,256]{1,2,0:T(8,128)(2,1)S(1)} %copy.43) | copy-start | bytes 2752516
  80.9 26.8 %collective-permute-start.5 = (bf16[24,32,256]{2,1,0:T(8,128)(2,1)S(1)}, bf16[24,32,256]{2,1,0:T(8,128)(2,1)S(1)}, u32[]{:S(2)}, u32[]{:S(2)}) collective-permute-start(bf16[24,32,256]{2,1,0:T(8,128)(2,1)S(1)} %get-tuple-element.33), channel_id=1, source_target_pairs={{0,1},{1,2},{2,3},{3,4},{4,5},{5,6},{6,7},{8,9},{9,10},{10,11},{11... | collective-permute-start | bytes 1179656 | tf_op jit(solution)/shard_map/ppermute | solution.py:174
  85.4 22.4 %collective-permute-start.6 = (bf16[24,32,256]{2,1,0:T(8,128)(2,1)S(1)}, bf16[24,32,256]{2,1,0:T(8,128)(2,1)S(1)}, u32[]{:S(2)}, u32[]{:S(2)}) collective-permute-start(bf16[24,32,256]{2,1,0:T(8,128)(2,1)S(1)} %get-tuple-element.34), channel_id=1, source_target_pairs={{1,0},{2,1},{3,2},{4,3},{5,4},{6,5},{7,6},{9,8},{10,9},{11,10},{12... | collective-permute-start | bytes 1179656 | tf_op jit(solution)/shard_map/ppermute | solution.py:175
  106.3 1.3 copy-start.4
  106.7 67.8 %copy-start.5 = (f32[32,32,170]{2,1,0:T(8,128)}, f32[32,32,170]{2,1,0:T(8,128)S(1)}, u32[]{:S(2)}) copy-start(f32[32,32,170]{2,1,0:T(8,128)S(1)} %slice.97) | copy-start | bytes 2088964
  107.7 1.3 copy-start.6
  129.2 3.1 %collective-permute-start.7 = (bf16[32,32,24]{2,1,0:T(8,128)(2,1)S(1)}, bf16[32,32,24]{2,1,0:T(8,128)(2,1)S(1)}, u32[]{:S(2)}, u32[]{:S(2)}) collective-permute-start(bf16[32,32,24]{2,1,0:T(8,128)(2,1)S(1)} %get-tuple-element.31), channel_id=1, source_target_pairs={{0,8},{8,16},{16,24},{1,9},{9,17},{17,25},{2,10},{10,18},{18,26},{... | collective-permute-start | bytes 147464 | tf_op jit(solution)/shard_map/ppermute | solution.py:174
  131.0 4.7 %collective-permute-start.8 = (bf16[32,32,24]{2,1,0:T(8,128)(2,1)S(1)}, bf16[32,32,24]{2,1,0:T(8,128)(2,1)S(1)}, u32[]{:S(2)}, u32[]{:S(2)}) collective-permute-start(bf16[32,32,24]{2,1,0:T(8,128)(2,1)S(1)} %get-tuple-element.32), channel_id=1, source_target_pairs={{8,0},{16,8},{24,16},{9,1},{17,9},{25,17},{10,2},{18,10},{26,18},{... | collective-permute-start | bytes 147464 | tf_op jit(solution)/shard_map/ppermute | solution.py:175
  136.3 11.3 %collective-permute-start.9 = (bf16[24,32,256]{2,1,0:T(8,128)(2,1)S(1)}, bf16[24,32,256]{2,1,0:T(8,128)(2,1)S(1)}, u32[]{:S(2)}, u32[]{:S(2)}) collective-permute-start(bf16[24,32,256]{2,1,0:T(8,128)(2,1)S(1)} %get-tuple-element.29), channel_id=1, source_target_pairs={{0,1},{1,2},{2,3},{3,4},{4,5},{5,6},{6,7},{8,9},{9,10},{10,11},{11... | collective-permute-start | bytes 1179656 | tf_op jit(solution)/shard_map/ppermute | solution.py:174
  142.0 12.6 %copy-start.3 = (bf16[7,256,256]{1,2,0:T(8,128)(2,1)S(1)}, bf16[7,256,256]{1,2,0:T(8,128)(2,1)}, u32[]{:S(2)}) copy-start(bf16[7,256,256]{1,2,0:T(8,128)(2,1)} %copy-done.2) | copy-start | bytes 2752516
  142.0 11.0 %collective-permute-start.10 = (bf16[24,32,256]{2,1,0:T(8,128)(2,1)S(1)}, bf16[24,32,256]{2,1,0:T(8,128)(2,1)S(1)}, u32[]{:S(2)}, u32[]{:S(2)}) collective-permute-start(bf16[24,32,256]{2,1,0:T(8,128)(2,1)S(1)} %get-tuple-element.30), channel_id=1, source_target_pairs={{1,0},{2,1},{3,2},{4,3},{5,4},{6,5},{7,6},{9,8},{10,9},{11,10},{12... | collective-permute-start | bytes 1179656 | tf_op jit(solution)/shard_map/ppermute | solution.py:175
  209.3 3.2 %copy-start.1 = (bf16[224,32]{0,1:T(8,128)(2,1)S(1)}, bf16[224,32]{0,1:T(8,128)(2,1)}, u32[]{:S(2)}) copy-start(bf16[224,32]{0,1:T(8,128)(2,1)} %param.8) | copy-start | bytes 43012

commit v2 on v1

v2 whole, which is shorter than its diff:
```python
import functools

import jax
import jax.numpy as jnp
from jax import lax
from jax.experimental import pallas as pl
from jax.experimental.pallas import tpu as pltpu
from jax.sharding import PartitionSpec as P

LANES = 128
SUB = 8
BF = jnp.bfloat16
F32 = jnp.float32
VMEM_LIMIT = 50 * 1024 * 1024


def round_up(value, unit):
    return (value + unit - 1) // unit * unit


def group_size(count, most):
    return max(size for size in range(1, most + 1) if count % size == 0)


def dot(lhs, rhs):
    return lax.dot_general(lhs, rhs, (((1,), (0,)), ((), ())), preferred_element_type=F32)


def toeplitz(taps, rows, shift):
    lanes = taps.shape[1]
    pieces = []
    for first in range(0, rows, LANES):
        count = min(LANES, rows - first)
        wide = jnp.broadcast_to(taps, (count, lanes))
        pieces.append(pltpu.roll(wide, (shift + first) % lanes, 1, stride=1, stride_axis=0))
    return jnp.concatenate(pieces, axis=0) if len(pieces) > 1 else pieces[0]


def spread_basis(basis, group, kinds):
    bands = basis.shape[0]
    rows = jnp.arange(bands * SUB)
    lanes = jnp.arange(SUB * kinds)
    up = (rows[:, None] // SUB == jnp.arange(bands)[None, :]).astype(BF)
    out = (jnp.arange(kinds)[:, None] == lanes[None, :] % kinds).astype(BF)
    same = (rows[:, None] % SUB) == (lanes[None, :] // kinds)
    wide = dot(dot(up, basis).astype(BF), out)
    return jnp.where(same, wide, 0.0).astype(BF).reshape(bands // group, group * SUB, SUB * kinds)


def component_first(spread, kinds):
    groups, deep, _ = spread.shape
    split = spread.reshape(groups, deep, SUB, kinds)
    return split.transpose(0, 3, 2, 1).reshape(groups, kinds * SUB, deep)


def adjoint_kernel(columns, radius, obs_ref, taps_ref, mix_ref, out_ref, acc, ys, mats, rows):
    step = pl.program_id(0)
    group, height, _ = obs_ref.shape
    span = ys.shape[3]
    width = 2 * LANES
    tiles = span // width
    chunks = ys.shape[0]
    ext = chunks * SUB
    edge = 2 * SUB
    last = columns // LANES * LANES
    batch = group_size(group, 4)

    @pl.when(step == 0)
    def _():
        acc[...] = jnp.zeros_like(acc)
        mats[...] = jnp.zeros_like(mats)

    @pl.loop(0, group, step=batch)
    def _(start):
        near = lax.broadcasted_iota(jnp.int32, (edge, width), 1) < LANES
        blank = jnp.zeros((edge, width), BF)
        for b in range(batch):
            b = start + b
            ring = toeplitz(taps_ref[b, 4:5], width, -round_up(radius, SUB)).astype(BF)
            top, bottom = ring[:edge], ring[width - edge :]
            mats[b, LANES - edge : LANES] = jnp.where(near, bottom, blank)
            mats[b, LANES : LANES + edge] = jnp.where(near, top, blank)
            mats[b, LANES + edge : LANES + width - edge] = ring[edge : width - edge]
            mats[b, LANES + width - edge : LANES + width] = jnp.where(near, blank, bottom)
            mats[b, LANES + width : LANES + width + edge] = jnp.where(near, blank, top)
            reach = toeplitz(taps_ref[b, 1:2, :LANES], ext, -2 * radius)[:, :height]
            high = reach.astype(BF)
            rows[b, 0] = high
            rows[b, 1] = (reach - high.astype(F32)).astype(BF)

    @pl.loop(0, group, step=batch)
    def _(start):
        fields = []
        for b in range(batch):
            cells = obs_ref[start + b]
            pieces = [jnp.zeros((height, LANES), BF), cells[:, :last]]
            if columns > last:
                fill = jnp.zeros((height, LANES - (columns - last)), BF)
                pieces.append(jnp.concatenate([cells[:, last:], fill], axis=1))
            have = sum(piece.shape[1] for piece in pieces)
            if have < span + width:
                pieces.append(jnp.zeros((height, span + width - have), BF))
            padded = jnp.concatenate(pieces, axis=1)
            stacked = jnp.concatenate(
                [padded[:, t * width : t * width + 2 * width] for t in range(tiles)], axis=0
            )
            mixed = dot(stacked, mats[start + b]).astype(BF)
            fields.append(
                jnp.concatenate([mixed[t * height : (t + 1) * height] for t in range(tiles)], axis=1)
            )
        for b in range(batch):
            done = dot(rows[start + b, 0], fields[b]) + dot(rows[start + b, 1], fields[b])
            for c in range(chunks):
                ys[c, start + b] = done[c * SUB : (c + 1) * SUB]

    for c in range(chunks):
        cells = ys[c].reshape(group * SUB, span).astype(BF)
        acc[c] += dot(mix_ref[0], cells)

    @pl.when(step == pl.num_programs(0) - 1)
    def _():
        out_ref[...] = acc[...].reshape(out_ref.shape).astype(out_ref.dtype)


def gram_kernel(halo, taps_ref, row_mask_ref, col_mask_ref, gr_ref, gl_ref):
    group, height, row_lanes = gr_ref.shape
    size = gl_ref.shape[1]
    for b in range(group):
        left = (toeplitz(taps_ref[b, 3:4, :size], size, -halo) * col_mask_ref[...]).astype(BF)
        right = toeplitz(taps_ref[b, 2:3, :size], size, -halo).astype(BF)
        gl_ref[b] = dot(left, right).astype(BF)
        left = (toeplitz(taps_ref[b, 1:2, :row_lanes], height, 0) * row_mask_ref[...]).astype(BF)
        right = toeplitz(taps_ref[b, 0:1, :row_lanes], row_lanes, 0).astype(BF)
        gr_ref[b] = dot(left, right).astype(BF)


def normal_kernel(
    columns, first, p_ref, own_ref, ridge_ref, sk_ref, pk_ref, gr_ref, gl_ref, out_ref, sums_ref, acc, xs, ys
):
    step = pl.program_id(0)
    group, height, _ = gr_ref.shape
    ext, kinds, lanes = p_ref.shape
    chunks = height // SUB

    @pl.when(step == 0)
    def _():
        acc[...] = jnp.zeros_like(acc)
        xs[...] = jnp.zeros_like(xs)

    for c in range(0, ext, 2 * SUB):
        halves = []
        for s in (c, c + SUB):
            cells = p_ref[s : s + SUB].reshape(SUB * kinds, lanes)
            halves.append(dot(sk_ref[0], cells).reshape(group, SUB, lanes))
        xs[:, c : c + 2 * SUB, :] = jnp.concatenate(halves, axis=1).astype(BF)

    @pl.loop(0, group, step=8)
    def _(start):
        mids = []
        for b in range(8):
            mids.append(dot(gr_ref[start + b], xs[start + b]).astype(BF))
        for b in range(8):
            done = dot(mids[b], gl_ref[start + b])
            for c in range(chunks):
                ys[c, start + b] = done[c * SUB : (c + 1) * SUB]

    for c in range(chunks):
        acc[c] += dot(pk_ref[0], ys[c].reshape(group * SUB, lanes).astype(BF))

    @pl.when(step == pl.num_programs(0) - 1)
    def _():
        lane = lax.broadcasted_iota(jnp.int32, (kinds, SUB, lanes), 2)
        totals = [jnp.zeros((SUB, lanes), F32) for _ in range(3)]
        for c in range(chunks):
            own = own_ref[:, c * SUB : (c + 1) * SUB, :]
            image = acc[c].reshape(kinds, SUB, lanes) + ridge_ref[...] * own
            image = jnp.where(lane < columns, image, 0.0)
            out_ref[:, c * SUB : (c + 1) * SUB, :] = image
            pairs = [own * image]
            if first:
                pairs += [own * own, image * image]
            for i, pair in enumerate(pairs):
                totals[i] = totals[i] + jnp.sum(pair, axis=0)
        flat = [
            jnp.sum(
                jnp.concatenate(
                    [total[:, i : i + LANES] for i in range(0, lanes, LANES)], axis=0
                ),
                axis=0,
                keepdims=True,
            )
            for total in totals
        ]
        row = lax.broadcasted_iota(jnp.int32, (SUB, LANES), 0)
        packed = jnp.zeros((SUB, LANES), F32)
        for i, line in enumerate(flat):
            packed = packed + jnp.where(row == i, jnp.broadcast_to(line, (SUB, LANES)), 0.0)
        sums_ref[...] = packed


def combine_kernel(shared_ref, v0_ref, v1_ref, v2_ref, coef_ref, res_ref):
    columns = coef_ref.shape[2]
    lines = jnp.sum(shared_ref[...], axis=0)
    v01, v00, v11, v12 = [jnp.sum(lines[i : i + 1], axis=1, keepdims=True) for i in range(4)]
    alpha = v00 / v01
    norm = v00 - 2.0 * alpha * v01 + alpha * alpha * v11
    lead = 1.0 + norm / v00
    product = lead * lead * v01 - 2.0 * lead * alpha * v11 + alpha * alpha * v12
    second = norm / product
    one = alpha + second * lead
    two = second * alpha
    for k in range(coef_ref.shape[0]):
        v0, v1, v2 = v0_ref[k], v1_ref[k], v2_ref[k]
        coef_ref[k] = (one * v0 - two * v1)[:, :columns]
        res_ref[k] = (v0 - one * v1 + two * v2)[:, :columns]


def shift_both(low_edge, high_edge, axis):
    count = lax.axis_size(axis)
    from_before = lax.ppermute(high_edge, axis, [(i, i + 1) for i in range(count - 1)])
    from_after = lax.ppermute(low_edge, axis, [(i + 1, i) for i in range(count - 1)])
    return from_before, from_after


def local(observed, row_taps, col_taps, spectral_basis, ridge_weights):
    bands_here, height, columns_all = observed.shape
    taps = row_taps.shape[1]
    radius = (taps - 1) // 2
    halo = 2 * radius
    bands, kinds = spectral_basis.shape
    n_band = lax.axis_size("band")
    n_row = lax.axis_size("row")
    columns = columns_all // n_band
    lanes = round_up(columns + 2 * halo, 2 * LANES)
    me_band = lax.axis_index("band")
    me_row = lax.axis_index("row")
    core = me_band % 2
    chip = me_band // 2
    chips = n_band // 2

    size = lanes

    def widen(values, lead=0):
        return jnp.pad(values, ((0, 0), (lead, 2 * LANES - taps - lead)))[:, None]

    plain = jnp.concatenate([row_taps, col_taps], axis=1)
    everyone = [(plain, me_band)]
    for hop in range(1, n_band):
        moves = [(i, (i + hop) % n_band) for i in range(n_band)]
        everyone.append((lax.ppermute(plain, "band", moves), (me_band - hop) % n_band))
    basis_here = lax.dynamic_slice_in_dim(spectral_basis, me_band * bands_here, bands_here, 0)
    basis_all = jnp.concatenate(
        [lax.dynamic_slice_in_dim(spectral_basis, at * bands_here, bands_here, 0) for _, at in everyone]
    )
    every = jnp.concatenate([values for values, _ in everyone])

    def variants(values):
        row, col = values[:, :taps], values[:, taps:]
        return [widen(row), widen(row[:, ::-1]), widen(col), widen(col[:, ::-1])]

    taps_all = jnp.concatenate(variants(every), axis=1)
    taps_here = jnp.concatenate(variants(plain) + [widen(col_taps, -radius % SUB)], axis=1)

    at = jnp.arange(size)
    edge = me_band * columns - radius + at
    col_mask = ((edge >= 0) & (edge < columns_all) & (at < columns + 2 * radius)).astype(F32)[None]
    at = jnp.arange(LANES)
    edge = me_row * height - radius + at
    row_mask = ((edge >= 0) & (edge < height * n_row) & (at < height + 2 * radius)).astype(F32)[None]
    part = group_size(bands, 16)
    whole = lambda shape: pl.BlockSpec(shape, lambda i: (0,) * len(shape))
    gr, gl = pl.pallas_call(
        functools.partial(gram_kernel, halo),
        grid=(bands // part,),
        in_specs=[
            pl.BlockSpec((part,) + taps_all.shape[1:], lambda i: (i, 0, 0)),
            whole((1, LANES)),
            whole((1, size)),
        ],
        out_specs=[
            pl.BlockSpec((part, height, LANES), lambda i: (i, 0, 0)),
            pl.BlockSpec((part, size, size), lambda i: (i, 0, 0)),
        ],
        out_shape=[
            jax.ShapeDtypeStruct((bands, height, LANES), BF),
            jax.ShapeDtypeStruct((bands, size, size), BF),
        ],
        compiler_params=pltpu.CompilerParams(vmem_limit_bytes=VMEM_LIMIT),
        cost_estimate=pl.CostEstimate(
            flops=bands * 2 * size**3, bytes_accessed=bands * size * size * 2, transcendentals=0
        ),
        name="gram",
    )(taps_all, row_mask, col_mask)

    few = group_size(bands_here, 32)
    span = round_up(columns_all, 2 * LANES)
    ext = height + 2 * radius
    chunks = ext // SUB
    mix = jnp.swapaxes(spread_basis(basis_here, few, kinds), 1, 2)
    summed = pl.pallas_call(
        functools.partial(adjoint_kernel, columns_all, radius),
        grid=(bands_here // few,),
        in_specs=[
            pl.BlockSpec((few, height, columns_all), lambda i: (i, 0, 0)),
            pl.BlockSpec((few,) + taps_here.shape[1:], lambda i: (i, 0, 0)),
            pl.BlockSpec((1,) + mix.shape[1:], lambda i: (i, 0, 0)),
        ],
        out_specs=whole((ext, kinds, span)),
        out_shape=jax.ShapeDtypeStruct((ext, kinds, span), BF),
        scratch_shapes=[
            pltpu.VMEM((chunks, SUB * kinds, span), F32),
            pltpu.VMEM((chunks, few, SUB, span), F32),
            pltpu.VMEM((few, 4 * LANES, 2 * LANES), BF),
            pltpu.VMEM((few, 2, ext, height), BF),
        ],
        compiler_params=pltpu.CompilerParams(vmem_limit_bytes=VMEM_LIMIT),
        cost_estimate=pl.CostEstimate(
            flops=bands_here * 2 * 96 * 512 * 256, bytes_accessed=observed.size * 2, transcendentals=0
        ),
        name="adjoint",
    )(observed, taps_here, mix)

    half = kinds // 2
    keep = lax.dynamic_slice_in_dim(summed, core * half, half, 1)
    give = lax.dynamic_slice_in_dim(summed, (1 - core) * half, half, 1)
    pairs = [(i, i ^ 1) for i in range(n_band)]
    got = lax.ppermute(give, "band", pairs)
    pair = keep.astype(F32) + got.astype(F32)
    before, after = shift_both(pair[:radius].astype(BF), pair[ext - radius :].astype(BF), "row")
    rows = pair[radius : ext - radius]
    pad = ((0, height - radius), (0, 0), (0, 0))
    rows = rows + jnp.pad(before.astype(F32), pad) + jnp.pad(after.astype(F32), (pad[0][::-1],) + pad[1:])
    rows = jnp.pad(rows[:, :, :columns_all], ((0, 0), (0, 0), (halo, halo)))
    wide = 2 * columns + 2 * halo
    total = lax.dynamic_slice_in_dim(rows, chip * 2 * columns, wide, 2)
    for hop in range(1, chips):
        target = (chip + hop) % chips
        piece = lax.dynamic_slice_in_dim(rows, target * 2 * columns, wide, 2).astype(BF)
        moves = [(i, (i + 2 * hop) % n_band) for i in range(n_band)]
        total = total + lax.ppermute(piece, "band", moves).astype(F32)
    other = lax.ppermute(total, "band", pairs)
    first = jnp.where(core == 0, total, other)
    second = jnp.where(core == 0, other, total)
    total = jnp.concatenate([first, second], axis=1)
    window = lax.dynamic_slice_in_dim(total, core * columns, columns + 2 * halo, 2)
    v0 = jnp.pad(window[:, :, halo : halo + columns], ((0, 0), (0, 0), (0, lanes - columns)))
    v0 = jnp.swapaxes(v0, 0, 1)
    window = jnp.pad(window.astype(BF), ((0, 0), (0, 0), (0, lanes - columns - 2 * halo)))

    group = group_size(bands, 32)
    sk = spread_basis(basis_all, group, kinds)
    pk = component_first(sk, kinds)
    ridge = jnp.broadcast_to(ridge_weights[:, None, None], (kinds, SUB, lanes))
    tall = height + 2 * halo
    block = lambda shape: pl.BlockSpec((group,) + shape, lambda i: (i, 0, 0))

    def normal_map(window, own, first):
        before, after = shift_both(window[:halo], window[height - halo :], "row")
        cells = jnp.concatenate([before, window, after], axis=0)
        return pl.pallas_call(
            functools.partial(normal_kernel, columns, first),
            grid=(bands // group,),
            in_specs=[
                whole((tall, kinds, lanes)),
                whole((kinds, height, lanes)),
                whole((kinds, SUB, lanes)),
                pl.BlockSpec((1,) + sk.shape[1:], lambda i: (i, 0, 0)),
                pl.BlockSpec((1,) + pk.shape[1:], lambda i: (i, 0, 0)),
                block((height, LANES)),
                block((size, size)),
            ],
            out_specs=[whole((kinds, height, lanes)), whole((SUB, LANES))],
            out_shape=[
                jax.ShapeDtypeStruct((kinds, height, lanes), F32),
                jax.ShapeDtypeStruct((SUB, LANES), F32),
            ],
            scratch_shapes=[
                pltpu.VMEM((height // SUB, SUB * kinds, lanes), F32),
                pltpu.VMEM((group, LANES, lanes), BF),
                pltpu.VMEM((height // SUB, group, SUB, lanes), F32),
            ],
            compiler_params=pltpu.CompilerParams(vmem_limit_bytes=VMEM_LIMIT),
            cost_estimate=pl.CostEstimate(
                flops=bands * 2 * 32 * 512 * 256, bytes_accessed=bands * size * size * 2, transcendentals=0
            ),
            name="normal",
        )(cells, own, ridge, sk, pk, gr, gl)

    v1, sums1 = normal_map(window, v0, True)
    near = jnp.swapaxes(v1[:, :, :columns].astype(BF), 0, 1)
    before, after = shift_both(near[:, :, :halo], near[:, :, columns - halo :], "band")
    window = jnp.concatenate(
        [before, near, after, jnp.zeros((height, kinds, lanes - columns - 2 * halo), BF)], axis=2
    )
    v2, sums2 = normal_map(window, v1, False)

    sums = jnp.concatenate([sums1[:3], sums2[:1], jnp.zeros((SUB - 4, LANES), F32)])
    mine = jnp.broadcast_to(sums[None], (n_band * n_row, SUB, LANES))
    shared = lax.all_to_all(mine, ("band", "row"), 0, 0, tiled=True)
    out = jax.ShapeDtypeStruct((kinds, height, columns), F32)
    return pl.pallas_call(
        combine_kernel,
        out_shape=[out, out],
        compiler_params=pltpu.CompilerParams(vmem_limit_bytes=VMEM_LIMIT),
        name="combine",
    )(shared, v0, v1, v2)


def solution(mesh):
    in_specs = (P("band", "row", None), P("band", None), P("band", None), P(), P())
    out_specs = (P(None, "row", "band"), P(None, "row", "band"))
    return jax.shard_map(local, mesh=mesh, in_specs=in_specs, out_specs=out_specs, check_vma=False)
```

time: 213 us -> 194 us (0.911)
  waiting for transfers between devices: 25.9 us -> 39.3 us
  blocking collectives: 34.5 us -> 21.6 us
  Pallas kernels: 89 us -> 76.9 us
  between operations: 7.54 us -> 1.38 us
  other arithmetic: 13.9 us -> 10.5 us
  starting transfers between devices: 24.6 us -> 27 us
    pallas_call x1, Pallas kernels: 29.5 us -> 14.3 us  [local(): pl.pallas_call(functools.partial(adjoint_kernel, columns_all, radius), gr...]
    all_gather x1 -> x0, blocking collectives: 13 us -> none  [local(): lax.all_gather(jnp.concatenate([row_taps, col_taps], axis=1), 'band', til...]
    ppermute x1, waiting for transfers between devices: 0.01 us -> 10.9 us  [local(): total = total + lax.ppermute(piece, 'band', moves).astype(F32)]
    ppermute x4, waiting for transfers between devices: 14 us -> 17.6 us  [shift_both(): lax.ppermute(high_edge, axis, [(i, i + 1) for i in range(count - 1)])]
    another operation x2 -> x1, other arithmetic: 3.45 us -> 0.58 us
    pallas_call x2 -> x3, Pallas kernels: 39.8 us -> 42.7 us  [the longest x2 40.9 us: normal_map(): pl.pallas_call(functools.partial(normal_kernel, columns, first), grid=(ba...]
    unnamed x18 -> x31, local copies, waits for them, and re-layouts: 5.61 us -> 3.05 us
    another operation x1, local copies, waits for them, and re-layouts: 3.21 us -> 0.99 us  [component_first(): split = spread.reshape(groups, deep, SUB, kinds)]
  transfers between devices with their start and end apart: 11 -> 14, of which waited for: 5 -> 6; matrix products, arithmetic and copies ran while one was open for 2% -> 6% of each run, Pallas kernels for 9% -> 10%
where the time goes in v2:
time: 194 us; the launch traced here: 193 us
  Pallas kernels  76.9 us (40%)
  waiting for transfers between devices  39.3 us (20%)
  starting transfers between devices  27 us (14%)
  blocking collectives  21.6 us (11%)
  local copies, waits for them, and re-layouts  15.3 us (8%)
  other arithmetic  10.5 us (5%)
    pallas_call x2, Pallas kernels, normal_map(): pl.pallas_call(functools.partial(normal_kernel, columns, first), grid=(ba...  40.9 us
    all_to_all x1, blocking collectives, local(): shared = lax.all_to_all(mine, ('band', 'row'), 0, 0, tiled=True)  21.6 us
    pallas_call x1, Pallas kernels, local(): pl.pallas_call(functools.partial(gram_kernel, halo), grid=(bands // part,...  19.9 us
    ppermute x4, starting transfers between devices, shift_both(): lax.ppermute(high_edge, axis, [(i, i + 1) for i in range(count - 1)])  17.7 us
    ppermute x4, waiting for transfers between devices, shift_both(): lax.ppermute(high_edge, axis, [(i, i + 1) for i in range(count - 1)])  17.6 us
    pallas_call x1, Pallas kernels, local(): pl.pallas_call(functools.partial(adjoint_kernel, columns_all, radius), gr...  14.3 us
    ppermute x1, waiting for transfers between devices, local(): total = total + lax.ppermute(piece, 'band', moves).astype(F32)  10.9 us
    ppermute x4, waiting for transfers between devices, shift_both(): lax.ppermute(low_edge, axis, [(i + 1, i) for i in range(count - 1)])  8.11 us
  transfers between devices with their start and end apart: 14, of which 6 were waited for; matrix products, arithmetic and copies ran while one was open for 6% of the time, Pallas kernels for 10%

profile of v2, /device:TPU:0, one launch (start us, length us, event | category | flops | bytes accessed | tf_op | source)
XLA Modules:
  0.0 193.2 jit_solution(1725690255397460637)
XLA Ops:
  0.8 0.8 copy.24
  1.7 0.8 copy.22
  2.9 1.6 constant_dynamic-slice_fusion.2
  4.5 0.4 fusion.2
  4.9 0.1 copy.27
  5.1 0.5 concatenate.30.taps_ref
  5.6 14.3 %adjoint.1 = bf16[56,32,768]{2,1,0:T(8,128)(2,1)S(1)} custom-call(bf16[56,32,680]{2,1,0:T(8,128)(2,1)} %obs_ref.1, f32[56,5,256]{2,1,0:T(8,128)S(1)} %concatenate.30.taps_ref, bf16[2,256,224]{2,1,0:T(8,128)(2,1)S(1)} %bitcast.24), custom_call_target="tpu_custom_call" | custom-call | flops 1409286144 | bytes 2437120 | tf_op jit(solution)/shard_map/adjoint/pallas_call | solution.py:300
  19.9 0.3 constant_dynamic-slice_fusion.4
  20.2 0.4 copy.40
  20.6 0.5 collective-permute-start
  21.1 2.8 %collective-permute-done = bf16[56,16,768]{2,0,1:T(8,128)(2,1)S(1)} collective-permute-done((bf16[56,16,768]{2,0,1:T(8,128)(2,1)S(1)}, bf16[56,16,768]{2,0,1:T(8,128)(2,1)S(1)}, u32[]{:S(2)}, u32[]{:S(2)}) %collective-permute-start) | collective-permute-done | bytes 1376288 | tf_op jit(solution)/shard_map/ppermute | solution.py:327
  23.9 0.6 fusion.41
  24.5 0.8 fusion.44
  25.3 5.5 %collective-permute-start.1 = (bf16[12,16,768]{2,0,1:T(8,128)(2,1)}, bf16[12,16,768]{2,0,1:T(8,128)(2,1)}, u32[]{:S(2)}, u32[]{:S(2)}) collective-permute-start(bf16[12,16,768]{2,0,1:T(8,128)(2,1)} %get-tuple-element.22), channel_id=1, source_target_pairs={{0,1},{1,2},{2,3},{3,4},{4,5},{5,6},{6,7},{8,9},{9,10},{10,11},{11... | collective-permute-start | bytes 884744 | tf_op jit(solution)/shard_map/ppermute | solution.py:220
  30.8 1.3 collective-permute-start.2
  32.2 1.0 collective-permute-start.9
  33.2 0.6 collective-permute-start.8
  33.8 0.2 collective-permute-start.7
  34.0 0.2 slice.67
  34.1 13.4 %collective-permute-done.1 = bf16[12,16,768]{2,0,1:T(8,128)(2,1)} collective-permute-done((bf16[12,16,768]{2,0,1:T(8,128)(2,1)}, bf16[12,16,768]{2,0,1:T(8,128)(2,1)}, u32[]{:S(2)}, u32[]{:S(2)}) %collective-permute-start.1) | collective-permute-done | bytes 294944 | tf_op jit(solution)/shard_map/ppermute | solution.py:220
  47.5 1.3 fusion.1
  48.9 0.3 fusion.4
  49.2 1.6 collective-permute-start.3
  50.8 0.8 fusion
  51.6 10.9 %collective-permute-done.3 = bf16[32,16,388]{2,0,1:T(8,128)(2,1)} collective-permute-done((bf16[32,16,388]{2,0,1:T(8,128)(2,1)S(1)}, bf16[32,16,388]{2,0,1:T(8,128)(2,1)}, u32[]{:S(2)}, u32[]{:S(2)}) %collective-permute-start.3) | collective-permute-done | bytes 397344 | tf_op jit(solution)/shard_map/ppermute | solution.py:340
  62.5 2.4 %fusion.3 = f32[32,16,388]{2,0,1:T(8,128)} fusion(s32[]{:T(128)S(6)} %select_n.156, f32[32,16,680]{2,0,1:T(8,128)S(1)} %fusion.1, bf16[32,16,388]{2,0,1:T(8,128)(2,1)} %collective-permute-done.3), kind=kLoop, calls=%fused_computation.16 | loop fusion | flops 397312 | bytes 2584580 | tf_op jit(solution)/shard_map/add | solution.py:340
  64.8 0.6 copy.30
  65.5 1.0 reshape_reshape.3
  66.5 0.6 copy.45
  67.1 0.8 pad_maximum_fusion.4
  68.0 0.4 rev.14
  68.4 0.2 copy.35
  68.7 0.4 rev.15
  69.1 0.2 broadcast_in_dim.78
  69.3 0.2 copy.36
  69.5 0.2 copy.34
  69.8 0.9 pad_maximum_fusion.2.taps_ref
  70.6 1.8 broadcast_select_fusion.1
  72.5 0.4 fusion.42
  72.9 0.1 pad_slice_fusion.1
  73.0 4.4 %collective-permute-start.5 = (bf16[24,32,256]{2,0,1:T(8,128)(2,1)S(1)}, bf16[24,32,256]{2,0,1:T(8,128)(2,1)S(1)}, u32[]{:S(2)}, u32[]{:S(2)}) collective-permute-start(bf16[24,32,256]{2,0,1:T(8,128)(2,1)S(1)} %get-tuple-element.28), channel_id=1, source_target_pairs={{0,1},{1,2},{2,3},{3,4},{4,5},{5,6},{6,7},{8,9},{9,10},{10,11},{11... | collective-permute-start | bytes 1179656 | tf_op jit(solution)/shard_map/ppermute | solution.py:220
  77.4 1.3 collective-permute-start.6
  78.7 19.9 %gram.1 = (bf16[224,32,128]{2,1,0:T(8,128)(2,1)S(1)}, bf16[224,256,256]{2,1,0:T(8,128)(2,1)}) custom-call(f32[224,4,256]{2,1,0:T(4,128)S(1)} %pad_maximum_fusion.2.taps_ref, f32[1,128]{1,0:T(1,128)S(1)} %and_convert_fusion.1.row_mask_ref, f32[1,256]{1,0:T(1,128)S(1)} %and_convert_fusion.col_mask_ref), custom_call_target="tpu_custom_call" | custom-call | flops 7516192768 | bytes 29360128 | tf_op jit(solution)/shard_map/gram/pallas_call | solution.py:272
  98.6 0.3 slice.71
  98.9 0.1 pad.66
  99.0 0.8 copy-done.3
  99.8 1.1 pad_bitcast_fusion.own_ref.v0_ref
  101.0 1.5 copy.37.p_ref
  102.6 20.5 %normal.2 = (f32[32,32,256]{2,1,0:T(8,128)S(1)}, f32[8,128]{1,0:T(8,128)S(1)}) custom-call(bf16[80,32,256]{2,1,0:T(8,128)(2,1)} %copy.37.p_ref, f32[32,32,256]{2,1,0:T(8,128)} %pad_bitcast_fusion.own_ref.v0_ref, f32[32,8,256]{2,1,0:T(8,128)S(1)} %broadcast_in_dim.73.ridge_ref, bf16[7,256,256]{2,1,0:T(8,128)(2,1)S(1)} %bitcast.20, ...), custom_call_target="tpu_custom_call" | custom-call | flops 1879048192 | bytes 29360128 | tf_op jit(solution)/shard_map/normal/pallas_call | solution.py:360
  123.1 0.6 copy.38
  123.7 0.1 fusion.46
  123.8 0.2 copy-done.1
  124.1 2.1 %collective-permute-start.10 = (bf16[32,32,24]{2,1,0:T(8,128)(2,1)S(1)}, bf16[32,32,24]{2,1,0:T(8,128)(2,1)S(1)}, u32[]{:S(2)}, u32[]{:S(2)}) collective-permute-start(bf16[32,32,24]{2,1,0:T(8,128)(2,1)S(1)} %get-tuple-element.26), channel_id=1, source_target_pairs={{0,8},{8,16},{16,24},{1,9},{9,17},{17,25},{2,10},{10,18},{18,26},{... | collective-permute-start | bytes 147464 | tf_op jit(solution)/shard_map/ppermute | solution.py:220
  126.2 1.5 collective-permute-start.11
  127.7 2.8 %collective-permute-done.11 = bf16[32,32,24]{2,1,0:T(8,128)(2,1)S(1)} collective-permute-done((bf16[32,32,24]{2,1,0:T(8,128)(2,1)S(1)}, bf16[32,32,24]{2,1,0:T(8,128)(2,1)S(1)}, u32[]{:S(2)}, u32[]{:S(2)}) %collective-permute-start.11) | collective-permute-done | bytes 49184 | tf_op jit(solution)/shard_map/ppermute | solution.py:221
  130.6 0.5 pad_maximum_fusion.3
  131.1 5.7 %collective-permute-start.12 = (bf16[24,32,256]{2,1,0:T(8,128)(2,1)S(1)}, bf16[24,32,256]{2,1,0:T(8,128)(2,1)S(1)}, u32[]{:S(2)}, u32[]{:S(2)}) collective-permute-start(bf16[24,32,256]{2,1,0:T(8,128)(2,1)S(1)} %get-tuple-element.24), channel_id=1, source_target_pairs={{0,1},{1,2},{2,3},{3,4},{4,5},{5,6},{6,7},{8,9},{9,10},{10,11},{11... | collective-permute-start | bytes 1179656 | tf_op jit(solution)/shard_map/ppermute | solution.py:220
  136.8 1.3 collective-permute-start.13
  138.2 4.2 %collective-permute-done.12 = bf16[24,32,256]{2,1,0:T(8,128)(2,1)S(1)} collective-permute-done((bf16[24,32,256]{2,1,0:T(8,128)(2,1)S(1)}, bf16[24,32,256]{2,1,0:T(8,128)(2,1)S(1)}, u32[]{:S(2)}, u32[]{:S(2)}) %collective-permute-start.12) | collective-permute-done | bytes 393248 | tf_op jit(solution)/shard_map/ppermute | solution.py:220
  142.4 5.3 %collective-permute-done.13 = bf16[24,32,256]{2,1,0:T(8,128)(2,1)S(1)} collective-permute-done((bf16[24,32,256]{2,1,0:T(8,128)(2,1)S(1)}, bf16[24,32,256]{2,1,0:T(8,128)(2,1)S(1)}, u32[]{:S(2)}, u32[]{:S(2)}) %collective-permute-start.13) | collective-permute-done | bytes 393248 | tf_op jit(solution)/shard_map/ppermute | solution.py:221
  147.7 1.6 pad_maximum_fusion.1.p_ref
  149.3 20.4 %normal.3 = (f32[32,32,256]{2,1,0:T(8,128)S(1)}, f32[8,128]{1,0:T(8,128)S(1)}) custom-call(bf16[80,32,256]{2,1,0:T(8,128)(2,1)} %pad_maximum_fusion.1.p_ref, f32[32,32,256]{2,1,0:T(8,128)} %copy-done.1, f32[32,8,256]{2,1,0:T(8,128)S(1)} %broadcast_in_dim.73.ridge_ref, bf16[7,256,256]{2,1,0:T(8,128)(2,1)S(1)} %bitcast.21, bf16[7,256,256]{2,1,0:T(8,128)(2,1)S(1)} %bitcast.23, ...), custom_call_target="tpu_custom_call" | custom-call | flops 1879048192 | bytes 29360128 | tf_op jit(solution)/shard_map/normal/pallas_call | solution.py:360
  169.8 21.6 %all_to_all.5.shared_ref = f32[32,8,128]{2,1,0:T(8,128)S(1)} all-to-all(f32[32,8,128]{2,1,0:T(8,128)S(1)} %broadcast_in_dim.81), channel_id=1, replica_groups=mesh['band'=4,'row'=8] {'band','row'}, dimensions={0} | all-to-all | bytes 262144 | tf_op jit(solution)/shard_map/all_to_all | solution.py:399
  191.5 1.8 combine.1
  (67 shorter events, 1.3 us)
Async XLA Ops:
  0.7 4.3 %copy-start.9 = (s32[256]{0:T(256)}, s32[256]{0:T(256)S(1)}, u32[]{:S(2)}) copy-start(s32[256]{0:T(256)S(1)} %get-tuple-element.40) | copy-start | bytes 3076
  0.7 4.3 %copy-start.11 = (s32[256]{0:T(256)}, s32[256]{0:T(256)S(1)}, u32[]{:S(2)}) copy-start(s32[256]{0:T(256)S(1)} %get-tuple-element.41) | copy-start | bytes 3076
  4.5 0.6 copy-start.5
  20.6 3.3 %collective-permute-start = (bf16[56,16,768]{2,0,1:T(8,128)(2,1)S(1)}, bf16[56,16,768]{2,0,1:T(8,128)(2,1)S(1)}, u32[]{:S(2)}, u32[]{:S(2)}) collective-permute-start(bf16[56,16,768]{2,0,1:T(8,128)(2,1)S(1)} %copy.40), channel_id=1, source_target_pairs={{0,8},{8,0},{16,24},{24,16},{1,9},{9,1},{17,25},{25,17},{2,10},{10... | collective-permute-start | bytes 4128776 | tf_op jit(solution)/shard_map/ppermute | solution.py:327
  25.3 22.2 %collective-permute-start.1 = (bf16[12,16,768]{2,0,1:T(8,128)(2,1)}, bf16[12,16,768]{2,0,1:T(8,128)(2,1)}, u32[]{:S(2)}, u32[]{:S(2)}) collective-permute-start(bf16[12,16,768]{2,0,1:T(8,128)(2,1)} %get-tuple-element.22), channel_id=1, source_target_pairs={{0,1},{1,2},{2,3},{3,4},{4,5},{5,6},{6,7},{8,9},{9,10},{10,11},{11... | collective-permute-start | bytes 884744 | tf_op jit(solution)/shard_map/ppermute | solution.py:220
  30.8 16.6 %collective-permute-start.2 = (bf16[12,16,768]{2,0,1:T(8,128)(2,1)S(1)}, bf16[12,16,768]{2,0,1:T(8,128)(2,1)}, u32[]{:S(2)}, u32[]{:S(2)}) collective-permute-start(bf16[12,16,768]{2,0,1:T(8,128)(2,1)S(1)} %get-tuple-element.23), channel_id=1, source_target_pairs={{1,0},{2,1},{3,2},{4,3},{5,4},{6,5},{7,6},{9,8},{10,9},{11,10},{12... | collective-permute-start | bytes 884744 | tf_op jit(solution)/shard_map/ppermute | solution.py:221
  32.2 34.8 %collective-permute-start.9 = (f32[56,50]{1,0:T(8,128)S(1)}, f32[56,50]{1,0:T(8,128)S(1)}, u32[]{:S(2)}, u32[]{:S(2)}) collective-permute-start(f32[56,50]{1,0:T(8,128)S(1)} %pad_maximum_fusion.5), channel_id=1, source_target_pairs={{0,24},{8,0},{16,8},{24,16},{1,25},{9,1},{17,9},{25,17},{2,26},{10... | collective-permute-start | bytes 33608 | tf_op jit(solution)/shard_map/ppermute | solution.py:250
  33.2 33.9 %collective-permute-start.8 = (f32[56,50]{1,0:T(8,128)S(1)}, f32[56,50]{1,0:T(8,128)S(1)}, u32[]{:S(2)}, u32[]{:S(2)}) collective-permute-start(f32[56,50]{1,0:T(8,128)S(1)} %pad_maximum_fusion.5), channel_id=1, source_target_pairs={{0,16},{8,24},{16,0},{24,8},{1,17},{9,25},{17,1},{25,9},{2,18},{10... | collective-permute-start | bytes 33608 | tf_op jit(solution)/shard_map/ppermute | solution.py:250
  33.8 33.3 %collective-permute-start.7 = (f32[56,50]{1,0:T(8,128)S(1)}, f32[56,50]{1,0:T(8,128)}, u32[]{:S(2)}, u32[]{:S(2)}) collective-permute-start(f32[56,50]{1,0:T(8,128)S(1)} %pad_maximum_fusion.5), channel_id=1, source_target_pairs={{0,8},{8,16},{16,24},{24,0},{1,9},{9,17},{17,25},{25,1},{2,10},{10... | collective-permute-start | bytes 33608 | tf_op jit(solution)/shard_map/ppermute | solution.py:250
  48.8 1.9 copy-start.4
  48.8 1.9 copy-start.6
  48.9 1.9 copy-start.7
  48.9 1.9 copy-start.8
  48.9 1.9 copy-start.10
  48.9 1.9 copy-start.12
  49.2 13.3 %collective-permute-start.3 = (bf16[32,16,388]{2,0,1:T(8,128)(2,1)S(1)}, bf16[32,16,388]{2,0,1:T(8,128)(2,1)}, u32[]{:S(2)}, u32[]{:S(2)}) collective-permute-start(bf16[32,16,388]{2,0,1:T(8,128)(2,1)S(1)} %fusion.4), channel_id=1, source_target_pairs={{0,16},{8,24},{16,0},{24,8},{1,17},{9,25},{17,1},{25,9},{2,18},{10... | collective-permute-start | bytes 1191944 | tf_op jit(solution)/shard_map/ppermute | solution.py:340
  64.8 5.8 %collective-permute-start.4 = (f32[32,16,388]{2,0,1:T(8,128)}, f32[32,16,388]{2,0,1:T(8,128)}, u32[]{:S(2)}, u32[]{:S(2)}) collective-permute-start(f32[32,16,388]{2,0,1:T(8,128)} %fusion.3), channel_id=1, source_target_pairs={{0,8},{8,0},{16,24},{24,16},{1,9},{9,1},{17,25},{25,17},{2,10},{10... | collective-permute-start | bytes 2383880 | tf_op jit(solution)/shard_map/ppermute | solution.py:341
  73.0 27.9 %collective-permute-start.5 = (bf16[24,32,256]{2,0,1:T(8,128)(2,1)S(1)}, bf16[24,32,256]{2,0,1:T(8,128)(2,1)S(1)}, u32[]{:S(2)}, u32[]{:S(2)}) collective-permute-start(bf16[24,32,256]{2,0,1:T(8,128)(2,1)S(1)} %get-tuple-element.28), channel_id=1, source_target_pairs={{0,1},{1,2},{2,3},{3,4},{4,5},{5,6},{6,7},{8,9},{9,10},{10,11},{11... | collective-permute-start | bytes 1179656 | tf_op jit(solution)/shard_map/ppermute | solution.py:220
  77.4 23.5 %collective-permute-start.6 = (bf16[24,32,256]{2,0,1:T(8,128)(2,1)S(1)}, bf16[24,32,256]{2,0,1:T(8,128)(2,1)S(1)}, u32[]{:S(2)}, u32[]{:S(2)}) collective-permute-start(bf16[24,32,256]{2,0,1:T(8,128)(2,1)S(1)} %get-tuple-element.29), channel_id=1, source_target_pairs={{1,0},{2,1},{3,2},{4,3},{5,4},{6,5},{7,6},{9,8},{10,9},{11,10},{12... | collective-permute-start | bytes 1179656 | tf_op jit(solution)/shard_map/ppermute | solution.py:221
  98.6 1.2 copy-start.3
  101.0 1.5 copy-start.13
  123.1 1.0 copy-start.1
  124.1 3.6 %collective-permute-start.10 = (bf16[32,32,24]{2,1,0:T(8,128)(2,1)S(1)}, bf16[32,32,24]{2,1,0:T(8,128)(2,1)S(1)}, u32[]{:S(2)}, u32[]{:S(2)}) collective-permute-start(bf16[32,32,24]{2,1,0:T(8,128)(2,1)S(1)} %get-tuple-element.26), channel_id=1, source_target_pairs={{0,8},{8,16},{16,24},{1,9},{9,17},{17,25},{2,10},{10,18},{18,26},{... | collective-permute-start | bytes 147464 | tf_op jit(solution)/shard_map/ppermute | solution.py:220
  126.2 4.3 %collective-permute-start.11 = (bf16[32,32,24]{2,1,0:T(8,128)(2,1)S(1)}, bf16[32,32,24]{2,1,0:T(8,128)(2,1)S(1)}, u32[]{:S(2)}, u32[]{:S(2)}) collective-permute-start(bf16[32,32,24]{2,1,0:T(8,128)(2,1)S(1)} %get-tuple-element.27), channel_id=1, source_target_pairs={{8,0},{16,8},{24,16},{9,1},{17,9},{25,17},{10,2},{18,10},{26,18},{... | collective-permute-start | bytes 147464 | tf_op jit(solution)/shard_map/ppermute | solution.py:221
  131.1 11.3 %collective-permute-start.12 = (bf16[24,32,256]{2,1,0:T(8,128)(2,1)S(1)}, bf16[24,32,256]{2,1,0:T(8,128)(2,1)S(1)}, u32[]{:S(2)}, u32[]{:S(2)}) collective-permute-start(bf16[24,32,256]{2,1,0:T(8,128)(2,1)S(1)} %get-tuple-element.24), channel_id=1, source_target_pairs={{0,1},{1,2},{2,3},{3,4},{4,5},{5,6},{6,7},{8,9},{9,10},{10,11},{11... | collective-permute-start | bytes 1179656 | tf_op jit(solution)/shard_map/ppermute | solution.py:220
  136.8 10.9 %collective-permute-start.13 = (bf16[24,32,256]{2,1,0:T(8,128)(2,1)S(1)}, bf16[24,32,256]{2,1,0:T(8,128)(2,1)S(1)}, u32[]{:S(2)}, u32[]{:S(2)}) collective-permute-start(bf16[24,32,256]{2,1,0:T(8,128)(2,1)S(1)} %get-tuple-element.25), channel_id=1, source_target_pairs={{1,0},{2,1},{3,2},{4,3},{5,4},{6,5},{7,6},{9,8},{10,9},{11,10},{12... | collective-permute-start | bytes 1179656 | tf_op jit(solution)/shard_map/ppermute | solution.py:221
  149.3 42.2 %copy-start = (f32[32,32,256]{2,1,0:T(8,128)S(1)}, f32[32,32,256]{2,1,0:T(8,128)}, u32[]{:S(2)}) copy-start(f32[32,32,256]{2,1,0:T(8,128)} %pad_bitcast_fusion.own_ref.v0_ref) | copy-start | bytes 3145732
  149.3 42.2 %copy-start.2 = (f32[32,32,256]{2,1,0:T(8,128)S(1)}, f32[32,32,256]{2,1,0:T(8,128)}, u32[]{:S(2)}) copy-start(f32[32,32,256]{2,1,0:T(8,128)} %copy-done.1) | copy-start | bytes 3145732

commit v3 on v2

--- a/solution.py
+++ b/solution.py
@@ -20,6 +20,13 @@
 
 def group_size(count, most):
     return max(size for size in range(1, most + 1) if count % size == 0)
+
+
+def packed_blocks(columns, halo):
+    out = []
+    for first in range(0, columns, LANES):
+        out.append((first, round_up(min(first + LANES, columns) + 2 * halo, 2 * SUB)))
+    return out
 
 
 def dot(lhs, rhs):
@@ -122,20 +129,28 @@
         out_ref[...] = acc[...].reshape(out_ref.shape).astype(out_ref.dtype)
 
 
-def gram_kernel(halo, taps_ref, row_mask_ref, col_mask_ref, gr_ref, gl_ref):
+def gram_kernel(columns, halo, taps_ref, row_mask_ref, col_mask_ref, gr_ref, gl_ref):
     group, height, row_lanes = gr_ref.shape
-    size = gl_ref.shape[1]
+    size = col_mask_ref.shape[1]
+    blocks = packed_blocks(columns, halo)
+    tall = max(end for _, end in blocks)
+    inner = round_up(columns + halo, 2 * SUB)
     for b in range(group):
-        left = (toeplitz(taps_ref[b, 3:4, :size], size, -halo) * col_mask_ref[...]).astype(BF)
-        right = toeplitz(taps_ref[b, 2:3, :size], size, -halo).astype(BF)
-        gl_ref[b] = dot(left, right).astype(BF)
+        left = (toeplitz(taps_ref[b, 3:4, :size], tall, -halo) * col_mask_ref[...]).astype(BF)
+        right = toeplitz(taps_ref[b, 2:3, :size], inner, -halo).astype(BF)
+        right = jnp.concatenate([right, jnp.zeros((size - inner, size), BF)], axis=0)
+        done = dot(left, right).astype(BF)
+        at = 0
+        for i, (start, end) in enumerate(blocks):
+            gl_ref[b, at : at + end - start] = done[start:end, i * LANES : (i + 1) * LANES]
+            at += end - start
         left = (toeplitz(taps_ref[b, 1:2, :row_lanes], height, 0) * row_mask_ref[...]).astype(BF)
         right = toeplitz(taps_ref[b, 0:1, :row_lanes], row_lanes, 0).astype(BF)
         gr_ref[b] = dot(left, right).astype(BF)
 
 
 def normal_kernel(
-    columns, first, p_ref, own_ref, ridge_ref, sk_ref, pk_ref, gr_ref, gl_ref, out_ref, sums_ref, acc, xs, ys
+    columns, halo, first, p_ref, own_ref, ridge_ref, sk_ref, pk_ref, gr_ref, gl_ref, out_ref, sums_ref, acc, xs, ys
 ):
     step = pl.program_id(0)
     group, height, _ = gr_ref.shape
@@ -145,7 +160,6 @@
     @pl.when(step == 0)
     def _():
         acc[...] = jnp.zeros_like(acc)
-        xs[...] = jnp.zeros_like(xs)
 
     for c in range(0, ext, 2 * SUB):
         halves = []
@@ -154,15 +168,26 @@
             halves.append(dot(sk_ref[0], cells).reshape(group, SUB, lanes))
         xs[:, c : c + 2 * SUB, :] = jnp.concatenate(halves, axis=1).astype(BF)
 
-    @pl.loop(0, group, step=8)
-    def _(start):
-        mids = []
-        for b in range(8):
-            mids.append(dot(gr_ref[start + b], xs[start + b]).astype(BF))
-        for b in range(8):
-            done = dot(mids[b], gl_ref[start + b])
-            for c in range(chunks):
-                ys[c, start + b] = done[c * SUB : (c + 1) * SUB]
+    blocks = packed_blocks(columns, halo)
+    mids = [dot(gr_ref[b, :, :ext], xs[b]).astype(BF) for b in range(group)]
+    for b in range(group):
+        parts = []
+        at = 0
+        for i in range(lanes // LANES):
+            if i < len(blocks):
+                start, end = blocks[i]
+                part = [gl_ref[b, at : at + end - start]]
+                at += end - start
+                if start:
+                    part = [jnp.zeros((start, LANES), BF)] + part
+                if end < lanes:
+                    part = part + [jnp.zeros((lanes - end, LANES), BF)]
+                parts.append(jnp.concatenate(part, axis=0))
+            else:
+                parts.append(jnp.zeros((lanes, LANES), BF))
+        done = dot(mids[b], jnp.concatenate(parts, axis=1))
+        for c in range(chunks):
+            ys[c, b] = done[c * SUB : (c + 1) * SUB]
 
     for c in range(chunks):
         acc[c] += dot(pk_ref[0], ys[c].reshape(group * SUB, lanes).astype(BF))
@@ -258,39 +283,9 @@
         row, col = values[:, :taps], values[:, taps:]
         return [widen(row), widen(row[:, ::-1]), widen(col), widen(col[:, ::-1])]
 
-    taps_all = jnp.concatenate(variants(every), axis=1)
     taps_here = jnp.concatenate(variants(plain) + [widen(col_taps, -radius % SUB)], axis=1)
 
-    at = jnp.arange(size)
-    edge = me_band * columns - radius + at
-    col_mask = ((edge >= 0) & (edge < columns_all) & (at < columns + 2 * radius)).astype(F32)[None]
-    at = jnp.arange(LANES)
-    edge = me_row * height - radius + at
-    row_mask = ((edge >= 0) & (edge < height * n_row) & (at < height + 2 * radius)).astype(F32)[None]
-    part = group_size(bands, 16)
     whole = lambda shape: pl.BlockSpec(shape, lambda i: (0,) * len(shape))
-    gr, gl = pl.pallas_call(
-        functools.partial(gram_kernel, halo),
-        grid=(bands // part,),
-        in_specs=[
-            pl.BlockSpec((part,) + taps_all.shape[1:], lambda i: (i, 0, 0)),
-            whole((1, LANES)),
-            whole((1, size)),
-        ],
-        out_specs=[
-            pl.BlockSpec((part, height, LANES), lambda i: (i, 0, 0)),
-            pl.BlockSpec((part, size, size), lambda i: (i, 0, 0)),
-        ],
-        out_shape=[
-            jax.ShapeDtypeStruct((bands, height, LANES), BF),
-            jax.ShapeDtypeStruct((bands, size, size), BF),
-        ],
-        compiler_params=pltpu.CompilerParams(vmem_limit_bytes=VMEM_LIMIT),
-        cost_estimate=pl.CostEstimate(
-            flops=bands * 2 * size**3, bytes_accessed=bands * size * size * 2, transcendentals=0
-        ),
-        name="gram",
-    )(taps_all, row_mask, col_mask)
 
     few = group_size(bands_here, 32)
     span = round_up(columns_all, 2 * LANES)
@@ -320,29 +315,77 @@
         name="adjoint",
     )(observed, taps_here, mix)
 
+    summed, every = lax.optimization_barrier((summed, every))
+    taps_all = jnp.concatenate(variants(every), axis=1)
+
+    at = jnp.arange(size)
+    edge = me_band * columns - radius + at
+    col_mask = ((edge >= 0) & (edge < columns_all) & (at < columns + 2 * radius)).astype(F32)[None]
+    at = jnp.arange(LANES)
+    edge = me_row * height - radius + at
+    row_mask = ((edge >= 0) & (edge < height * n_row) & (at < height + 2 * radius)).astype(F32)[None]
+    part = group_size(bands, 16)
+    deep = sum(end - start for start, end in packed_blocks(columns, halo))
+    gr, gl = pl.pallas_call(
+        functools.partial(gram_kernel, columns, halo),
+        grid=(bands // part,),
+        in_specs=[
+            pl.BlockSpec((part,) + taps_all.shape[1:], lambda i: (i, 0, 0)),
+            whole((1, LANES)),
+            whole((1, size)),
+        ],
+        out_specs=[
+            pl.BlockSpec((part, height, LANES), lambda i: (i, 0, 0)),
+            pl.BlockSpec((part, deep, LANES), lambda i: (i, 0, 0)),
+        ],
+        out_shape=[
+            jax.ShapeDtypeStruct((bands, height, LANES), BF),
+            jax.ShapeDtypeStruct((bands, deep, LANES), BF),
+        ],
+        compiler_params=pltpu.CompilerParams(vmem_limit_bytes=VMEM_LIMIT),
+        cost_estimate=pl.CostEstimate(
+            flops=bands * 2 * size**3, bytes_accessed=bands * deep * LANES * 2, transcendentals=0
+        ),
+        name="gram",
+    )(taps_all, row_mask, col_mask)
+
     half = kinds // 2
     keep = lax.dynamic_slice_in_dim(summed, core * half, half, 1)
     give = lax.dynamic_slice_in_dim(summed, (1 - core) * half, half, 1)
     pairs = [(i, i ^ 1) for i in range(n_band)]
     got = lax.ppermute(give, "band", pairs)
     pair = keep.astype(F32) + got.astype(F32)
-    before, after = shift_both(pair[:radius].astype(BF), pair[ext - radius :].astype(BF), "row")
-    rows = pair[radius : ext - radius]
-    pad = ((0, height - radius), (0, 0), (0, 0))
-    rows = rows + jnp.pad(before.astype(F32), pad) + jnp.pad(after.astype(F32), (pad[0][::-1],) + pad[1:])
-    rows = jnp.pad(rows[:, :, :columns_all], ((0, 0), (0, 0), (halo, halo)))
-    wide = 2 * columns + 2 * halo
-    total = lax.dynamic_slice_in_dim(rows, chip * 2 * columns, wide, 2)
-    for hop in range(1, chips):
-        target = (chip + hop) % chips
-        piece = lax.dynamic_slice_in_dim(rows, target * 2 * columns, wide, 2).astype(BF)
-        moves = [(i, (i + 2 * hop) % n_band) for i in range(n_band)]
-        total = total + lax.ppermute(piece, "band", moves).astype(F32)
+    wide = min(columns_all, 2 * columns + (2 * halo if chips > 2 else halo))
+
+    def window_start(which):
+        return jnp.clip(2 * columns * which - halo, 0, columns_all - wide)
+
+    def moves(hop, step):
+        return [
+            (b * n_row + r, (b + 2 * hop) % n_band * n_row + r + step)
+            for b in range(n_band)
+            for r in range(n_row)
+            if 0 <= r + step < n_row
+        ]
+
+    total = None
+    for hop in range(chips):
+        piece = lax.dynamic_slice_in_dim(pair, window_start((chip + hop) % chips), wide, 2)
+        above, here, below = piece[:radius], piece[radius : ext - radius], piece[ext - radius :]
+        axes = ("band", "row")
+        after = lax.ppermute(above.astype(BF), axes, moves(hop, -1)).astype(F32)
+        before = lax.ppermute(below.astype(BF), axes, moves(hop, 1)).astype(F32)
+        if hop:
+            here = lax.ppermute(here.astype(BF), axes, moves(hop, 0)).astype(F32)
+        rest = jnp.zeros((height - radius,) + here.shape[1:], F32)
+        here = here + jnp.concatenate([before, rest]) + jnp.concatenate([rest, after])
+        total = here if total is None else total + here
     other = lax.ppermute(total, "band", pairs)
     first = jnp.where(core == 0, total, other)
     second = jnp.where(core == 0, other, total)
     total = jnp.concatenate([first, second], axis=1)
-    window = lax.dynamic_slice_in_dim(total, core * columns, columns + 2 * halo, 2)
+    total = jnp.pad(total, ((0, 0), (0, 0), (halo, halo)))
+    window = lax.dynamic_slice_in_dim(total, me_band * columns - window_start(chip), columns + 2 * halo, 2)
     v0 = jnp.pad(window[:, :, halo : halo + columns], ((0, 0), (0, 0), (0, lanes - columns)))
     v0 = jnp.swapaxes(v0, 0, 1)
     window = jnp.pad(window.astype(BF), ((0, 0), (0, 0), (0, lanes - columns - 2 * halo)))
@@ -358,7 +401,7 @@
         before, after = shift_both(window[:halo], window[height - halo :], "row")
         cells = jnp.concatenate([before, window, after], axis=0)
         return pl.pallas_call(
-            functools.partial(normal_kernel, columns, first),
+            functools.partial(normal_kernel, columns, halo, first),
             grid=(bands // group,),
             in_specs=[
                 whole((tall, kinds, lanes)),
@@ -367,7 +410,7 @@
                 pl.BlockSpec((1,) + sk.shape[1:], lambda i: (i, 0, 0)),
                 pl.BlockSpec((1,) + pk.shape[1:], lambda i: (i, 0, 0)),
                 block((height, LANES)),
-                block((size, size)),
+                block((deep, LANES)),
             ],
             out_specs=[whole((kinds, height, lanes)), whole((SUB, LANES))],
             out_shape=[
@@ -376,12 +419,12 @@
             ],
             scratch_shapes=[
                 pltpu.VMEM((height // SUB, SUB * kinds, lanes), F32),
-                pltpu.VMEM((group, LANES, lanes), BF),
+                pltpu.VMEM((group, tall, lanes), BF),
                 pltpu.VMEM((height // SUB, group, SUB, lanes), F32),
             ],
             compiler_params=pltpu.CompilerParams(vmem_limit_bytes=VMEM_LIMIT),
             cost_estimate=pl.CostEstimate(
-                flops=bands * 2 * 32 * 512 * 256, bytes_accessed=bands * size * size * 2, transcendentals=0
+                flops=bands * 2 * 32 * 512 * 256, bytes_accessed=bands * deep * LANES * 2, transcendentals=0
             ),
             name="normal",
         )(cells, own, ridge, sk, pk, gr, gl)

time: 194 us -> 174 us (0.90)
  waiting for transfers between devices: 39.3 us -> 22.3 us
  Pallas kernels: 76.9 us -> 64.2 us
  starting transfers between devices: 27 us -> 33.3 us
  local copies, waits for them, and re-layouts: 15.3 us -> 17.8 us
    ppermute x4 -> x3, waiting for transfers between devices: 17.6 us -> 4.23 us  [shift_both(): lax.ppermute(high_edge, axis, [(i, i + 1) for i in range(count - 1)])]
    pallas_call x3, Pallas kernels: 60.8 us -> 48.1 us  [the longest x2 29.2 us: normal_map(): pl.pallas_call(functools.partial(normal_kernel, columns, halo, first), gr...]
    ppermute x1 -> x5, starting transfers between devices: 1.57 us -> 12.2 us  [the longest x2 8.83 us: local(): before = lax.ppermute(below.astype(BF), axes, moves(hop, 1)).astype(F32)]
    ppermute x4 -> x3, starting transfers between devices: 17.7 us -> 12.4 us  [shift_both(): lax.ppermute(high_edge, axis, [(i, i + 1) for i in range(count - 1)])]
    ppermute x1 -> x5, waiting for transfers between devices: 10.9 us -> 8.13 us  [the longest x2 8.12 us: local(): before = lax.ppermute(below.astype(BF), axes, moves(hop, 1)).astype(F32)]
    ppermute x4 -> x3, starting transfers between devices: 5.38 us -> 4.1 us  [shift_both(): lax.ppermute(low_edge, axis, [(i + 1, i) for i in range(count - 1)])]
    ppermute x4 -> x3, waiting for transfers between devices: 8.11 us -> 7.19 us  [shift_both(): lax.ppermute(low_edge, axis, [(i + 1, i) for i in range(count - 1)])]
    unnamed x31 -> x26, local copies, waits for them, and re-layouts: 3.05 us -> 3.92 us
  transfers between devices with their start and end apart: 14 -> 16, of which waited for: 6 -> 5; matrix products, arithmetic and copies ran while one was open for 6% -> 6% of each run, Pallas kernels for 10% -> 19%
where the time goes in v3:
time: 174 us; the launch traced here: 173 us
  Pallas kernels  64.2 us (37%)
  starting transfers between devices  33.3 us (19%)
  waiting for transfers between devices  22.3 us (13%)
  blocking collectives  21.6 us (12%)
  local copies, waits for them, and re-layouts  17.8 us (10%)
  other arithmetic  11 us (6%)
    pallas_call x2, Pallas kernels, normal_map(): pl.pallas_call(functools.partial(normal_kernel, columns, halo, first), gr...  29.2 us
    all_to_all x1, blocking collectives, local(): shared = lax.all_to_all(mine, ('band', 'row'), 0, 0, tiled=True)  21.6 us
    pallas_call x1, Pallas kernels, local(): pl.pallas_call(functools.partial(gram_kernel, columns, halo), grid=(bands...  18.9 us
    pallas_call x1, Pallas kernels, local(): pl.pallas_call(functools.partial(adjoint_kernel, columns_all, radius), gr...  14.4 us
    ppermute x3, starting transfers between devices, shift_both(): lax.ppermute(high_edge, axis, [(i, i + 1) for i in range(count - 1)])  12.4 us
    ppermute x2, starting transfers between devices, local(): before = lax.ppermute(below.astype(BF), axes, moves(hop, 1)).astype(F32)  8.83 us
    ppermute x2, waiting for transfers between devices, local(): before = lax.ppermute(below.astype(BF), axes, moves(hop, 1)).astype(F32)  8.12 us
    ppermute x3, waiting for transfers between devices, shift_both(): lax.ppermute(low_edge, axis, [(i + 1, i) for i in range(count - 1)])  7.19 us
  transfers between devices with their start and end apart: 16, of which 5 were waited for; matrix products, arithmetic and copies ran while one was open for 6% of the time, Pallas kernels for 19%

profile of v3, /device:TPU:0, one launch (start us, length us, event | category | flops | bytes accessed | tf_op | source)
XLA Modules:
  0.0 172.7 jit_solution(2331319051785130967)
XLA Ops:
  0.6 0.8 copy.22
  1.4 0.8 copy.24
  2.2 0.7 pad_maximum_fusion.5
  2.9 2.4 %collective-permute-start.2 = (f32[56,50]{1,0:T(8,128)}, f32[56,50]{1,0:T(8,128)}, u32[]{:S(2)}, u32[]{:S(2)}) collective-permute-start(f32[56,50]{1,0:T(8,128)} %pad_maximum_fusion.5), channel_id=1, source_target_pairs={{0,24},{8,0},{16,8},{24,16},{1,25},{9,1},{17,9},{25,17},{2,26},{10... | collective-permute-start | bytes 33608 | tf_op jit(solution)/shard_map/ppermute | solution.py:275
  5.3 0.6 collective-permute-start.1
  5.9 0.2 collective-permute-start
  6.7 1.6 constant_dynamic-slice_fusion.2
  8.2 0.4 fusion.1
  8.7 0.1 copy.27
  8.8 0.5 concatenate.50.taps_ref
  9.3 14.4 %adjoint.1 = bf16[56,32,768]{2,1,0:T(8,128)(2,1)S(1)} custom-call(bf16[56,32,680]{2,1,0:T(8,128)(2,1)} %obs_ref.1, f32[56,5,256]{2,1,0:T(8,128)S(1)} %concatenate.50.taps_ref, bf16[2,256,224]{2,1,0:T(8,128)(2,1)S(1)} %bitcast.24), custom_call_target="tpu_custom_call" | custom-call | flops 1409286144 | bytes 2437120 | tf_op jit(solution)/shard_map/adjoint/pallas_call | solution.py:295
  23.7 0.9 pad_maximum_fusion.4
  24.6 1.5 copy.30
  26.1 1.5 copy-done.4
  27.7 1.4 collective-permute-start.3
  29.1 2.8 %collective-permute-done.3 = bf16[56,16,768]{2,0,1:T(8,128)(2,1)S(1)} collective-permute-done((bf16[56,16,768]{2,0,1:T(8,128)(2,1)S(1)}, bf16[56,16,768]{2,0,1:T(8,128)(2,1)S(1)}, u32[]{:S(2)}, u32[]{:S(2)}) %collective-permute-start.3) | collective-permute-done | bytes 1376288 | tf_op jit(solution)/shard_map/ppermute | solution.py:356
  31.9 1.6 convert_add_fusion
  33.5 0.6 dynamic-slice_convert_fusion.1
  34.1 0.1 slice.80
  34.3 0.7 copy-done.5
  35.0 0.6 collective-permute-start.6
  35.6 0.7 fusion.47
  36.4 3.4 %collective-permute-start.4 = (bf16[12,16,364]{2,0,1:T(8,128)(2,1)}, bf16[12,16,364]{2,0,1:T(8,128)(2,1)S(1)}, u32[]{:S(2)}, u32[]{:S(2)}) collective-permute-start(bf16[12,16,364]{2,0,1:T(8,128)(2,1)} %get-tuple-element.24), channel_id=1, source_target_pairs={{0,1},{1,2},{2,3},{3,4},{4,5},{5,6},{6,7},{8,9},{9,10},{10,11},{11... | collective-permute-start | bytes 419336 | tf_op jit(solution)/shard_map/ppermute | solution.py:377
  39.8 1.3 collective-permute-start.5
  41.1 5.4 %collective-permute-start.7 = (bf16[12,16,364]{2,0,1:T(8,128)(2,1)S(1)}, bf16[12,16,364]{2,0,1:T(8,128)(2,1)S(1)}, u32[]{:S(2)}, u32[]{:S(2)}) collective-permute-start(bf16[12,16,364]{2,0,1:T(8,128)(2,1)S(1)} %get-tuple-element.26), channel_id=1, source_target_pairs={{0,17},{1,18},{2,19},{3,20},{4,21},{5,22},{6,23},{8,25},{9,26},{10... | collective-permute-start | bytes 419336 | tf_op jit(solution)/shard_map/ppermute | solution.py:377
  46.5 1.5 collective-permute-start.8
  48.0 0.8 fusion
  48.9 8.1 %collective-permute-done.7 = bf16[12,16,364]{2,0,1:T(8,128)(2,1)S(1)} collective-permute-done((bf16[12,16,364]{2,0,1:T(8,128)(2,1)S(1)}, bf16[12,16,364]{2,0,1:T(8,128)(2,1)S(1)}, u32[]{:S(2)}, u32[]{:S(2)}) %collective-permute-start.7) | collective-permute-done | bytes 139808 | tf_op jit(solution)/shard_map/ppermute | solution.py:377
  57.0 2.6 %fusion.11 = f32[32,16,364]{2,0,1:T(8,128)} fusion(f32[56,16,768]{2,0,1:T(8,128)} %copy-done.5, s32[]{:T(128)S(6)} %add.213, s32[]{:T(128)S(6)} %min.10, bf16[32,16,364]{2,0,1:T(8,128)(2,1)S(1)} %collective-permute-done.6, bf16[12,16,364]{2,0,1:T(8,128)(2,1)S(1)} %collective-permute-done.8, bf16[12,16,364]{2,0,1:T(8,128)(2,1)S(1)} %collective-permute-done.7, ...), kind=kLoop, calls=%fused_computation.28 | loop fusion | flops 1863680 | bytes 2422792 | tf_op jit(solution)/shard_map/add | solution.py:382
  59.7 0.6 copy.32
  60.3 1.0 reshape_reshape.3
  61.3 0.6 copy.40
  62.0 0.4 rev.14
  62.4 0.2 copy.34
  62.6 0.2 copy.35
  62.9 0.4 rev.15
  63.3 0.2 copy.36
  63.6 0.2 broadcast_in_dim.78
  63.7 0.9 pad_maximum_fusion.2.taps_ref
  64.6 1.5 broadcast_select_fusion.1
  66.1 0.6 fusion.45
  66.8 5.3 %collective-permute-start.10 = (bf16[24,32,256]{2,0,1:T(8,128)(2,1)S(1)}, bf16[24,32,256]{2,0,1:T(8,128)(2,1)S(1)}, u32[]{:S(2)}, u32[]{:S(2)}) collective-permute-start(bf16[24,32,256]{2,0,1:T(8,128)(2,1)S(1)} %get-tuple-element.32), channel_id=1, source_target_pairs={{0,1},{1,2},{2,3},{3,4},{4,5},{5,6},{6,7},{8,9},{9,10},{10,11},{11... | collective-permute-start | bytes 1179656 | tf_op jit(solution)/shard_map/ppermute | solution.py:245
  72.1 1.3 collective-permute-start.11
  73.4 18.9 %gram.1 = (bf16[224,32,128]{2,1,0:T(8,128)(2,1)S(1)}, bf16[224,272,128]{2,1,0:T(8,128)(2,1)}) custom-call(f32[224,4,256]{2,1,0:T(4,128)S(1)} %pad_maximum_fusion.2.taps_ref, f32[1,128]{1,0:T(1,128)S(1)} %and_convert_fusion.1.row_mask_ref, f32[1,256]{1,0:T(1,128)S(1)} %and_convert_fusion.col_mask_ref), custom_call_target="tpu_custom_call" | custom-call | flops 7516192768 | bytes 15597568 | tf_op jit(solution)/shard_map/gram/pallas_call | solution.py:329
  92.3 0.3 slice.83
  92.7 0.1 pad.56
  92.8 1.1 pad_bitcast_fusion.own_ref.v0_ref
  94.0 1.5 copy.37.p_ref
  95.5 0.1 broadcast_in_dim.73.ridge_ref
  95.6 14.6 %normal.2 = (f32[32,32,256]{2,1,0:T(8,128)S(1)}, f32[8,128]{1,0:T(8,128)S(1)}) custom-call(bf16[80,32,256]{2,1,0:T(8,128)(2,1)} %copy.37.p_ref, f32[32,32,256]{2,1,0:T(8,128)} %pad_bitcast_fusion.own_ref.v0_ref, f32[32,8,256]{2,1,0:T(8,128)S(1)} %broadcast_in_dim.73.ridge_ref, bf16[7,256,256]{2,1,0:T(8,128)(2,1)S(1)} %bitcast.20, ...), custom_call_target="tpu_custom_call" | custom-call | flops 1879048192 | bytes 15597568 | tf_op jit(solution)/shard_map/normal/pallas_call | solution.py:403
  110.2 0.6 copy.38
  110.8 0.1 fusion.50
  111.0 2.1 %collective-permute-start.12 = (bf16[32,32,24]{2,1,0:T(8,128)(2,1)S(1)}, bf16[32,32,24]{2,1,0:T(8,128)(2,1)S(1)}, u32[]{:S(2)}, u32[]{:S(2)}) collective-permute-start(bf16[32,32,24]{2,1,0:T(8,128)(2,1)S(1)} %get-tuple-element.30), channel_id=1, source_target_pairs={{0,8},{8,16},{16,24},{1,9},{9,17},{17,25},{2,10},{10,18},{18,26},{... | collective-permute-start | bytes 147464 | tf_op jit(solution)/shard_map/ppermute | solution.py:245
  113.1 1.5 collective-permute-start.13
  114.6 1.9 %collective-permute-done.13 = bf16[32,32,24]{2,1,0:T(8,128)(2,1)S(1)} collective-permute-done((bf16[32,32,24]{2,1,0:T(8,128)(2,1)S(1)}, bf16[32,32,24]{2,1,0:T(8,128)(2,1)S(1)}, u32[]{:S(2)}, u32[]{:S(2)}) %collective-permute-start.13) | collective-permute-done | bytes 49184 | tf_op jit(solution)/shard_map/ppermute | solution.py:246
  116.6 0.5 pad_maximum_fusion.3
  117.2 5.0 %collective-permute-start.14 = (bf16[24,32,256]{2,1,0:T(8,128)(2,1)S(1)}, bf16[24,32,256]{2,1,0:T(8,128)(2,1)S(1)}, u32[]{:S(2)}, u32[]{:S(2)}) collective-permute-start(bf16[24,32,256]{2,1,0:T(8,128)(2,1)S(1)} %get-tuple-element.28), channel_id=1, source_target_pairs={{0,1},{1,2},{2,3},{3,4},{4,5},{5,6},{6,7},{8,9},{9,10},{10,11},{11... | collective-permute-start | bytes 1179656 | tf_op jit(solution)/shard_map/ppermute | solution.py:245
  122.2 1.3 collective-permute-start.15
  123.5 4.2 %collective-permute-done.14 = bf16[24,32,256]{2,1,0:T(8,128)(2,1)S(1)} collective-permute-done((bf16[24,32,256]{2,1,0:T(8,128)(2,1)S(1)}, bf16[24,32,256]{2,1,0:T(8,128)(2,1)S(1)}, u32[]{:S(2)}, u32[]{:S(2)}) %collective-permute-start.14) | collective-permute-done | bytes 393248 | tf_op jit(solution)/shard_map/ppermute | solution.py:245
  127.8 5.3 %collective-permute-done.15 = bf16[24,32,256]{2,1,0:T(8,128)(2,1)S(1)} collective-permute-done((bf16[24,32,256]{2,1,0:T(8,128)(2,1)S(1)}, bf16[24,32,256]{2,1,0:T(8,128)(2,1)S(1)}, u32[]{:S(2)}, u32[]{:S(2)}) %collective-permute-start.15) | collective-permute-done | bytes 393248 | tf_op jit(solution)/shard_map/ppermute | solution.py:246
  133.1 1.6 pad_maximum_fusion.1.p_ref
  134.6 14.6 %normal.3 = (f32[32,32,256]{2,1,0:T(8,128)S(1)}, f32[8,128]{1,0:T(8,128)S(1)}) custom-call(bf16[80,32,256]{2,1,0:T(8,128)(2,1)} %pad_maximum_fusion.1.p_ref, f32[32,32,256]{2,1,0:T(8,128)} %copy-done.1, f32[32,8,256]{2,1,0:T(8,128)S(1)} %broadcast_in_dim.73.ridge_ref, bf16[7,256,256]{2,1,0:T(8,128)(2,1)S(1)} %bitcast.21, bf16[7,256,256]{2,1,0:T(8,128)(2,1)S(1)} %bitcast.23, ...), custom_call_target="tpu_custom_call" | custom-call | flops 1879048192 | bytes 15597568 | tf_op jit(solution)/shard_map/normal/pallas_call | solution.py:403
  149.3 21.6 %all_to_all.5.shared_ref = f32[32,8,128]{2,1,0:T(8,128)S(1)} all-to-all(f32[32,8,128]{2,1,0:T(8,128)S(1)} %broadcast_in_dim.81), channel_id=1, replica_groups=mesh['band'=4,'row'=8] {'band','row'}, dimensions={0} | all-to-all | bytes 262144 | tf_op jit(solution)/shard_map/all_to_all | solution.py:442
  170.9 1.8 %combine.1 = (f32[32,32,170]{2,1,0:T(8,128)}, f32[32,32,170]{2,1,0:T(8,128)}) custom-call(f32[32,8,128]{2,1,0:T(8,128)S(1)} %all_to_all.5.shared_ref, f32[32,32,256]{2,1,0:T(8,128)S(1)} %copy-done, f32[32,32,256]{2,1,0:T(8,128)S(1)} %copy-done.2, f32[32,32,256]{2,1,0:T(8,128)S(1)} %get-tuple-element.17.v2_ref), custom_call_target="tpu_custom_call" | custom-call | tf_op jit(solution)/shard_map/combine/pallas_call | solution.py:444
  (68 shorter events, 1.4 us)
Async XLA Ops:
  2.9 20.8 %collective-permute-start.2 = (f32[56,50]{1,0:T(8,128)}, f32[56,50]{1,0:T(8,128)}, u32[]{:S(2)}, u32[]{:S(2)}) collective-permute-start(f32[56,50]{1,0:T(8,128)} %pad_maximum_fusion.5), channel_id=1, source_target_pairs={{0,24},{8,0},{16,8},{24,16},{1,25},{9,1},{17,9},{25,17},{2,26},{10... | collective-permute-start | bytes 33608 | tf_op jit(solution)/shard_map/ppermute | solution.py:275
  5.3 18.4 %collective-permute-start.1 = (f32[56,50]{1,0:T(8,128)}, f32[56,50]{1,0:T(8,128)}, u32[]{:S(2)}, u32[]{:S(2)}) collective-permute-start(f32[56,50]{1,0:T(8,128)} %pad_maximum_fusion.5), channel_id=1, source_target_pairs={{0,16},{8,24},{16,0},{24,8},{1,17},{9,25},{17,1},{25,9},{2,18},{10... | collective-permute-start | bytes 33608 | tf_op jit(solution)/shard_map/ppermute | solution.py:275
  5.9 17.8 %collective-permute-start = (f32[56,50]{1,0:T(8,128)}, f32[56,50]{1,0:T(8,128)}, u32[]{:S(2)}, u32[]{:S(2)}) collective-permute-start(f32[56,50]{1,0:T(8,128)} %pad_maximum_fusion.5), channel_id=1, source_target_pairs={{0,8},{8,16},{16,24},{24,0},{1,9},{9,17},{17,25},{25,1},{2,10},{10... | collective-permute-start | bytes 33608 | tf_op jit(solution)/shard_map/ppermute | solution.py:275
  6.1 2.5 %copy-start.7 = (s32[256]{0:T(256)}, s32[256]{0:T(256)S(1)}, u32[]{:S(2)}) copy-start(s32[256]{0:T(256)S(1)} %get-tuple-element.44) | copy-start | bytes 3076
  6.1 2.5 %copy-start.9 = (s32[256]{0:T(256)}, s32[256]{0:T(256)S(1)}, u32[]{:S(2)}) copy-start(s32[256]{0:T(256)S(1)} %get-tuple-element.45) | copy-start | bytes 3076
  26.1 1.5 copy-start.4
  27.7 4.1 %collective-permute-start.3 = (bf16[56,16,768]{2,0,1:T(8,128)(2,1)S(1)}, bf16[56,16,768]{2,0,1:T(8,128)(2,1)S(1)}, u32[]{:S(2)}, u32[]{:S(2)}) collective-permute-start(bf16[56,16,768]{2,0,1:T(8,128)(2,1)S(1)} %constant_dynamic-slice_fusion.3), channel_id=1, source_target_pairs={{0,8},{8,0},{16,24},{24,16},{1,9},{9,1},{17,25},{25,17},{2,10},{10... | collective-permute-start | bytes 4128776 | tf_op jit(solution)/shard_map/ppermute | solution.py:356
  33.5 1.5 copy-start.5
  33.5 14.5 %copy-start.6 = (bf16[56,32]{0,1:T(8,128)(2,1)S(1)}, bf16[56,32]{0,1:T(8,128)(2,1)}, u32[]{:S(2)}) copy-start(bf16[56,32]{0,1:T(8,128)(2,1)} %get-tuple-element.41) | copy-start | bytes 10756
  33.5 14.5 %copy-start.8 = (s32[256]{0:T(256)S(1)}, s32[256]{0:T(256)}, u32[]{:S(2)}) copy-start(s32[256]{0:T(256)} %copy-done.7) | copy-start | bytes 3076
  33.5 14.5 %copy-start.10 = (s32[256]{0:T(256)S(1)}, s32[256]{0:T(256)}, u32[]{:S(2)}) copy-start(s32[256]{0:T(256)} %copy-done.9) | copy-start | bytes 3076
  35.0 22.0 %collective-permute-start.6 = (bf16[32,16,364]{2,0,1:T(8,128)(2,1)S(1)}, bf16[32,16,364]{2,0,1:T(8,128)(2,1)S(1)}, u32[]{:S(2)}, u32[]{:S(2)}) collective-permute-start(bf16[32,16,364]{2,0,1:T(8,128)(2,1)S(1)} %slice.80), channel_id=1, source_target_pairs={{0,16},{1,17},{2,18},{3,19},{4,20},{5,21},{6,22},{7,23},{8,24},{9,... | collective-permute-start | bytes 1118216 | tf_op jit(solution)/shard_map/ppermute | solution.py:379
  36.4 12.5 %collective-permute-start.4 = (bf16[12,16,364]{2,0,1:T(8,128)(2,1)}, bf16[12,16,364]{2,0,1:T(8,128)(2,1)S(1)}, u32[]{:S(2)}, u32[]{:S(2)}) collective-permute-start(bf16[12,16,364]{2,0,1:T(8,128)(2,1)} %get-tuple-element.24), channel_id=1, source_target_pairs={{0,1},{1,2},{2,3},{3,4},{4,5},{5,6},{6,7},{8,9},{9,10},{10,11},{11... | collective-permute-start | bytes 419336 | tf_op jit(solution)/shard_map/ppermute | solution.py:377
  39.8 9.1 %collective-permute-start.5 = (bf16[12,16,364]{2,0,1:T(8,128)(2,1)S(1)}, bf16[12,16,364]{2,0,1:T(8,128)(2,1)S(1)}, u32[]{:S(2)}, u32[]{:S(2)}) collective-permute-start(bf16[12,16,364]{2,0,1:T(8,128)(2,1)S(1)} %get-tuple-element.25), channel_id=1, source_target_pairs={{1,0},{2,1},{3,2},{4,3},{5,4},{6,5},{7,6},{9,8},{10,9},{11,10},{12... | collective-permute-start | bytes 419336 | tf_op jit(solution)/shard_map/ppermute | solution.py:376
  41.1 15.9 %collective-permute-start.7 = (bf16[12,16,364]{2,0,1:T(8,128)(2,1)S(1)}, bf16[12,16,364]{2,0,1:T(8,128)(2,1)S(1)}, u32[]{:S(2)}, u32[]{:S(2)}) collective-permute-start(bf16[12,16,364]{2,0,1:T(8,128)(2,1)S(1)} %get-tuple-element.26), channel_id=1, source_target_pairs={{0,17},{1,18},{2,19},{3,20},{4,21},{5,22},{6,23},{8,25},{9,26},{10... | collective-permute-start | bytes 419336 | tf_op jit(solution)/shard_map/ppermute | solution.py:377
  46.5 10.5 %collective-permute-start.8 = (bf16[12,16,364]{2,0,1:T(8,128)(2,1)S(1)}, bf16[12,16,364]{2,0,1:T(8,128)(2,1)S(1)}, u32[]{:S(2)}, u32[]{:S(2)}) collective-permute-start(bf16[12,16,364]{2,0,1:T(8,128)(2,1)S(1)} %get-tuple-element.27), channel_id=1, source_target_pairs={{1,16},{2,17},{3,18},{4,19},{5,20},{6,21},{7,22},{9,24},{10,25},{1... | collective-permute-start | bytes 419336 | tf_op jit(solution)/shard_map/ppermute | solution.py:376
  59.6 5.0 %collective-permute-start.9 = (f32[32,16,364]{2,0,1:T(8,128)}, f32[32,16,364]{2,0,1:T(8,128)}, u32[]{:S(2)}, u32[]{:S(2)}) collective-permute-start(f32[32,16,364]{2,0,1:T(8,128)} %fusion.11), channel_id=1, source_target_pairs={{0,8},{8,0},{16,24},{24,16},{1,9},{9,1},{17,25},{25,17},{2,10},{10... | collective-permute-start | bytes 2236424 | tf_op jit(solution)/shard_map/ppermute | solution.py:383
  66.8 27.1 %collective-permute-start.10 = (bf16[24,32,256]{2,0,1:T(8,128)(2,1)S(1)}, bf16[24,32,256]{2,0,1:T(8,128)(2,1)S(1)}, u32[]{:S(2)}, u32[]{:S(2)}) collective-permute-start(bf16[24,32,256]{2,0,1:T(8,128)(2,1)S(1)} %get-tuple-element.32), channel_id=1, source_target_pairs={{0,1},{1,2},{2,3},{3,4},{4,5},{5,6},{6,7},{8,9},{9,10},{10,11},{11... | collective-permute-start | bytes 1179656 | tf_op jit(solution)/shard_map/ppermute | solution.py:245
  72.1 21.8 %collective-permute-start.11 = (bf16[24,32,256]{2,0,1:T(8,128)(2,1)S(1)}, bf16[24,32,256]{2,0,1:T(8,128)(2,1)S(1)}, u32[]{:S(2)}, u32[]{:S(2)}) collective-permute-start(bf16[24,32,256]{2,0,1:T(8,128)(2,1)S(1)} %get-tuple-element.33), channel_id=1, source_target_pairs={{1,0},{2,1},{3,2},{4,3},{5,4},{6,5},{7,6},{9,8},{10,9},{11,10},{12... | collective-permute-start | bytes 1179656 | tf_op jit(solution)/shard_map/ppermute | solution.py:246
  92.3 1.6 copy-start.3
  93.9 1.6 copy-start.11
  110.2 6.9 %copy-start.1 = (f32[32,32,256]{2,1,0:T(8,128)}, f32[32,32,256]{2,1,0:T(8,128)S(1)}, u32[]{:S(2)}) copy-start(f32[32,32,256]{2,1,0:T(8,128)S(1)} %get-tuple-element.15.own_ref.v1_ref) | copy-start | bytes 3145732
  111.0 3.6 %collective-permute-start.12 = (bf16[32,32,24]{2,1,0:T(8,128)(2,1)S(1)}, bf16[32,32,24]{2,1,0:T(8,128)(2,1)S(1)}, u32[]{:S(2)}, u32[]{:S(2)}) collective-permute-start(bf16[32,32,24]{2,1,0:T(8,128)(2,1)S(1)} %get-tuple-element.30), channel_id=1, source_target_pairs={{0,8},{8,16},{16,24},{1,9},{9,17},{17,25},{2,10},{10,18},{18,26},{... | collective-permute-start | bytes 147464 | tf_op jit(solution)/shard_map/ppermute | solution.py:245
  113.1 3.4 %collective-permute-start.13 = (bf16[32,32,24]{2,1,0:T(8,128)(2,1)S(1)}, bf16[32,32,24]{2,1,0:T(8,128)(2,1)S(1)}, u32[]{:S(2)}, u32[]{:S(2)}) collective-permute-start(bf16[32,32,24]{2,1,0:T(8,128)(2,1)S(1)} %get-tuple-element.31), channel_id=1, source_target_pairs={{8,0},{16,8},{24,16},{9,1},{17,9},{25,17},{10,2},{18,10},{26,18},{... | collective-permute-start | bytes 147464 | tf_op jit(solution)/shard_map/ppermute | solution.py:246
  117.2 10.6 %collective-permute-start.14 = (bf16[24,32,256]{2,1,0:T(8,128)(2,1)S(1)}, bf16[24,32,256]{2,1,0:T(8,128)(2,1)S(1)}, u32[]{:S(2)}, u32[]{:S(2)}) collective-permute-start(bf16[24,32,256]{2,1,0:T(8,128)(2,1)S(1)} %get-tuple-element.28), channel_id=1, source_target_pairs={{0,1},{1,2},{2,3},{3,4},{4,5},{5,6},{6,7},{8,9},{9,10},{10,11},{11... | collective-permute-start | bytes 1179656 | tf_op jit(solution)/shard_map/ppermute | solution.py:245
  122.2 10.9 %collective-permute-start.15 = (bf16[24,32,256]{2,1,0:T(8,128)(2,1)S(1)}, bf16[24,32,256]{2,1,0:T(8,128)(2,1)S(1)}, u32[]{:S(2)}, u32[]{:S(2)}) collective-permute-start(bf16[24,32,256]{2,1,0:T(8,128)(2,1)S(1)} %get-tuple-element.29), channel_id=1, source_target_pairs={{1,0},{2,1},{3,2},{4,3},{5,4},{6,5},{7,6},{9,8},{10,9},{11,10},{12... | collective-permute-start | bytes 1179656 | tf_op jit(solution)/shard_map/ppermute | solution.py:246
  134.6 36.3 %copy-start = (f32[32,32,256]{2,1,0:T(8,128)S(1)}, f32[32,32,256]{2,1,0:T(8,128)}, u32[]{:S(2)}) copy-start(f32[32,32,256]{2,1,0:T(8,128)} %pad_bitcast_fusion.own_ref.v0_ref) | copy-start | bytes 3145732
  134.6 36.3 %copy-start.2 = (f32[32,32,256]{2,1,0:T(8,128)S(1)}, f32[32,32,256]{2,1,0:T(8,128)}, u32[]{:S(2)}) copy-start(f32[32,32,256]{2,1,0:T(8,128)} %copy-done.1) | copy-start | bytes 3145732

commit v4 on v3

--- a/solution.py
+++ b/solution.py
@@ -43,24 +43,140 @@
     return jnp.concatenate(pieces, axis=0) if len(pieces) > 1 else pieces[0]
 
 
-def spread_basis(basis, group, kinds):
-    bands = basis.shape[0]
-    rows = jnp.arange(bands * SUB)
-    lanes = jnp.arange(SUB * kinds)
-    up = (rows[:, None] // SUB == jnp.arange(bands)[None, :]).astype(BF)
-    out = (jnp.arange(kinds)[:, None] == lanes[None, :] % kinds).astype(BF)
-    same = (rows[:, None] % SUB) == (lanes[None, :] // kinds)
-    wide = dot(dot(up, basis).astype(BF), out)
-    return jnp.where(same, wide, 0.0).astype(BF).reshape(bands // group, group * SUB, SUB * kinds)
-
-
-def component_first(spread, kinds):
-    groups, deep, _ = spread.shape
-    split = spread.reshape(groups, deep, SUB, kinds)
-    return split.transpose(0, 3, 2, 1).reshape(groups, kinds * SUB, deep)
-
-
-def adjoint_kernel(columns, radius, obs_ref, taps_ref, mix_ref, out_ref, acc, ys, mats, rows):
+def chosen(shape, rule, kind=BF):
+    row = lax.broadcasted_iota(jnp.int32, shape, 0)
+    lane = lax.broadcasted_iota(jnp.int32, shape, 1)
+    return jnp.where(rule(row, lane), 1.0, 0.0).astype(kind)
+
+
+def placed_taps(both, places, kind):
+    count = both.shape[1] // 2
+    picks = []
+    for first, lead, flip in places:
+
+        def rule(row, lane):
+            at = lane - lead
+            here = (at >= 0) & (at < count)
+            return here & (row == first + (count - 1 - at if flip else at))
+
+        picks.append(chosen((both.shape[1], 2 * LANES), rule, kind))
+    done = lax.dot_general(
+        both.astype(kind),
+        jnp.concatenate(picks, axis=1),
+        (((1,), (0,)), ((), ())),
+        precision=lax.Precision.HIGHEST if kind == F32 else None,
+        preferred_element_type=F32,
+    )
+    return [done[:, i * 2 * LANES : (i + 1) * 2 * LANES] for i in range(len(places))]
+
+
+def dot_rows(lhs, rhs):
+    return lax.dot_general(lhs, rhs, (((1,), (1,)), ((), ())), preferred_element_type=F32)
+
+
+def strip_plan(rows, width):
+    beside = max(n for n in range(1, rows + 1) if rows % n == 0 and n * width <= LANES)
+    return beside, rows // beside
+
+
+def turn_lanes(cells, amount):
+    rows, kinds, lanes = cells.shape
+    flat = pltpu.roll(cells.reshape(rows * kinds, lanes), amount % lanes, 1)
+    return flat.reshape(rows, kinds, lanes)
+
+
+def keep_lanes(cells, first, width):
+    lane = lax.broadcasted_iota(jnp.int32, cells.shape, 2)
+    return jnp.where((lane >= first) & (lane < first + width), cells, 0.0)
+
+
+def packed_strip(cells, first, width):
+    beside, rows = strip_plan(cells.shape[0], width)
+    total = None
+    for g in range(beside):
+        part = turn_lanes(cells[g * rows : (g + 1) * rows], g * width - first)[:, :, :LANES]
+        part = keep_lanes(part, g * width, width)
+        total = part if total is None else total + part
+    return total
+
+
+def unpacked_strip(packed, count, width, first, lanes):
+    beside, rows = strip_plan(count, width)
+    wide = packed.astype(F32)
+    if lanes > LANES:
+        rest = jnp.zeros(packed.shape[:2] + (lanes - LANES,), F32)
+        wide = jnp.concatenate([wide, rest], axis=2)
+    return jnp.concatenate(
+        [keep_lanes(turn_lanes(wide, first - g * width), first, width) for g in range(beside)], axis=0
+    )
+
+
+def main_rows(columns, halo):
+    full = columns // LANES
+    rest = columns - full * LANES
+    return full * halo + (strip_plan(halo, rest)[1] if rest else 0)
+
+
+def packed_main(cells, columns):
+    full = columns // LANES
+    rest = columns - full * LANES
+    parts = [cells[:, :, t * LANES : (t + 1) * LANES] for t in range(full)]
+    if rest:
+        parts.append(packed_strip(cells, full * LANES, rest))
+    return jnp.concatenate(parts, axis=0)
+
+
+def unpacked_main(packed, columns, halo, lanes):
+    full = columns // LANES
+    rest = columns - full * LANES
+    kinds = packed.shape[1]
+    total = jnp.zeros((halo, kinds, lanes), F32)
+    for t in range(full):
+        part = packed[t * halo : (t + 1) * halo]
+        total = total + unpacked_wide(part, t * LANES + halo, lanes)
+    if rest:
+        total = total + unpacked_strip(packed[full * halo :], halo, rest, full * LANES + halo, lanes)
+    return total
+
+
+def unpacked_wide(part, first, lanes):
+    wide = part.astype(F32)
+    if lanes > LANES:
+        rest = jnp.zeros(part.shape[:2] + (lanes - LANES,), F32)
+        wide = jnp.concatenate([wide, rest], axis=2)
+    return turn_lanes(wide, first)
+
+
+def pack_kernel(columns, halo, near_ref, up_ref, down_ref, left_ref, right_ref):
+    cells = near_ref[...].astype(F32)
+    height = cells.shape[0]
+    up_ref[...] = packed_main(cells[:halo], columns).astype(BF)
+    down_ref[...] = packed_main(cells[height - halo :], columns).astype(BF)
+    left_ref[...] = packed_strip(cells, 0, halo).astype(BF)
+    right_ref[...] = packed_strip(cells, columns - halo, halo).astype(BF)
+
+
+def window_pieces(columns, halo, near_ref, main_refs, side_refs, corner_refs, p_ref):
+    height, _, lanes = near_ref.shape
+    right = columns + halo
+    own = turn_lanes(near_ref[...].astype(F32), halo)
+    own = own + unpacked_strip(side_refs[0][...], height, halo, 0, lanes)
+    own = own + unpacked_strip(side_refs[1][...], height, halo, right, lanes)
+    p_ref[halo : halo + height] = own.astype(BF)
+    rows = strip_plan(height, halo)[1]
+    for main, corner, first, at in (
+        (main_refs[0], corner_refs[0], height - halo, 0),
+        (main_refs[1], corner_refs[1], 0, halo + height),
+    ):
+        total = unpacked_main(main[...], columns, halo, lanes)
+        for packed, lane in ((corner[:rows], 0), (corner[rows:], right)):
+            total = total + unpacked_strip(packed, height, halo, lane, lanes)[first : first + halo]
+        p_ref[at : at + halo] = total.astype(BF)
+
+
+def adjoint_kernel(
+    columns, radius, place_ref, obs_ref, taps_ref, basis_ref, give_ref, keep_ref, acc, ys, mats, rows, lines
+):
     step = pl.program_id(0)
     group, height, _ = obs_ref.shape
     span = ys.shape[3]
@@ -76,6 +192,10 @@
     def _():
         acc[...] = jnp.zeros_like(acc)
         mats[...] = jnp.zeros_like(mats)
+        both = taps_ref[...]
+        taps = both.shape[1] // 2
+        for i, line in enumerate(placed_taps(both, [(taps, -radius % SUB, False), (0, 0, True)], F32)):
+            lines[i] = line[:, None]
 
     @pl.loop(0, group, step=batch)
     def _(start):
@@ -83,14 +203,14 @@
         blank = jnp.zeros((edge, width), BF)
         for b in range(batch):
             b = start + b
-            ring = toeplitz(taps_ref[b, 4:5], width, -round_up(radius, SUB)).astype(BF)
+            ring = toeplitz(lines[0, step * group + b], width, -round_up(radius, SUB)).astype(BF)
             top, bottom = ring[:edge], ring[width - edge :]
             mats[b, LANES - edge : LANES] = jnp.where(near, bottom, blank)
             mats[b, LANES : LANES + edge] = jnp.where(near, top, blank)
             mats[b, LANES + edge : LANES + width - edge] = ring[edge : width - edge]
             mats[b, LANES + width - edge : LANES + width] = jnp.where(near, blank, bottom)
             mats[b, LANES + width : LANES + width + edge] = jnp.where(near, blank, top)
-            reach = toeplitz(taps_ref[b, 1:2, :LANES], ext, -2 * radius)[:, :height]
+            reach = toeplitz(lines[1, step * group + b][:, :LANES], ext, -2 * radius)[:, :height]
             high = reach.astype(BF)
             rows[b, 0] = high
             rows[b, 1] = (reach - high.astype(F32)).astype(BF)
@@ -120,33 +240,85 @@
             for c in range(chunks):
                 ys[c, start + b] = done[c * SUB : (c + 1) * SUB]
 
+    bands, kinds = basis_ref.shape
+    first = place_ref[0] + step * group
+    turn = place_ref[1]
+    pick = chosen((SUB * kinds, kinds), lambda row, lane: lane == (row + turn) % kinds)
+    wide = dot_rows(pick, basis_ref[...]).astype(BF)
+    here = chosen((bands, group * SUB), lambda row, lane: row == first + lane // SUB)
+    same = chosen((SUB * kinds, group * SUB), lambda row, lane: row // kinds == lane % SUB, F32)
+    mix = (dot(wide, here) * same).astype(BF)
     for c in range(chunks):
         cells = ys[c].reshape(group * SUB, span).astype(BF)
-        acc[c] += dot(mix_ref[0], cells)
+        acc[c] += dot(mix, cells)
 
     @pl.when(step == pl.num_programs(0) - 1)
     def _():
-        out_ref[...] = acc[...].reshape(out_ref.shape).astype(out_ref.dtype)
-
-
-def gram_kernel(columns, halo, taps_ref, row_mask_ref, col_mask_ref, gr_ref, gl_ref):
+        half = kinds // 2
+        total = acc[...].reshape(ext, kinds, span).astype(BF)
+        give_ref[...] = total[:, :half]
+        keep_ref[...] = total[:, half:]
+
+
+def gram_kernel(sizes, radius, place_ref, taps_ref, basis_ref, gr_ref, gl_ref, sk_ref, pk_ref):
+    columns, columns_all, rows_all = sizes
+    halo = 2 * radius
     group, height, row_lanes = gr_ref.shape
-    size = col_mask_ref.shape[1]
+    size = 2 * LANES
     blocks = packed_blocks(columns, halo)
     tall = max(end for _, end in blocks)
     inner = round_up(columns + halo, 2 * SUB)
+    both = taps_ref[...]
+    taps = both.shape[1] // 2
+    places = [(0, 0, False), (0, 0, True), (taps, 0, False), (taps, 0, True)]
+    row_line, row_back, col_line, col_back = placed_taps(both, places, BF)
+    row_line, row_back = row_line[:, :row_lanes], row_back[:, :row_lanes]
+
+    def inside(lanes, first, count, limit):
+        lane = lax.broadcasted_iota(jnp.int32, (1, lanes), 1)
+        at = lane + first
+        return jnp.where((at >= 0) & (at < limit) & (lane < count), 1.0, 0.0)
+
+    col_mask = inside(size, place_ref[2], columns + halo, columns_all)
+    row_mask = inside(row_lanes, place_ref[3], height + halo, rows_all)
     for b in range(group):
-        left = (toeplitz(taps_ref[b, 3:4, :size], tall, -halo) * col_mask_ref[...]).astype(BF)
-        right = toeplitz(taps_ref[b, 2:3, :size], inner, -halo).astype(BF)
+        left = (toeplitz(col_back[b : b + 1], tall, -halo) * col_mask).astype(BF)
+        right = toeplitz(col_line[b : b + 1], inner, -halo).astype(BF)
         right = jnp.concatenate([right, jnp.zeros((size - inner, size), BF)], axis=0)
         done = dot(left, right).astype(BF)
         at = 0
         for i, (start, end) in enumerate(blocks):
             gl_ref[b, at : at + end - start] = done[start:end, i * LANES : (i + 1) * LANES]
             at += end - start
-        left = (toeplitz(taps_ref[b, 1:2, :row_lanes], height, 0) * row_mask_ref[...]).astype(BF)
-        right = toeplitz(taps_ref[b, 0:1, :row_lanes], row_lanes, 0).astype(BF)
+        left = (toeplitz(row_back[b : b + 1], height, 0) * row_mask).astype(BF)
+        right = toeplitz(row_line[b : b + 1], row_lanes, 0).astype(BF)
         gr_ref[b] = dot(left, right).astype(BF)
+    basis = basis_ref[...]
+    kinds = basis.shape[1]
+    up = chosen((group * SUB, group), lambda row, lane: row // SUB == lane)
+    out = chosen((kinds, SUB * kinds), lambda row, lane: row == lane % kinds)
+    same = chosen((group * SUB, SUB * kinds), lambda row, lane: row % SUB == lane // kinds, F32)
+    sk_ref[...] = (dot(dot(up, basis).astype(BF), out) * same).astype(BF)
+    up = chosen((SUB * kinds, kinds), lambda row, lane: row // SUB == lane)
+    out = chosen((group, group * SUB), lambda row, lane: row == lane // SUB)
+    same = chosen((SUB * kinds, group * SUB), lambda row, lane: row % SUB == lane % SUB, F32)
+    pk_ref[0] = (dot(dot_rows(up, basis).astype(BF), out) * same).astype(BF)
+
+
+def first_kernel(columns, halo, p_ref, *rest):
+    normal_kernel(columns, halo, True, p_ref, *rest)
+
+
+def second_kernel(columns, halo, near_ref, before, after, left, right, corner_before, corner_after, *rest):
+    *rest, p_ref = rest
+
+    @pl.when(pl.program_id(0) == 0)
+    def _():
+        window_pieces(
+            columns, halo, near_ref, (before, after), (left, right), (corner_before, corner_after), p_ref
+        )
+
+    normal_kernel(columns, halo, False, p_ref, *rest)
 
 
 def normal_kernel(
@@ -165,7 +337,7 @@
         halves = []
         for s in (c, c + SUB):
             cells = p_ref[s : s + SUB].reshape(SUB * kinds, lanes)
-            halves.append(dot(sk_ref[0], cells).reshape(group, SUB, lanes))
+            halves.append(dot(sk_ref[...], cells).reshape(group, SUB, lanes))
         xs[:, c : c + 2 * SUB, :] = jnp.concatenate(halves, axis=1).astype(BF)
 
     blocks = packed_blocks(columns, halo)
@@ -189,8 +361,9 @@
         for c in range(chunks):
             ys[c, b] = done[c * SUB : (c + 1) * SUB]
 
+    gather = jnp.concatenate([pk_ref[i] for i in range(pk_ref.shape[0])], axis=1)
     for c in range(chunks):
-        acc[c] += dot(pk_ref[0], ys[c].reshape(group * SUB, lanes).astype(BF))
+        acc[c] += dot(gather, ys[c].reshape(group * SUB, lanes).astype(BF))
 
     @pl.when(step == pl.num_programs(0) - 1)
     def _():
@@ -263,95 +436,82 @@
     chip = me_band // 2
     chips = n_band // 2
 
-    size = lanes
-
-    def widen(values, lead=0):
-        return jnp.pad(values, ((0, 0), (lead, 2 * LANES - taps - lead)))[:, None]
-
     plain = jnp.concatenate([row_taps, col_taps], axis=1)
     everyone = [(plain, me_band)]
     for hop in range(1, n_band):
         moves = [(i, (i + hop) % n_band) for i in range(n_band)]
         everyone.append((lax.ppermute(plain, "band", moves), (me_band - hop) % n_band))
-    basis_here = lax.dynamic_slice_in_dim(spectral_basis, me_band * bands_here, bands_here, 0)
     basis_all = jnp.concatenate(
         [lax.dynamic_slice_in_dim(spectral_basis, at * bands_here, bands_here, 0) for _, at in everyone]
     )
     every = jnp.concatenate([values for values, _ in everyone])
 
-    def variants(values):
-        row, col = values[:, :taps], values[:, taps:]
-        return [widen(row), widen(row[:, ::-1]), widen(col), widen(col[:, ::-1])]
-
-    taps_here = jnp.concatenate(variants(plain) + [widen(col_taps, -radius % SUB)], axis=1)
-
+    half = kinds // 2
+    place = jnp.stack(
+        [me_band * bands_here, half * (1 - core), me_band * columns - radius, me_row * height - radius]
+    ).astype(jnp.int32)
     whole = lambda shape: pl.BlockSpec(shape, lambda i: (0,) * len(shape))
 
     few = group_size(bands_here, 32)
     span = round_up(columns_all, 2 * LANES)
     ext = height + 2 * radius
     chunks = ext // SUB
-    mix = jnp.swapaxes(spread_basis(basis_here, few, kinds), 1, 2)
-    summed = pl.pallas_call(
+    give, keep = pl.pallas_call(
         functools.partial(adjoint_kernel, columns_all, radius),
         grid=(bands_here // few,),
         in_specs=[
+            pl.BlockSpec(memory_space=pltpu.SMEM),
             pl.BlockSpec((few, height, columns_all), lambda i: (i, 0, 0)),
-            pl.BlockSpec((few,) + taps_here.shape[1:], lambda i: (i, 0, 0)),
-            pl.BlockSpec((1,) + mix.shape[1:], lambda i: (i, 0, 0)),
+            whole(plain.shape),
+            whole((bands, kinds)),
         ],
-        out_specs=whole((ext, kinds, span)),
-        out_shape=jax.ShapeDtypeStruct((ext, kinds, span), BF),
+        out_specs=[whole((ext, half, span))] * 2,
+        out_shape=[jax.ShapeDtypeStruct((ext, half, span), BF)] * 2,
         scratch_shapes=[
             pltpu.VMEM((chunks, SUB * kinds, span), F32),
             pltpu.VMEM((chunks, few, SUB, span), F32),
             pltpu.VMEM((few, 4 * LANES, 2 * LANES), BF),
             pltpu.VMEM((few, 2, ext, height), BF),
+            pltpu.VMEM((2, bands_here, 1, 2 * LANES), F32),
         ],
         compiler_params=pltpu.CompilerParams(vmem_limit_bytes=VMEM_LIMIT),
         cost_estimate=pl.CostEstimate(
             flops=bands_here * 2 * 96 * 512 * 256, bytes_accessed=observed.size * 2, transcendentals=0
         ),
         name="adjoint",
-    )(observed, taps_here, mix)
-
-    summed, every = lax.optimization_barrier((summed, every))
-    taps_all = jnp.concatenate(variants(every), axis=1)
-
-    at = jnp.arange(size)
-    edge = me_band * columns - radius + at
-    col_mask = ((edge >= 0) & (edge < columns_all) & (at < columns + 2 * radius)).astype(F32)[None]
-    at = jnp.arange(LANES)
-    edge = me_row * height - radius + at
-    row_mask = ((edge >= 0) & (edge < height * n_row) & (at < height + 2 * radius)).astype(F32)[None]
-    part = group_size(bands, 16)
+    )(place, observed, plain, spectral_basis)
+
+    give, every = lax.optimization_barrier((give, every))
+
+    part = group_size(bands, 32)
     deep = sum(end - start for start, end in packed_blocks(columns, halo))
-    gr, gl = pl.pallas_call(
-        functools.partial(gram_kernel, columns, halo),
+    gr, gl, sk, pk = pl.pallas_call(
+        functools.partial(gram_kernel, (columns, columns_all, height * n_row), radius),
         grid=(bands // part,),
         in_specs=[
-            pl.BlockSpec((part,) + taps_all.shape[1:], lambda i: (i, 0, 0)),
-            whole((1, LANES)),
-            whole((1, size)),
+            pl.BlockSpec(memory_space=pltpu.SMEM),
+            pl.BlockSpec((part, 2 * taps), lambda i: (i, 0)),
+            pl.BlockSpec((part, kinds), lambda i: (i, 0)),
         ],
         out_specs=[
             pl.BlockSpec((part, height, LANES), lambda i: (i, 0, 0)),
             pl.BlockSpec((part, deep, LANES), lambda i: (i, 0, 0)),
+            pl.BlockSpec((part * SUB, SUB * kinds), lambda i: (i, 0)),
+            pl.BlockSpec((1, SUB * kinds, part * SUB), lambda i: (i, 0, 0)),
         ],
         out_shape=[
             jax.ShapeDtypeStruct((bands, height, LANES), BF),
             jax.ShapeDtypeStruct((bands, deep, LANES), BF),
+            jax.ShapeDtypeStruct((bands * SUB, SUB * kinds), BF),
+            jax.ShapeDtypeStruct((bands // part, SUB * kinds, part * SUB), BF),
         ],
         compiler_params=pltpu.CompilerParams(vmem_limit_bytes=VMEM_LIMIT),
         cost_estimate=pl.CostEstimate(
-            flops=bands * 2 * size**3, bytes_accessed=bands * deep * LANES * 2, transcendentals=0
+            flops=bands * 2 * (2 * LANES) ** 3, bytes_accessed=bands * deep * LANES * 2, transcendentals=0
         ),
         name="gram",
-    )(taps_all, row_mask, col_mask)
-
-    half = kinds // 2
-    keep = lax.dynamic_slice_in_dim(summed, core * half, half, 1)
-    give = lax.dynamic_slice_in_dim(summed, (1 - core) * half, half, 1)
+    )(place, every, basis_all)
+
     pairs = [(i, i ^ 1) for i in range(n_band)]
     got = lax.ppermute(give, "band", pairs)
     pair = keep.astype(F32) + got.astype(F32)
@@ -390,25 +550,22 @@
     v0 = jnp.swapaxes(v0, 0, 1)
     window = jnp.pad(window.astype(BF), ((0, 0), (0, 0), (0, lanes - columns - 2 * halo)))
 
-    group = group_size(bands, 32)
-    sk = spread_basis(basis_all, group, kinds)
-    pk = component_first(sk, kinds)
+    group = part
     ridge = jnp.broadcast_to(ridge_weights[:, None, None], (kinds, SUB, lanes))
     tall = height + 2 * halo
     block = lambda shape: pl.BlockSpec((group,) + shape, lambda i: (i, 0, 0))
 
-    def normal_map(window, own, first):
-        before, after = shift_both(window[:halo], window[height - halo :], "row")
-        cells = jnp.concatenate([before, window, after], axis=0)
+    def normal_map(pieces, own, first):
+        window = [pltpu.VMEM((tall, kinds, lanes), BF)] if not first else []
         return pl.pallas_call(
-            functools.partial(normal_kernel, columns, halo, first),
+            functools.partial(first_kernel if first else second_kernel, columns, halo),
             grid=(bands // group,),
-            in_specs=[
-                whole((tall, kinds, lanes)),
+            in_specs=[whole(piece.shape) for piece in pieces]
+            + [
                 whole((kinds, height, lanes)),
                 whole((kinds, SUB, lanes)),
-                pl.BlockSpec((1,) + sk.shape[1:], lambda i: (i, 0, 0)),
-                pl.BlockSpec((1,) + pk.shape[1:], lambda i: (i, 0, 0)),
+                pl.BlockSpec((group * SUB, SUB * kinds), lambda i: (i, 0)),
+                pl.BlockSpec((group // part, SUB * kinds, part * SUB), lambda i: (i, 0, 0)),
                 block((height, LANES)),
                 block((deep, LANES)),
             ],
@@ -421,21 +578,32 @@
                 pltpu.VMEM((height // SUB, SUB * kinds, lanes), F32),
                 pltpu.VMEM((group, tall, lanes), BF),
                 pltpu.VMEM((height // SUB, group, SUB, lanes), F32),
-            ],
+            ]
+            + window,
             compiler_params=pltpu.CompilerParams(vmem_limit_bytes=VMEM_LIMIT),
             cost_estimate=pl.CostEstimate(
                 flops=bands * 2 * 32 * 512 * 256, bytes_accessed=bands * deep * LANES * 2, transcendentals=0
             ),
             name="normal",
-        )(cells, own, ridge, sk, pk, gr, gl)
-
-    v1, sums1 = normal_map(window, v0, True)
-    near = jnp.swapaxes(v1[:, :, :columns].astype(BF), 0, 1)
-    before, after = shift_both(near[:, :, :halo], near[:, :, columns - halo :], "band")
-    window = jnp.concatenate(
-        [before, near, after, jnp.zeros((height, kinds, lanes - columns - 2 * halo), BF)], axis=2
-    )
-    v2, sums2 = normal_map(window, v1, False)
+        )(*pieces, own, ridge, sk, pk, gr, gl)
+
+    before, after = shift_both(window[:halo], window[height - halo :], "row")
+    v1, sums1 = normal_map([jnp.concatenate([before, window, after], axis=0)], v0, True)
+    near = jnp.swapaxes(v1.astype(BF), 0, 1)
+    main = jax.ShapeDtypeStruct((main_rows(columns, halo), kinds, LANES), BF)
+    side = jax.ShapeDtypeStruct((strip_plan(height, halo)[1], kinds, LANES), BF)
+    up, down, left, right = pl.pallas_call(
+        functools.partial(pack_kernel, columns, halo),
+        out_shape=[main, main, side, side],
+        compiler_params=pltpu.CompilerParams(vmem_limit_bytes=VMEM_LIMIT),
+        name="pack",
+    )(near)
+    before, after = shift_both(up, down, "row")
+    from_left, from_right = shift_both(left, right, "band")
+    corners = jnp.concatenate([from_left, from_right], axis=0)
+    corner_before, corner_after = shift_both(corners, corners, "row")
+    pieces = [near, before, after, from_left, from_right, corner_before, corner_after]
+    v2, sums2 = normal_map(pieces, v1, False)
 
     sums = jnp.concatenate([sums1[:3], sums2[:1], jnp.zeros((SUB - 4, LANES), F32)])
     mine = jnp.broadcast_to(sums[None], (n_band * n_row, SUB, LANES))

time: 174 us -> 166 us (0.954)
  starting transfers between devices: 33.3 us -> 42.5 us
  other arithmetic: 11 us -> 3.5 us
  blocking collectives: 21.6 us -> 15.1 us
  local copies, waits for them, and re-layouts: 17.8 us -> 11.4 us
  Pallas kernels: 64.2 us -> 68.6 us
    ppermute x3 -> x4, starting transfers between devices: 12.4 us -> 20.6 us  [shift_both(): lax.ppermute(high_edge, axis, [(i, i + 1) for i in range(count - 1)])]
    all_to_all x1, blocking collectives: 21.6 us -> 15.1 us  [local(): shared = lax.all_to_all(mine, ('band', 'row'), 0, 0, tiled=True)]
    pallas_call x3 -> x4, Pallas kernels: 48.1 us -> 51.7 us  [the longest x2 30.7 us: normal_map(): pl.pallas_call(functools.partial(first_kernel if first else second_kernel...]
    concatenate x4 -> x2, other arithmetic: 3.01 us -> 0.17 us  [the longest x1 0.09 us: local(): jnp.concatenate([before, window, after], axis=0)]
    ppermute x3 -> x4, waiting for transfers between devices: 7.19 us -> 5.27 us  [shift_both(): lax.ppermute(low_edge, axis, [(i + 1, i) for i in range(count - 1)])]
    ppermute x1, waiting for transfers between devices: 0.01 us -> 1.86 us  [local(): other = lax.ppermute(total, 'band', pairs)]
    ppermute x3 -> x4, starting transfers between devices: 4.1 us -> 5.35 us  [shift_both(): lax.ppermute(low_edge, axis, [(i + 1, i) for i in range(count - 1)])]
    unnamed x26 -> x20, local copies, waits for them, and re-layouts: 3.92 us -> 4.91 us
  transfers between devices with their start and end apart: 16 -> 18, of which waited for: 5 -> 5; matrix products, arithmetic and copies ran while one was open for 6% -> 2% of each run, Pallas kernels for 19% -> 22%
where the time goes in v4:
time: 166 us; the launch traced here: 165 us
  Pallas kernels  68.6 us (41%)
  starting transfers between devices  42.5 us (26%)
  waiting for transfers between devices  22.7 us (14%)
  blocking collectives  15.1 us (9%)
  local copies, waits for them, and re-layouts  11.4 us (7%)
  other arithmetic  3.5 us (2%)
    pallas_call x2, Pallas kernels, normal_map(): pl.pallas_call(functools.partial(first_kernel if first else second_kernel...  30.7 us
    ppermute x4, starting transfers between devices, shift_both(): lax.ppermute(high_edge, axis, [(i, i + 1) for i in range(count - 1)])  20.6 us
    pallas_call x1, Pallas kernels, local(): pl.pallas_call(functools.partial(gram_kernel, (columns, columns_all, heig...  20.5 us
    pallas_call x1, Pallas kernels, local(): pl.pallas_call(functools.partial(adjoint_kernel, columns_all, radius), gr...  15.2 us
    all_to_all x1, blocking collectives, local(): shared = lax.all_to_all(mine, ('band', 'row'), 0, 0, tiled=True)  15.1 us
    ppermute x2, starting transfers between devices, local(): before = lax.ppermute(below.astype(BF), axes, moves(hop, 1)).astype(F32)  8.69 us
    ppermute x2, waiting for transfers between devices, local(): before = lax.ppermute(below.astype(BF), axes, moves(hop, 1)).astype(F32)  8.44 us
    ppermute x4, starting transfers between devices, shift_both(): lax.ppermute(low_edge, axis, [(i + 1, i) for i in range(count - 1)])  5.35 us
  transfers between devices with their start and end apart: 18, of which 5 were waited for; matrix products, arithmetic and copies ran while one was open for 2% of the time, Pallas kernels for 22%

profile of v4, /device:TPU:0, one launch (start us, length us, event | category | flops | bytes accessed | tf_op | source)
XLA Modules:
  0.0 164.8 jit_solution(17257965858557101678)
XLA Ops:
  0.6 0.8 copy.18
  1.4 0.8 copy.19
  2.2 0.1 pad_maximum_fusion.2.taps_ref
  2.3 2.4 %collective-permute-start.2 = (f32[56,50]{1,0:T(8,128)S(1)}, f32[56,50]{1,0:T(8,128)S(1)}, u32[]{:S(2)}, u32[]{:S(2)}) collective-permute-start(f32[56,50]{1,0:T(8,128)S(1)} %pad_maximum_fusion.2.taps_ref), channel_id=1, source_target_pairs={{0,24},{8,0},{16,8},{24,16},{1,25},{9,1},{17,9},{25,17},{2,26},{10... | collective-permute-start | bytes 33608 | tf_op jit(solution)/shard_map/ppermute | solution.py:443
  4.7 0.6 collective-permute-start.1
  5.3 0.2 collective-permute-start
  5.5 0.8 copy.20.basis_ref
  6.3 0.1 pad_add_fusion.place_ref
  6.4 15.2 %adjoint.1 = (bf16[56,16,768]{2,1,0:T(8,128)(2,1)S(1)}, bf16[56,16,768]{2,1,0:T(8,128)(2,1)S(1)}) custom-call(s32[4]{0:T(128)S(1)} %pad_add_fusion.place_ref, bf16[56,32,680]{2,1,0:T(8,128)(2,1)} %obs_ref.1, f32[56,50]{1,0:T(8,128)S(1)} %pad_maximum_fusion.2.taps_ref, bf16[224,32]{1,0:T(8,128)(2,1)S(1)} %copy.20.basis_ref), custom_call_target="tpu_custom_call" | custom-call | flops 1409286144 | bytes 2437120 | tf_op jit(solution)/shard_map/adjoint/pallas_call | solution.py:459
  21.6 0.0 collective-permute-done.2
  21.6 0.0 collective-permute-done.1
  21.6 0.1 pad_maximum_fusion.1.taps_ref
  21.7 1.5 copy.22
  23.2 1.4 collective-permute-start.3
  24.6 3.0 %collective-permute-done.3 = bf16[56,16,768]{2,0,1:T(8,128)(2,1)S(1)} collective-permute-done((bf16[56,16,768]{2,0,1:T(8,128)(2,1)}, bf16[56,16,768]{2,0,1:T(8,128)(2,1)S(1)}, u32[]{:S(2)}, u32[]{:S(2)}) %collective-permute-start.3) | collective-permute-done | bytes 1376288 | tf_op jit(solution)/shard_map/ppermute | solution.py:516
  27.6 0.5 convert_add_fusion
  28.1 0.6 dynamic-slice_convert_fusion.1
  28.7 0.1 fusion.11
  28.7 3.3 %collective-permute-start.4 = (bf16[12,16,364]{2,0,1:T(8,128)(2,1)S(1)}, bf16[12,16,364]{2,0,1:T(8,128)(2,1)S(1)}, u32[]{:S(2)}, u32[]{:S(2)}) collective-permute-start(bf16[12,16,364]{2,0,1:T(8,128)(2,1)S(1)} %get-tuple-element.40), channel_id=1, source_target_pairs={{0,1},{1,2},{2,3},{3,4},{4,5},{5,6},{6,7},{8,9},{9,10},{10,11},{11... | collective-permute-start | bytes 419336 | tf_op jit(solution)/shard_map/ppermute | solution.py:537
  32.1 1.3 collective-permute-start.5
  33.4 0.0 copy-start.6
  33.4 0.1 slice.51
  33.5 0.7 collective-permute-start.6
  34.2 0.1 fusion.12
  34.3 5.4 %collective-permute-start.7 = (bf16[12,16,364]{2,0,1:T(8,128)(2,1)S(1)}, bf16[12,16,364]{2,0,1:T(8,128)(2,1)S(1)}, u32[]{:S(2)}, u32[]{:S(2)}) collective-permute-start(bf16[12,16,364]{2,0,1:T(8,128)(2,1)S(1)} %get-tuple-element.42), channel_id=1, source_target_pairs={{0,17},{1,18},{2,19},{3,20},{4,21},{5,22},{6,23},{8,25},{9,26},{10... | collective-permute-start | bytes 419336 | tf_op jit(solution)/shard_map/ppermute | solution.py:537
  39.7 1.3 collective-permute-start.8
  41.0 8.4 %collective-permute-done.7 = bf16[12,16,364]{2,0,1:T(8,128)(2,1)S(1)} collective-permute-done((bf16[12,16,364]{2,0,1:T(8,128)(2,1)S(1)}, bf16[12,16,364]{2,0,1:T(8,128)(2,1)S(1)}, u32[]{:S(2)}, u32[]{:S(2)}) %collective-permute-start.7) | collective-permute-done | bytes 139808 | tf_op jit(solution)/shard_map/ppermute | solution.py:537
  49.4 1.8 %fusion.7 = f32[32,16,364]{2,0,1:T(8,128)S(1)} fusion(f32[56,16,768]{2,0,1:T(8,128)} %copy-done.5, s32[]{:T(128)S(6)} %add.101, s32[]{:T(128)S(6)} %min.10, bf16[32,16,364]{2,0,1:T(8,128)(2,1)S(1)} %collective-permute-done.6, bf16[12,16,364]{2,0,1:T(8,128)(2,1)S(1)} %collective-permute-done.8, bf16[12,16,364]{2,0,1:T(8,128)(2,1)S(1)} %collective-permute-done.7, ...), kind=kLoop, calls=%fused_computation.17 | loop fusion | flops 1863680 | bytes 2422792 | tf_op jit(solution)/shard_map/add | solution.py:542
  51.2 0.1 collective-permute-start.9
  51.3 0.1 constant_dynamic-slice_fusion.3
  51.5 0.1 pad_maximum_fusion.3
  51.5 0.1 copy.23.basis_ref
  51.7 1.9 %collective-permute-done.9 = f32[32,16,364]{2,0,1:T(8,128)S(1)} collective-permute-done((f32[32,16,364]{2,0,1:T(8,128)S(1)}, f32[32,16,364]{2,0,1:T(8,128)S(1)}, u32[]{:S(2)}, u32[]{:S(2)}) %collective-permute-start.9) | collective-permute-done | bytes 745504 | tf_op jit(solution)/shard_map/ppermute | solution.py:543
  53.5 0.1 broadcast_select_fusion.1
  53.7 0.6 fusion.9
  54.3 0.1 pad_slice_fusion.1
  54.4 8.0 %collective-permute-start.10 = (bf16[24,32,256]{2,0,1:T(8,128)(2,1)S(1)}, bf16[24,32,256]{2,0,1:T(8,128)(2,1)S(1)}, u32[]{:S(2)}, u32[]{:S(2)}) collective-permute-start(bf16[24,32,256]{2,0,1:T(8,128)(2,1)S(1)} %get-tuple-element.44), channel_id=1, source_target_pairs={{0,1},{1,2},{2,3},{3,4},{4,5},{5,6},{6,7},{8,9},{9,10},{10,11},{11... | collective-permute-start | bytes 1179656 | tf_op jit(solution)/shard_map/ppermute | solution.py:418
  62.3 1.5 collective-permute-start.11
  63.8 20.5 %gram.1 = (bf16[224,32,128]{2,1,0:T(8,128)(2,1)S(1)}, bf16[224,272,128]{2,1,0:T(8,128)(2,1)}, bf16[1792,256]{1,0:T(8,128)(2,1)S(1)}, bf16[7,256,256]{2,1,0:T(8,128)(2,1)S(1)}) custom-call(s32[4]{0:T(128)S(1)} %pad_add_fusion.place_ref, f32[224,50]{1,0:T(8,128)S(1)} %pad_maximum_fusion.1.taps_ref, bf16[224,32]{1,0:T(8,128)(2,1)S(1)} %copy.23.basis_ref), custom_call_target="tpu_custom_call" | custom-call | flops 7516192768 | bytes 15597568 | tf_op jit(solution)/shard_map/gram/pallas_call | solution.py:488
  84.3 0.3 slice.54
  84.6 0.1 pad.21
  84.8 1.1 pad_bitcast_fusion.rest_0_.v0_ref
  85.9 0.1 pad_maximum_fusion
  86.0 1.5 copy.24.p_ref
  87.5 0.1 broadcast_in_dim.6.rest_1_
  87.6 14.6 %normal.2 = (f32[32,32,256]{2,1,0:T(8,128)S(1)}, f32[8,128]{1,0:T(8,128)S(1)}) custom-call(bf16[80,32,256]{2,1,0:T(8,128)(2,1)} %copy.24.p_ref, f32[32,32,256]{2,1,0:T(8,128)} %pad_bitcast_fusion.rest_0_.v0_ref, f32[32,8,256]{2,1,0:T(8,128)S(1)} %broadcast_in_dim.6.rest_1_, bf16[1792,256]{1,0:T(8,128)(2,1)S(1)} %get-tuple-element.22.rest_2_, ...), custom_call_target="tpu_custom_call" | custom-call | flops 1879048192 | bytes 15597568 | tf_op jit(solution)/shard_map/normal/pallas_call | solution.py:560
  102.3 0.0 copy-start.1
  102.3 0.6 copy.30
  102.9 0.5 pack.1
  103.4 1.8 %collective-permute-start.14 = (bf16[8,32,128]{2,1,0:T(8,128)(2,1)S(1)}, bf16[8,32,128]{2,1,0:T(8,128)(2,1)S(1)}, u32[]{:S(2)}, u32[]{:S(2)}) collective-permute-start(bf16[8,32,128]{2,1,0:T(8,128)(2,1)S(1)} %get-tuple-element.30), channel_id=1, source_target_pairs={{0,8},{8,16},{16,24},{1,9},{9,17},{17,25},{2,10},{10,18},{18,26},{... | collective-permute-start | bytes 196616 | tf_op jit(solution)/shard_map/ppermute | solution.py:418
  105.1 1.3 collective-permute-start.15
  106.4 5.1 %collective-permute-start.12 = (bf16[32,32,128]{2,1,0:T(8,128)(2,1)S(1)}, bf16[32,32,128]{2,1,0:T(8,128)(2,1)S(1)}, u32[]{:S(2)}, u32[]{:S(2)}) collective-permute-start(bf16[32,32,128]{2,1,0:T(8,128)(2,1)S(1)} %get-tuple-element.28), channel_id=1, source_target_pairs={{0,1},{1,2},{2,3},{3,4},{4,5},{5,6},{6,7},{8,9},{9,10},{10,11},{11... | collective-permute-start | bytes 786440 | tf_op jit(solution)/shard_map/ppermute | solution.py:418
  111.5 1.3 collective-permute-start.13
  112.9 1.3 collective-permute-start.17
  114.2 5.8 %collective-permute-start.16 = (bf16[16,32,128]{2,1,0:T(8,128)(2,1)S(1)}, bf16[16,32,128]{2,1,0:T(8,128)(2,1)S(1)}, u32[]{:S(2)}, u32[]{:S(2)}) collective-permute-start(bf16[16,32,128]{2,1,0:T(8,128)(2,1)S(1)} %constant_dynamic-update-slice_fusion), channel_id=1, source_target_pairs={{0,1},{1,2},{2,3},{3,4},{4,5},{5,6},{6,7},{8,9},{9,10},{10,11},{11... | collective-permute-start | bytes 393224 | tf_op jit(solution)/shard_map/ppermute | solution.py:418
  120.0 0.1 pad.25.clone
  120.0 5.3 %collective-permute-done.17.corner_after = bf16[16,32,128]{2,1,0:T(8,128)(2,1)S(1)} collective-permute-done((bf16[16,32,128]{2,1,0:T(8,128)(2,1)S(1)}, bf16[16,32,128]{2,1,0:T(8,128)(2,1)S(1)}, u32[]{:S(2)}, u32[]{:S(2)}) %collective-permute-start.17) | collective-permute-done | bytes 131104 | tf_op jit(solution)/shard_map/ppermute | solution.py:419
  125.3 4.1 %collective-permute-done.16.corner_before = bf16[16,32,128]{2,1,0:T(8,128)(2,1)S(1)} collective-permute-done((bf16[16,32,128]{2,1,0:T(8,128)(2,1)S(1)}, bf16[16,32,128]{2,1,0:T(8,128)(2,1)S(1)}, u32[]{:S(2)}, u32[]{:S(2)}) %collective-permute-start.16) | collective-permute-done | bytes 131104 | tf_op jit(solution)/shard_map/ppermute | solution.py:418
  129.4 16.0 %normal.3 = (f32[32,32,256]{2,1,0:T(8,128)}, f32[8,128]{1,0:T(8,128)S(1)}) custom-call(bf16[32,32,256]{2,1,0:T(8,128)(2,1)S(1)} %bitcast.10, bf16[32,32,128]{2,1,0:T(8,128)(2,1)S(1)} %collective-permute-done.12.before, bf16[32,32,128]{2,1,0:T(8,128)(2,1)S(1)} %collective-permute-done.13.after, bf16[8,32,128]{2,1,0:T(8,128)(2,1)S(1)} %collective-permute-done.14.left, ...), custom_call_target="tpu_custom_call" | custom-call | flops 1879048192 | bytes 15597568 | tf_op jit(solution)/shard_map/normal/pallas_call | solution.py:560
  145.5 0.1 maximum_maximum_fusion
  145.5 15.1 %all_to_all.5.shared_ref = f32[32,8,128]{2,1,0:T(8,128)S(1)} all-to-all(f32[32,8,128]{2,1,0:T(8,128)S(1)} %broadcast_in_dim.8), channel_id=1, replica_groups=mesh['band'=4,'row'=8] {'band','row'}, dimensions={0} | all-to-all | bytes 262144 | tf_op jit(solution)/shard_map/all_to_all | solution.py:610
  160.6 1.2 copy-done.2
  161.8 1.2 copy-done.4
  163.1 1.8 %combine.1 = (f32[32,32,170]{2,1,0:T(8,128)}, f32[32,32,170]{2,1,0:T(8,128)}) custom-call(f32[32,8,128]{2,1,0:T(8,128)S(1)} %all_to_all.5.shared_ref, f32[32,32,256]{2,1,0:T(8,128)S(1)} %copy-done, f32[32,32,256]{2,1,0:T(8,128)S(1)} %copy-done.2, f32[32,32,256]{2,1,0:T(8,128)S(1)} %copy-done.4), custom_call_target="tpu_custom_call" | custom-call | tf_op jit(solution)/shard_map/combine/pallas_call | solution.py:612
  (29 shorter events, 0.1 us)
Async XLA Ops:
  2.3 19.3 %collective-permute-start.2 = (f32[56,50]{1,0:T(8,128)S(1)}, f32[56,50]{1,0:T(8,128)S(1)}, u32[]{:S(2)}, u32[]{:S(2)}) collective-permute-start(f32[56,50]{1,0:T(8,128)S(1)} %pad_maximum_fusion.2.taps_ref), channel_id=1, source_target_pairs={{0,24},{8,0},{16,8},{24,16},{1,25},{9,1},{17,9},{25,17},{2,26},{10... | collective-permute-start | bytes 33608 | tf_op jit(solution)/shard_map/ppermute | solution.py:443
  4.7 16.9 %collective-permute-start.1 = (f32[56,50]{1,0:T(8,128)S(1)}, f32[56,50]{1,0:T(8,128)S(1)}, u32[]{:S(2)}, u32[]{:S(2)}) collective-permute-start(f32[56,50]{1,0:T(8,128)S(1)} %pad_maximum_fusion.2.taps_ref), channel_id=1, source_target_pairs={{0,16},{8,24},{16,0},{24,8},{1,17},{9,25},{17,1},{25,9},{2,18},{10... | collective-permute-start | bytes 33608 | tf_op jit(solution)/shard_map/ppermute | solution.py:443
  5.3 16.3 %collective-permute-start = (f32[56,50]{1,0:T(8,128)S(1)}, f32[56,50]{1,0:T(8,128)S(1)}, u32[]{:S(2)}, u32[]{:S(2)}) collective-permute-start(f32[56,50]{1,0:T(8,128)S(1)} %pad_maximum_fusion.2.taps_ref), channel_id=1, source_target_pairs={{0,8},{8,16},{16,24},{24,0},{1,9},{9,17},{17,25},{25,1},{2,10},{10... | collective-permute-start | bytes 33608 | tf_op jit(solution)/shard_map/ppermute | solution.py:443
  23.2 4.3 %collective-permute-start.3 = (bf16[56,16,768]{2,0,1:T(8,128)(2,1)}, bf16[56,16,768]{2,0,1:T(8,128)(2,1)S(1)}, u32[]{:S(2)}, u32[]{:S(2)}) collective-permute-start(bf16[56,16,768]{2,0,1:T(8,128)(2,1)} %copy.22), channel_id=1, source_target_pairs={{0,8},{8,0},{16,24},{24,16},{1,9},{9,1},{17,25},{25,17},{2,10},{10... | collective-permute-start | bytes 4128776 | tf_op jit(solution)/shard_map/ppermute | solution.py:516
  28.1 5.4 %copy-start.5 = (f32[56,16,768]{2,0,1:T(8,128)}, f32[56,16,768]{2,0,1:T(8,128)S(1)}, u32[]{:S(2)}) copy-start(f32[56,16,768]{2,0,1:T(8,128)S(1)} %convert_add_fusion) | copy-start | bytes 8257540
  28.7 12.2 %collective-permute-start.4 = (bf16[12,16,364]{2,0,1:T(8,128)(2,1)S(1)}, bf16[12,16,364]{2,0,1:T(8,128)(2,1)S(1)}, u32[]{:S(2)}, u32[]{:S(2)}) collective-permute-start(bf16[12,16,364]{2,0,1:T(8,128)(2,1)S(1)} %get-tuple-element.40), channel_id=1, source_target_pairs={{0,1},{1,2},{2,3},{3,4},{4,5},{5,6},{6,7},{8,9},{9,10},{10,11},{11... | collective-permute-start | bytes 419336 | tf_op jit(solution)/shard_map/ppermute | solution.py:537
  32.1 8.9 %collective-permute-start.5 = (bf16[12,16,364]{2,0,1:T(8,128)(2,1)S(1)}, bf16[12,16,364]{2,0,1:T(8,128)(2,1)S(1)}, u32[]{:S(2)}, u32[]{:S(2)}) collective-permute-start(bf16[12,16,364]{2,0,1:T(8,128)(2,1)S(1)} %get-tuple-element.41), channel_id=1, source_target_pairs={{1,0},{2,1},{3,2},{4,3},{5,4},{6,5},{7,6},{9,8},{10,9},{11,10},{12... | collective-permute-start | bytes 419336 | tf_op jit(solution)/shard_map/ppermute | solution.py:536
  33.4 18.0 %copy-start.6 = (bf16[224,32]{0,1:T(8,128)(2,1)S(1)}, bf16[224,32]{0,1:T(8,128)(2,1)}, u32[]{:S(2)}) copy-start(bf16[224,32]{0,1:T(8,128)(2,1)} %param.8) | copy-start | bytes 43012
  33.5 15.9 %collective-permute-start.6 = (bf16[32,16,364]{2,0,1:T(8,128)(2,1)S(1)}, bf16[32,16,364]{2,0,1:T(8,128)(2,1)S(1)}, u32[]{:S(2)}, u32[]{:S(2)}) collective-permute-start(bf16[32,16,364]{2,0,1:T(8,128)(2,1)S(1)} %slice.51), channel_id=1, source_target_pairs={{0,16},{1,17},{2,18},{3,19},{4,20},{5,21},{6,22},{7,23},{8,24},{9,... | collective-permute-start | bytes 1118216 | tf_op jit(solution)/shard_map/ppermute | solution.py:539
  34.3 15.2 %collective-permute-start.7 = (bf16[12,16,364]{2,0,1:T(8,128)(2,1)S(1)}, bf16[12,16,364]{2,0,1:T(8,128)(2,1)S(1)}, u32[]{:S(2)}, u32[]{:S(2)}) collective-permute-start(bf16[12,16,364]{2,0,1:T(8,128)(2,1)S(1)} %get-tuple-element.42), channel_id=1, source_target_pairs={{0,17},{1,18},{2,19},{3,20},{4,21},{5,22},{6,23},{8,25},{9,26},{10... | collective-permute-start | bytes 419336 | tf_op jit(solution)/shard_map/ppermute | solution.py:537
  39.7 9.8 %collective-permute-start.8 = (bf16[12,16,364]{2,0,1:T(8,128)(2,1)S(1)}, bf16[12,16,364]{2,0,1:T(8,128)(2,1)S(1)}, u32[]{:S(2)}, u32[]{:S(2)}) collective-permute-start(bf16[12,16,364]{2,0,1:T(8,128)(2,1)S(1)} %get-tuple-element.43), channel_id=1, source_target_pairs={{1,16},{2,17},{3,18},{4,19},{5,20},{6,21},{7,22},{9,24},{10,25},{1... | collective-permute-start | bytes 419336 | tf_op jit(solution)/shard_map/ppermute | solution.py:536
  51.2 2.4 %collective-permute-start.9 = (f32[32,16,364]{2,0,1:T(8,128)S(1)}, f32[32,16,364]{2,0,1:T(8,128)S(1)}, u32[]{:S(2)}, u32[]{:S(2)}) collective-permute-start(f32[32,16,364]{2,0,1:T(8,128)S(1)} %fusion.7), channel_id=1, source_target_pairs={{0,8},{8,0},{16,24},{24,16},{1,9},{9,1},{17,25},{25,17},{2,10},{10... | collective-permute-start | bytes 2236424 | tf_op jit(solution)/shard_map/ppermute | solution.py:543
  54.4 31.5 %collective-permute-start.10 = (bf16[24,32,256]{2,0,1:T(8,128)(2,1)S(1)}, bf16[24,32,256]{2,0,1:T(8,128)(2,1)S(1)}, u32[]{:S(2)}, u32[]{:S(2)}) collective-permute-start(bf16[24,32,256]{2,0,1:T(8,128)(2,1)S(1)} %get-tuple-element.44), channel_id=1, source_target_pairs={{0,1},{1,2},{2,3},{3,4},{4,5},{5,6},{6,7},{8,9},{9,10},{10,11},{11... | collective-permute-start | bytes 1179656 | tf_op jit(solution)/shard_map/ppermute | solution.py:418
  62.3 23.5 %collective-permute-start.11 = (bf16[24,32,256]{2,0,1:T(8,128)(2,1)S(1)}, bf16[24,32,256]{2,0,1:T(8,128)(2,1)S(1)}, u32[]{:S(2)}, u32[]{:S(2)}) collective-permute-start(bf16[24,32,256]{2,0,1:T(8,128)(2,1)S(1)} %get-tuple-element.45), channel_id=1, source_target_pairs={{1,0},{2,1},{3,2},{4,3},{5,4},{6,5},{7,6},{9,8},{10,9},{11,10},{12... | collective-permute-start | bytes 1179656 | tf_op jit(solution)/shard_map/ppermute | solution.py:419
  84.3 1.6 copy-start.3
  85.9 1.7 %copy-start.7 = (f32[32]{0:T(128)S(1)}, f32[32]{0:T(128)}, u32[]{:S(2)}) copy-start(f32[32]{0:T(128)} %param.9) | copy-start | bytes 388
  102.3 27.1 %copy-start.1 = (f32[32,32,256]{2,1,0:T(8,128)}, f32[32,32,256]{2,1,0:T(8,128)S(1)}, u32[]{:S(2)}) copy-start(f32[32,32,256]{2,1,0:T(8,128)S(1)} %get-tuple-element.27.rest_0_.v1_ref) | copy-start | bytes 3145732
  103.4 9.5 %collective-permute-start.14 = (bf16[8,32,128]{2,1,0:T(8,128)(2,1)S(1)}, bf16[8,32,128]{2,1,0:T(8,128)(2,1)S(1)}, u32[]{:S(2)}, u32[]{:S(2)}) collective-permute-start(bf16[8,32,128]{2,1,0:T(8,128)(2,1)S(1)} %get-tuple-element.30), channel_id=1, source_target_pairs={{0,8},{8,16},{16,24},{1,9},{9,17},{17,25},{2,10},{10,18},{18,26},{... | collective-permute-start | bytes 196616 | tf_op jit(solution)/shard_map/ppermute | solution.py:418
  105.1 7.7 %collective-permute-start.15 = (bf16[8,32,128]{2,1,0:T(8,128)(2,1)S(1)}, bf16[8,32,128]{2,1,0:T(8,128)(2,1)S(1)}, u32[]{:S(2)}, u32[]{:S(2)}) collective-permute-start(bf16[8,32,128]{2,1,0:T(8,128)(2,1)S(1)} %get-tuple-element.31), channel_id=1, source_target_pairs={{8,0},{16,8},{24,16},{9,1},{17,9},{25,17},{10,2},{18,10},{26,18},{... | collective-permute-start | bytes 196616 | tf_op jit(solution)/shard_map/ppermute | solution.py:419
  106.4 23.0 %collective-permute-start.12 = (bf16[32,32,128]{2,1,0:T(8,128)(2,1)S(1)}, bf16[32,32,128]{2,1,0:T(8,128)(2,1)S(1)}, u32[]{:S(2)}, u32[]{:S(2)}) collective-permute-start(bf16[32,32,128]{2,1,0:T(8,128)(2,1)S(1)} %get-tuple-element.28), channel_id=1, source_target_pairs={{0,1},{1,2},{2,3},{3,4},{4,5},{5,6},{6,7},{8,9},{9,10},{10,11},{11... | collective-permute-start | bytes 786440 | tf_op jit(solution)/shard_map/ppermute | solution.py:418
  111.5 17.9 %collective-permute-start.13 = (bf16[32,32,128]{2,1,0:T(8,128)(2,1)S(1)}, bf16[32,32,128]{2,1,0:T(8,128)(2,1)S(1)}, u32[]{:S(2)}, u32[]{:S(2)}) collective-permute-start(bf16[32,32,128]{2,1,0:T(8,128)(2,1)S(1)} %get-tuple-element.29), channel_id=1, source_target_pairs={{1,0},{2,1},{3,2},{4,3},{5,4},{6,5},{7,6},{9,8},{10,9},{11,10},{12... | collective-permute-start | bytes 786440 | tf_op jit(solution)/shard_map/ppermute | solution.py:419
  112.9 12.4 %collective-permute-start.17 = (bf16[16,32,128]{2,1,0:T(8,128)(2,1)S(1)}, bf16[16,32,128]{2,1,0:T(8,128)(2,1)S(1)}, u32[]{:S(2)}, u32[]{:S(2)}) collective-permute-start(bf16[16,32,128]{2,1,0:T(8,128)(2,1)S(1)} %constant_dynamic-update-slice_fusion), channel_id=1, source_target_pairs={{1,0},{2,1},{3,2},{4,3},{5,4},{6,5},{7,6},{9,8},{10,9},{11,10},{12... | collective-permute-start | bytes 393224 | tf_op jit(solution)/shard_map/ppermute | solution.py:419
  114.2 15.2 %collective-permute-start.16 = (bf16[16,32,128]{2,1,0:T(8,128)(2,1)S(1)}, bf16[16,32,128]{2,1,0:T(8,128)(2,1)S(1)}, u32[]{:S(2)}, u32[]{:S(2)}) collective-permute-start(bf16[16,32,128]{2,1,0:T(8,128)(2,1)S(1)} %constant_dynamic-update-slice_fusion), channel_id=1, source_target_pairs={{0,1},{1,2},{2,3},{3,4},{4,5},{5,6},{6,7},{8,9},{9,10},{10,11},{11... | collective-permute-start | bytes 393224 | tf_op jit(solution)/shard_map/ppermute | solution.py:418
  120.0 40.6 %copy-start = (f32[32,32,256]{2,1,0:T(8,128)S(1)}, f32[32,32,256]{2,1,0:T(8,128)}, u32[]{:S(2)}) copy-start(f32[32,32,256]{2,1,0:T(8,128)} %pad_bitcast_fusion.rest_0_.v0_ref) | copy-start | bytes 3145732
  160.6 1.2 copy-start.2
  161.8 1.2 copy-start.4

commit v5 on v4

--- a/solution.py
+++ b/solution.py
@@ -260,38 +260,42 @@
         keep_ref[...] = total[:, half:]
 
 
-def gram_kernel(sizes, radius, place_ref, taps_ref, basis_ref, gr_ref, gl_ref, sk_ref, pk_ref):
-    columns, columns_all, rows_all = sizes
+def inside(lanes, first, count, limit):
+    lane = lax.broadcasted_iota(jnp.int32, (1, lanes), 1)
+    at = lane + first
+    return jnp.where((at >= 0) & (at < limit) & (lane < count), 1.0, 0.0)
+
+
+def gram_columns_kernel(columns, columns_all, radius, place_ref, taps_ref, gl_ref):
     halo = 2 * radius
-    group, height, row_lanes = gr_ref.shape
     size = 2 * LANES
     blocks = packed_blocks(columns, halo)
     tall = max(end for _, end in blocks)
     inner = round_up(columns + halo, 2 * SUB)
     both = taps_ref[...]
     taps = both.shape[1] // 2
-    places = [(0, 0, False), (0, 0, True), (taps, 0, False), (taps, 0, True)]
-    row_line, row_back, col_line, col_back = placed_taps(both, places, BF)
-    row_line, row_back = row_line[:, :row_lanes], row_back[:, :row_lanes]
-
-    def inside(lanes, first, count, limit):
-        lane = lax.broadcasted_iota(jnp.int32, (1, lanes), 1)
-        at = lane + first
-        return jnp.where((at >= 0) & (at < limit) & (lane < count), 1.0, 0.0)
-
-    col_mask = inside(size, place_ref[2], columns + halo, columns_all)
-    row_mask = inside(row_lanes, place_ref[3], height + halo, rows_all)
-    for b in range(group):
-        left = (toeplitz(col_back[b : b + 1], tall, -halo) * col_mask).astype(BF)
-        right = toeplitz(col_line[b : b + 1], inner, -halo).astype(BF)
+    line, back = placed_taps(both, [(taps, 0, False), (taps, 0, True)], BF)
+    mask = inside(size, place_ref[2], columns + halo, columns_all)
+    for b in range(both.shape[0]):
+        left = (toeplitz(back[b : b + 1], tall, -halo) * mask).astype(BF)
+        right = toeplitz(line[b : b + 1], inner, -halo).astype(BF)
         right = jnp.concatenate([right, jnp.zeros((size - inner, size), BF)], axis=0)
         done = dot(left, right).astype(BF)
         at = 0
         for i, (start, end) in enumerate(blocks):
             gl_ref[b, at : at + end - start] = done[start:end, i * LANES : (i + 1) * LANES]
             at += end - start
-        left = (toeplitz(row_back[b : b + 1], height, 0) * row_mask).astype(BF)
-        right = toeplitz(row_line[b : b + 1], row_lanes, 0).astype(BF)
+
+
+def gram_rows_kernel(rows_all, radius, place_ref, taps_ref, basis_ref, gr_ref, sk_ref, pk_ref):
+    halo = 2 * radius
+    group, height, lanes = gr_ref.shape
+    both = taps_ref[...]
+    line, back = [part[:, :lanes] for part in placed_taps(both, [(0, 0, False), (0, 0, True)], BF)]
+    mask = inside(lanes, place_ref[3], height + halo, rows_all)
+    for b in range(group):
+        left = (toeplitz(back[b : b + 1], height, 0) * mask).astype(BF)
+        right = toeplitz(line[b : b + 1], lanes, 0).astype(BF)
         gr_ref[b] = dot(left, right).astype(BF)
     basis = basis_ref[...]
     kinds = basis.shape[1]
@@ -305,8 +309,80 @@
     pk_ref[0] = (dot(dot_rows(up, basis).astype(BF), out) * same).astype(BF)
 
 
-def first_kernel(columns, halo, p_ref, *rest):
-    normal_kernel(columns, halo, True, p_ref, *rest)
+def lane_window(cells, first, width, lanes):
+    have = cells.shape[1]
+    base = max(first, 0) // LANES * LANES
+    stop = min(have, round_up(first + width, LANES))
+    part = cells[:, base:stop]
+    size = max(stop - base, lanes)
+    if size > stop - base:
+        part = jnp.concatenate([part, jnp.zeros((cells.shape[0], size - (stop - base)), F32)], axis=1)
+    if (base - first) % size:
+        part = pltpu.roll(part, (base - first) % size, 1)
+    lane = lax.broadcasted_iota(jnp.int32, (cells.shape[0], lanes), 1)
+    low, high = max(0, -first), min(width, have - first)
+    return jnp.where((lane >= low) & (lane < high), part[:, :lanes], 0.0)
+
+
+def split_kernel(starts, wide, radius, place_ref, keep_ref, got_ref, *out_refs):
+    chips = len(starts)
+    ext, half, span = keep_ref.shape
+    lanes = out_refs[0].shape[2]
+    unit = 4
+    for chip in range(chips):
+
+        @pl.when(place_ref[4] == chip)
+        def _():
+            for r in range(0, ext, unit):
+                pair = keep_ref[r : r + unit].astype(F32) + got_ref[r : r + unit].astype(F32)
+                flat = pair.reshape(unit * half, span)
+                for hop in range(chips):
+                    part = lane_window(flat, starts[(chip + hop) % chips], wide, lanes)
+                    part = part.reshape(unit, half, lanes)
+                    above, here, below = out_refs[3 * hop : 3 * hop + 3]
+                    if r < radius:
+                        above[r : r + unit] = part.astype(above.dtype)
+                    elif r < ext - radius:
+                        here[r - radius : r - radius + unit] = part.astype(here.dtype)
+                    else:
+                        below[r - ext + radius : r - ext + radius + unit] = part.astype(below.dtype)
+
+
+def merge_kernel(radius, *refs):
+    *in_refs, out_ref = refs
+    height = out_ref.shape[0]
+    total = in_refs[1][...].astype(F32)
+    for i in range(4, len(in_refs), 3):
+        total = total + in_refs[i][...].astype(F32)
+    first = sum(in_refs[i][...].astype(F32) for i in range(0, len(in_refs), 3))
+    last = sum(in_refs[i][...].astype(F32) for i in range(2, len(in_refs), 3))
+    out_ref[:radius] = total[:radius] + first
+    out_ref[radius : height - radius] = total[radius : height - radius]
+    out_ref[height - radius :] = total[height - radius :] + last
+
+
+def window_kernel(starts, wide, columns, halo, place_ref, mine_ref, other_ref, window_ref, own_ref):
+    height, half, lanes_in = mine_ref.shape
+    lanes = window_ref.shape[2]
+    unit = 4
+    for band in range(2 * len(starts)):
+        first = band * columns - starts[band // 2]
+
+        @pl.when(place_ref[5] == band)
+        def _():
+            for r in range(0, height, unit):
+                for core in range(2):
+                    source = mine_ref if core == band % 2 else other_ref
+                    flat = source[r : r + unit].reshape(unit * half, lanes_in)
+                    kinds = slice(core * half, (core + 1) * half)
+                    part = lane_window(flat, first - halo, columns + 2 * halo, lanes)
+                    window_ref[r : r + unit, kinds] = part.reshape(unit, half, lanes).astype(BF)
+                    part = lane_window(flat, first, columns, lanes)
+                    own_ref[r : r + unit, kinds] = part.reshape(unit, half, lanes)
+
+
+def first_kernel(columns, halo, before, window, after, *rest):
+    normal_kernel(columns, halo, True, (before, window, after), *rest)
 
 
 def second_kernel(columns, halo, near_ref, before, after, left, right, corner_before, corner_after, *rest):
@@ -318,15 +394,17 @@
             columns, halo, near_ref, (before, after), (left, right), (corner_before, corner_after), p_ref
         )
 
-    normal_kernel(columns, halo, False, p_ref, *rest)
+    normal_kernel(columns, halo, False, (p_ref,), *rest)
 
 
 def normal_kernel(
-    columns, halo, first, p_ref, own_ref, ridge_ref, sk_ref, pk_ref, gr_ref, gl_ref, out_ref, sums_ref, acc, xs, ys
+    columns, halo, first, p_refs, own_ref, ridge_ref, sk_ref, pk_ref, gr_ref, gl_ref, out_ref, sums_ref, acc, xs, ys
 ):
     step = pl.program_id(0)
     group, height, _ = gr_ref.shape
-    ext, kinds, lanes = p_ref.shape
+    _, kinds, lanes = p_refs[0].shape
+    sources = [(ref, s) for ref in p_refs for s in range(0, ref.shape[0], SUB)]
+    ext = SUB * len(sources)
     chunks = height // SUB
 
     @pl.when(step == 0)
@@ -335,8 +413,8 @@
 
     for c in range(0, ext, 2 * SUB):
         halves = []
-        for s in (c, c + SUB):
-            cells = p_ref[s : s + SUB].reshape(SUB * kinds, lanes)
+        for ref, s in sources[c // SUB : c // SUB + 2]:
+            cells = ref[s : s + SUB].reshape(SUB * kinds, lanes)
             halves.append(dot(sk_ref[...], cells).reshape(group, SUB, lanes))
         xs[:, c : c + 2 * SUB, :] = jnp.concatenate(halves, axis=1).astype(BF)
 
@@ -448,7 +526,14 @@
 
     half = kinds // 2
     place = jnp.stack(
-        [me_band * bands_here, half * (1 - core), me_band * columns - radius, me_row * height - radius]
+        [
+            me_band * bands_here,
+            half * (1 - core),
+            me_band * columns - radius,
+            me_row * height - radius,
+            chip,
+            me_band,
+        ]
     ).astype(jnp.int32)
     whole = lambda shape: pl.BlockSpec(shape, lambda i: (0,) * len(shape))
 
@@ -481,44 +566,63 @@
         name="adjoint",
     )(place, observed, plain, spectral_basis)
 
-    give, every = lax.optimization_barrier((give, every))
 
     part = group_size(bands, 32)
     deep = sum(end - start for start, end in packed_blocks(columns, halo))
-    gr, gl, sk, pk = pl.pallas_call(
-        functools.partial(gram_kernel, (columns, columns_all, height * n_row), radius),
+    taps_spec = pl.BlockSpec((part, 2 * taps), lambda i: (i, 0))
+    smem = pl.BlockSpec(memory_space=pltpu.SMEM)
+    params = pltpu.CompilerParams(vmem_limit_bytes=VMEM_LIMIT)
+    gr, sk, pk = pl.pallas_call(
+        functools.partial(gram_rows_kernel, height * n_row, radius),
         grid=(bands // part,),
-        in_specs=[
-            pl.BlockSpec(memory_space=pltpu.SMEM),
-            pl.BlockSpec((part, 2 * taps), lambda i: (i, 0)),
-            pl.BlockSpec((part, kinds), lambda i: (i, 0)),
-        ],
+        in_specs=[smem, taps_spec, pl.BlockSpec((part, kinds), lambda i: (i, 0))],
         out_specs=[
             pl.BlockSpec((part, height, LANES), lambda i: (i, 0, 0)),
-            pl.BlockSpec((part, deep, LANES), lambda i: (i, 0, 0)),
             pl.BlockSpec((part * SUB, SUB * kinds), lambda i: (i, 0)),
             pl.BlockSpec((1, SUB * kinds, part * SUB), lambda i: (i, 0, 0)),
         ],
         out_shape=[
             jax.ShapeDtypeStruct((bands, height, LANES), BF),
-            jax.ShapeDtypeStruct((bands, deep, LANES), BF),
             jax.ShapeDtypeStruct((bands * SUB, SUB * kinds), BF),
             jax.ShapeDtypeStruct((bands // part, SUB * kinds, part * SUB), BF),
         ],
-        compiler_params=pltpu.CompilerParams(vmem_limit_bytes=VMEM_LIMIT),
+        compiler_params=params,
+        cost_estimate=pl.CostEstimate(
+            flops=bands * 2 * LANES**3, bytes_accessed=bands * height * LANES * 2, transcendentals=0
+        ),
+        name="gram_rows",
+    )(place, every, basis_all)
+    gl = pl.pallas_call(
+        functools.partial(gram_columns_kernel, columns, columns_all, radius),
+        grid=(bands // part,),
+        in_specs=[smem, taps_spec],
+        out_specs=pl.BlockSpec((part, deep, LANES), lambda i: (i, 0, 0)),
+        out_shape=jax.ShapeDtypeStruct((bands, deep, LANES), BF),
+        compiler_params=params,
         cost_estimate=pl.CostEstimate(
             flops=bands * 2 * (2 * LANES) ** 3, bytes_accessed=bands * deep * LANES * 2, transcendentals=0
         ),
-        name="gram",
-    )(place, every, basis_all)
+        name="gram_columns",
+    )(place, every)
 
     pairs = [(i, i ^ 1) for i in range(n_band)]
     got = lax.ppermute(give, "band", pairs)
-    pair = keep.astype(F32) + got.astype(F32)
     wide = min(columns_all, 2 * columns + (2 * halo if chips > 2 else halo))
-
-    def window_start(which):
-        return jnp.clip(2 * columns * which - halo, 0, columns_all - wide)
+    wide_lanes = round_up(wide, LANES)
+    starts = [min(max(2 * columns * c - halo, 0), columns_all - wide) for c in range(chips)]
+    vmem = pl.BlockSpec(memory_space=pltpu.VMEM)
+    shape = lambda rows, kind: jax.ShapeDtypeStruct((rows, half, wide_lanes), kind)
+    sends = pl.pallas_call(
+        functools.partial(split_kernel, starts, wide, radius),
+        in_specs=[smem, vmem, vmem],
+        out_shape=[
+            shape(rows, F32 if rows == height and hop == 0 else BF)
+            for hop in range(chips)
+            for rows in (radius, height, radius)
+        ],
+        compiler_params=params,
+        name="split",
+    )(place, keep, got)
 
     def moves(hop, step):
         return [
@@ -528,27 +632,34 @@
             if 0 <= r + step < n_row
         ]
 
-    total = None
+    parts = []
+    axes = ("band", "row")
     for hop in range(chips):
-        piece = lax.dynamic_slice_in_dim(pair, window_start((chip + hop) % chips), wide, 2)
-        above, here, below = piece[:radius], piece[radius : ext - radius], piece[ext - radius :]
-        axes = ("band", "row")
-        after = lax.ppermute(above.astype(BF), axes, moves(hop, -1)).astype(F32)
-        before = lax.ppermute(below.astype(BF), axes, moves(hop, 1)).astype(F32)
+        above, here, below = sends[3 * hop : 3 * hop + 3]
+        after = lax.ppermute(above, axes, moves(hop, -1))
+        before = lax.ppermute(below, axes, moves(hop, 1))
         if hop:
-            here = lax.ppermute(here.astype(BF), axes, moves(hop, 0)).astype(F32)
-        rest = jnp.zeros((height - radius,) + here.shape[1:], F32)
-        here = here + jnp.concatenate([before, rest]) + jnp.concatenate([rest, after])
-        total = here if total is None else total + here
+            here = lax.ppermute(here, axes, moves(hop, 0))
+        parts += [before, here, after]
+    parts[1], gr, sk, pk = lax.optimization_barrier((parts[1], gr, sk, pk))
+    total = pl.pallas_call(
+        functools.partial(merge_kernel, radius),
+        out_shape=shape(height, F32),
+        compiler_params=params,
+        name="merge",
+    )(*parts)
     other = lax.ppermute(total, "band", pairs)
-    first = jnp.where(core == 0, total, other)
-    second = jnp.where(core == 0, other, total)
-    total = jnp.concatenate([first, second], axis=1)
-    total = jnp.pad(total, ((0, 0), (0, 0), (halo, halo)))
-    window = lax.dynamic_slice_in_dim(total, me_band * columns - window_start(chip), columns + 2 * halo, 2)
-    v0 = jnp.pad(window[:, :, halo : halo + columns], ((0, 0), (0, 0), (0, lanes - columns)))
+    window, v0 = pl.pallas_call(
+        functools.partial(window_kernel, starts, wide, columns, halo),
+        in_specs=[smem, vmem, vmem],
+        out_shape=[
+            jax.ShapeDtypeStruct((height, kinds, lanes), BF),
+            jax.ShapeDtypeStruct((height, kinds, lanes), F32),
+        ],
+        compiler_params=params,
+        name="window",
+    )(place, total, other)
     v0 = jnp.swapaxes(v0, 0, 1)
-    window = jnp.pad(window.astype(BF), ((0, 0), (0, 0), (0, lanes - columns - 2 * halo)))
 
     group = part
     ridge = jnp.broadcast_to(ridge_weights[:, None, None], (kinds, SUB, lanes))
@@ -588,7 +699,7 @@
         )(*pieces, own, ridge, sk, pk, gr, gl)
 
     before, after = shift_both(window[:halo], window[height - halo :], "row")
-    v1, sums1 = normal_map([jnp.concatenate([before, window, after], axis=0)], v0, True)
+    v1, sums1 = normal_map([before, window, after], v0, True)
     near = jnp.swapaxes(v1.astype(BF), 0, 1)
     main = jax.ShapeDtypeStruct((main_rows(columns, halo), kinds, LANES), BF)
     side = jax.ShapeDtypeStruct((strip_plan(height, halo)[1], kinds, LANES), BF)

time: 166 us -> 154 us (0.928)
  waiting for transfers between devices: 22.7 us -> 12.3 us
  Pallas kernels: 68.6 us -> 75.8 us
  other arithmetic: 3.5 us -> 0.32 us
  local copies, waits for them, and re-layouts: 11.4 us -> 8.82 us
  starting transfers between devices: 42.5 us -> 40.8 us
    ppermute x5, waiting for transfers between devices: 8.45 us -> 0.01 us  [the longest x2 0.01 us: local(): before = lax.ppermute(below, axes, moves(hop, 1))]
    pallas_call x1 -> x5, Pallas kernels: 20.5 us -> 26.2 us  [the longest x1 16.2 us: local(): pl.pallas_call(functools.partial(gram_columns_kernel, columns, columns_al...]
    ppermute x1, waiting for transfers between devices: 2.97 us -> 0.32 us  [local(): got = lax.ppermute(give, 'band', pairs)]
    add x2 -> x0, other arithmetic: 2.29 us -> none  [the longest x1 1.76 us: local(): total = here if total is None else total + here]
    ppermute x4, starting transfers between devices: 20.6 us -> 18.8 us  [shift_both(): lax.ppermute(high_edge, axis, [(i, i + 1) for i in range(count - 1)])]
    unnamed x20 -> x16, local copies, waits for them, and re-layouts: 4.91 us -> 4.89 us
  transfers between devices with their start and end apart: 18 -> 18, of which waited for: 5 -> 4; matrix products, arithmetic and copies ran while one was open for 2% -> 1% of each run, Pallas kernels for 22% -> 16%
where the time goes in v5:
time: 154 us; the launch traced here: 153 us
  Pallas kernels  75.8 us (49%)
  starting transfers between devices  40.8 us (26%)
  blocking collectives  14.2 us (9%)
  waiting for transfers between devices  12.3 us (8%)
  local copies, waits for them, and re-layouts  8.82 us (6%)
    pallas_call x2, Pallas kernels, normal_map(): pl.pallas_call(functools.partial(first_kernel if first else second_kernel...  31.2 us
    ppermute x4, starting transfers between devices, shift_both(): lax.ppermute(high_edge, axis, [(i, i + 1) for i in range(count - 1)])  18.8 us
    pallas_call x1, Pallas kernels, local(): pl.pallas_call(functools.partial(gram_columns_kernel, columns, columns_al...  16.2 us
    pallas_call x1, Pallas kernels, local(): pl.pallas_call(functools.partial(adjoint_kernel, columns_all, radius), gr...  16.2 us
    all_to_all x1, blocking collectives, local(): shared = lax.all_to_all(mine, ('band', 'row'), 0, 0, tiled=True)  14.2 us
    ppermute x2, starting transfers between devices, local(): before = lax.ppermute(below, axes, moves(hop, 1))  7.91 us
    pallas_call x1, Pallas kernels, local(): pl.pallas_call(functools.partial(gram_rows_kernel, height * n_row, radius...  7.2 us
    ppermute x4, waiting for transfers between devices, shift_both(): lax.ppermute(low_edge, axis, [(i + 1, i) for i in range(count - 1)])  5.77 us
  transfers between devices with their start and end apart: 18, of which 4 were waited for; matrix products, arithmetic and copies ran while one was open for 1% of the time, Pallas kernels for 16%

profile of v5, /device:TPU:0, one launch (start us, length us, event | category | flops | bytes accessed | tf_op | source)
XLA Modules:
  0.0 153.2 jit_solution(8787450891734680625)
XLA Ops:
  0.6 0.8 copy.16
  1.4 0.8 copy.17
  2.2 0.8 copy.18.basis_ref
  3.1 0.1 pad_maximum_fusion.1.taps_ref
  3.2 0.1 stack.27.place_ref
  3.3 16.2 %adjoint.1 = (bf16[56,16,768]{2,1,0:T(8,128)(2,1)}, bf16[56,16,768]{2,1,0:T(8,128)(2,1)S(1)}) custom-call(s32[6]{0:T(128)S(1)} %stack.27.place_ref, bf16[56,32,680]{2,1,0:T(8,128)(2,1)} %obs_ref.1, f32[56,50]{1,0:T(8,128)S(1)} %pad_maximum_fusion.1.taps_ref, bf16[224,32]{1,0:T(8,128)(2,1)S(1)} %copy.18.basis_ref), custom_call_target="tpu_custom_call" | custom-call | flops 1409286144 | bytes 2437120 | tf_op jit(solution)/shard_map/adjoint/pallas_call | solution.py:544
  19.4 0.5 collective-permute-start
  19.9 2.6 %collective-permute-start.4 = (f32[56,50]{1,0:T(8,128)S(1)}, f32[56,50]{1,0:T(8,128)S(1)}, u32[]{:S(2)}, u32[]{:S(2)}) collective-permute-start(f32[56,50]{1,0:T(8,128)S(1)} %pad_maximum_fusion.1.taps_ref), channel_id=1, source_target_pairs={{0,24},{8,0},{16,8},{24,16},{1,25},{9,1},{17,9},{25,17},{2,26},{10... | collective-permute-start | bytes 33608 | tf_op jit(solution)/shard_map/ppermute | solution.py:521
  22.5 0.0 collective-permute-start.3
  22.5 0.1 collective-permute-start.2
  22.6 0.3 collective-permute-done.got_ref
  23.0 1.8 %split.1 = (bf16[12,16,384]{2,1,0:T(8,128)(2,1)S(1)}, f32[32,16,384]{2,1,0:T(8,128)S(1)}, bf16[12,16,384]{2,1,0:T(8,128)(2,1)S(1)}, bf16[12,16,384]{2,1,0:T(8,12...) custom-call(s32[6]{0:T(128)S(1)} %stack.27.place_ref, ...), custom_call_target="tpu_custom_call" | custom-call | tf_op jit(solution)/shard_map/split/pallas_call | solution.py:615
  24.8 3.0 %collective-permute-start.7 = (bf16[32,16,384]{2,1,0:T(8,128)(2,1)S(1)}, bf16[32,16,384]{2,1,0:T(8,128)(2,1)S(1)}, u32[]{:S(2)}, u32[]{:S(2)}) collective-permute-start(bf16[32,16,384]{2,1,0:T(8,128)(2,1)S(1)} %get-tuple-element.37), channel_id=1, source_target_pairs={{0,16},{1,17},{2,18},{3,19},{4,20},{5,21},{6,22},{7,23},{8,24},{9,... | collective-permute-start | bytes 1179656 | tf_op jit(solution)/shard_map/ppermute | solution.py:642
  27.8 0.1 constant_dynamic-slice_fusion.3
  27.9 0.1 pad_maximum_fusion.2
  28.0 0.1 copy.19.basis_ref
  28.1 3.4 %collective-permute-start.1 = (bf16[12,16,384]{2,1,0:T(8,128)(2,1)S(1)}, bf16[12,16,384]{2,1,0:T(8,128)(2,1)S(1)}, u32[]{:S(2)}, u32[]{:S(2)}) collective-permute-start(bf16[12,16,384]{2,1,0:T(8,128)(2,1)S(1)} %get-tuple-element.29), channel_id=1, source_target_pairs={{0,1},{1,2},{2,3},{3,4},{4,5},{5,6},{6,7},{8,9},{9,10},{10,11},{11... | collective-permute-start | bytes 442376 | tf_op jit(solution)/shard_map/ppermute | solution.py:640
  31.6 0.0 collective-permute-done.4
  31.6 1.3 collective-permute-start.5
  32.9 0.0 collective-permute-done.3
  32.9 4.5 %collective-permute-start.6 = (bf16[12,16,384]{2,1,0:T(8,128)(2,1)S(1)}, bf16[12,16,384]{2,1,0:T(8,128)(2,1)S(1)}, u32[]{:S(2)}, u32[]{:S(2)}) collective-permute-start(bf16[12,16,384]{2,1,0:T(8,128)(2,1)S(1)} %get-tuple-element.36), channel_id=1, source_target_pairs={{0,17},{1,18},{2,19},{3,20},{4,21},{5,22},{6,23},{8,25},{9,26},{10... | collective-permute-start | bytes 442376 | tf_op jit(solution)/shard_map/ppermute | solution.py:640
  37.4 0.0 collective-permute-done.2
  37.4 1.3 collective-permute-start.8
  38.7 0.1 pad_maximum_fusion.taps_ref
  38.8 7.2 %gram_rows.1 = (bf16[224,32,128]{2,1,0:T(8,128)(2,1)S(1)}, bf16[1792,256]{1,0:T(8,128)(2,1)S(1)}, bf16[7,256,256]{2,1,0:T(8,128)(2,1)S(1)}) custom-call(s32[6]{0:T(128)S(1)} %stack.27.place_ref, f32[224,50]{1,0:T(8,128)S(1)} %pad_maximum_fusion.taps_ref, bf16[224,32]{1,0:T(8,128)(2,1)S(1)} %copy.19.basis_ref), custom_call_target="tpu_custom_call" | custom-call | flops 939524096 | bytes 1835008 | tf_op jit(solution)/shard_map/gram_rows/pallas_call | solution.py:575
  46.0 1.2 copy-done.2
  47.2 0.0 collective-permute-done.1.refs_0_
  47.2 0.0 collective-permute-done.5.refs_2_
  47.2 0.0 collective-permute-done.6.refs_3_
  47.2 0.0 collective-permute-done.8.refs_5_
  47.2 0.0 collective-permute-done.7.refs_4_
  47.2 0.1 merge.1.mine_ref
  47.4 0.1 collective-permute-start.9
  47.5 2.3 %collective-permute-done.9.other_ref = f32[32,16,384]{2,1,0:T(8,128)S(1)} collective-permute-done((f32[32,16,384]{2,1,0:T(8,128)S(1)}, f32[32,16,384]{2,1,0:T(8,128)S(1)}, u32[]{:S(2)}, u32[]{:S(2)}) %collective-permute-start.9) | collective-permute-done | bytes 786464 | tf_op jit(solution)/shard_map/ppermute | solution.py:651
  49.7 0.8 window.1
  50.6 0.1 fusion.1
  50.6 1.3 collective-permute-start.11
  51.9 6.4 %collective-permute-start.10 = (bf16[24,32,256]{2,1,0:T(8,128)(2,1)S(1)}, bf16[24,32,256]{2,1,0:T(8,128)(2,1)S(1)}, u32[]{:S(2)}, u32[]{:S(2)}) collective-permute-start(bf16[24,32,256]{2,1,0:T(8,128)(2,1)S(1)} %get-tuple-element.53), channel_id=1, source_target_pairs={{0,1},{1,2},{2,3},{3,4},{4,5},{5,6},{6,7},{8,9},{9,10},{10,11},{11... | collective-permute-start | bytes 1179656 | tf_op jit(solution)/shard_map/ppermute | solution.py:496
  58.3 16.2 %gram_columns.1.rest_5_ = bf16[224,272,128]{2,1,0:T(8,128)(2,1)} custom-call(s32[6]{0:T(128)S(1)} %stack.27.place_ref, f32[224,50]{1,0:T(8,128)S(1)} %pad_maximum_fusion.taps_ref), custom_call_target="tpu_custom_call" | custom-call | flops 7516192768 | bytes 15597568 | tf_op jit(solution)/shard_map/gram_columns/pallas_call | solution.py:595
  74.5 1.6 %copy.26 = f32[32,32,256]{2,0,1:T(8,128)} copy(f32[32,32,256]{2,1,0:T(8,128)S(1)} %get-tuple-element.40) | data formatting | bytes 2097152 | tf_op jit(solution)/shard_map/window/pallas_call | solution.py:652
  76.1 0.0 collective-permute-done.11.after
  76.1 0.0 collective-permute-done.10.before
  76.1 0.1 broadcast_in_dim.6.rest_1_
  76.2 15.2 %normal.2 = (f32[32,32,256]{2,1,0:T(8,128)}, f32[8,128]{1,0:T(8,128)S(1)}) custom-call(bf16[24,32,256]{2,1,0:T(8,128)(2,1)S(1)} %collective-permute-done.10.before, bf16[32,32,256]{2,1,0:T(8,128)(2,1)S(1)} %get-tuple-element.39.window, bf16[24,32,256]{2,1,0:T(8,128)(2,1)S(1)} %collective-permute-done.11.after, f32[32,32,256]{2,1,0:T(8,128)} %bitcast.12, ...), custom_call_target="tpu_custom_call" | custom-call | flops 1879048192 | bytes 15597568 | tf_op jit(solution)/shard_map/normal/pallas_call | solution.py:671
  91.4 1.8 %copy.27 = bf16[32,32,256]{2,0,1:T(8,128)(2,1)S(1)} copy(f32[32,32,256]{2,1,0:T(8,128)} %get-tuple-element.45.rest_0_.v1_ref) | data formatting | bytes 1572864 | tf_op jit(solution)/shard_map/normal/pallas_call | solution.py:671
  93.2 0.5 pack.1
  93.7 2.0 %collective-permute-start.14 = (bf16[8,32,128]{2,1,0:T(8,128)(2,1)S(1)}, bf16[8,32,128]{2,1,0:T(8,128)(2,1)S(1)}, u32[]{:S(2)}, u32[]{:S(2)}) collective-permute-start(bf16[8,32,128]{2,1,0:T(8,128)(2,1)S(1)} %get-tuple-element.48), channel_id=1, source_target_pairs={{0,8},{8,16},{16,24},{1,9},{9,17},{17,25},{2,10},{10,18},{18,26},{... | collective-permute-start | bytes 196616 | tf_op jit(solution)/shard_map/ppermute | solution.py:496
  95.6 1.3 collective-permute-start.15
  96.9 5.3 %collective-permute-start.12 = (bf16[32,32,128]{2,1,0:T(8,128)(2,1)S(1)}, bf16[32,32,128]{2,1,0:T(8,128)(2,1)S(1)}, u32[]{:S(2)}, u32[]{:S(2)}) collective-permute-start(bf16[32,32,128]{2,1,0:T(8,128)(2,1)S(1)} %get-tuple-element.46), channel_id=1, source_target_pairs={{0,1},{1,2},{2,3},{3,4},{4,5},{5,6},{6,7},{8,9},{9,10},{10,11},{11... | collective-permute-start | bytes 786440 | tf_op jit(solution)/shard_map/ppermute | solution.py:496
  102.2 1.3 collective-permute-start.13
  103.5 0.0 collective-permute-done.14.left
  103.6 0.0 collective-permute-done.15.right
  103.6 1.3 collective-permute-start.17
  104.9 5.2 %collective-permute-start.16 = (bf16[16,32,128]{2,1,0:T(8,128)(2,1)S(1)}, bf16[16,32,128]{2,1,0:T(8,128)(2,1)S(1)}, u32[]{:S(2)}, u32[]{:S(2)}) collective-permute-start(bf16[16,32,128]{2,1,0:T(8,128)(2,1)S(1)} %constant_dynamic-update-slice_fusion), channel_id=1, source_target_pairs={{0,1},{1,2},{2,3},{3,4},{4,5},{5,6},{6,7},{8,9},{9,10},{10,11},{11... | collective-permute-start | bytes 393224 | tf_op jit(solution)/shard_map/ppermute | solution.py:496
  110.1 0.1 pad.2.clone
  110.2 5.8 %collective-permute-done.17.corner_after = bf16[16,32,128]{2,1,0:T(8,128)(2,1)S(1)} collective-permute-done((bf16[16,32,128]{2,1,0:T(8,128)(2,1)S(1)}, bf16[16,32,128]{2,1,0:T(8,128)(2,1)S(1)}, u32[]{:S(2)}, u32[]{:S(2)}) %collective-permute-start.17) | collective-permute-done | bytes 131104 | tf_op jit(solution)/shard_map/ppermute | solution.py:497
  115.9 3.9 %collective-permute-done.16.corner_before = bf16[16,32,128]{2,1,0:T(8,128)(2,1)S(1)} collective-permute-done((bf16[16,32,128]{2,1,0:T(8,128)(2,1)S(1)}, bf16[16,32,128]{2,1,0:T(8,128)(2,1)S(1)}, u32[]{:S(2)}, u32[]{:S(2)}) %collective-permute-start.16) | collective-permute-done | bytes 131104 | tf_op jit(solution)/shard_map/ppermute | solution.py:496
  119.9 0.0 collective-permute-done.12.before
  119.9 0.0 collective-permute-done.13.after
  119.9 16.0 %normal.3 = (f32[32,32,256]{2,1,0:T(8,128)}, f32[8,128]{1,0:T(8,128)S(1)}) custom-call(bf16[32,32,256]{2,1,0:T(8,128)(2,1)S(1)} %bitcast.15, bf16[32,32,128]{2,1,0:T(8,128)(2,1)S(1)} %collective-permute-done.12.before, bf16[32,32,128]{2,1,0:T(8,128)(2,1)S(1)} %collective-permute-done.13.after, bf16[8,32,128]{2,1,0:T(8,128)(2,1)S(1)} %collective-permute-done.14.left, ...), custom_call_target="tpu_custom_call" | custom-call | flops 1879048192 | bytes 15597568 | tf_op jit(solution)/shard_map/normal/pallas_call | solution.py:671
  135.9 0.1 maximum_maximum_fusion
  136.0 14.2 %all_to_all.5.shared_ref = f32[32,8,128]{2,1,0:T(8,128)S(1)} all-to-all(f32[32,8,128]{2,1,0:T(8,128)S(1)} %broadcast_in_dim.8), channel_id=1, replica_groups=mesh['band'=4,'row'=8] {'band','row'}, dimensions={0} | all-to-all | bytes 262144 | tf_op jit(solution)/shard_map/all_to_all | solution.py:721
  150.2 1.2 copy-done.3
  151.5 1.8 %combine.1 = (f32[32,32,170]{2,1,0:T(8,128)}, f32[32,32,170]{2,1,0:T(8,128)}) custom-call(f32[32,8,128]{2,1,0:T(8,128)S(1)} %all_to_all.5.shared_ref, f32[32,32,256]{2,1,0:T(8,128)S(1)} %bitcast.13, f32[32,32,256]{2,1,0:T(8,128)S(1)} %copy-done.1, f32[32,32,256]{2,1,0:T(8,128)S(1)} %copy-done.3), custom_call_target="tpu_custom_call" | custom-call | tf_op jit(solution)/shard_map/combine/pallas_call | solution.py:723
  (16 shorter events, 0.1 us)
Async XLA Ops:
  19.4 8.4 %copy-start.4 = (bf16[224,32]{0,1:T(8,128)(2,1)S(1)}, bf16[224,32]{0,1:T(8,128)(2,1)}, u32[]{:S(2)}) copy-start(bf16[224,32]{0,1:T(8,128)(2,1)} %param.8) | copy-start | bytes 43012
  19.4 3.5 %collective-permute-start = (bf16[56,16,768]{2,1,0:T(8,128)(2,1)}, bf16[56,16,768]{2,1,0:T(8,128)(2,1)}, u32[]{:S(2)}, u32[]{:S(2)}) collective-permute-start(bf16[56,16,768]{2,1,0:T(8,128)(2,1)} %get-tuple-element.28), channel_id=1, source_target_pairs={{0,8},{8,0},{16,24},{24,16},{1,9},{9,1},{17,25},{25,17},{2,10},{10... | collective-permute-start | bytes 4128776 | tf_op jit(solution)/shard_map/ppermute | solution.py:609
  19.9 11.7 %collective-permute-start.4 = (f32[56,50]{1,0:T(8,128)S(1)}, f32[56,50]{1,0:T(8,128)S(1)}, u32[]{:S(2)}, u32[]{:S(2)}) collective-permute-start(f32[56,50]{1,0:T(8,128)S(1)} %pad_maximum_fusion.1.taps_ref), channel_id=1, source_target_pairs={{0,24},{8,0},{16,8},{24,16},{1,25},{9,1},{17,9},{25,17},{2,26},{10... | collective-permute-start | bytes 33608 | tf_op jit(solution)/shard_map/ppermute | solution.py:521
  22.5 10.4 %collective-permute-start.3 = (f32[56,50]{1,0:T(8,128)S(1)}, f32[56,50]{1,0:T(8,128)S(1)}, u32[]{:S(2)}, u32[]{:S(2)}) collective-permute-start(f32[56,50]{1,0:T(8,128)S(1)} %pad_maximum_fusion.1.taps_ref), channel_id=1, source_target_pairs={{0,16},{8,24},{16,0},{24,8},{1,17},{9,25},{17,1},{25,9},{2,18},{10... | collective-permute-start | bytes 33608 | tf_op jit(solution)/shard_map/ppermute | solution.py:521
  22.5 14.9 %collective-permute-start.2 = (f32[56,50]{1,0:T(8,128)S(1)}, f32[56,50]{1,0:T(8,128)S(1)}, u32[]{:S(2)}, u32[]{:S(2)}) collective-permute-start(f32[56,50]{1,0:T(8,128)S(1)} %pad_maximum_fusion.1.taps_ref), channel_id=1, source_target_pairs={{0,8},{8,16},{16,24},{24,0},{1,9},{9,17},{17,25},{25,1},{2,10},{10... | collective-permute-start | bytes 33608 | tf_op jit(solution)/shard_map/ppermute | solution.py:521
  24.8 22.4 %collective-permute-start.7 = (bf16[32,16,384]{2,1,0:T(8,128)(2,1)S(1)}, bf16[32,16,384]{2,1,0:T(8,128)(2,1)S(1)}, u32[]{:S(2)}, u32[]{:S(2)}) collective-permute-start(bf16[32,16,384]{2,1,0:T(8,128)(2,1)S(1)} %get-tuple-element.37), channel_id=1, source_target_pairs={{0,16},{1,17},{2,18},{3,19},{4,20},{5,21},{6,22},{7,23},{8,24},{9,... | collective-permute-start | bytes 1179656 | tf_op jit(solution)/shard_map/ppermute | solution.py:642
  28.1 19.1 %collective-permute-start.1 = (bf16[12,16,384]{2,1,0:T(8,128)(2,1)S(1)}, bf16[12,16,384]{2,1,0:T(8,128)(2,1)S(1)}, u32[]{:S(2)}, u32[]{:S(2)}) collective-permute-start(bf16[12,16,384]{2,1,0:T(8,128)(2,1)S(1)} %get-tuple-element.29), channel_id=1, source_target_pairs={{0,1},{1,2},{2,3},{3,4},{4,5},{5,6},{6,7},{8,9},{9,10},{10,11},{11... | collective-permute-start | bytes 442376 | tf_op jit(solution)/shard_map/ppermute | solution.py:640
  31.6 15.6 %collective-permute-start.5 = (bf16[12,16,384]{2,1,0:T(8,128)(2,1)S(1)}, bf16[12,16,384]{2,1,0:T(8,128)(2,1)S(1)}, u32[]{:S(2)}, u32[]{:S(2)}) collective-permute-start(bf16[12,16,384]{2,1,0:T(8,128)(2,1)S(1)} %get-tuple-element.35), channel_id=1, source_target_pairs={{1,0},{2,1},{3,2},{4,3},{5,4},{6,5},{7,6},{9,8},{10,9},{11,10},{12... | collective-permute-start | bytes 442376 | tf_op jit(solution)/shard_map/ppermute | solution.py:639
  32.9 14.3 %collective-permute-start.6 = (bf16[12,16,384]{2,1,0:T(8,128)(2,1)S(1)}, bf16[12,16,384]{2,1,0:T(8,128)(2,1)S(1)}, u32[]{:S(2)}, u32[]{:S(2)}) collective-permute-start(bf16[12,16,384]{2,1,0:T(8,128)(2,1)S(1)} %get-tuple-element.36), channel_id=1, source_target_pairs={{0,17},{1,18},{2,19},{3,20},{4,21},{5,22},{6,23},{8,25},{9,26},{10... | collective-permute-start | bytes 442376 | tf_op jit(solution)/shard_map/ppermute | solution.py:640
  37.4 9.8 %collective-permute-start.8 = (bf16[12,16,384]{2,1,0:T(8,128)(2,1)S(1)}, bf16[12,16,384]{2,1,0:T(8,128)(2,1)S(1)}, u32[]{:S(2)}, u32[]{:S(2)}) collective-permute-start(bf16[12,16,384]{2,1,0:T(8,128)(2,1)S(1)} %get-tuple-element.38), channel_id=1, source_target_pairs={{1,16},{2,17},{3,18},{4,19},{5,20},{6,21},{7,22},{9,24},{10,25},{1... | collective-permute-start | bytes 442376 | tf_op jit(solution)/shard_map/ppermute | solution.py:639
  46.0 1.2 copy-start.2
  47.4 2.4 %collective-permute-start.9 = (f32[32,16,384]{2,1,0:T(8,128)S(1)}, f32[32,16,384]{2,1,0:T(8,128)S(1)}, u32[]{:S(2)}, u32[]{:S(2)}) collective-permute-start(f32[32,16,384]{2,1,0:T(8,128)S(1)} %merge.1.mine_ref), channel_id=1, source_target_pairs={{0,8},{8,0},{16,24},{24,16},{1,9},{9,1},{17,25},{25,17},{2,10},{10... | collective-permute-start | bytes 2359304 | tf_op jit(solution)/shard_map/ppermute | solution.py:651
  50.6 25.5 %collective-permute-start.11 = (bf16[24,32,256]{2,1,0:T(8,128)(2,1)S(1)}, bf16[24,32,256]{2,1,0:T(8,128)(2,1)S(1)}, u32[]{:S(2)}, u32[]{:S(2)}) collective-permute-start(bf16[24,32,256]{2,1,0:T(8,128)(2,1)S(1)} %get-tuple-element.52), channel_id=1, source_target_pairs={{1,0},{2,1},{3,2},{4,3},{5,4},{6,5},{7,6},{9,8},{10,9},{11,10},{12... | collective-permute-start | bytes 1179656 | tf_op jit(solution)/shard_map/ppermute | solution.py:497
  51.9 24.2 %collective-permute-start.10 = (bf16[24,32,256]{2,1,0:T(8,128)(2,1)S(1)}, bf16[24,32,256]{2,1,0:T(8,128)(2,1)S(1)}, u32[]{:S(2)}, u32[]{:S(2)}) collective-permute-start(bf16[24,32,256]{2,1,0:T(8,128)(2,1)S(1)} %get-tuple-element.53), channel_id=1, source_target_pairs={{0,1},{1,2},{2,3},{3,4},{4,5},{5,6},{6,7},{8,9},{9,10},{10,11},{11... | collective-permute-start | bytes 1179656 | tf_op jit(solution)/shard_map/ppermute | solution.py:496
  74.5 1.6 %copy-start.5 = (f32[32]{0:T(128)S(1)}, f32[32]{0:T(128)}, u32[]{:S(2)}) copy-start(f32[32]{0:T(128)} %param.9) | copy-start | bytes 388
  93.7 9.9 %collective-permute-start.14 = (bf16[8,32,128]{2,1,0:T(8,128)(2,1)S(1)}, bf16[8,32,128]{2,1,0:T(8,128)(2,1)S(1)}, u32[]{:S(2)}, u32[]{:S(2)}) collective-permute-start(bf16[8,32,128]{2,1,0:T(8,128)(2,1)S(1)} %get-tuple-element.48), channel_id=1, source_target_pairs={{0,8},{8,16},{16,24},{1,9},{9,17},{17,25},{2,10},{10,18},{18,26},{... | collective-permute-start | bytes 196616 | tf_op jit(solution)/shard_map/ppermute | solution.py:496
  95.6 7.9 %collective-permute-start.15 = (bf16[8,32,128]{2,1,0:T(8,128)(2,1)S(1)}, bf16[8,32,128]{2,1,0:T(8,128)(2,1)S(1)}, u32[]{:S(2)}, u32[]{:S(2)}) collective-permute-start(bf16[8,32,128]{2,1,0:T(8,128)(2,1)S(1)} %get-tuple-element.49), channel_id=1, source_target_pairs={{8,0},{16,8},{24,16},{9,1},{17,9},{25,17},{10,2},{18,10},{26,18},{... | collective-permute-start | bytes 196616 | tf_op jit(solution)/shard_map/ppermute | solution.py:497
  96.9 22.9 %collective-permute-start.12 = (bf16[32,32,128]{2,1,0:T(8,128)(2,1)S(1)}, bf16[32,32,128]{2,1,0:T(8,128)(2,1)S(1)}, u32[]{:S(2)}, u32[]{:S(2)}) collective-permute-start(bf16[32,32,128]{2,1,0:T(8,128)(2,1)S(1)} %get-tuple-element.46), channel_id=1, source_target_pairs={{0,1},{1,2},{2,3},{3,4},{4,5},{5,6},{6,7},{8,9},{9,10},{10,11},{11... | collective-permute-start | bytes 786440 | tf_op jit(solution)/shard_map/ppermute | solution.py:496
  102.2 17.6 %collective-permute-start.13 = (bf16[32,32,128]{2,1,0:T(8,128)(2,1)S(1)}, bf16[32,32,128]{2,1,0:T(8,128)(2,1)S(1)}, u32[]{:S(2)}, u32[]{:S(2)}) collective-permute-start(bf16[32,32,128]{2,1,0:T(8,128)(2,1)S(1)} %get-tuple-element.47), channel_id=1, source_target_pairs={{1,0},{2,1},{3,2},{4,3},{5,4},{6,5},{7,6},{9,8},{10,9},{11,10},{12... | collective-permute-start | bytes 786440 | tf_op jit(solution)/shard_map/ppermute | solution.py:497
  103.6 12.3 %collective-permute-start.17 = (bf16[16,32,128]{2,1,0:T(8,128)(2,1)S(1)}, bf16[16,32,128]{2,1,0:T(8,128)(2,1)S(1)}, u32[]{:S(2)}, u32[]{:S(2)}) collective-permute-start(bf16[16,32,128]{2,1,0:T(8,128)(2,1)S(1)} %constant_dynamic-update-slice_fusion), channel_id=1, source_target_pairs={{1,0},{2,1},{3,2},{4,3},{5,4},{6,5},{7,6},{9,8},{10,9},{11,10},{12... | collective-permute-start | bytes 393224 | tf_op jit(solution)/shard_map/ppermute | solution.py:497
  104.9 15.0 %collective-permute-start.16 = (bf16[16,32,128]{2,1,0:T(8,128)(2,1)S(1)}, bf16[16,32,128]{2,1,0:T(8,128)(2,1)S(1)}, u32[]{:S(2)}, u32[]{:S(2)}) collective-permute-start(bf16[16,32,128]{2,1,0:T(8,128)(2,1)S(1)} %constant_dynamic-update-slice_fusion), channel_id=1, source_target_pairs={{0,1},{1,2},{2,3},{3,4},{4,5},{5,6},{6,7},{8,9},{9,10},{10,11},{11... | collective-permute-start | bytes 393224 | tf_op jit(solution)/shard_map/ppermute | solution.py:496
  110.2 40.1 %copy-start = (f32[32,32,256]{2,0,1:T(8,128)S(1)}, f32[32,32,256]{2,0,1:T(8,128)}, u32[]{:S(2)}) copy-start(f32[32,32,256]{2,0,1:T(8,128)} %copy.26) | copy-start | bytes 3145732
  110.2 40.1 %copy-start.1 = (f32[32,32,256]{2,1,0:T(8,128)S(1)}, f32[32,32,256]{2,1,0:T(8,128)}, u32[]{:S(2)}) copy-start(f32[32,32,256]{2,1,0:T(8,128)} %get-tuple-element.45.rest_0_.v1_ref) | copy-start | bytes 3145732
  150.2 1.2 copy-start.3

commit v6 on v5

--- a/solution.py
+++ b/solution.py
@@ -12,6 +12,7 @@
 BF = jnp.bfloat16
 F32 = jnp.float32
 VMEM_LIMIT = 50 * 1024 * 1024
+SMALL_LIMIT = 20 * 1024 * 1024
 
 
 def round_up(value, unit):
@@ -186,7 +187,7 @@
     ext = chunks * SUB
     edge = 2 * SUB
     last = columns // LANES * LANES
-    batch = group_size(group, 4)
+    batch = group_size(group, 7)
 
     @pl.when(step == 0)
     def _():
@@ -381,11 +382,13 @@
                     own_ref[r : r + unit, kinds] = part.reshape(unit, half, lanes)
 
 
-def first_kernel(columns, halo, before, window, after, *rest):
-    normal_kernel(columns, halo, True, (before, window, after), *rest)
-
-
-def second_kernel(columns, halo, near_ref, before, after, left, right, corner_before, corner_after, *rest):
+def first_kernel(columns, halo, group, before, window, after, *rest):
+    normal_kernel(columns, halo, group, True, (before, window, after), *rest)
+
+
+def second_kernel(
+    columns, halo, group, near_ref, before, after, left, right, corner_before, corner_after, *rest
+):
     *rest, p_ref = rest
 
     @pl.when(pl.program_id(0) == 0)
@@ -394,14 +397,15 @@
             columns, halo, near_ref, (before, after), (left, right), (corner_before, corner_after), p_ref
         )
 
-    normal_kernel(columns, halo, False, (p_ref,), *rest)
+    normal_kernel(columns, halo, group, False, (p_ref,), *rest)
 
 
 def normal_kernel(
-    columns, halo, first, p_refs, own_ref, ridge_ref, sk_ref, pk_ref, gr_ref, gl_ref, out_ref, sums_ref, acc, xs, ys
+    columns, halo, group, first, p_refs, own_ref, ridge_ref, sk_ref, pk_ref, gr_ref, gl_ref, out_ref, sums_ref, acc, xs, ys
 ):
     step = pl.program_id(0)
-    group, height, _ = gr_ref.shape
+    height = gr_ref.shape[1]
+    from_band = step * group
     _, kinds, lanes = p_refs[0].shape
     sources = [(ref, s) for ref in p_refs for s in range(0, ref.shape[0], SUB)]
     ext = SUB * len(sources)
@@ -411,22 +415,23 @@
     def _():
         acc[...] = jnp.zeros_like(acc)
 
+    spread = sk_ref[pl.ds(pl.multiple_of(from_band * SUB, group * SUB), group * SUB)]
     for c in range(0, ext, 2 * SUB):
         halves = []
         for ref, s in sources[c // SUB : c // SUB + 2]:
             cells = ref[s : s + SUB].reshape(SUB * kinds, lanes)
-            halves.append(dot(sk_ref[...], cells).reshape(group, SUB, lanes))
+            halves.append(dot(spread, cells).reshape(group, SUB, lanes))
         xs[:, c : c + 2 * SUB, :] = jnp.concatenate(halves, axis=1).astype(BF)
 
     blocks = packed_blocks(columns, halo)
-    mids = [dot(gr_ref[b, :, :ext], xs[b]).astype(BF) for b in range(group)]
+    mids = [dot(gr_ref[from_band + b, :, :ext], xs[b]).astype(BF) for b in range(group)]
     for b in range(group):
         parts = []
         at = 0
         for i in range(lanes // LANES):
             if i < len(blocks):
                 start, end = blocks[i]
-                part = [gl_ref[b, at : at + end - start]]
+                part = [gl_ref[from_band + b, at : at + end - start]]
                 at += end - start
                 if start:
                     part = [jnp.zeros((start, LANES), BF)] + part
@@ -439,7 +444,7 @@
         for c in range(chunks):
             ys[c, b] = done[c * SUB : (c + 1) * SUB]
 
-    gather = jnp.concatenate([pk_ref[i] for i in range(pk_ref.shape[0])], axis=1)
+    gather = pk_ref[step]
     for c in range(chunks):
         acc[c] += dot(gather, ys[c].reshape(group * SUB, lanes).astype(BF))
 
@@ -571,7 +576,7 @@
     deep = sum(end - start for start, end in packed_blocks(columns, halo))
     taps_spec = pl.BlockSpec((part, 2 * taps), lambda i: (i, 0))
     smem = pl.BlockSpec(memory_space=pltpu.SMEM)
-    params = pltpu.CompilerParams(vmem_limit_bytes=VMEM_LIMIT)
+    params = pltpu.CompilerParams(vmem_limit_bytes=SMALL_LIMIT)
     gr, sk, pk = pl.pallas_call(
         functools.partial(gram_rows_kernel, height * n_row, radius),
         grid=(bands // part,),
@@ -620,7 +625,7 @@
             for hop in range(chips)
             for rows in (radius, height, radius)
         ],
-        compiler_params=params,
+        compiler_params=pltpu.CompilerParams(vmem_limit_bytes=VMEM_LIMIT),
         name="split",
     )(place, keep, got)
 
@@ -664,23 +669,14 @@
     group = part
     ridge = jnp.broadcast_to(ridge_weights[:, None, None], (kinds, SUB, lanes))
     tall = height + 2 * halo
-    block = lambda shape: pl.BlockSpec((group,) + shape, lambda i: (i, 0, 0))
 
     def normal_map(pieces, own, first):
         window = [pltpu.VMEM((tall, kinds, lanes), BF)] if not first else []
         return pl.pallas_call(
-            functools.partial(first_kernel if first else second_kernel, columns, halo),
+            functools.partial(first_kernel if first else second_kernel, columns, halo, group),
             grid=(bands // group,),
-            in_specs=[whole(piece.shape) for piece in pieces]
-            + [
-                whole((kinds, height, lanes)),
-                whole((kinds, SUB, lanes)),
-                pl.BlockSpec((group * SUB, SUB * kinds), lambda i: (i, 0)),
-                pl.BlockSpec((group // part, SUB * kinds, part * SUB), lambda i: (i, 0, 0)),
-                block((height, LANES)),
-                block((deep, LANES)),
-            ],
-            out_specs=[whole((kinds, height, lanes)), whole((SUB, LANES))],
+            in_specs=[vmem] * (len(pieces) + 6),
+            out_specs=[vmem, vmem],
             out_shape=[
                 jax.ShapeDtypeStruct((kinds, height, lanes), F32),
                 jax.ShapeDtypeStruct((SUB, LANES), F32),
@@ -691,7 +687,7 @@
                 pltpu.VMEM((height // SUB, group, SUB, lanes), F32),
             ]
             + window,
-            compiler_params=pltpu.CompilerParams(vmem_limit_bytes=VMEM_LIMIT),
+            compiler_params=pltpu.CompilerParams(vmem_limit_bytes=SMALL_LIMIT),
             cost_estimate=pl.CostEstimate(
                 flops=bands * 2 * 32 * 512 * 256, bytes_accessed=bands * deep * LANES * 2, transcendentals=0
             ),
@@ -706,7 +702,7 @@
     up, down, left, right = pl.pallas_call(
         functools.partial(pack_kernel, columns, halo),
         out_shape=[main, main, side, side],
-        compiler_params=pltpu.CompilerParams(vmem_limit_bytes=VMEM_LIMIT),
+        compiler_params=pltpu.CompilerParams(vmem_limit_bytes=SMALL_LIMIT),
         name="pack",
     )(near)
     before, after = shift_both(up, down, "row")
@@ -723,7 +719,7 @@
     return pl.pallas_call(
         combine_kernel,
         out_shape=[out, out],
-        compiler_params=pltpu.CompilerParams(vmem_limit_bytes=VMEM_LIMIT),
+        compiler_params=pltpu.CompilerParams(vmem_limit_bytes=SMALL_LIMIT),
         name="combine",
     )(shared, v0, v1, v2)
 

time: 154 us -> 140 us (0.909)
  Pallas kernels: 75.8 us -> 66.2 us
  local copies, waits for them, and re-layouts: 8.82 us -> 4.19 us
    pallas_call x2, Pallas kernels: 31.2 us -> 24.8 us  [normal_map(): pl.pallas_call(functools.partial(first_kernel if first else second_kernel...]
    unnamed x16 -> x8, local copies, waits for them, and re-layouts: 4.89 us -> 2.45 us
    pallas_call x1, Pallas kernels: 16.2 us -> 14.4 us  [local(): pl.pallas_call(functools.partial(adjoint_kernel, columns_all, radius), gr...]
  transfers between devices with their start and end apart: 18 -> 18, of which waited for: 4 -> 5; matrix products, arithmetic and copies ran while one was open for 1% -> 1% of each run, Pallas kernels for 16% -> 17%
where the time goes in v6:
time: 140 us; the launch traced here: 139 us
  Pallas kernels  66.2 us (47%)
  starting transfers between devices  39.9 us (28%)
  blocking collectives  13.8 us (10%)
  waiting for transfers between devices  13.7 us (10%)
  local copies, waits for them, and re-layouts  4.19 us (3%)
    pallas_call x2, Pallas kernels, normal_map(): pl.pallas_call(functools.partial(first_kernel if first else second_kernel...  24.8 us
    ppermute x4, starting transfers between devices, shift_both(): lax.ppermute(high_edge, axis, [(i, i + 1) for i in range(count - 1)])  17.9 us
    pallas_call x1, Pallas kernels, local(): pl.pallas_call(functools.partial(gram_columns_kernel, columns, columns_al...  14.8 us
    pallas_call x1, Pallas kernels, local(): pl.pallas_call(functools.partial(adjoint_kernel, columns_all, radius), gr...  14.4 us
    all_to_all x1, blocking collectives, local(): shared = lax.all_to_all(mine, ('band', 'row'), 0, 0, tiled=True)  13.8 us
    ppermute x2, starting transfers between devices, local(): before = lax.ppermute(below, axes, moves(hop, 1))  7.86 us
    pallas_call x1, Pallas kernels, local(): pl.pallas_call(functools.partial(gram_rows_kernel, height * n_row, radius...  7.2 us
    ppermute x4, waiting for transfers between devices, shift_both(): lax.ppermute(low_edge, axis, [(i + 1, i) for i in range(count - 1)])  5.87 us
  transfers between devices with their start and end apart: 18, of which 5 were waited for; matrix products, arithmetic and copies ran while one was open for 1% of the time, Pallas kernels for 17%

profile of v6, /device:TPU:0, one launch (start us, length us, event | category | flops | bytes accessed | tf_op | source)
XLA Modules:
  0.0 139.1 jit_solution(8293480293819698861)
XLA Ops:
  0.6 0.8 copy.16
  1.4 0.8 copy.17
  2.2 0.8 copy.18.basis_ref
  3.1 0.1 pad_maximum_fusion.1.taps_ref
  3.2 0.1 stack.27.place_ref
  3.3 14.4 %adjoint.1 = (bf16[56,16,768]{2,1,0:T(8,128)(2,1)}, bf16[56,16,768]{2,1,0:T(8,128)(2,1)S(1)}) custom-call(s32[6]{0:T(128)S(1)} %stack.27.place_ref, bf16[56,32,680]{2,1,0:T(8,128)(2,1)} %obs_ref.1, f32[56,50]{1,0:T(8,128)S(1)} %pad_maximum_fusion.1.taps_ref, bf16[224,32]{1,0:T(8,128)(2,1)S(1)} %copy.18.basis_ref), custom_call_target="tpu_custom_call" | custom-call | flops 1409286144 | bytes 2437120 | tf_op jit(solution)/shard_map/adjoint/pallas_call | solution.py:549
  17.6 0.5 collective-permute-start
  18.1 2.6 %collective-permute-start.4 = (f32[56,50]{1,0:T(8,128)S(1)}, f32[56,50]{1,0:T(8,128)S(1)}, u32[]{:S(2)}, u32[]{:S(2)}) collective-permute-start(f32[56,50]{1,0:T(8,128)S(1)} %pad_maximum_fusion.1.taps_ref), channel_id=1, source_target_pairs={{0,24},{8,0},{16,8},{24,16},{1,25},{9,1},{17,9},{25,17},{2,26},{10... | collective-permute-start | bytes 33608 | tf_op jit(solution)/shard_map/ppermute | solution.py:526
  20.7 0.0 collective-permute-start.3
  20.7 0.1 collective-permute-start.2
  20.9 0.3 collective-permute-done.got_ref
  21.2 1.8 %split.1 = (bf16[12,16,384]{2,1,0:T(8,128)(2,1)S(1)}, f32[32,16,384]{2,1,0:T(8,128)S(1)}, bf16[12,16,384]{2,1,0:T(8,128)(2,1)S(1)}, bf16[12,16,384]{2,1,0:T(8,12...) custom-call(s32[6]{0:T(128)S(1)} %stack.27.place_ref, ...), custom_call_target="tpu_custom_call" | custom-call | tf_op jit(solution)/shard_map/split/pallas_call | solution.py:620
  23.0 3.0 %collective-permute-start.7 = (bf16[32,16,384]{2,1,0:T(8,128)(2,1)S(1)}, bf16[32,16,384]{2,1,0:T(8,128)(2,1)S(1)}, u32[]{:S(2)}, u32[]{:S(2)}) collective-permute-start(bf16[32,16,384]{2,1,0:T(8,128)(2,1)S(1)} %get-tuple-element.37), channel_id=1, source_target_pairs={{0,16},{1,17},{2,18},{3,19},{4,20},{5,21},{6,22},{7,23},{8,24},{9,... | collective-permute-start | bytes 1179656 | tf_op jit(solution)/shard_map/ppermute | solution.py:647
  26.1 0.1 constant_dynamic-slice_fusion.3
  26.2 0.1 pad_maximum_fusion.2
  26.3 0.1 copy.19.basis_ref
  26.4 3.4 %collective-permute-start.1 = (bf16[12,16,384]{2,1,0:T(8,128)(2,1)S(1)}, bf16[12,16,384]{2,1,0:T(8,128)(2,1)S(1)}, u32[]{:S(2)}, u32[]{:S(2)}) collective-permute-start(bf16[12,16,384]{2,1,0:T(8,128)(2,1)S(1)} %get-tuple-element.29), channel_id=1, source_target_pairs={{0,1},{1,2},{2,3},{3,4},{4,5},{5,6},{6,7},{8,9},{9,10},{10,11},{11... | collective-permute-start | bytes 442376 | tf_op jit(solution)/shard_map/ppermute | solution.py:645
  29.8 0.0 collective-permute-done.4
  29.8 1.3 collective-permute-start.5
  31.1 0.0 collective-permute-done.3
  31.1 4.5 %collective-permute-start.6 = (bf16[12,16,384]{2,1,0:T(8,128)(2,1)S(1)}, bf16[12,16,384]{2,1,0:T(8,128)(2,1)S(1)}, u32[]{:S(2)}, u32[]{:S(2)}) collective-permute-start(bf16[12,16,384]{2,1,0:T(8,128)(2,1)S(1)} %get-tuple-element.36), channel_id=1, source_target_pairs={{0,17},{1,18},{2,19},{3,20},{4,21},{5,22},{6,23},{8,25},{9,26},{10... | collective-permute-start | bytes 442376 | tf_op jit(solution)/shard_map/ppermute | solution.py:645
  35.6 0.0 collective-permute-done.2
  35.6 1.3 collective-permute-start.8
  36.9 0.1 pad_maximum_fusion.taps_ref
  37.0 7.2 %gram_rows.1 = (bf16[224,32,128]{2,1,0:T(8,128)(2,1)S(1)}, bf16[1792,256]{1,0:T(8,128)(2,1)S(1)}, bf16[7,256,256]{2,1,0:T(8,128)(2,1)S(1)}) custom-call(s32[6]{0:T(128)S(1)} %stack.27.place_ref, f32[224,50]{1,0:T(8,128)S(1)} %pad_maximum_fusion.taps_ref, bf16[224,32]{1,0:T(8,128)(2,1)S(1)} %copy.19.basis_ref), custom_call_target="tpu_custom_call" | custom-call | flops 939524096 | bytes 1835008 | tf_op jit(solution)/shard_map/gram_rows/pallas_call | solution.py:580
  44.2 0.0 collective-permute-done.1.refs_0_
  44.2 0.0 collective-permute-done.5.refs_2_
  44.2 0.0 collective-permute-done.6.refs_3_
  44.2 0.0 collective-permute-done.8.refs_5_
  44.2 0.0 collective-permute-done.7.refs_4_
  44.2 0.1 merge.1.mine_ref
  44.4 0.1 collective-permute-start.9
  44.4 2.3 %collective-permute-done.9.other_ref = f32[32,16,384]{2,1,0:T(8,128)S(1)} collective-permute-done((f32[32,16,384]{2,1,0:T(8,128)S(1)}, f32[32,16,384]{2,1,0:T(8,128)S(1)}, u32[]{:S(2)}, u32[]{:S(2)}) %collective-permute-start.9) | collective-permute-done | bytes 786464 | tf_op jit(solution)/shard_map/ppermute | solution.py:656
  46.7 0.8 window.1
  47.5 0.1 fusion.1
  47.6 1.3 collective-permute-start.11
  48.9 6.4 %collective-permute-start.10 = (bf16[24,32,256]{2,1,0:T(8,128)(2,1)S(1)}, bf16[24,32,256]{2,1,0:T(8,128)(2,1)S(1)}, u32[]{:S(2)}, u32[]{:S(2)}) collective-permute-start(bf16[24,32,256]{2,1,0:T(8,128)(2,1)S(1)} %get-tuple-element.53), channel_id=1, source_target_pairs={{0,1},{1,2},{2,3},{3,4},{4,5},{5,6},{6,7},{8,9},{9,10},{10,11},{11... | collective-permute-start | bytes 1179656 | tf_op jit(solution)/shard_map/ppermute | solution.py:501
  55.3 14.8 %gram_columns.1.rest_5_ = bf16[224,272,128]{2,1,0:T(8,128)(2,1)S(1)} custom-call(s32[6]{0:T(128)S(1)} %stack.27.place_ref, f32[224,50]{1,0:T(8,128)S(1)} %pad_maximum_fusion.taps_ref), custom_call_target="tpu_custom_call" | custom-call | flops 7516192768 | bytes 15597568 | tf_op jit(solution)/shard_map/gram_columns/pallas_call | solution.py:600
  70.1 0.0 copy-start.1
  70.1 0.6 copy.26
  70.8 0.0 collective-permute-done.11.after
  70.8 1.3 collective-permute-done.10.before
  72.1 0.0 copy-done.1
  72.1 0.1 broadcast_in_dim.6.rest_1_
  72.2 12.0 %normal.2 = (f32[32,32,256]{2,1,0:T(8,128)S(1)}, f32[8,128]{1,0:T(8,128)S(1)}) custom-call(bf16[24,32,256]{2,1,0:T(8,128)(2,1)S(1)} %collective-permute-done.10.before, bf16[32,32,256]{2,1,0:T(8,128)(2,1)S(1)} %get-tuple-element.39.window, bf16[24,32,256]{2,1,0:T(8,128)(2,1)S(1)} %collective-permute-done.11.after, f32[32,32,256]{2,1,0:T(8,128)S(1)} %bitcast.12, ...), custom_call_target="tpu_custom_call" | custom-call | flops 1879048192 | bytes 15597568 | tf_op jit(solution)/shard_map/normal/pallas_call | solution.py:675
  84.2 0.6 copy.27
  84.8 0.5 pack.1
  85.3 1.9 %collective-permute-start.14 = (bf16[8,32,128]{2,1,0:T(8,128)(2,1)S(1)}, bf16[8,32,128]{2,1,0:T(8,128)(2,1)S(1)}, u32[]{:S(2)}, u32[]{:S(2)}) collective-permute-start(bf16[8,32,128]{2,1,0:T(8,128)(2,1)S(1)} %get-tuple-element.48), channel_id=1, source_target_pairs={{0,8},{8,16},{16,24},{1,9},{9,17},{17,25},{2,10},{10,18},{18,26},{... | collective-permute-start | bytes 196616 | tf_op jit(solution)/shard_map/ppermute | solution.py:501
  87.2 1.3 collective-permute-start.15
  88.5 4.4 %collective-permute-start.12 = (bf16[32,32,128]{2,1,0:T(8,128)(2,1)S(1)}, bf16[32,32,128]{2,1,0:T(8,128)(2,1)S(1)}, u32[]{:S(2)}, u32[]{:S(2)}) collective-permute-start(bf16[32,32,128]{2,1,0:T(8,128)(2,1)S(1)} %get-tuple-element.46), channel_id=1, source_target_pairs={{0,1},{1,2},{2,3},{3,4},{4,5},{5,6},{6,7},{8,9},{9,10},{10,11},{11... | collective-permute-start | bytes 786440 | tf_op jit(solution)/shard_map/ppermute | solution.py:501
  92.9 1.3 collective-permute-start.13
  94.2 0.0 collective-permute-done.14.left
  94.3 0.0 collective-permute-done.15.right
  94.3 1.3 collective-permute-start.17
  95.6 5.2 %collective-permute-start.16 = (bf16[16,32,128]{2,1,0:T(8,128)(2,1)S(1)}, bf16[16,32,128]{2,1,0:T(8,128)(2,1)S(1)}, u32[]{:S(2)}, u32[]{:S(2)}) collective-permute-start(bf16[16,32,128]{2,1,0:T(8,128)(2,1)S(1)} %constant_dynamic-update-slice_fusion), channel_id=1, source_target_pairs={{0,1},{1,2},{2,3},{3,4},{4,5},{5,6},{6,7},{8,9},{9,10},{10,11},{11... | collective-permute-start | bytes 393224 | tf_op jit(solution)/shard_map/ppermute | solution.py:501
  100.8 0.1 pad.2.clone
  100.9 5.9 %collective-permute-done.17.corner_after = bf16[16,32,128]{2,1,0:T(8,128)(2,1)S(1)} collective-permute-done((bf16[16,32,128]{2,1,0:T(8,128)(2,1)S(1)}, bf16[16,32,128]{2,1,0:T(8,128)(2,1)S(1)}, u32[]{:S(2)}, u32[]{:S(2)}) %collective-permute-start.17) | collective-permute-done | bytes 131104 | tf_op jit(solution)/shard_map/ppermute | solution.py:502
  106.7 3.9 %collective-permute-done.16.corner_before = bf16[16,32,128]{2,1,0:T(8,128)(2,1)S(1)} collective-permute-done((bf16[16,32,128]{2,1,0:T(8,128)(2,1)S(1)}, bf16[16,32,128]{2,1,0:T(8,128)(2,1)S(1)}, u32[]{:S(2)}, u32[]{:S(2)}) %collective-permute-start.16) | collective-permute-done | bytes 131104 | tf_op jit(solution)/shard_map/ppermute | solution.py:501
  110.6 0.0 collective-permute-done.12.before
  110.6 0.0 collective-permute-done.13.after
  110.7 12.8 %normal.3 = (f32[32,32,256]{2,1,0:T(8,128)S(1)}, f32[8,128]{1,0:T(8,128)S(1)}) custom-call(bf16[32,32,256]{2,1,0:T(8,128)(2,1)S(1)} %bitcast.15, bf16[32,32,128]{2,1,0:T(8,128)(2,1)S(1)} %collective-permute-done.12.before, bf16[32,32,128]{2,1,0:T(8,128)(2,1)S(1)} %collective-permute-done.13.after, bf16[8,32,128]{2,1,0:T(8,128)(2,1)S(1)} %collective-permute-done.14.left, ...), custom_call_target="tpu_custom_call" | custom-call | flops 1879048192 | bytes 15597568 | tf_op jit(solution)/shard_map/normal/pallas_call | solution.py:675
  123.5 0.1 maximum_maximum_fusion
  123.6 13.8 %all_to_all.5.shared_ref = f32[32,8,128]{2,1,0:T(8,128)S(1)} all-to-all(f32[32,8,128]{2,1,0:T(8,128)S(1)} %broadcast_in_dim.8), channel_id=1, replica_groups=mesh['band'=4,'row'=8] {'band','row'}, dimensions={0} | all-to-all | bytes 262144 | tf_op jit(solution)/shard_map/all_to_all | solution.py:717
  137.4 1.8 %combine.1 = (f32[32,32,170]{2,1,0:T(8,128)}, f32[32,32,170]{2,1,0:T(8,128)}) custom-call(f32[32,8,128]{2,1,0:T(8,128)S(1)} %all_to_all.5.shared_ref, f32[32,32,256]{2,1,0:T(8,128)S(1)} %bitcast.13, f32[32,32,256]{2,1,0:T(8,128)S(1)} %get-tuple-element.45.rest_0_.v1_ref, f32[32,32,256]{2,1,0:T(8,128)S(1)} %get-tuple-element.51.v2_ref), custom_call_target="tpu_custom_call" | custom-call | tf_op jit(solution)/shard_map/combine/pallas_call | solution.py:719
  (8 shorter events, 0.0 us)
Async XLA Ops:
  17.6 8.4 %copy-start = (bf16[224,32]{0,1:T(8,128)(2,1)S(1)}, bf16[224,32]{0,1:T(8,128)(2,1)}, u32[]{:S(2)}) copy-start(bf16[224,32]{0,1:T(8,128)(2,1)} %param.8) | copy-start | bytes 43012
  17.6 3.5 %collective-permute-start = (bf16[56,16,768]{2,1,0:T(8,128)(2,1)}, bf16[56,16,768]{2,1,0:T(8,128)(2,1)}, u32[]{:S(2)}, u32[]{:S(2)}) collective-permute-start(bf16[56,16,768]{2,1,0:T(8,128)(2,1)} %get-tuple-element.28), channel_id=1, source_target_pairs={{0,8},{8,0},{16,24},{24,16},{1,9},{9,1},{17,25},{25,17},{2,10},{10... | collective-permute-start | bytes 4128776 | tf_op jit(solution)/shard_map/ppermute | solution.py:614
  18.1 11.7 %collective-permute-start.4 = (f32[56,50]{1,0:T(8,128)S(1)}, f32[56,50]{1,0:T(8,128)S(1)}, u32[]{:S(2)}, u32[]{:S(2)}) collective-permute-start(f32[56,50]{1,0:T(8,128)S(1)} %pad_maximum_fusion.1.taps_ref), channel_id=1, source_target_pairs={{0,24},{8,0},{16,8},{24,16},{1,25},{9,1},{17,9},{25,17},{2,26},{10... | collective-permute-start | bytes 33608 | tf_op jit(solution)/shard_map/ppermute | solution.py:526
  20.7 10.4 %collective-permute-start.3 = (f32[56,50]{1,0:T(8,128)S(1)}, f32[56,50]{1,0:T(8,128)S(1)}, u32[]{:S(2)}, u32[]{:S(2)}) collective-permute-start(f32[56,50]{1,0:T(8,128)S(1)} %pad_maximum_fusion.1.taps_ref), channel_id=1, source_target_pairs={{0,16},{8,24},{16,0},{24,8},{1,17},{9,25},{17,1},{25,9},{2,18},{10... | collective-permute-start | bytes 33608 | tf_op jit(solution)/shard_map/ppermute | solution.py:526
  20.7 14.8 %collective-permute-start.2 = (f32[56,50]{1,0:T(8,128)S(1)}, f32[56,50]{1,0:T(8,128)S(1)}, u32[]{:S(2)}, u32[]{:S(2)}) collective-permute-start(f32[56,50]{1,0:T(8,128)S(1)} %pad_maximum_fusion.1.taps_ref), channel_id=1, source_target_pairs={{0,8},{8,16},{16,24},{24,0},{1,9},{9,17},{17,25},{25,1},{2,10},{10... | collective-permute-start | bytes 33608 | tf_op jit(solution)/shard_map/ppermute | solution.py:526
  23.0 21.2 %collective-permute-start.7 = (bf16[32,16,384]{2,1,0:T(8,128)(2,1)S(1)}, bf16[32,16,384]{2,1,0:T(8,128)(2,1)S(1)}, u32[]{:S(2)}, u32[]{:S(2)}) collective-permute-start(bf16[32,16,384]{2,1,0:T(8,128)(2,1)S(1)} %get-tuple-element.37), channel_id=1, source_target_pairs={{0,16},{1,17},{2,18},{3,19},{4,20},{5,21},{6,22},{7,23},{8,24},{9,... | collective-permute-start | bytes 1179656 | tf_op jit(solution)/shard_map/ppermute | solution.py:647
  26.4 17.8 %collective-permute-start.1 = (bf16[12,16,384]{2,1,0:T(8,128)(2,1)S(1)}, bf16[12,16,384]{2,1,0:T(8,128)(2,1)S(1)}, u32[]{:S(2)}, u32[]{:S(2)}) collective-permute-start(bf16[12,16,384]{2,1,0:T(8,128)(2,1)S(1)} %get-tuple-element.29), channel_id=1, source_target_pairs={{0,1},{1,2},{2,3},{3,4},{4,5},{5,6},{6,7},{8,9},{9,10},{10,11},{11... | collective-permute-start | bytes 442376 | tf_op jit(solution)/shard_map/ppermute | solution.py:645
  29.8 14.4 %collective-permute-start.5 = (bf16[12,16,384]{2,1,0:T(8,128)(2,1)S(1)}, bf16[12,16,384]{2,1,0:T(8,128)(2,1)S(1)}, u32[]{:S(2)}, u32[]{:S(2)}) collective-permute-start(bf16[12,16,384]{2,1,0:T(8,128)(2,1)S(1)} %get-tuple-element.35), channel_id=1, source_target_pairs={{1,0},{2,1},{3,2},{4,3},{5,4},{6,5},{7,6},{9,8},{10,9},{11,10},{12... | collective-permute-start | bytes 442376 | tf_op jit(solution)/shard_map/ppermute | solution.py:644
  31.1 13.1 %collective-permute-start.6 = (bf16[12,16,384]{2,1,0:T(8,128)(2,1)S(1)}, bf16[12,16,384]{2,1,0:T(8,128)(2,1)S(1)}, u32[]{:S(2)}, u32[]{:S(2)}) collective-permute-start(bf16[12,16,384]{2,1,0:T(8,128)(2,1)S(1)} %get-tuple-element.36), channel_id=1, source_target_pairs={{0,17},{1,18},{2,19},{3,20},{4,21},{5,22},{6,23},{8,25},{9,26},{10... | collective-permute-start | bytes 442376 | tf_op jit(solution)/shard_map/ppermute | solution.py:645
  35.6 8.6 %collective-permute-start.8 = (bf16[12,16,384]{2,1,0:T(8,128)(2,1)S(1)}, bf16[12,16,384]{2,1,0:T(8,128)(2,1)S(1)}, u32[]{:S(2)}, u32[]{:S(2)}) collective-permute-start(bf16[12,16,384]{2,1,0:T(8,128)(2,1)S(1)} %get-tuple-element.38), channel_id=1, source_target_pairs={{1,16},{2,17},{3,18},{4,19},{5,20},{6,21},{7,22},{9,24},{10,25},{1... | collective-permute-start | bytes 442376 | tf_op jit(solution)/shard_map/ppermute | solution.py:644
  44.4 2.4 %collective-permute-start.9 = (f32[32,16,384]{2,1,0:T(8,128)S(1)}, f32[32,16,384]{2,1,0:T(8,128)S(1)}, u32[]{:S(2)}, u32[]{:S(2)}) collective-permute-start(f32[32,16,384]{2,1,0:T(8,128)S(1)} %merge.1.mine_ref), channel_id=1, source_target_pairs={{0,8},{8,0},{16,24},{24,16},{1,9},{9,1},{17,25},{25,17},{2,10},{10... | collective-permute-start | bytes 2359304 | tf_op jit(solution)/shard_map/ppermute | solution.py:656
  47.6 23.2 %collective-permute-start.11 = (bf16[24,32,256]{2,1,0:T(8,128)(2,1)S(1)}, bf16[24,32,256]{2,1,0:T(8,128)(2,1)S(1)}, u32[]{:S(2)}, u32[]{:S(2)}) collective-permute-start(bf16[24,32,256]{2,1,0:T(8,128)(2,1)S(1)} %get-tuple-element.52), channel_id=1, source_target_pairs={{1,0},{2,1},{3,2},{4,3},{5,4},{6,5},{7,6},{9,8},{10,9},{11,10},{12... | collective-permute-start | bytes 1179656 | tf_op jit(solution)/shard_map/ppermute | solution.py:502
  48.9 23.2 %collective-permute-start.10 = (bf16[24,32,256]{2,1,0:T(8,128)(2,1)S(1)}, bf16[24,32,256]{2,1,0:T(8,128)(2,1)S(1)}, u32[]{:S(2)}, u32[]{:S(2)}) collective-permute-start(bf16[24,32,256]{2,1,0:T(8,128)(2,1)S(1)} %get-tuple-element.53), channel_id=1, source_target_pairs={{0,1},{1,2},{2,3},{3,4},{4,5},{5,6},{6,7},{8,9},{9,10},{10,11},{11... | collective-permute-start | bytes 1179656 | tf_op jit(solution)/shard_map/ppermute | solution.py:501
  70.1 2.0 %copy-start.1 = (f32[32]{0:T(128)S(1)}, f32[32]{0:T(128)}, u32[]{:S(2)}) copy-start(f32[32]{0:T(128)} %param.9) | copy-start | bytes 388
  85.3 9.0 %collective-permute-start.14 = (bf16[8,32,128]{2,1,0:T(8,128)(2,1)S(1)}, bf16[8,32,128]{2,1,0:T(8,128)(2,1)S(1)}, u32[]{:S(2)}, u32[]{:S(2)}) collective-permute-start(bf16[8,32,128]{2,1,0:T(8,128)(2,1)S(1)} %get-tuple-element.48), channel_id=1, source_target_pairs={{0,8},{8,16},{16,24},{1,9},{9,17},{17,25},{2,10},{10,18},{18,26},{... | collective-permute-start | bytes 196616 | tf_op jit(solution)/shard_map/ppermute | solution.py:501
  87.2 7.0 %collective-permute-start.15 = (bf16[8,32,128]{2,1,0:T(8,128)(2,1)S(1)}, bf16[8,32,128]{2,1,0:T(8,128)(2,1)S(1)}, u32[]{:S(2)}, u32[]{:S(2)}) collective-permute-start(bf16[8,32,128]{2,1,0:T(8,128)(2,1)S(1)} %get-tuple-element.49), channel_id=1, source_target_pairs={{8,0},{16,8},{24,16},{9,1},{17,9},{25,17},{10,2},{18,10},{26,18},{... | collective-permute-start | bytes 196616 | tf_op jit(solution)/shard_map/ppermute | solution.py:502
  88.5 22.1 %collective-permute-start.12 = (bf16[32,32,128]{2,1,0:T(8,128)(2,1)S(1)}, bf16[32,32,128]{2,1,0:T(8,128)(2,1)S(1)}, u32[]{:S(2)}, u32[]{:S(2)}) collective-permute-start(bf16[32,32,128]{2,1,0:T(8,128)(2,1)S(1)} %get-tuple-element.46), channel_id=1, source_target_pairs={{0,1},{1,2},{2,3},{3,4},{4,5},{5,6},{6,7},{8,9},{9,10},{10,11},{11... | collective-permute-start | bytes 786440 | tf_op jit(solution)/shard_map/ppermute | solution.py:501
  92.9 17.7 %collective-permute-start.13 = (bf16[32,32,128]{2,1,0:T(8,128)(2,1)S(1)}, bf16[32,32,128]{2,1,0:T(8,128)(2,1)S(1)}, u32[]{:S(2)}, u32[]{:S(2)}) collective-permute-start(bf16[32,32,128]{2,1,0:T(8,128)(2,1)S(1)} %get-tuple-element.47), channel_id=1, source_target_pairs={{1,0},{2,1},{3,2},{4,3},{5,4},{6,5},{7,6},{9,8},{10,9},{11,10},{12... | collective-permute-start | bytes 786440 | tf_op jit(solution)/shard_map/ppermute | solution.py:502
  94.3 12.4 %collective-permute-start.17 = (bf16[16,32,128]{2,1,0:T(8,128)(2,1)S(1)}, bf16[16,32,128]{2,1,0:T(8,128)(2,1)S(1)}, u32[]{:S(2)}, u32[]{:S(2)}) collective-permute-start(bf16[16,32,128]{2,1,0:T(8,128)(2,1)S(1)} %constant_dynamic-update-slice_fusion), channel_id=1, source_target_pairs={{1,0},{2,1},{3,2},{4,3},{5,4},{6,5},{7,6},{9,8},{10,9},{11,10},{12... | collective-permute-start | bytes 393224 | tf_op jit(solution)/shard_map/ppermute | solution.py:502
  95.6 15.1 %collective-permute-start.16 = (bf16[16,32,128]{2,1,0:T(8,128)(2,1)S(1)}, bf16[16,32,128]{2,1,0:T(8,128)(2,1)S(1)}, u32[]{:S(2)}, u32[]{:S(2)}) collective-permute-start(bf16[16,32,128]{2,1,0:T(8,128)(2,1)S(1)} %constant_dynamic-update-slice_fusion), channel_id=1, source_target_pairs={{0,1},{1,2},{2,3},{3,4},{4,5},{5,6},{6,7},{8,9},{9,10},{10,11},{11... | collective-permute-start | bytes 393224 | tf_op jit(solution)/shard_map/ppermute | solution.py:501

commit v7 on v6

--- a/solution.py
+++ b/solution.py
@@ -148,31 +148,36 @@
     return turn_lanes(wide, first)
 
 
-def pack_kernel(columns, halo, near_ref, up_ref, down_ref, left_ref, right_ref):
+def pack_kernel(columns, halo, near_ref, up_ref, down_ref):
     cells = near_ref[...].astype(F32)
     height = cells.shape[0]
     up_ref[...] = packed_main(cells[:halo], columns).astype(BF)
     down_ref[...] = packed_main(cells[height - halo :], columns).astype(BF)
-    left_ref[...] = packed_strip(cells, 0, halo).astype(BF)
-    right_ref[...] = packed_strip(cells, columns - halo, halo).astype(BF)
-
-
-def window_pieces(columns, halo, near_ref, main_refs, side_refs, corner_refs, p_ref):
+
+
+def tall_rows(columns, halo, near_ref, before_ref, after_ref):
+    lanes = near_ref.shape[2]
+    return [turn_lanes(near_ref[...].astype(F32), halo)] + [
+        unpacked_main(ref[...], columns, halo, lanes) for ref in (before_ref, after_ref)
+    ]
+
+
+def side_kernel(columns, halo, near_ref, before_ref, after_ref, left_ref, right_ref):
+    cells = jnp.concatenate(tall_rows(columns, halo, near_ref, before_ref, after_ref), axis=0)
+    left_ref[...] = packed_strip(cells, halo, halo).astype(BF)
+    right_ref[...] = packed_strip(cells, columns, halo).astype(BF)
+
+
+def window_pieces(columns, halo, near_ref, before_ref, after_ref, left_ref, right_ref, p_ref):
     height, _, lanes = near_ref.shape
-    right = columns + halo
-    own = turn_lanes(near_ref[...].astype(F32), halo)
-    own = own + unpacked_strip(side_refs[0][...], height, halo, 0, lanes)
-    own = own + unpacked_strip(side_refs[1][...], height, halo, right, lanes)
-    p_ref[halo : halo + height] = own.astype(BF)
-    rows = strip_plan(height, halo)[1]
-    for main, corner, first, at in (
-        (main_refs[0], corner_refs[0], height - halo, 0),
-        (main_refs[1], corner_refs[1], 0, halo + height),
-    ):
-        total = unpacked_main(main[...], columns, halo, lanes)
-        for packed, lane in ((corner[:rows], 0), (corner[rows:], right)):
-            total = total + unpacked_strip(packed, height, halo, lane, lanes)[first : first + halo]
-        p_ref[at : at + halo] = total.astype(BF)
+    tall = height + 2 * halo
+    sides = unpacked_strip(left_ref[...], tall, halo, 0, lanes)
+    sides = sides + unpacked_strip(right_ref[...], tall, halo, columns + halo, lanes)
+    at = 0
+    for rows, to in zip(tall_rows(columns, halo, near_ref, before_ref, after_ref), (halo, 0, halo + height)):
+        count = rows.shape[0]
+        p_ref[to : to + count] = (rows + sides[at : at + count]).astype(BF)
+        at += count
 
 
 def adjoint_kernel(
@@ -189,10 +194,13 @@
     last = columns // LANES * LANES
     batch = group_size(group, 7)
 
+    blank_rows = jnp.zeros((LANES - edge, width), BF)
+
     @pl.when(step == 0)
     def _():
-        acc[...] = jnp.zeros_like(acc)
-        mats[...] = jnp.zeros_like(mats)
+        for b in range(group):
+            mats[b, : LANES - edge] = blank_rows
+            mats[b, LANES + width + edge :] = blank_rows
         both = taps_ref[...]
         taps = both.shape[1] // 2
         for i, line in enumerate(placed_taps(both, [(taps, -radius % SUB, False), (0, 0, True)], F32)):
@@ -251,14 +259,22 @@
     mix = (dot(wide, here) * same).astype(BF)
     for c in range(chunks):
         cells = ys[c].reshape(group * SUB, span).astype(BF)
-        acc[c] += dot(mix, cells)
-
-    @pl.when(step == pl.num_programs(0) - 1)
-    def _():
+        total = dot(mix, cells).reshape(SUB, kinds, span)
         half = kinds // 2
-        total = acc[...].reshape(ext, kinds, span).astype(BF)
-        give_ref[...] = total[:, :half]
-        keep_ref[...] = total[:, half:]
+        here = slice(c * SUB, (c + 1) * SUB)
+
+        if acc.shape[0] == ext:
+            @pl.when(step == 0)
+            def _():
+                acc[here] = total
+
+            @pl.when(step > 0)
+            def _():
+                acc[here] += total
+
+            total = acc[here]
+        give_ref[here] = total[:, :half].astype(BF)
+        keep_ref[here] = total[:, half:].astype(BF)
 
 
 def inside(lanes, first, count, limit):
@@ -386,16 +402,12 @@
     normal_kernel(columns, halo, group, True, (before, window, after), *rest)
 
 
-def second_kernel(
-    columns, halo, group, near_ref, before, after, left, right, corner_before, corner_after, *rest
-):
+def second_kernel(columns, halo, group, near_ref, before, after, left, right, *rest):
     *rest, p_ref = rest
 
     @pl.when(pl.program_id(0) == 0)
     def _():
-        window_pieces(
-            columns, halo, near_ref, (before, after), (left, right), (corner_before, corner_after), p_ref
-        )
+        window_pieces(columns, halo, near_ref, before, after, left, right, p_ref)
 
     normal_kernel(columns, halo, group, False, (p_ref,), *rest)
 
@@ -542,7 +554,7 @@
     ).astype(jnp.int32)
     whole = lambda shape: pl.BlockSpec(shape, lambda i: (0,) * len(shape))
 
-    few = group_size(bands_here, 32)
+    few = group_size(bands_here, 64)
     span = round_up(columns_all, 2 * LANES)
     ext = height + 2 * radius
     chunks = ext // SUB
@@ -558,7 +570,7 @@
         out_specs=[whole((ext, half, span))] * 2,
         out_shape=[jax.ShapeDtypeStruct((ext, half, span), BF)] * 2,
         scratch_shapes=[
-            pltpu.VMEM((chunks, SUB * kinds, span), F32),
+            pltpu.VMEM((ext if few < bands_here else SUB, kinds, span), F32),
             pltpu.VMEM((chunks, few, SUB, span), F32),
             pltpu.VMEM((few, 4 * LANES, 2 * LANES), BF),
             pltpu.VMEM((few, 2, ext, height), BF),
@@ -698,18 +710,22 @@
     v1, sums1 = normal_map([before, window, after], v0, True)
     near = jnp.swapaxes(v1.astype(BF), 0, 1)
     main = jax.ShapeDtypeStruct((main_rows(columns, halo), kinds, LANES), BF)
-    side = jax.ShapeDtypeStruct((strip_plan(height, halo)[1], kinds, LANES), BF)
-    up, down, left, right = pl.pallas_call(
+    up, down = pl.pallas_call(
         functools.partial(pack_kernel, columns, halo),
-        out_shape=[main, main, side, side],
-        compiler_params=pltpu.CompilerParams(vmem_limit_bytes=SMALL_LIMIT),
+        out_shape=[main, main],
+        compiler_params=params,
         name="pack",
     )(near)
     before, after = shift_both(up, down, "row")
-    from_left, from_right = shift_both(left, right, "band")
-    corners = jnp.concatenate([from_left, from_right], axis=0)
-    corner_before, corner_after = shift_both(corners, corners, "row")
-    pieces = [near, before, after, from_left, from_right, corner_before, corner_after]
+    side = jax.ShapeDtypeStruct((strip_plan(tall, halo)[1], kinds, LANES), BF)
+    left, right = pl.pallas_call(
+        functools.partial(side_kernel, columns, halo),
+        out_shape=[side, side],
+        compiler_params=params,
+        name="sides",
+    )(near, before, after)
+    left, right = shift_both(left, right, "band")
+    pieces = [near, before, after, left, right]
     v2, sums2 = normal_map(pieces, v1, False)
 
     sums = jnp.concatenate([sums1[:3], sums2[:1], jnp.zeros((SUB - 4, LANES), F32)])

time: 140 us -> 138 us (0.986)
  starting transfers between devices: 39.9 us -> 32.7 us
  waiting for transfers between devices: 13.7 us -> 16.5 us
  blocking collectives: 13.8 us -> 16.3 us
    ppermute x4 -> x3, waiting for transfers between devices: 5.24 us -> 11.4 us  [shift_both(): lax.ppermute(high_edge, axis, [(i, i + 1) for i in range(count - 1)])]
    ppermute x4 -> x3, starting transfers between devices: 17.9 us -> 12.1 us  [shift_both(): lax.ppermute(high_edge, axis, [(i, i + 1) for i in range(count - 1)])]
    ppermute x4 -> x3, waiting for transfers between devices: 5.87 us -> 2.55 us  [shift_both(): lax.ppermute(low_edge, axis, [(i + 1, i) for i in range(count - 1)])]
    all_to_all x1, blocking collectives: 13.8 us -> 16.3 us  [local(): shared = lax.all_to_all(mine, ('band', 'row'), 0, 0, tiled=True)]
    ppermute x4 -> x3, starting transfers between devices: 5.17 us -> 3.88 us  [shift_both(): lax.ppermute(low_edge, axis, [(i + 1, i) for i in range(count - 1)])]
  transfers between devices with their start and end apart: 18 -> 16, of which waited for: 5 -> 5; matrix products, arithmetic and copies ran while one was open for 1% -> 1% of each run, Pallas kernels for 17% -> 17%
where the time goes in v7:
time: 138 us
  Pallas kernels  66.7 us (48%)
  starting transfers between devices  32.7 us (24%)
  waiting for transfers between devices  16.5 us (12%)
  blocking collectives  16.3 us (12%)
  local copies, waits for them, and re-layouts  4.17 us (3%)
    pallas_call x2, Pallas kernels, normal_map(): pl.pallas_call(functools.partial(first_kernel if first else second_kernel...  24.9 us
    all_to_all x1, blocking collectives, local(): shared = lax.all_to_all(mine, ('band', 'row'), 0, 0, tiled=True)  16.3 us
    pallas_call x1, Pallas kernels, local(): pl.pallas_call(functools.partial(gram_columns_kernel, columns, columns_al...  14.8 us
    pallas_call x1, Pallas kernels, local(): pl.pallas_call(functools.partial(adjoint_kernel, columns_all, radius), gr...  13.7 us
    ppermute x3, starting transfers between devices, shift_both(): lax.ppermute(high_edge, axis, [(i, i + 1) for i in range(count - 1)])  12.1 us
    ppermute x3, waiting for transfers between devices, shift_both(): lax.ppermute(high_edge, axis, [(i, i + 1) for i in range(count - 1)])  11.4 us
    ppermute x2, starting transfers between devices, local(): before = lax.ppermute(below, axes, moves(hop, 1))  7.86 us
    pallas_call x1, Pallas kernels, local(): pl.pallas_call(functools.partial(gram_rows_kernel, height * n_row, radius...  7.2 us
  transfers between devices with their start and end apart: 16, of which 5 were waited for; matrix products, arithmetic and copies ran while one was open for 1% of the time, Pallas kernels for 17%

profile of v7, /device:TPU:0, one launch (start us, length us, event | category | flops | bytes accessed | tf_op | source)
XLA Modules:
  0.0 137.7 jit_solution(10503633043701052833)
XLA Ops:
  0.6 0.8 copy.16
  1.4 0.8 copy.17
  2.2 0.8 copy.18.basis_ref
  3.1 0.1 pad_maximum_fusion.1.taps_ref
  3.2 0.1 stack.27.place_ref
  3.3 13.7 %adjoint.1 = (bf16[56,16,768]{2,1,0:T(8,128)(2,1)}, bf16[56,16,768]{2,1,0:T(8,128)(2,1)S(1)}) custom-call(s32[6]{0:T(128)S(1)} %stack.27.place_ref, bf16[56,32,680]{2,1,0:T(8,128)(2,1)} %obs_ref.1, f32[56,50]{1,0:T(8,128)S(1)} %pad_maximum_fusion.1.taps_ref, bf16[224,32]{1,0:T(8,128)(2,1)S(1)} %copy.18.basis_ref), custom_call_target="tpu_custom_call" | custom-call | flops 1409286144 | bytes 2437120 | tf_op jit(solution)/shard_map/adjoint/pallas_call | solution.py:561
  16.9 0.0 copy-start
  16.9 0.5 collective-permute-start
  17.4 2.6 %collective-permute-start.4 = (f32[56,50]{1,0:T(8,128)S(1)}, f32[56,50]{1,0:T(8,128)S(1)}, u32[]{:S(2)}, u32[]{:S(2)}) collective-permute-start(f32[56,50]{1,0:T(8,128)S(1)} %pad_maximum_fusion.1.taps_ref), channel_id=1, source_target_pairs={{0,24},{8,0},{16,8},{24,16},{1,25},{9,1},{17,9},{25,17},{2,26},{10... | collective-permute-start | bytes 33608 | tf_op jit(solution)/shard_map/ppermute | solution.py:538
  20.0 0.0 collective-permute-start.3
  20.0 0.1 collective-permute-start.2
  20.2 0.3 collective-permute-done.got_ref
  20.5 1.8 %split.1 = (bf16[12,16,384]{2,1,0:T(8,128)(2,1)S(1)}, f32[32,16,384]{2,1,0:T(8,128)S(1)}, bf16[12,16,384]{2,1,0:T(8,128)(2,1)S(1)}, bf16[12,16,384]{2,1,0:T(8,12...) custom-call(s32[6]{0:T(128)S(1)} %stack.27.place_ref, ...), custom_call_target="tpu_custom_call" | custom-call | tf_op jit(solution)/shard_map/split/pallas_call | solution.py:632
  22.3 3.0 %collective-permute-start.7 = (bf16[32,16,384]{2,1,0:T(8,128)(2,1)S(1)}, bf16[32,16,384]{2,1,0:T(8,128)(2,1)S(1)}, u32[]{:S(2)}, u32[]{:S(2)}) collective-permute-start(bf16[32,16,384]{2,1,0:T(8,128)(2,1)S(1)} %get-tuple-element.37), channel_id=1, source_target_pairs={{0,16},{1,17},{2,18},{3,19},{4,20},{5,21},{6,22},{7,23},{8,24},{9,... | collective-permute-start | bytes 1179656 | tf_op jit(solution)/shard_map/ppermute | solution.py:659
  25.4 0.0 copy-done
  25.4 0.1 constant_dynamic-slice_fusion.3
  25.5 0.1 pad_maximum_fusion.2
  25.6 0.1 copy.19.basis_ref
  25.7 3.4 %collective-permute-start.1 = (bf16[12,16,384]{2,1,0:T(8,128)(2,1)S(1)}, bf16[12,16,384]{2,1,0:T(8,128)(2,1)S(1)}, u32[]{:S(2)}, u32[]{:S(2)}) collective-permute-start(bf16[12,16,384]{2,1,0:T(8,128)(2,1)S(1)} %get-tuple-element.29), channel_id=1, source_target_pairs={{0,1},{1,2},{2,3},{3,4},{4,5},{5,6},{6,7},{8,9},{9,10},{10,11},{11... | collective-permute-start | bytes 442376 | tf_op jit(solution)/shard_map/ppermute | solution.py:657
  29.1 0.0 collective-permute-done.4
  29.1 1.3 collective-permute-start.5
  30.4 0.0 collective-permute-done.3
  30.4 4.5 %collective-permute-start.6 = (bf16[12,16,384]{2,1,0:T(8,128)(2,1)S(1)}, bf16[12,16,384]{2,1,0:T(8,128)(2,1)S(1)}, u32[]{:S(2)}, u32[]{:S(2)}) collective-permute-start(bf16[12,16,384]{2,1,0:T(8,128)(2,1)S(1)} %get-tuple-element.36), channel_id=1, source_target_pairs={{0,17},{1,18},{2,19},{3,20},{4,21},{5,22},{6,23},{8,25},{9,26},{10... | collective-permute-start | bytes 442376 | tf_op jit(solution)/shard_map/ppermute | solution.py:657
  34.9 0.0 collective-permute-done.2
  34.9 1.3 collective-permute-start.8
  36.2 0.1 pad_maximum_fusion.taps_ref
  36.3 7.2 %gram_rows.1 = (bf16[224,32,128]{2,1,0:T(8,128)(2,1)S(1)}, bf16[1792,256]{1,0:T(8,128)(2,1)S(1)}, bf16[7,256,256]{2,1,0:T(8,128)(2,1)S(1)}) custom-call(s32[6]{0:T(128)S(1)} %stack.27.place_ref, f32[224,50]{1,0:T(8,128)S(1)} %pad_maximum_fusion.taps_ref, bf16[224,32]{1,0:T(8,128)(2,1)S(1)} %copy.19.basis_ref), custom_call_target="tpu_custom_call" | custom-call | flops 939524096 | bytes 1835008 | tf_op jit(solution)/shard_map/gram_rows/pallas_call | solution.py:592
  43.5 0.0 collective-permute-done.1.refs_0_
  43.5 0.0 collective-permute-done.5.refs_2_
  43.5 0.0 collective-permute-done.6.refs_3_
  43.5 0.0 collective-permute-done.8.refs_5_
  43.5 0.0 collective-permute-done.7.refs_4_
  43.5 0.1 merge.1.mine_ref
  43.7 0.1 collective-permute-start.9
  43.7 2.3 %collective-permute-done.9.other_ref = f32[32,16,384]{2,1,0:T(8,128)S(1)} collective-permute-done((f32[32,16,384]{2,1,0:T(8,128)S(1)}, f32[32,16,384]{2,1,0:T(8,128)S(1)}, u32[]{:S(2)}, u32[]{:S(2)}) %collective-permute-start.9) | collective-permute-done | bytes 786464 | tf_op jit(solution)/shard_map/ppermute | solution.py:668
  46.0 0.8 window.1
  46.8 0.1 fusion.1
  46.9 1.3 collective-permute-start.11
  48.2 6.4 %collective-permute-start.10 = (bf16[24,32,256]{2,1,0:T(8,128)(2,1)S(1)}, bf16[24,32,256]{2,1,0:T(8,128)(2,1)S(1)}, u32[]{:S(2)}, u32[]{:S(2)}) collective-permute-start(bf16[24,32,256]{2,1,0:T(8,128)(2,1)S(1)} %get-tuple-element.53), channel_id=1, source_target_pairs={{0,1},{1,2},{2,3},{3,4},{4,5},{5,6},{6,7},{8,9},{9,10},{10,11},{11... | collective-permute-start | bytes 1179656 | tf_op jit(solution)/shard_map/ppermute | solution.py:513
  54.6 14.8 %gram_columns.1.rest_5_ = bf16[224,272,128]{2,1,0:T(8,128)(2,1)S(1)} custom-call(s32[6]{0:T(128)S(1)} %stack.27.place_ref, f32[224,50]{1,0:T(8,128)S(1)} %pad_maximum_fusion.taps_ref), custom_call_target="tpu_custom_call" | custom-call | flops 7516192768 | bytes 15597568 | tf_op jit(solution)/shard_map/gram_columns/pallas_call | solution.py:612
  69.4 0.0 copy-start.1
  69.5 0.6 copy.26
  70.1 0.0 collective-permute-done.11.after
  70.1 1.3 collective-permute-done.10.before
  71.4 0.0 copy-done.1
  71.4 0.1 broadcast_in_dim.6.rest_1_
  71.5 12.0 %normal.2 = (f32[32,32,256]{2,1,0:T(8,128)S(1)}, f32[8,128]{1,0:T(8,128)S(1)}) custom-call(bf16[24,32,256]{2,1,0:T(8,128)(2,1)S(1)} %collective-permute-done.10.before, bf16[32,32,256]{2,1,0:T(8,128)(2,1)S(1)} %get-tuple-element.39.window, bf16[24,32,256]{2,1,0:T(8,128)(2,1)S(1)} %collective-permute-done.11.after, f32[32,32,256]{2,1,0:T(8,128)S(1)} %bitcast.12, ...), custom_call_target="tpu_custom_call" | custom-call | flops 1879048192 | bytes 15597568 | tf_op jit(solution)/shard_map/normal/pallas_call | solution.py:687
  83.5 0.6 copy.27
  84.1 0.2 pack.1
  84.3 4.4 %collective-permute-start.12 = (bf16[32,32,128]{2,1,0:T(8,128)(2,1)S(1)}, bf16[32,32,128]{2,1,0:T(8,128)(2,1)S(1)}, u32[]{:S(2)}, u32[]{:S(2)}) collective-permute-start(bf16[32,32,128]{2,1,0:T(8,128)(2,1)S(1)} %get-tuple-element.46), channel_id=1, source_target_pairs={{0,1},{1,2},{2,3},{3,4},{4,5},{5,6},{6,7},{8,9},{9,10},{10,11},{11... | collective-permute-start | bytes 786440 | tf_op jit(solution)/shard_map/ppermute | solution.py:513
  88.7 1.3 collective-permute-start.13
  90.0 10.1 %collective-permute-done.12.before_ref.before = bf16[32,32,128]{2,1,0:T(8,128)(2,1)S(1)} collective-permute-done((bf16[32,32,128]{2,1,0:T(8,128)(2,1)S(1)}, bf16[32,32,128]{2,1,0:T(8,128)(2,1)S(1)}, u32[]{:S(2)}, u32[]{:S(2)}) %collective-permute-start.12) | collective-permute-done | bytes 262176 | tf_op jit(solution)/shard_map/ppermute | solution.py:513
  100.1 0.0 collective-permute-done.13.after_ref.after
  100.1 1.3 sides.1
  101.4 1.3 collective-permute-start.14
  102.7 1.3 collective-permute-start.15
  104.0 0.1 pad.2.clone
  104.1 0.0 collective-permute-done.14.left
  104.1 2.5 %collective-permute-done.15.right = bf16[16,32,128]{2,1,0:T(8,128)(2,1)S(1)} collective-permute-done((bf16[16,32,128]{2,1,0:T(8,128)(2,1)S(1)}, bf16[16,32,128]{2,1,0:T(8,128)(2,1)S(1)}, u32[]{:S(2)}, u32[]{:S(2)}) %collective-permute-start.15) | collective-permute-done | bytes 131104 | tf_op jit(solution)/shard_map/ppermute | solution.py:514
  106.7 12.9 %normal.3 = (f32[32,32,256]{2,1,0:T(8,128)S(1)}, f32[8,128]{1,0:T(8,128)S(1)}) custom-call(bf16[32,32,256]{2,1,0:T(8,128)(2,1)S(1)} %bitcast.16, bf16[32,32,128]{2,1,0:T(8,128)(2,1)S(1)} %collective-permute-done.12.before_ref.before, bf16[32,32,128]{2,1,0:T(8,128)(2,1)S(1)} %collective-permute-done.13.after_ref.after, ...), custom_call_target="tpu_custom_call" | custom-call | flops 1879048192 | bytes 15597568 | tf_op jit(solution)/shard_map/normal/pallas_call | solution.py:687
  119.6 0.1 maximum_maximum_fusion
  119.6 16.3 %all_to_all.5.shared_ref = f32[32,8,128]{2,1,0:T(8,128)S(1)} all-to-all(f32[32,8,128]{2,1,0:T(8,128)S(1)} %broadcast_in_dim.8), channel_id=1, replica_groups=mesh['band'=4,'row'=8] {'band','row'}, dimensions={0} | all-to-all | bytes 262144 | tf_op jit(solution)/shard_map/all_to_all | solution.py:733
  136.0 1.8 %combine.1 = (f32[32,32,170]{2,1,0:T(8,128)}, f32[32,32,170]{2,1,0:T(8,128)}) custom-call(f32[32,8,128]{2,1,0:T(8,128)S(1)} %all_to_all.5.shared_ref, f32[32,32,256]{2,1,0:T(8,128)S(1)} %bitcast.13, f32[32,32,256]{2,1,0:T(8,128)S(1)} %get-tuple-element.45.rest_0_.v1_ref, f32[32,32,256]{2,1,0:T(8,128)S(1)} %get-tuple-element.51.v2_ref), custom_call_target="tpu_custom_call" | custom-call | tf_op jit(solution)/shard_map/combine/pallas_call | solution.py:735
  (4 shorter events, 0.0 us)
Async XLA Ops:
  16.9 8.4 %copy-start = (bf16[224,32]{0,1:T(8,128)(2,1)S(1)}, bf16[224,32]{0,1:T(8,128)(2,1)}, u32[]{:S(2)}) copy-start(bf16[224,32]{0,1:T(8,128)(2,1)} %param.8) | copy-start | bytes 43012
  16.9 3.5 %collective-permute-start = (bf16[56,16,768]{2,1,0:T(8,128)(2,1)}, bf16[56,16,768]{2,1,0:T(8,128)(2,1)}, u32[]{:S(2)}, u32[]{:S(2)}) collective-permute-start(bf16[56,16,768]{2,1,0:T(8,128)(2,1)} %get-tuple-element.28), channel_id=1, source_target_pairs={{0,8},{8,0},{16,24},{24,16},{1,9},{9,1},{17,25},{25,17},{2,10},{10... | collective-permute-start | bytes 4128776 | tf_op jit(solution)/shard_map/ppermute | solution.py:626
  17.4 11.7 %collective-permute-start.4 = (f32[56,50]{1,0:T(8,128)S(1)}, f32[56,50]{1,0:T(8,128)S(1)}, u32[]{:S(2)}, u32[]{:S(2)}) collective-permute-start(f32[56,50]{1,0:T(8,128)S(1)} %pad_maximum_fusion.1.taps_ref), channel_id=1, source_target_pairs={{0,24},{8,0},{16,8},{24,16},{1,25},{9,1},{17,9},{25,17},{2,26},{10... | collective-permute-start | bytes 33608 | tf_op jit(solution)/shard_map/ppermute | solution.py:538
  20.0 10.4 %collective-permute-start.3 = (f32[56,50]{1,0:T(8,128)S(1)}, f32[56,50]{1,0:T(8,128)S(1)}, u32[]{:S(2)}, u32[]{:S(2)}) collective-permute-start(f32[56,50]{1,0:T(8,128)S(1)} %pad_maximum_fusion.1.taps_ref), channel_id=1, source_target_pairs={{0,16},{8,24},{16,0},{24,8},{1,17},{9,25},{17,1},{25,9},{2,18},{10... | collective-permute-start | bytes 33608 | tf_op jit(solution)/shard_map/ppermute | solution.py:538
  20.0 14.8 %collective-permute-start.2 = (f32[56,50]{1,0:T(8,128)S(1)}, f32[56,50]{1,0:T(8,128)S(1)}, u32[]{:S(2)}, u32[]{:S(2)}) collective-permute-start(f32[56,50]{1,0:T(8,128)S(1)} %pad_maximum_fusion.1.taps_ref), channel_id=1, source_target_pairs={{0,8},{8,16},{16,24},{24,0},{1,9},{9,17},{17,25},{25,1},{2,10},{10... | collective-permute-start | bytes 33608 | tf_op jit(solution)/shard_map/ppermute | solution.py:538
  22.3 21.2 %collective-permute-start.7 = (bf16[32,16,384]{2,1,0:T(8,128)(2,1)S(1)}, bf16[32,16,384]{2,1,0:T(8,128)(2,1)S(1)}, u32[]{:S(2)}, u32[]{:S(2)}) collective-permute-start(bf16[32,16,384]{2,1,0:T(8,128)(2,1)S(1)} %get-tuple-element.37), channel_id=1, source_target_pairs={{0,16},{1,17},{2,18},{3,19},{4,20},{5,21},{6,22},{7,23},{8,24},{9,... | collective-permute-start | bytes 1179656 | tf_op jit(solution)/shard_map/ppermute | solution.py:659
  25.7 17.8 %collective-permute-start.1 = (bf16[12,16,384]{2,1,0:T(8,128)(2,1)S(1)}, bf16[12,16,384]{2,1,0:T(8,128)(2,1)S(1)}, u32[]{:S(2)}, u32[]{:S(2)}) collective-permute-start(bf16[12,16,384]{2,1,0:T(8,128)(2,1)S(1)} %get-tuple-element.29), channel_id=1, source_target_pairs={{0,1},{1,2},{2,3},{3,4},{4,5},{5,6},{6,7},{8,9},{9,10},{10,11},{11... | collective-permute-start | bytes 442376 | tf_op jit(solution)/shard_map/ppermute | solution.py:657
  29.1 14.4 %collective-permute-start.5 = (bf16[12,16,384]{2,1,0:T(8,128)(2,1)S(1)}, bf16[12,16,384]{2,1,0:T(8,128)(2,1)S(1)}, u32[]{:S(2)}, u32[]{:S(2)}) collective-permute-start(bf16[12,16,384]{2,1,0:T(8,128)(2,1)S(1)} %get-tuple-element.35), channel_id=1, source_target_pairs={{1,0},{2,1},{3,2},{4,3},{5,4},{6,5},{7,6},{9,8},{10,9},{11,10},{12... | collective-permute-start | bytes 442376 | tf_op jit(solution)/shard_map/ppermute | solution.py:656
  30.4 13.1 %collective-permute-start.6 = (bf16[12,16,384]{2,1,0:T(8,128)(2,1)S(1)}, bf16[12,16,384]{2,1,0:T(8,128)(2,1)S(1)}, u32[]{:S(2)}, u32[]{:S(2)}) collective-permute-start(bf16[12,16,384]{2,1,0:T(8,128)(2,1)S(1)} %get-tuple-element.36), channel_id=1, source_target_pairs={{0,17},{1,18},{2,19},{3,20},{4,21},{5,22},{6,23},{8,25},{9,26},{10... | collective-permute-start | bytes 442376 | tf_op jit(solution)/shard_map/ppermute | solution.py:657
  34.9 8.6 %collective-permute-start.8 = (bf16[12,16,384]{2,1,0:T(8,128)(2,1)S(1)}, bf16[12,16,384]{2,1,0:T(8,128)(2,1)S(1)}, u32[]{:S(2)}, u32[]{:S(2)}) collective-permute-start(bf16[12,16,384]{2,1,0:T(8,128)(2,1)S(1)} %get-tuple-element.38), channel_id=1, source_target_pairs={{1,16},{2,17},{3,18},{4,19},{5,20},{6,21},{7,22},{9,24},{10,25},{1... | collective-permute-start | bytes 442376 | tf_op jit(solution)/shard_map/ppermute | solution.py:656
  43.7 2.4 %collective-permute-start.9 = (f32[32,16,384]{2,1,0:T(8,128)S(1)}, f32[32,16,384]{2,1,0:T(8,128)S(1)}, u32[]{:S(2)}, u32[]{:S(2)}) collective-permute-start(f32[32,16,384]{2,1,0:T(8,128)S(1)} %merge.1.mine_ref), channel_id=1, source_target_pairs={{0,8},{8,0},{16,24},{24,16},{1,9},{9,1},{17,25},{25,17},{2,10},{10... | collective-permute-start | bytes 2359304 | tf_op jit(solution)/shard_map/ppermute | solution.py:668
  46.9 23.2 %collective-permute-start.11 = (bf16[24,32,256]{2,1,0:T(8,128)(2,1)S(1)}, bf16[24,32,256]{2,1,0:T(8,128)(2,1)S(1)}, u32[]{:S(2)}, u32[]{:S(2)}) collective-permute-start(bf16[24,32,256]{2,1,0:T(8,128)(2,1)S(1)} %get-tuple-element.52), channel_id=1, source_target_pairs={{1,0},{2,1},{3,2},{4,3},{5,4},{6,5},{7,6},{9,8},{10,9},{11,10},{12... | collective-permute-start | bytes 1179656 | tf_op jit(solution)/shard_map/ppermute | solution.py:514
  48.2 23.2 %collective-permute-start.10 = (bf16[24,32,256]{2,1,0:T(8,128)(2,1)S(1)}, bf16[24,32,256]{2,1,0:T(8,128)(2,1)S(1)}, u32[]{:S(2)}, u32[]{:S(2)}) collective-permute-start(bf16[24,32,256]{2,1,0:T(8,128)(2,1)S(1)} %get-tuple-element.53), channel_id=1, source_target_pairs={{0,1},{1,2},{2,3},{3,4},{4,5},{5,6},{6,7},{8,9},{9,10},{10,11},{11... | collective-permute-start | bytes 1179656 | tf_op jit(solution)/shard_map/ppermute | solution.py:513
  69.4 2.0 %copy-start.1 = (f32[32]{0:T(128)S(1)}, f32[32]{0:T(128)}, u32[]{:S(2)}) copy-start(f32[32]{0:T(128)} %param.9) | copy-start | bytes 388
  84.3 15.8 %collective-permute-start.12 = (bf16[32,32,128]{2,1,0:T(8,128)(2,1)S(1)}, bf16[32,32,128]{2,1,0:T(8,128)(2,1)S(1)}, u32[]{:S(2)}, u32[]{:S(2)}) collective-permute-start(bf16[32,32,128]{2,1,0:T(8,128)(2,1)S(1)} %get-tuple-element.46), channel_id=1, source_target_pairs={{0,1},{1,2},{2,3},{3,4},{4,5},{5,6},{6,7},{8,9},{9,10},{10,11},{11... | collective-permute-start | bytes 786440 | tf_op jit(solution)/shard_map/ppermute | solution.py:513
  88.7 11.4 %collective-permute-start.13 = (bf16[32,32,128]{2,1,0:T(8,128)(2,1)S(1)}, bf16[32,32,128]{2,1,0:T(8,128)(2,1)S(1)}, u32[]{:S(2)}, u32[]{:S(2)}) collective-permute-start(bf16[32,32,128]{2,1,0:T(8,128)(2,1)S(1)} %get-tuple-element.47), channel_id=1, source_target_pairs={{1,0},{2,1},{3,2},{4,3},{5,4},{6,5},{7,6},{9,8},{10,9},{11,10},{12... | collective-permute-start | bytes 786440 | tf_op jit(solution)/shard_map/ppermute | solution.py:514
  101.4 2.7 %collective-permute-start.14 = (bf16[16,32,128]{2,1,0:T(8,128)(2,1)S(1)}, bf16[16,32,128]{2,1,0:T(8,128)(2,1)S(1)}, u32[]{:S(2)}, u32[]{:S(2)}) collective-permute-start(bf16[16,32,128]{2,1,0:T(8,128)(2,1)S(1)} %get-tuple-element.48), channel_id=1, source_target_pairs={{0,8},{8,16},{16,24},{1,9},{9,17},{17,25},{2,10},{10,18},{18,26},{... | collective-permute-start | bytes 393224 | tf_op jit(solution)/shard_map/ppermute | solution.py:513
  102.7 3.9 %collective-permute-start.15 = (bf16[16,32,128]{2,1,0:T(8,128)(2,1)S(1)}, bf16[16,32,128]{2,1,0:T(8,128)(2,1)S(1)}, u32[]{:S(2)}, u32[]{:S(2)}) collective-permute-start(bf16[16,32,128]{2,1,0:T(8,128)(2,1)S(1)} %get-tuple-element.49), channel_id=1, source_target_pairs={{8,0},{16,8},{24,16},{9,1},{17,9},{25,17},{10,2},{18,10},{26,18},{... | collective-permute-start | bytes 393224 | tf_op jit(solution)/shard_map/ppermute | solution.py:514

commit v8 on v7

--- a/solution.py
+++ b/solution.py
@@ -314,7 +314,7 @@
         left = (toeplitz(back[b : b + 1], height, 0) * mask).astype(BF)
         right = toeplitz(line[b : b + 1], lanes, 0).astype(BF)
         gr_ref[b] = dot(left, right).astype(BF)
-    basis = basis_ref[...]
+    basis = basis_ref[...].astype(BF)
     kinds = basis.shape[1]
     up = chosen((group * SUB, group), lambda row, lane: row // SUB == lane)
     out = chosen((kinds, SUB * kinds), lambda row, lane: row == lane % kinds)
@@ -584,7 +584,7 @@
     )(place, observed, plain, spectral_basis)
 
 
-    part = group_size(bands, 32)
+    part = group_size(bands, 64)
     deep = sum(end - start for start, end in packed_blocks(columns, halo))
     taps_spec = pl.BlockSpec((part, 2 * taps), lambda i: (i, 0))
     smem = pl.BlockSpec(memory_space=pltpu.SMEM)
@@ -608,7 +608,7 @@
             flops=bands * 2 * LANES**3, bytes_accessed=bands * height * LANES * 2, transcendentals=0
         ),
         name="gram_rows",
-    )(place, every, basis_all)
+    )(place, every, basis_all.astype(F32))
     gl = pl.pallas_call(
         functools.partial(gram_columns_kernel, columns, columns_all, radius),
         grid=(bands // part,),

time: 138 us -> 134 us (0.971)
  Pallas kernels: 66.7 us -> 61.3 us
  waiting for transfers between devices: 16.5 us -> 19.3 us
    pallas_call x2, Pallas kernels: 24.9 us -> 22.3 us  [normal_map(): pl.pallas_call(functools.partial(first_kernel if first else second_kernel...]
    pallas_call x1, Pallas kernels: 7.2 us -> 5.57 us  [local(): pl.pallas_call(functools.partial(gram_rows_kernel, height * n_row, radius...]
    ppermute x2, waiting for transfers between devices: 0.01 us -> 1.47 us  [local(): after = lax.ppermute(above, axes, moves(hop, -1))]
  transfers between devices with their start and end apart: 16 -> 16, of which waited for: 5 -> 6; matrix products, arithmetic and copies ran while one was open for 1% -> 1% of each run, Pallas kernels for 17% -> 16%
where the time goes in v8:
time: 134 us
  Pallas kernels  61.3 us (46%)
  starting transfers between devices  32.1 us (24%)
  waiting for transfers between devices  19.3 us (14%)
  blocking collectives  15.5 us (12%)
  local copies, waits for them, and re-layouts  4.15 us (3%)
    pallas_call x2, Pallas kernels, normal_map(): pl.pallas_call(functools.partial(first_kernel if first else second_kernel...  22.3 us
    all_to_all x1, blocking collectives, local(): shared = lax.all_to_all(mine, ('band', 'row'), 0, 0, tiled=True)  15.5 us
    pallas_call x1, Pallas kernels, local(): pl.pallas_call(functools.partial(gram_columns_kernel, columns, columns_al...  13.7 us
    pallas_call x1, Pallas kernels, local(): pl.pallas_call(functools.partial(adjoint_kernel, columns_all, radius), gr...  13.7 us
    ppermute x3, waiting for transfers between devices, shift_both(): lax.ppermute(high_edge, axis, [(i, i + 1) for i in range(count - 1)])  11.9 us
    ppermute x3, starting transfers between devices, shift_both(): lax.ppermute(high_edge, axis, [(i, i + 1) for i in range(count - 1)])  11.3 us
    ppermute x2, starting transfers between devices, local(): before = lax.ppermute(below, axes, moves(hop, 1))  7.86 us
    pallas_call x1, Pallas kernels, local(): pl.pallas_call(functools.partial(gram_rows_kernel, height * n_row, radius...  5.57 us
  transfers between devices with their start and end apart: 16, of which 6 were waited for; matrix products, arithmetic and copies ran while one was open for 1% of the time, Pallas kernels for 16%

profile of v8, /device:TPU:0, one launch (start us, length us, event | category | flops | bytes accessed | tf_op | source)
XLA Modules:
  0.0 133.7 jit_solution(1992018432693449002)
XLA Ops:
  0.6 0.8 copy.22
  1.4 0.8 copy.23
  2.2 0.8 copy.24.basis_ref
  3.1 0.1 pad_maximum_fusion.1.taps_ref
  3.2 0.1 stack.27.place_ref
  3.3 13.7 %adjoint.1 = (bf16[56,16,768]{2,1,0:T(8,128)(2,1)}, bf16[56,16,768]{2,1,0:T(8,128)(2,1)S(1)}) custom-call(s32[6]{0:T(128)S(1)} %stack.27.place_ref, bf16[56,32,680]{2,1,0:T(8,128)(2,1)} %obs_ref.1, f32[56,50]{1,0:T(8,128)S(1)} %pad_maximum_fusion.1.taps_ref, bf16[224,32]{1,0:T(8,128)(2,1)S(1)} %copy.24.basis_ref), custom_call_target="tpu_custom_call" | custom-call | flops 1409286144 | bytes 2437120 | tf_op jit(solution)/shard_map/adjoint/pallas_call | solution.py:561
  16.9 0.0 copy-start
  16.9 0.5 collective-permute-start
  17.4 2.6 %collective-permute-start.4 = (f32[56,50]{1,0:T(8,128)S(1)}, f32[56,50]{1,0:T(8,128)S(1)}, u32[]{:S(2)}, u32[]{:S(2)}) collective-permute-start(f32[56,50]{1,0:T(8,128)S(1)} %pad_maximum_fusion.1.taps_ref), channel_id=1, source_target_pairs={{0,24},{8,0},{16,8},{24,16},{1,25},{9,1},{17,9},{25,17},{2,26},{10... | collective-permute-start | bytes 33608 | tf_op jit(solution)/shard_map/ppermute | solution.py:538
  20.0 0.0 collective-permute-start.3
  20.0 0.1 collective-permute-start.2
  20.2 0.3 collective-permute-done.got_ref
  20.5 1.8 %split.1 = (bf16[12,16,384]{2,1,0:T(8,128)(2,1)S(1)}, f32[32,16,384]{2,1,0:T(8,128)S(1)}, bf16[12,16,384]{2,1,0:T(8,128)(2,1)S(1)}, bf16[12,16,384]{2,1,0:T(8,12...) custom-call(s32[6]{0:T(128)S(1)} %stack.27.place_ref, ...), custom_call_target="tpu_custom_call" | custom-call | tf_op jit(solution)/shard_map/split/pallas_call | solution.py:632
  22.3 3.0 %collective-permute-start.7 = (bf16[32,16,384]{2,1,0:T(8,128)(2,1)S(1)}, bf16[32,16,384]{2,1,0:T(8,128)(2,1)S(1)}, u32[]{:S(2)}, u32[]{:S(2)}) collective-permute-start(bf16[32,16,384]{2,1,0:T(8,128)(2,1)S(1)} %get-tuple-element.37), channel_id=1, source_target_pairs={{0,16},{1,17},{2,18},{3,19},{4,20},{5,21},{6,22},{7,23},{8,24},{9,... | collective-permute-start | bytes 1179656 | tf_op jit(solution)/shard_map/ppermute | solution.py:659
  25.4 0.0 copy-done
  25.4 0.1 constant_dynamic-slice_fusion.3
  25.5 0.1 maximum_convert_fusion
  25.6 0.1 copy.25.basis_ref
  25.7 3.4 %collective-permute-start.1 = (bf16[12,16,384]{2,1,0:T(8,128)(2,1)S(1)}, bf16[12,16,384]{2,1,0:T(8,128)(2,1)S(1)}, u32[]{:S(2)}, u32[]{:S(2)}) collective-permute-start(bf16[12,16,384]{2,1,0:T(8,128)(2,1)S(1)} %get-tuple-element.29), channel_id=1, source_target_pairs={{0,1},{1,2},{2,3},{3,4},{4,5},{5,6},{6,7},{8,9},{9,10},{10,11},{11... | collective-permute-start | bytes 442376 | tf_op jit(solution)/shard_map/ppermute | solution.py:657
  29.1 0.0 collective-permute-done.4
  29.1 1.3 collective-permute-start.5
  30.4 0.0 collective-permute-done.3
  30.4 4.5 %collective-permute-start.6 = (bf16[12,16,384]{2,1,0:T(8,128)(2,1)S(1)}, bf16[12,16,384]{2,1,0:T(8,128)(2,1)S(1)}, u32[]{:S(2)}, u32[]{:S(2)}) collective-permute-start(bf16[12,16,384]{2,1,0:T(8,128)(2,1)S(1)} %get-tuple-element.36), channel_id=1, source_target_pairs={{0,17},{1,18},{2,19},{3,20},{4,21},{5,22},{6,23},{8,25},{9,26},{10... | collective-permute-start | bytes 442376 | tf_op jit(solution)/shard_map/ppermute | solution.py:657
  34.9 0.0 collective-permute-done.2
  34.9 1.3 collective-permute-start.8
  36.2 0.1 pad_maximum_fusion.taps_ref
  36.2 5.6 %gram_rows.1 = (bf16[224,32,128]{2,1,0:T(8,128)(2,1)S(1)}, bf16[1792,256]{1,0:T(8,128)(2,1)S(1)}, bf16[4,256,448]{2,1,0:T(8,128)(2,1)S(1)}) custom-call(s32[6]{0:T(128)S(1)} %stack.27.place_ref, f32[224,50]{1,0:T(8,128)S(1)} %pad_maximum_fusion.taps_ref, f32[224,32]{1,0:T(8,128)S(1)} %copy.25.basis_ref), custom_call_target="tpu_custom_call" | custom-call | flops 939524096 | bytes 1835008 | tf_op jit(solution)/shard_map/gram_rows/pallas_call | solution.py:592
  41.8 0.0 collective-permute-done.1.refs_0_
  41.8 0.0 collective-permute-done.5.refs_2_
  41.8 0.0 collective-permute-done.6.refs_3_
  41.9 1.5 %collective-permute-done.8.refs_5_ = bf16[12,16,384]{2,1,0:T(8,128)(2,1)S(1)} collective-permute-done((bf16[12,16,384]{2,1,0:T(8,128)(2,1)S(1)}, bf16[12,16,384]{2,1,0:T(8,128)(2,1)S(1)}, u32[]{:S(2)}, u32[]{:S(2)}) %collective-permute-start.8) | collective-permute-done | bytes 147488 | tf_op jit(solution)/shard_map/ppermute | solution.py:656
  43.3 0.0 collective-permute-done.7.refs_4_
  43.3 0.1 merge.1.mine_ref
  43.5 0.1 collective-permute-start.9
  43.6 2.3 %collective-permute-done.9.other_ref = f32[32,16,384]{2,1,0:T(8,128)S(1)} collective-permute-done((f32[32,16,384]{2,1,0:T(8,128)S(1)}, f32[32,16,384]{2,1,0:T(8,128)S(1)}, u32[]{:S(2)}, u32[]{:S(2)}) %collective-permute-start.9) | collective-permute-done | bytes 786464 | tf_op jit(solution)/shard_map/ppermute | solution.py:668
  45.8 0.8 window.1
  46.6 0.1 fusion.1
  46.7 1.3 collective-permute-start.11
  48.0 5.6 %collective-permute-start.10 = (bf16[24,32,256]{2,1,0:T(8,128)(2,1)S(1)}, bf16[24,32,256]{2,1,0:T(8,128)(2,1)S(1)}, u32[]{:S(2)}, u32[]{:S(2)}) collective-permute-start(bf16[24,32,256]{2,1,0:T(8,128)(2,1)S(1)} %get-tuple-element.53), channel_id=1, source_target_pairs={{0,1},{1,2},{2,3},{3,4},{4,5},{5,6},{6,7},{8,9},{9,10},{10,11},{11... | collective-permute-start | bytes 1179656 | tf_op jit(solution)/shard_map/ppermute | solution.py:513
  53.6 13.7 %gram_columns.1.rest_5_ = bf16[224,272,128]{2,1,0:T(8,128)(2,1)S(1)} custom-call(s32[6]{0:T(128)S(1)} %stack.27.place_ref, f32[224,50]{1,0:T(8,128)S(1)} %pad_maximum_fusion.taps_ref), custom_call_target="tpu_custom_call" | custom-call | flops 7516192768 | bytes 15597568 | tf_op jit(solution)/shard_map/gram_columns/pallas_call | solution.py:612
  67.3 0.0 copy-start.1
  67.3 0.6 copy.32
  67.9 0.0 collective-permute-done.11.after
  67.9 1.8 %collective-permute-done.10.before = bf16[24,32,256]{2,1,0:T(8,128)(2,1)S(1)} collective-permute-done((bf16[24,32,256]{2,1,0:T(8,128)(2,1)S(1)}, bf16[24,32,256]{2,1,0:T(8,128)(2,1)S(1)}, u32[]{:S(2)}, u32[]{:S(2)}) %collective-permute-start.10) | collective-permute-done | bytes 393248 | tf_op jit(solution)/shard_map/ppermute | solution.py:513
  69.8 0.0 copy-done.1
  69.8 0.1 broadcast_in_dim.6.rest_1_
  69.9 10.7 %normal.2 = (f32[32,32,256]{2,1,0:T(8,128)S(1)}, f32[8,128]{1,0:T(8,128)S(1)}) custom-call(bf16[24,32,256]{2,1,0:T(8,128)(2,1)S(1)} %collective-permute-done.10.before, bf16[32,32,256]{2,1,0:T(8,128)(2,1)S(1)} %get-tuple-element.39.window, bf16[24,32,256]{2,1,0:T(8,128)(2,1)S(1)} %collective-permute-done.11.after, f32[32,32,256]{2,1,0:T(8,128)S(1)} %bitcast.12, ...), custom_call_target="tpu_custom_call" | custom-call | flops 1879048192 | bytes 15597568 | tf_op jit(solution)/shard_map/normal/pallas_call | solution.py:687
  80.6 0.6 copy.33
  81.1 0.2 pack.1
  81.4 4.4 %collective-permute-start.12 = (bf16[32,32,128]{2,1,0:T(8,128)(2,1)S(1)}, bf16[32,32,128]{2,1,0:T(8,128)(2,1)S(1)}, u32[]{:S(2)}, u32[]{:S(2)}) collective-permute-start(bf16[32,32,128]{2,1,0:T(8,128)(2,1)S(1)} %get-tuple-element.46), channel_id=1, source_target_pairs={{0,1},{1,2},{2,3},{3,4},{4,5},{5,6},{6,7},{8,9},{9,10},{10,11},{11... | collective-permute-start | bytes 786440 | tf_op jit(solution)/shard_map/ppermute | solution.py:513
  85.8 1.3 collective-permute-start.13
  87.1 10.1 %collective-permute-done.12.before_ref.before = bf16[32,32,128]{2,1,0:T(8,128)(2,1)S(1)} collective-permute-done((bf16[32,32,128]{2,1,0:T(8,128)(2,1)S(1)}, bf16[32,32,128]{2,1,0:T(8,128)(2,1)S(1)}, u32[]{:S(2)}, u32[]{:S(2)}) %collective-permute-start.12) | collective-permute-done | bytes 262176 | tf_op jit(solution)/shard_map/ppermute | solution.py:513
  97.1 0.0 collective-permute-done.13.after_ref.after
  97.1 1.3 sides.1
  98.5 1.3 collective-permute-start.14
  99.8 1.5 %collective-permute-start.15 = (bf16[16,32,128]{2,1,0:T(8,128)(2,1)S(1)}, bf16[16,32,128]{2,1,0:T(8,128)(2,1)S(1)}, u32[]{:S(2)}, u32[]{:S(2)}) collective-permute-start(bf16[16,32,128]{2,1,0:T(8,128)(2,1)S(1)} %get-tuple-element.49), channel_id=1, source_target_pairs={{8,0},{16,8},{24,16},{9,1},{17,9},{25,17},{10,2},{18,10},{26,18},{... | collective-permute-start | bytes 393224 | tf_op jit(solution)/shard_map/ppermute | solution.py:514
  101.3 0.1 pad.2.clone
  101.4 0.0 collective-permute-done.14.left
  101.4 3.3 %collective-permute-done.15.right = bf16[16,32,128]{2,1,0:T(8,128)(2,1)S(1)} collective-permute-done((bf16[16,32,128]{2,1,0:T(8,128)(2,1)S(1)}, bf16[16,32,128]{2,1,0:T(8,128)(2,1)S(1)}, u32[]{:S(2)}, u32[]{:S(2)}) %collective-permute-start.15) | collective-permute-done | bytes 131104 | tf_op jit(solution)/shard_map/ppermute | solution.py:514
  104.7 11.6 %normal.3 = (f32[32,32,256]{2,1,0:T(8,128)S(1)}, f32[8,128]{1,0:T(8,128)S(1)}) custom-call(bf16[32,32,256]{2,1,0:T(8,128)(2,1)S(1)} %bitcast.16, bf16[32,32,128]{2,1,0:T(8,128)(2,1)S(1)} %collective-permute-done.12.before_ref.before, bf16[32,32,128]{2,1,0:T(8,128)(2,1)S(1)} %collective-permute-done.13.after_ref.after, ...), custom_call_target="tpu_custom_call" | custom-call | flops 1879048192 | bytes 15597568 | tf_op jit(solution)/shard_map/normal/pallas_call | solution.py:687
  116.3 0.1 maximum_maximum_fusion
  116.4 15.5 %all_to_all.5.shared_ref = f32[32,8,128]{2,1,0:T(8,128)S(1)} all-to-all(f32[32,8,128]{2,1,0:T(8,128)S(1)} %broadcast_in_dim.8), channel_id=1, replica_groups=mesh['band'=4,'row'=8] {'band','row'}, dimensions={0} | all-to-all | bytes 262144 | tf_op jit(solution)/shard_map/all_to_all | solution.py:733
  131.9 1.8 %combine.1 = (f32[32,32,170]{2,1,0:T(8,128)}, f32[32,32,170]{2,1,0:T(8,128)}) custom-call(f32[32,8,128]{2,1,0:T(8,128)S(1)} %all_to_all.5.shared_ref, f32[32,32,256]{2,1,0:T(8,128)S(1)} %bitcast.13, f32[32,32,256]{2,1,0:T(8,128)S(1)} %get-tuple-element.45.rest_0_.v1_ref, f32[32,32,256]{2,1,0:T(8,128)S(1)} %get-tuple-element.51.v2_ref), custom_call_target="tpu_custom_call" | custom-call | tf_op jit(solution)/shard_map/combine/pallas_call | solution.py:735
  (4 shorter events, 0.0 us)
Async XLA Ops:
  16.9 8.4 %copy-start = (bf16[224,32]{0,1:T(8,128)(2,1)S(1)}, bf16[224,32]{0,1:T(8,128)(2,1)}, u32[]{:S(2)}) copy-start(bf16[224,32]{0,1:T(8,128)(2,1)} %param.8) | copy-start | bytes 43012
  16.9 3.5 %collective-permute-start = (bf16[56,16,768]{2,1,0:T(8,128)(2,1)}, bf16[56,16,768]{2,1,0:T(8,128)(2,1)}, u32[]{:S(2)}, u32[]{:S(2)}) collective-permute-start(bf16[56,16,768]{2,1,0:T(8,128)(2,1)} %get-tuple-element.28), channel_id=1, source_target_pairs={{0,8},{8,0},{16,24},{24,16},{1,9},{9,1},{17,25},{25,17},{2,10},{10... | collective-permute-start | bytes 4128776 | tf_op jit(solution)/shard_map/ppermute | solution.py:626
  17.4 11.7 %collective-permute-start.4 = (f32[56,50]{1,0:T(8,128)S(1)}, f32[56,50]{1,0:T(8,128)S(1)}, u32[]{:S(2)}, u32[]{:S(2)}) collective-permute-start(f32[56,50]{1,0:T(8,128)S(1)} %pad_maximum_fusion.1.taps_ref), channel_id=1, source_target_pairs={{0,24},{8,0},{16,8},{24,16},{1,25},{9,1},{17,9},{25,17},{2,26},{10... | collective-permute-start | bytes 33608 | tf_op jit(solution)/shard_map/ppermute | solution.py:538
  20.0 10.3 %collective-permute-start.3 = (f32[56,50]{1,0:T(8,128)S(1)}, f32[56,50]{1,0:T(8,128)S(1)}, u32[]{:S(2)}, u32[]{:S(2)}) collective-permute-start(f32[56,50]{1,0:T(8,128)S(1)} %pad_maximum_fusion.1.taps_ref), channel_id=1, source_target_pairs={{0,16},{8,24},{16,0},{24,8},{1,17},{9,25},{17,1},{25,9},{2,18},{10... | collective-permute-start | bytes 33608 | tf_op jit(solution)/shard_map/ppermute | solution.py:538
  20.0 14.8 %collective-permute-start.2 = (f32[56,50]{1,0:T(8,128)S(1)}, f32[56,50]{1,0:T(8,128)S(1)}, u32[]{:S(2)}, u32[]{:S(2)}) collective-permute-start(f32[56,50]{1,0:T(8,128)S(1)} %pad_maximum_fusion.1.taps_ref), channel_id=1, source_target_pairs={{0,8},{8,16},{16,24},{24,0},{1,9},{9,17},{17,25},{25,1},{2,10},{10... | collective-permute-start | bytes 33608 | tf_op jit(solution)/shard_map/ppermute | solution.py:538
  22.3 21.0 %collective-permute-start.7 = (bf16[32,16,384]{2,1,0:T(8,128)(2,1)S(1)}, bf16[32,16,384]{2,1,0:T(8,128)(2,1)S(1)}, u32[]{:S(2)}, u32[]{:S(2)}) collective-permute-start(bf16[32,16,384]{2,1,0:T(8,128)(2,1)S(1)} %get-tuple-element.37), channel_id=1, source_target_pairs={{0,16},{1,17},{2,18},{3,19},{4,20},{5,21},{6,22},{7,23},{8,24},{9,... | collective-permute-start | bytes 1179656 | tf_op jit(solution)/shard_map/ppermute | solution.py:659
  25.7 16.2 %collective-permute-start.1 = (bf16[12,16,384]{2,1,0:T(8,128)(2,1)S(1)}, bf16[12,16,384]{2,1,0:T(8,128)(2,1)S(1)}, u32[]{:S(2)}, u32[]{:S(2)}) collective-permute-start(bf16[12,16,384]{2,1,0:T(8,128)(2,1)S(1)} %get-tuple-element.29), channel_id=1, source_target_pairs={{0,1},{1,2},{2,3},{3,4},{4,5},{5,6},{6,7},{8,9},{9,10},{10,11},{11... | collective-permute-start | bytes 442376 | tf_op jit(solution)/shard_map/ppermute | solution.py:657
  29.1 12.8 %collective-permute-start.5 = (bf16[12,16,384]{2,1,0:T(8,128)(2,1)S(1)}, bf16[12,16,384]{2,1,0:T(8,128)(2,1)S(1)}, u32[]{:S(2)}, u32[]{:S(2)}) collective-permute-start(bf16[12,16,384]{2,1,0:T(8,128)(2,1)S(1)} %get-tuple-element.35), channel_id=1, source_target_pairs={{1,0},{2,1},{3,2},{4,3},{5,4},{6,5},{7,6},{9,8},{10,9},{11,10},{12... | collective-permute-start | bytes 442376 | tf_op jit(solution)/shard_map/ppermute | solution.py:656
  30.4 11.5 %collective-permute-start.6 = (bf16[12,16,384]{2,1,0:T(8,128)(2,1)S(1)}, bf16[12,16,384]{2,1,0:T(8,128)(2,1)S(1)}, u32[]{:S(2)}, u32[]{:S(2)}) collective-permute-start(bf16[12,16,384]{2,1,0:T(8,128)(2,1)S(1)} %get-tuple-element.36), channel_id=1, source_target_pairs={{0,17},{1,18},{2,19},{3,20},{4,21},{5,22},{6,23},{8,25},{9,26},{10... | collective-permute-start | bytes 442376 | tf_op jit(solution)/shard_map/ppermute | solution.py:657
  34.9 8.5 %collective-permute-start.8 = (bf16[12,16,384]{2,1,0:T(8,128)(2,1)S(1)}, bf16[12,16,384]{2,1,0:T(8,128)(2,1)S(1)}, u32[]{:S(2)}, u32[]{:S(2)}) collective-permute-start(bf16[12,16,384]{2,1,0:T(8,128)(2,1)S(1)} %get-tuple-element.38), channel_id=1, source_target_pairs={{1,16},{2,17},{3,18},{4,19},{5,20},{6,21},{7,22},{9,24},{10,25},{1... | collective-permute-start | bytes 442376 | tf_op jit(solution)/shard_map/ppermute | solution.py:656
  43.5 2.4 %collective-permute-start.9 = (f32[32,16,384]{2,1,0:T(8,128)S(1)}, f32[32,16,384]{2,1,0:T(8,128)S(1)}, u32[]{:S(2)}, u32[]{:S(2)}) collective-permute-start(f32[32,16,384]{2,1,0:T(8,128)S(1)} %merge.1.mine_ref), channel_id=1, source_target_pairs={{0,8},{8,0},{16,24},{24,16},{1,9},{9,1},{17,25},{25,17},{2,10},{10... | collective-permute-start | bytes 2359304 | tf_op jit(solution)/shard_map/ppermute | solution.py:668
  46.7 21.2 %collective-permute-start.11 = (bf16[24,32,256]{2,1,0:T(8,128)(2,1)S(1)}, bf16[24,32,256]{2,1,0:T(8,128)(2,1)S(1)}, u32[]{:S(2)}, u32[]{:S(2)}) collective-permute-start(bf16[24,32,256]{2,1,0:T(8,128)(2,1)S(1)} %get-tuple-element.52), channel_id=1, source_target_pairs={{1,0},{2,1},{3,2},{4,3},{5,4},{6,5},{7,6},{9,8},{10,9},{11,10},{12... | collective-permute-start | bytes 1179656 | tf_op jit(solution)/shard_map/ppermute | solution.py:514
  48.0 21.7 %collective-permute-start.10 = (bf16[24,32,256]{2,1,0:T(8,128)(2,1)S(1)}, bf16[24,32,256]{2,1,0:T(8,128)(2,1)S(1)}, u32[]{:S(2)}, u32[]{:S(2)}) collective-permute-start(bf16[24,32,256]{2,1,0:T(8,128)(2,1)S(1)} %get-tuple-element.53), channel_id=1, source_target_pairs={{0,1},{1,2},{2,3},{3,4},{4,5},{5,6},{6,7},{8,9},{9,10},{10,11},{11... | collective-permute-start | bytes 1179656 | tf_op jit(solution)/shard_map/ppermute | solution.py:513
  67.3 2.5 %copy-start.1 = (f32[32]{0:T(128)S(1)}, f32[32]{0:T(128)}, u32[]{:S(2)}) copy-start(f32[32]{0:T(128)} %param.9) | copy-start | bytes 388
  81.4 15.8 %collective-permute-start.12 = (bf16[32,32,128]{2,1,0:T(8,128)(2,1)S(1)}, bf16[32,32,128]{2,1,0:T(8,128)(2,1)S(1)}, u32[]{:S(2)}, u32[]{:S(2)}) collective-permute-start(bf16[32,32,128]{2,1,0:T(8,128)(2,1)S(1)} %get-tuple-element.46), channel_id=1, source_target_pairs={{0,1},{1,2},{2,3},{3,4},{4,5},{5,6},{6,7},{8,9},{9,10},{10,11},{11... | collective-permute-start | bytes 786440 | tf_op jit(solution)/shard_map/ppermute | solution.py:513
  85.8 11.4 %collective-permute-start.13 = (bf16[32,32,128]{2,1,0:T(8,128)(2,1)S(1)}, bf16[32,32,128]{2,1,0:T(8,128)(2,1)S(1)}, u32[]{:S(2)}, u32[]{:S(2)}) collective-permute-start(bf16[32,32,128]{2,1,0:T(8,128)(2,1)S(1)} %get-tuple-element.47), channel_id=1, source_target_pairs={{1,0},{2,1},{3,2},{4,3},{5,4},{6,5},{7,6},{9,8},{10,9},{11,10},{12... | collective-permute-start | bytes 786440 | tf_op jit(solution)/shard_map/ppermute | solution.py:514
  98.5 2.9 %collective-permute-start.14 = (bf16[16,32,128]{2,1,0:T(8,128)(2,1)S(1)}, bf16[16,32,128]{2,1,0:T(8,128)(2,1)S(1)}, u32[]{:S(2)}, u32[]{:S(2)}) collective-permute-start(bf16[16,32,128]{2,1,0:T(8,128)(2,1)S(1)} %get-tuple-element.48), channel_id=1, source_target_pairs={{0,8},{8,16},{16,24},{1,9},{9,17},{17,25},{2,10},{10,18},{18,26},{... | collective-permute-start | bytes 393224 | tf_op jit(solution)/shard_map/ppermute | solution.py:513
  99.8 4.9 %collective-permute-start.15 = (bf16[16,32,128]{2,1,0:T(8,128)(2,1)S(1)}, bf16[16,32,128]{2,1,0:T(8,128)(2,1)S(1)}, u32[]{:S(2)}, u32[]{:S(2)}) collective-permute-start(bf16[16,32,128]{2,1,0:T(8,128)(2,1)S(1)} %get-tuple-element.49), channel_id=1, source_target_pairs={{8,0},{16,8},{24,16},{9,1},{17,9},{25,17},{10,2},{18,10},{26,18},{... | collective-permute-start | bytes 393224 | tf_op jit(solution)/shard_map/ppermute | solution.py:514

commit v9 on v8

--- a/solution.py
+++ b/solution.py
@@ -50,8 +50,8 @@
     return jnp.where(rule(row, lane), 1.0, 0.0).astype(kind)
 
 
-def placed_taps(both, places, kind):
-    count = both.shape[1] // 2
+def placed_taps(both, places, kind, axis=1):
+    count = both.shape[axis] // 2
     picks = []
     for first, lead, flip in places:
 
@@ -60,11 +60,11 @@
             here = (at >= 0) & (at < count)
             return here & (row == first + (count - 1 - at if flip else at))
 
-        picks.append(chosen((both.shape[1], 2 * LANES), rule, kind))
+        picks.append(chosen((both.shape[axis], 2 * LANES), rule, kind))
     done = lax.dot_general(
         both.astype(kind),
         jnp.concatenate(picks, axis=1),
-        (((1,), (0,)), ((), ())),
+        (((axis,), (0,)), ((), ())),
         precision=lax.Precision.HIGHEST if kind == F32 else None,
         preferred_element_type=F32,
     )
@@ -202,8 +202,9 @@
             mats[b, : LANES - edge] = blank_rows
             mats[b, LANES + width + edge :] = blank_rows
         both = taps_ref[...]
-        taps = both.shape[1] // 2
-        for i, line in enumerate(placed_taps(both, [(taps, -radius % SUB, False), (0, 0, True)], F32)):
+        taps = both.shape[0] // 2
+        places = [(taps, -radius % SUB, False), (0, 0, True)]
+        for i, line in enumerate(placed_taps(both, places, F32, 0)):
             lines[i] = line[:, None]
 
     @pl.loop(0, group, step=batch)
@@ -249,11 +250,11 @@
             for c in range(chunks):
                 ys[c, start + b] = done[c * SUB : (c + 1) * SUB]
 
-    bands, kinds = basis_ref.shape
+    kinds, bands = basis_ref.shape
     first = place_ref[0] + step * group
     turn = place_ref[1]
     pick = chosen((SUB * kinds, kinds), lambda row, lane: lane == (row + turn) % kinds)
-    wide = dot_rows(pick, basis_ref[...]).astype(BF)
+    wide = dot(pick, basis_ref[...]).astype(BF)
     here = chosen((bands, group * SUB), lambda row, lane: row == first + lane // SUB)
     same = chosen((SUB * kinds, group * SUB), lambda row, lane: row // kinds == lane % SUB, F32)
     mix = (dot(wide, here) * same).astype(BF)
@@ -531,7 +532,7 @@
     chip = me_band // 2
     chips = n_band // 2
 
-    plain = jnp.concatenate([row_taps, col_taps], axis=1)
+    plain = jnp.concatenate([row_taps.T, col_taps.T], axis=0)
     everyone = [(plain, me_band)]
     for hop in range(1, n_band):
         moves = [(i, (i + hop) % n_band) for i in range(n_band)]
@@ -539,7 +540,7 @@
     basis_all = jnp.concatenate(
         [lax.dynamic_slice_in_dim(spectral_basis, at * bands_here, bands_here, 0) for _, at in everyone]
     )
-    every = jnp.concatenate([values for values, _ in everyone])
+    every = jnp.concatenate([values for values, _ in everyone], axis=1).T
 
     half = kinds // 2
     place = jnp.stack(
@@ -565,7 +566,7 @@
             pl.BlockSpec(memory_space=pltpu.SMEM),
             pl.BlockSpec((few, height, columns_all), lambda i: (i, 0, 0)),
             whole(plain.shape),
-            whole((bands, kinds)),
+            whole((kinds, bands)),
         ],
         out_specs=[whole((ext, half, span))] * 2,
         out_shape=[jax.ShapeDtypeStruct((ext, half, span), BF)] * 2,
@@ -581,7 +582,7 @@
             flops=bands_here * 2 * 96 * 512 * 256, bytes_accessed=observed.size * 2, transcendentals=0
         ),
         name="adjoint",
-    )(place, observed, plain, spectral_basis)
+    )(place, observed, plain, spectral_basis.T)
 
 
     part = group_size(bands, 64)

time: 134 us -> 134 us (level)
  no operation moved by 1% of the time
where the time goes in v9:
time: 134 us
  Pallas kernels  61.3 us (46%)
  starting transfers between devices  32.1 us (24%)
  waiting for transfers between devices  19.3 us (14%)
  blocking collectives  15.5 us (12%)
  local copies, waits for them, and re-layouts  4.14 us (3%)
    pallas_call x2, Pallas kernels, normal_map(): pl.pallas_call(functools.partial(first_kernel if first else second_kernel...  22.3 us
    all_to_all x1, blocking collectives, local(): shared = lax.all_to_all(mine, ('band', 'row'), 0, 0, tiled=True)  15.5 us
    pallas_call x1, Pallas kernels, local(): pl.pallas_call(functools.partial(adjoint_kernel, columns_all, radius), gr...  13.7 us
    pallas_call x1, Pallas kernels, local(): pl.pallas_call(functools.partial(gram_columns_kernel, columns, columns_al...  13.7 us
    ppermute x3, waiting for transfers between devices, shift_both(): lax.ppermute(high_edge, axis, [(i, i + 1) for i in range(count - 1)])  11.9 us
    ppermute x3, starting transfers between devices, shift_both(): lax.ppermute(high_edge, axis, [(i, i + 1) for i in range(count - 1)])  11.2 us
    ppermute x2, starting transfers between devices, local(): before = lax.ppermute(below, axes, moves(hop, 1))  7.86 us
    pallas_call x1, Pallas kernels, local(): pl.pallas_call(functools.partial(gram_rows_kernel, height * n_row, radius...  5.57 us
  transfers between devices with their start and end apart: 16, of which 6 were waited for; matrix products, arithmetic and copies ran while one was open for 1% of the time, Pallas kernels for 16%

profile of v9, /device:TPU:0, one launch (start us, length us, event | category | flops | bytes accessed | tf_op | source)
XLA Modules:
  0.0 133.7 jit_solution(3204381889699127661)
XLA Ops:
  0.6 0.8 copy.22
  1.4 0.8 copy.23
  2.2 0.1 pad_maximum_fusion
  2.3 0.1 copy.24.taps_ref
  2.4 0.1 stack.27.place_ref
  2.5 0.0 copy-start
  2.5 0.7 copy-done
  3.2 13.7 %adjoint.1 = (bf16[56,16,768]{2,1,0:T(8,128)(2,1)}, bf16[56,16,768]{2,1,0:T(8,128)(2,1)S(1)}) custom-call(s32[6]{0:T(128)S(1)} %stack.27.place_ref, bf16[56,32,680]{2,1,0:T(8,128)(2,1)} %obs_ref.1, f32[50,56]{1,0:T(8,128)S(1)} %copy.24.taps_ref, bf16[32,224]{1,0:T(8,128)(2,1)S(1)} %bitcast.22), custom_call_target="tpu_custom_call" | custom-call | flops 1409286144 | bytes 2437120 | tf_op jit(solution)/shard_map/adjoint/pallas_call | solution.py:562
  16.9 0.5 collective-permute-start
  17.4 2.6 %collective-permute-start.4 = (f32[50,56]{0,1:T(8,128)S(1)}, f32[50,56]{0,1:T(8,128)S(1)}, u32[]{:S(2)}, u32[]{:S(2)}) collective-permute-start(f32[50,56]{0,1:T(8,128)S(1)} %pad_maximum_fusion), channel_id=1, source_target_pairs={{0,24},{8,0},{16,8},{24,16},{1,25},{9,1},{17,9},{25,17},{2,26},{10... | collective-permute-start | bytes 33608 | tf_op jit(solution)/shard_map/ppermute | solution.py:539
  20.0 0.0 collective-permute-start.3
  20.0 0.1 collective-permute-start.2
  20.2 0.3 collective-permute-done.got_ref
  20.5 1.8 %split.1 = (bf16[12,16,384]{2,1,0:T(8,128)(2,1)S(1)}, f32[32,16,384]{2,1,0:T(8,128)S(1)}, bf16[12,16,384]{2,1,0:T(8,128)(2,1)S(1)}, bf16[12,16,384]{2,1,0:T(8,12...) custom-call(s32[6]{0:T(128)S(1)} %stack.27.place_ref, ...), custom_call_target="tpu_custom_call" | custom-call | tf_op jit(solution)/shard_map/split/pallas_call | solution.py:633
  22.3 3.0 %collective-permute-start.7 = (bf16[32,16,384]{2,1,0:T(8,128)(2,1)S(1)}, bf16[32,16,384]{2,1,0:T(8,128)(2,1)S(1)}, u32[]{:S(2)}, u32[]{:S(2)}) collective-permute-start(bf16[32,16,384]{2,1,0:T(8,128)(2,1)S(1)} %get-tuple-element.37), channel_id=1, source_target_pairs={{0,16},{1,17},{2,18},{3,19},{4,20},{5,21},{6,22},{7,23},{8,24},{9,... | collective-permute-start | bytes 1179656 | tf_op jit(solution)/shard_map/ppermute | solution.py:660
  25.4 0.0 copy-done.1
  25.4 0.1 constant_dynamic-slice_fusion.3
  25.5 0.1 maximum_convert_fusion
  25.5 0.1 copy.25.basis_ref
  25.6 3.4 %collective-permute-start.1 = (bf16[12,16,384]{2,1,0:T(8,128)(2,1)S(1)}, bf16[12,16,384]{2,1,0:T(8,128)(2,1)S(1)}, u32[]{:S(2)}, u32[]{:S(2)}) collective-permute-start(bf16[12,16,384]{2,1,0:T(8,128)(2,1)S(1)} %get-tuple-element.29), channel_id=1, source_target_pairs={{0,1},{1,2},{2,3},{3,4},{4,5},{5,6},{6,7},{8,9},{9,10},{10,11},{11... | collective-permute-start | bytes 442376 | tf_op jit(solution)/shard_map/ppermute | solution.py:658
  29.1 0.0 collective-permute-done.4
  29.1 1.3 collective-permute-start.5
  30.4 0.0 collective-permute-done.3
  30.4 4.5 %collective-permute-start.6 = (bf16[12,16,384]{2,1,0:T(8,128)(2,1)S(1)}, bf16[12,16,384]{2,1,0:T(8,128)(2,1)S(1)}, u32[]{:S(2)}, u32[]{:S(2)}) collective-permute-start(bf16[12,16,384]{2,1,0:T(8,128)(2,1)S(1)} %get-tuple-element.36), channel_id=1, source_target_pairs={{0,17},{1,18},{2,19},{3,20},{4,21},{5,22},{6,23},{8,25},{9,26},{10... | collective-permute-start | bytes 442376 | tf_op jit(solution)/shard_map/ppermute | solution.py:658
  34.8 0.0 collective-permute-done.2
  34.8 1.3 collective-permute-start.8
  36.1 0.1 maximum_bitcast_fusion.taps_ref
  36.2 5.6 %gram_rows.1 = (bf16[224,32,128]{2,1,0:T(8,128)(2,1)S(1)}, bf16[1792,256]{1,0:T(8,128)(2,1)S(1)}, bf16[4,256,448]{2,1,0:T(8,128)(2,1)S(1)}) custom-call(s32[6]{0:T(128)S(1)} %stack.27.place_ref, f32[224,50]{1,0:T(8,128)S(1)} %maximum_bitcast_fusion.taps_ref, f32[224,32]{1,0:T(8,128)S(1)} %copy.25.basis_ref), custom_call_target="tpu_custom_call" | custom-call | flops 939524096 | bytes 1835008 | tf_op jit(solution)/shard_map/gram_rows/pallas_call | solution.py:593
  41.8 0.0 collective-permute-done.1.refs_0_
  41.8 0.0 collective-permute-done.5.refs_2_
  41.8 0.0 collective-permute-done.6.refs_3_
  41.8 1.5 %collective-permute-done.8.refs_5_ = bf16[12,16,384]{2,1,0:T(8,128)(2,1)S(1)} collective-permute-done((bf16[12,16,384]{2,1,0:T(8,128)(2,1)S(1)}, bf16[12,16,384]{2,1,0:T(8,128)(2,1)S(1)}, u32[]{:S(2)}, u32[]{:S(2)}) %collective-permute-start.8) | collective-permute-done | bytes 147488 | tf_op jit(solution)/shard_map/ppermute | solution.py:657
  43.3 0.0 collective-permute-done.7.refs_4_
  43.3 0.1 merge.1.mine_ref
  43.5 0.1 collective-permute-start.9
  43.5 2.3 %collective-permute-done.9.other_ref = f32[32,16,384]{2,1,0:T(8,128)S(1)} collective-permute-done((f32[32,16,384]{2,1,0:T(8,128)S(1)}, f32[32,16,384]{2,1,0:T(8,128)S(1)}, u32[]{:S(2)}, u32[]{:S(2)}) %collective-permute-start.9) | collective-permute-done | bytes 786464 | tf_op jit(solution)/shard_map/ppermute | solution.py:669
  45.8 0.8 window.1
  46.6 0.1 fusion.1
  46.7 1.3 collective-permute-start.11
  48.0 5.6 %collective-permute-start.10 = (bf16[24,32,256]{2,1,0:T(8,128)(2,1)S(1)}, bf16[24,32,256]{2,1,0:T(8,128)(2,1)S(1)}, u32[]{:S(2)}, u32[]{:S(2)}) collective-permute-start(bf16[24,32,256]{2,1,0:T(8,128)(2,1)S(1)} %get-tuple-element.53), channel_id=1, source_target_pairs={{0,1},{1,2},{2,3},{3,4},{4,5},{5,6},{6,7},{8,9},{9,10},{10,11},{11... | collective-permute-start | bytes 1179656 | tf_op jit(solution)/shard_map/ppermute | solution.py:514
  53.6 13.7 %gram_columns.1.rest_5_ = bf16[224,272,128]{2,1,0:T(8,128)(2,1)S(1)} custom-call(s32[6]{0:T(128)S(1)} %stack.27.place_ref, f32[224,50]{1,0:T(8,128)S(1)} %maximum_bitcast_fusion.taps_ref), custom_call_target="tpu_custom_call" | custom-call | flops 7516192768 | bytes 15597568 | tf_op jit(solution)/shard_map/gram_columns/pallas_call | solution.py:613
  67.3 0.0 copy-start.2
  67.3 0.6 copy.32
  67.9 0.0 collective-permute-done.11.after
  67.9 1.8 %collective-permute-done.10.before = bf16[24,32,256]{2,1,0:T(8,128)(2,1)S(1)} collective-permute-done((bf16[24,32,256]{2,1,0:T(8,128)(2,1)S(1)}, bf16[24,32,256]{2,1,0:T(8,128)(2,1)S(1)}, u32[]{:S(2)}, u32[]{:S(2)}) %collective-permute-start.10) | collective-permute-done | bytes 393248 | tf_op jit(solution)/shard_map/ppermute | solution.py:514
  69.7 0.0 copy-done.2
  69.7 0.1 broadcast_in_dim.6.rest_1_
  69.9 10.7 %normal.2 = (f32[32,32,256]{2,1,0:T(8,128)S(1)}, f32[8,128]{1,0:T(8,128)S(1)}) custom-call(bf16[24,32,256]{2,1,0:T(8,128)(2,1)S(1)} %collective-permute-done.10.before, bf16[32,32,256]{2,1,0:T(8,128)(2,1)S(1)} %get-tuple-element.39.window, bf16[24,32,256]{2,1,0:T(8,128)(2,1)S(1)} %collective-permute-done.11.after, f32[32,32,256]{2,1,0:T(8,128)S(1)} %bitcast.17, ...), custom_call_target="tpu_custom_call" | custom-call | flops 1879048192 | bytes 15597568 | tf_op jit(solution)/shard_map/normal/pallas_call | solution.py:688
  80.6 0.6 copy.33
  81.1 0.2 pack.1
  81.4 4.4 %collective-permute-start.12 = (bf16[32,32,128]{2,1,0:T(8,128)(2,1)S(1)}, bf16[32,32,128]{2,1,0:T(8,128)(2,1)S(1)}, u32[]{:S(2)}, u32[]{:S(2)}) collective-permute-start(bf16[32,32,128]{2,1,0:T(8,128)(2,1)S(1)} %get-tuple-element.46), channel_id=1, source_target_pairs={{0,1},{1,2},{2,3},{3,4},{4,5},{5,6},{6,7},{8,9},{9,10},{10,11},{11... | collective-permute-start | bytes 786440 | tf_op jit(solution)/shard_map/ppermute | solution.py:514
  85.7 1.3 collective-permute-start.13
  87.0 10.1 %collective-permute-done.12.before_ref.before = bf16[32,32,128]{2,1,0:T(8,128)(2,1)S(1)} collective-permute-done((bf16[32,32,128]{2,1,0:T(8,128)(2,1)S(1)}, bf16[32,32,128]{2,1,0:T(8,128)(2,1)S(1)}, u32[]{:S(2)}, u32[]{:S(2)}) %collective-permute-start.12) | collective-permute-done | bytes 262176 | tf_op jit(solution)/shard_map/ppermute | solution.py:514
  97.1 0.0 collective-permute-done.13.after_ref.after
  97.1 1.3 sides.1
  98.5 1.3 collective-permute-start.14
  99.8 1.5 %collective-permute-start.15 = (bf16[16,32,128]{2,1,0:T(8,128)(2,1)S(1)}, bf16[16,32,128]{2,1,0:T(8,128)(2,1)S(1)}, u32[]{:S(2)}, u32[]{:S(2)}) collective-permute-start(bf16[16,32,128]{2,1,0:T(8,128)(2,1)S(1)} %get-tuple-element.49), channel_id=1, source_target_pairs={{8,0},{16,8},{24,16},{9,1},{17,9},{25,17},{10,2},{18,10},{26,18},{... | collective-permute-start | bytes 393224 | tf_op jit(solution)/shard_map/ppermute | solution.py:515
  101.3 0.1 pad.2.clone
  101.4 0.0 collective-permute-done.14.left
  101.4 3.3 %collective-permute-done.15.right = bf16[16,32,128]{2,1,0:T(8,128)(2,1)S(1)} collective-permute-done((bf16[16,32,128]{2,1,0:T(8,128)(2,1)S(1)}, bf16[16,32,128]{2,1,0:T(8,128)(2,1)S(1)}, u32[]{:S(2)}, u32[]{:S(2)}) %collective-permute-start.15) | collective-permute-done | bytes 131104 | tf_op jit(solution)/shard_map/ppermute | solution.py:515
  104.7 11.6 %normal.3 = (f32[32,32,256]{2,1,0:T(8,128)S(1)}, f32[8,128]{1,0:T(8,128)S(1)}) custom-call(bf16[32,32,256]{2,1,0:T(8,128)(2,1)S(1)} %bitcast.21, bf16[32,32,128]{2,1,0:T(8,128)(2,1)S(1)} %collective-permute-done.12.before_ref.before, bf16[32,32,128]{2,1,0:T(8,128)(2,1)S(1)} %collective-permute-done.13.after_ref.after, ...), custom_call_target="tpu_custom_call" | custom-call | flops 1879048192 | bytes 15597568 | tf_op jit(solution)/shard_map/normal/pallas_call | solution.py:688
  116.3 0.1 maximum_maximum_fusion
  116.4 15.5 %all_to_all.5.shared_ref = f32[32,8,128]{2,1,0:T(8,128)S(1)} all-to-all(f32[32,8,128]{2,1,0:T(8,128)S(1)} %broadcast_in_dim.8), channel_id=1, replica_groups=mesh['band'=4,'row'=8] {'band','row'}, dimensions={0} | all-to-all | bytes 262144 | tf_op jit(solution)/shard_map/all_to_all | solution.py:734
  131.9 1.8 %combine.1 = (f32[32,32,170]{2,1,0:T(8,128)}, f32[32,32,170]{2,1,0:T(8,128)}) custom-call(f32[32,8,128]{2,1,0:T(8,128)S(1)} %all_to_all.5.shared_ref, f32[32,32,256]{2,1,0:T(8,128)S(1)} %bitcast.18, f32[32,32,256]{2,1,0:T(8,128)S(1)} %get-tuple-element.45.rest_0_.v1_ref, f32[32,32,256]{2,1,0:T(8,128)S(1)} %get-tuple-element.51.v2_ref), custom_call_target="tpu_custom_call" | custom-call | tf_op jit(solution)/shard_map/combine/pallas_call | solution.py:736
  (5 shorter events, 0.0 us)
Async XLA Ops:
  2.5 0.7 copy-start
  16.9 8.4 %copy-start.1 = (bf16[224,32]{0,1:T(8,128)(2,1)S(1)}, bf16[224,32]{0,1:T(8,128)(2,1)}, u32[]{:S(2)}) copy-start(bf16[224,32]{0,1:T(8,128)(2,1)} %param.8) | copy-start | bytes 43012
  16.9 3.5 %collective-permute-start = (bf16[56,16,768]{2,1,0:T(8,128)(2,1)}, bf16[56,16,768]{2,1,0:T(8,128)(2,1)}, u32[]{:S(2)}, u32[]{:S(2)}) collective-permute-start(bf16[56,16,768]{2,1,0:T(8,128)(2,1)} %get-tuple-element.28), channel_id=1, source_target_pairs={{0,8},{8,0},{16,24},{24,16},{1,9},{9,1},{17,25},{25,17},{2,10},{10... | collective-permute-start | bytes 4128776 | tf_op jit(solution)/shard_map/ppermute | solution.py:627
  17.4 11.7 %collective-permute-start.4 = (f32[50,56]{0,1:T(8,128)S(1)}, f32[50,56]{0,1:T(8,128)S(1)}, u32[]{:S(2)}, u32[]{:S(2)}) collective-permute-start(f32[50,56]{0,1:T(8,128)S(1)} %pad_maximum_fusion), channel_id=1, source_target_pairs={{0,24},{8,0},{16,8},{24,16},{1,25},{9,1},{17,9},{25,17},{2,26},{10... | collective-permute-start | bytes 33608 | tf_op jit(solution)/shard_map/ppermute | solution.py:539
  20.0 10.3 %collective-permute-start.3 = (f32[50,56]{0,1:T(8,128)S(1)}, f32[50,56]{0,1:T(8,128)S(1)}, u32[]{:S(2)}, u32[]{:S(2)}) collective-permute-start(f32[50,56]{0,1:T(8,128)S(1)} %pad_maximum_fusion), channel_id=1, source_target_pairs={{0,16},{8,24},{16,0},{24,8},{1,17},{9,25},{17,1},{25,9},{2,18},{10... | collective-permute-start | bytes 33608 | tf_op jit(solution)/shard_map/ppermute | solution.py:539
  20.0 14.8 %collective-permute-start.2 = (f32[50,56]{0,1:T(8,128)S(1)}, f32[50,56]{0,1:T(8,128)S(1)}, u32[]{:S(2)}, u32[]{:S(2)}) collective-permute-start(f32[50,56]{0,1:T(8,128)S(1)} %pad_maximum_fusion), channel_id=1, source_target_pairs={{0,8},{8,16},{16,24},{24,0},{1,9},{9,17},{17,25},{25,1},{2,10},{10... | collective-permute-start | bytes 33608 | tf_op jit(solution)/shard_map/ppermute | solution.py:539
  22.3 21.0 %collective-permute-start.7 = (bf16[32,16,384]{2,1,0:T(8,128)(2,1)S(1)}, bf16[32,16,384]{2,1,0:T(8,128)(2,1)S(1)}, u32[]{:S(2)}, u32[]{:S(2)}) collective-permute-start(bf16[32,16,384]{2,1,0:T(8,128)(2,1)S(1)} %get-tuple-element.37), channel_id=1, source_target_pairs={{0,16},{1,17},{2,18},{3,19},{4,20},{5,21},{6,22},{7,23},{8,24},{9,... | collective-permute-start | bytes 1179656 | tf_op jit(solution)/shard_map/ppermute | solution.py:660
  25.6 16.2 %collective-permute-start.1 = (bf16[12,16,384]{2,1,0:T(8,128)(2,1)S(1)}, bf16[12,16,384]{2,1,0:T(8,128)(2,1)S(1)}, u32[]{:S(2)}, u32[]{:S(2)}) collective-permute-start(bf16[12,16,384]{2,1,0:T(8,128)(2,1)S(1)} %get-tuple-element.29), channel_id=1, source_target_pairs={{0,1},{1,2},{2,3},{3,4},{4,5},{5,6},{6,7},{8,9},{9,10},{10,11},{11... | collective-permute-start | bytes 442376 | tf_op jit(solution)/shard_map/ppermute | solution.py:658
  29.1 12.8 %collective-permute-start.5 = (bf16[12,16,384]{2,1,0:T(8,128)(2,1)S(1)}, bf16[12,16,384]{2,1,0:T(8,128)(2,1)S(1)}, u32[]{:S(2)}, u32[]{:S(2)}) collective-permute-start(bf16[12,16,384]{2,1,0:T(8,128)(2,1)S(1)} %get-tuple-element.35), channel_id=1, source_target_pairs={{1,0},{2,1},{3,2},{4,3},{5,4},{6,5},{7,6},{9,8},{10,9},{11,10},{12... | collective-permute-start | bytes 442376 | tf_op jit(solution)/shard_map/ppermute | solution.py:657
  30.4 11.5 %collective-permute-start.6 = (bf16[12,16,384]{2,1,0:T(8,128)(2,1)S(1)}, bf16[12,16,384]{2,1,0:T(8,128)(2,1)S(1)}, u32[]{:S(2)}, u32[]{:S(2)}) collective-permute-start(bf16[12,16,384]{2,1,0:T(8,128)(2,1)S(1)} %get-tuple-element.36), channel_id=1, source_target_pairs={{0,17},{1,18},{2,19},{3,20},{4,21},{5,22},{6,23},{8,25},{9,26},{10... | collective-permute-start | bytes 442376 | tf_op jit(solution)/shard_map/ppermute | solution.py:658
  34.8 8.5 %collective-permute-start.8 = (bf16[12,16,384]{2,1,0:T(8,128)(2,1)S(1)}, bf16[12,16,384]{2,1,0:T(8,128)(2,1)S(1)}, u32[]{:S(2)}, u32[]{:S(2)}) collective-permute-start(bf16[12,16,384]{2,1,0:T(8,128)(2,1)S(1)} %get-tuple-element.38), channel_id=1, source_target_pairs={{1,16},{2,17},{3,18},{4,19},{5,20},{6,21},{7,22},{9,24},{10,25},{1... | collective-permute-start | bytes 442376 | tf_op jit(solution)/shard_map/ppermute | solution.py:657
  43.5 2.4 %collective-permute-start.9 = (f32[32,16,384]{2,1,0:T(8,128)S(1)}, f32[32,16,384]{2,1,0:T(8,128)S(1)}, u32[]{:S(2)}, u32[]{:S(2)}) collective-permute-start(f32[32,16,384]{2,1,0:T(8,128)S(1)} %merge.1.mine_ref), channel_id=1, source_target_pairs={{0,8},{8,0},{16,24},{24,16},{1,9},{9,1},{17,25},{25,17},{2,10},{10... | collective-permute-start | bytes 2359304 | tf_op jit(solution)/shard_map/ppermute | solution.py:669
  46.7 21.2 %collective-permute-start.11 = (bf16[24,32,256]{2,1,0:T(8,128)(2,1)S(1)}, bf16[24,32,256]{2,1,0:T(8,128)(2,1)S(1)}, u32[]{:S(2)}, u32[]{:S(2)}) collective-permute-start(bf16[24,32,256]{2,1,0:T(8,128)(2,1)S(1)} %get-tuple-element.52), channel_id=1, source_target_pairs={{1,0},{2,1},{3,2},{4,3},{5,4},{6,5},{7,6},{9,8},{10,9},{11,10},{12... | collective-permute-start | bytes 1179656 | tf_op jit(solution)/shard_map/ppermute | solution.py:515
  48.0 21.7 %collective-permute-start.10 = (bf16[24,32,256]{2,1,0:T(8,128)(2,1)S(1)}, bf16[24,32,256]{2,1,0:T(8,128)(2,1)S(1)}, u32[]{:S(2)}, u32[]{:S(2)}) collective-permute-start(bf16[24,32,256]{2,1,0:T(8,128)(2,1)S(1)} %get-tuple-element.53), channel_id=1, source_target_pairs={{0,1},{1,2},{2,3},{3,4},{4,5},{5,6},{6,7},{8,9},{9,10},{10,11},{11... | collective-permute-start | bytes 1179656 | tf_op jit(solution)/shard_map/ppermute | solution.py:514
  67.3 2.5 %copy-start.2 = (f32[32]{0:T(128)S(1)}, f32[32]{0:T(128)}, u32[]{:S(2)}) copy-start(f32[32]{0:T(128)} %param.9) | copy-start | bytes 388
  81.4 15.8 %collective-permute-start.12 = (bf16[32,32,128]{2,1,0:T(8,128)(2,1)S(1)}, bf16[32,32,128]{2,1,0:T(8,128)(2,1)S(1)}, u32[]{:S(2)}, u32[]{:S(2)}) collective-permute-start(bf16[32,32,128]{2,1,0:T(8,128)(2,1)S(1)} %get-tuple-element.46), channel_id=1, source_target_pairs={{0,1},{1,2},{2,3},{3,4},{4,5},{5,6},{6,7},{8,9},{9,10},{10,11},{11... | collective-permute-start | bytes 786440 | tf_op jit(solution)/shard_map/ppermute | solution.py:514
  85.7 11.4 %collective-permute-start.13 = (bf16[32,32,128]{2,1,0:T(8,128)(2,1)S(1)}, bf16[32,32,128]{2,1,0:T(8,128)(2,1)S(1)}, u32[]{:S(2)}, u32[]{:S(2)}) collective-permute-start(bf16[32,32,128]{2,1,0:T(8,128)(2,1)S(1)} %get-tuple-element.47), channel_id=1, source_target_pairs={{1,0},{2,1},{3,2},{4,3},{5,4},{6,5},{7,6},{9,8},{10,9},{11,10},{12... | collective-permute-start | bytes 786440 | tf_op jit(solution)/shard_map/ppermute | solution.py:515
  98.5 2.9 %collective-permute-start.14 = (bf16[16,32,128]{2,1,0:T(8,128)(2,1)S(1)}, bf16[16,32,128]{2,1,0:T(8,128)(2,1)S(1)}, u32[]{:S(2)}, u32[]{:S(2)}) collective-permute-start(bf16[16,32,128]{2,1,0:T(8,128)(2,1)S(1)} %get-tuple-element.48), channel_id=1, source_target_pairs={{0,8},{8,16},{16,24},{1,9},{9,17},{17,25},{2,10},{10,18},{18,26},{... | collective-permute-start | bytes 393224 | tf_op jit(solution)/shard_map/ppermute | solution.py:514
  99.8 4.9 %collective-permute-start.15 = (bf16[16,32,128]{2,1,0:T(8,128)(2,1)S(1)}, bf16[16,32,128]{2,1,0:T(8,128)(2,1)S(1)}, u32[]{:S(2)}, u32[]{:S(2)}) collective-permute-start(bf16[16,32,128]{2,1,0:T(8,128)(2,1)S(1)} %get-tuple-element.49), channel_id=1, source_target_pairs={{8,0},{16,8},{24,16},{9,1},{17,9},{25,17},{10,2},{18,10},{26,18},{... | collective-permute-start | bytes 393224 | tf_op jit(solution)/shard_map/ppermute | solution.py:515
